TPU v7x, 32 devices: a whole 2x2x4 slice. The times are simulated.
32 devices in a mesh: expert: 8 (over y, x, core), tensor: 4 (over z).
Axes of the slice: x: 2, y: 2, z: 4, core: 2. Of those that a mesh axis runs over, the one named last changes fastest.
Arguments:
- layer_in: bfloat16 [4096, 1024], P('expert'), may hold values from -6 to 6
- seq_lengths: int32 [8, 3], P('expert'), may hold values from 1 to 384, 512 in all within a row
- routes: int32 [4096, 2], P('expert'), may hold values from 0 to 7, all different within a row; in each aligned block of 512 rows (0 to 511, 512 to 1023, ...) at most 256 rows name the same one
- gain_attn: float32 [1024], replicated, may hold values from 0.5 to 1.5
- w_qkv: bfloat16 [1024, 8, 256], P(None, 'tensor'), may hold values from -0.25 to 0.25
- w_output: bfloat16 [1024, 1024], P('tensor'), may hold values from -0.5 to 0.5
- gain_ffn: float32 [1024], replicated, may hold values from 0.5 to 1.5
- w_router: bfloat16 [1024, 8], replicated, may hold values from -0.09375 to 0.09375
- w_in: bfloat16 [8, 2, 512, 1024], P('expert', None, 'tensor'), may hold values from -0.1875 to 0.1875
- w_out: bfloat16 [8, 512, 1024], P('expert', 'tensor'), may hold values from -1.5 to 1.5
- out_grad: bfloat16 [4096, 1024], P('expert'), may hold values from -6 to 6
Outputs:
- layer_out: bfloat16 [4096, 1024], P('expert')
- in_grad: bfloat16 [4096, 1024], P('expert')
- gain_attn_grad: float32 [1024], replicated
- w_qkv_grad: float32 [1024, 8, 256], P(None, 'tensor')
- w_output_grad: float32 [1024, 1024], P('tensor')
- gain_ffn_grad: float32 [1024], replicated
- w_router_grad: float32 [1024, 8], replicated
- w_in_grad: float32 [8, 2, 512, 1024], P('expert', None, 'tensor')
- w_out_grad: float32 [8, 512, 1024], P('expert', 'tensor')
Inputs may be any that keep to these rules, and one draw needn't show every extreme that they name: `seq_lengths`: each row lists the sequence lengths of one device group in order; they sum to 512 and the longest of each row is 384. `routes`: each token names 2 different experts; among the tokens of one device group no expert is named by more than 256 tokens, and some expert reaches 256.
All inputs are finite; a program needn't handle non-finite values.
Results may differ from a plain program's by a relative error of at most 0.025.
Values may be sent and summed in bfloat16 or wider, within the bound.
No kernel may reach another device: no remote copies, remote signals or barrier semaphores. Data moves between devices by JAX's collectives and lax.ppermute only.
A program may use at most 192 MiB of HBM per device.

v0:
```python
import math

import jax
import jax.numpy as jnp
from jax import lax
from jax.sharding import PartitionSpec as P

HEADS = 16
KV_HEADS = 8
HEAD_DIM = 64


epsilon = 1e-06
rope_base = 10000.0
masked_out = -1e30


def rms_forward(values, gain_vec):
    inverse = lax.rsqrt(jnp.mean(values * values, axis=-1, keepdims=True) + epsilon)
    return (values * inverse * gain_vec, inverse)


def rms_backward(values, inverse, gain_vec, upstream):
    normal = values * inverse
    scaled = upstream * gain_vec
    gain_part = jnp.sum(upstream * normal, axis=0)
    inner_mean = jnp.mean(scaled * normal, axis=-1, keepdims=True)
    return (inverse * (scaled - normal * inner_mean), gain_part)


def positions(lengths, token_count):
    seq_ends = jnp.cumsum(lengths, dtype=jnp.int32)
    row_index = jnp.arange(token_count, dtype=jnp.int32)
    segment = jnp.sum(
        (row_index[:, None] >= seq_ends[None, :]).astype(jnp.int32), axis=1, dtype=jnp.int32
    )
    seq_ids = jnp.arange(lengths.shape[0], dtype=jnp.int32)
    seq_start = jnp.sum(
        jnp.where(segment[:, None] == seq_ids[None, :], (seq_ends - lengths)[None, :], 0),
        axis=1,
        dtype=jnp.int32,
    )
    return (segment, row_index - seq_start)


def rope_tables(position, head_dim):
    half_dim = head_dim // 2
    inverse_freq = jnp.exp(
        jnp.arange(half_dim, dtype=jnp.float32) * (-2.0 * math.log(rope_base) / head_dim)
    )
    angles = position.astype(jnp.float32)[:, None] * inverse_freq[None, :]
    cosine = jnp.cos(angles)
    sine_tab = jnp.sin(angles)
    return (jnp.concatenate([cosine, cosine], 1), jnp.concatenate([sine_tab, sine_tab], 1))


def rotate(values, cosine, sine_tab):
    half_dim = values.shape[-1] // 2
    turned = jnp.concatenate([-values[..., half_dim:], values[..., :half_dim]], -1)
    return values * cosine + turned * sine_tab


def slot_table(routes_part, experts_all, capacity):
    flat_routes = routes_part.reshape(-1)
    hot_table = (flat_routes[:, None] == jnp.arange(experts_all, dtype=jnp.int32)[None, :]).astype(
        jnp.int32
    )
    earlier = jnp.cumsum(hot_table, axis=0, dtype=jnp.int32) - hot_table
    slot_of = jnp.sum(earlier * hot_table, axis=1, dtype=jnp.int32)
    assign_ids = jnp.arange(flat_routes.shape[0], dtype=jnp.int32)
    return jnp.full((experts_all, capacity), -1, jnp.int32).at[flat_routes, slot_of].set(assign_ids)


def slot_fields(table_part, top_count):
    filled = table_part >= 0
    assign = jnp.where(filled, table_part, 0)
    return (filled, assign, assign // top_count)


def split_blocks(array_in, axis_at, block_count):
    dims_now = array_in.shape
    regrouped = array_in.reshape(
        dims_now[:axis_at]
        + (block_count, dims_now[axis_at] // block_count)
        + dims_now[axis_at + 1 :]
    )
    return jnp.moveaxis(regrouped, axis_at, 0)


def join_blocks(array_in, axis_at):
    regrouped = jnp.moveaxis(array_in, 0, axis_at)
    dims_now = regrouped.shape
    return regrouped.reshape(
        dims_now[:axis_at] + (dims_now[axis_at] * dims_now[axis_at + 1],) + dims_now[axis_at + 2 :]
    )


def block_scores(query_block, key_rows, segment_rows, row_start, segment, scaling):
    block_rows = query_block.shape[2]
    scores_raw = (
        jnp.einsum("kgbd,ksd->kgbs", query_block, key_rows, preferred_element_type=jnp.float32)
        * scaling
    )
    query_index = row_start + jnp.arange(block_rows, dtype=jnp.int32)
    key_index = jnp.arange(key_rows.shape[1], dtype=jnp.int32)
    allowed = (segment_rows[:, None] == segment[None, :]) & (
        key_index[None, :] <= query_index[:, None]
    )
    return jnp.where(allowed[None, None], scores_raw, masked_out)


def attention_forward(queries, key_rows, values, segment, scaling, block_size):
    block_count = queries.shape[2] // block_size
    starts_all = jnp.arange(block_count, dtype=jnp.int32) * block_size

    def one_block(packed):
        query_block, segment_rows, row_start = packed
        scores = block_scores(query_block, key_rows, segment_rows, row_start, segment, scaling)
        top_score = jnp.max(scores, -1)
        exponent = jnp.exp(scores - top_score[..., None])
        row_total = jnp.sum(exponent, -1)
        probs = (exponent / row_total[..., None]).astype(jnp.bfloat16)
        output = jnp.einsum("kgbs,ksd->kgbd", probs, values, preferred_element_type=jnp.float32)
        return (output.astype(jnp.bfloat16), top_score, row_total)

    outputs, top_blocks, total_blocks = lax.map(
        one_block,
        (
            split_blocks(queries, 2, block_count),
            segment.reshape(block_count, block_size),
            starts_all,
        ),
    )
    return (join_blocks(outputs, 2), join_blocks(top_blocks, 2), join_blocks(total_blocks, 2))


def attention_backward(
    queries, key_rows, values, heads_grad, segment, top_kept, total_kept, scaling, block_size
):
    block_count = queries.shape[2] // block_size
    starts_all = jnp.arange(block_count, dtype=jnp.int32) * block_size

    def one_block(running, packed):
        key_acc, value_acc = running
        query_block, grad_block, segment_rows, row_start, top_block, total_block = packed
        scores = block_scores(query_block, key_rows, segment_rows, row_start, segment, scaling)
        probs = jnp.exp(scores - top_block[..., None]) / total_block[..., None]
        probs_low = probs.astype(jnp.bfloat16)
        value_acc = value_acc + jnp.einsum(
            "kgbs,kgbd->ksd", probs_low, grad_block, preferred_element_type=jnp.float32
        )
        prob_grad = jnp.einsum(
            "kgbd,ksd->kgbs", grad_block, values, preferred_element_type=jnp.float32
        )
        inner_sum = jnp.sum(probs * prob_grad, -1, keepdims=True)
        score_grad = (probs * (prob_grad - inner_sum)).astype(jnp.bfloat16)
        query_grad = (
            jnp.einsum("kgbs,ksd->kgbd", score_grad, key_rows, preferred_element_type=jnp.float32)
            * scaling
        )
        key_acc = (
            key_acc
            + jnp.einsum(
                "kgbs,kgbd->ksd", score_grad, query_block, preferred_element_type=jnp.float32
            )
            * scaling
        )
        return ((key_acc, value_acc), query_grad)

    empty = jnp.zeros(key_rows.shape, jnp.float32)
    packed_all = (
        split_blocks(queries, 2, block_count),
        split_blocks(heads_grad, 2, block_count),
        segment.reshape(block_count, block_size),
        starts_all,
        split_blocks(top_kept, 2, block_count),
        split_blocks(total_kept, 2, block_count),
    )
    (key_grad, value_grad), query_blocks = lax.scan(one_block, (empty, empty), packed_all)
    return (join_blocks(query_blocks, 2), key_grad, value_grad)


def on_device(
    layer_in,
    seq_lengths,
    routes,
    gain_attn,
    w_qkv,
    w_output,
    gain_ffn,
    w_router,
    w_in,
    w_out,
    out_grad,
):
    token_count, model_width = layer_in.shape
    kv_here = w_qkv.shape[1]
    group_size = HEADS // KV_HEADS
    scaling = 1.0 / math.sqrt(HEAD_DIM)
    block_size = min(512, token_count)
    segment, position = positions(seq_lengths[0], token_count)
    cosine, sine_tab = rope_tables(position, HEAD_DIM)
    inputs = layer_in.astype(jnp.float32)
    normed_one, inverse_one = rms_forward(inputs, gain_attn)
    normed_one_low = normed_one.astype(jnp.bfloat16)
    qkv_flat = w_qkv.reshape(model_width, -1)
    projected = jnp.dot(normed_one_low, qkv_flat, preferred_element_type=jnp.float32)
    projected = projected.reshape(token_count, kv_here, group_size + 2, HEAD_DIM)
    queries = rotate(
        jnp.transpose(projected[:, :, :group_size], (1, 2, 0, 3)), cosine, sine_tab
    ).astype(jnp.bfloat16)
    key_rows = rotate(
        jnp.transpose(projected[:, :, group_size], (1, 0, 2)), cosine, sine_tab
    ).astype(jnp.bfloat16)
    values = jnp.transpose(projected[:, :, group_size + 1], (1, 0, 2)).astype(jnp.bfloat16)
    attended, top_kept, total_kept = attention_forward(
        queries, key_rows, values, segment, scaling, block_size
    )
    heads_out = jnp.transpose(attended, (2, 0, 1, 3)).reshape(token_count, -1)
    branch_part = jnp.dot(heads_out, w_output, preferred_element_type=jnp.float32)
    branch_here = lax.psum(branch_part, "tensor")
    residual = inputs + branch_here
    normed_two, inverse_two = rms_forward(residual, gain_ffn)
    normed_here_low = normed_two.astype(jnp.bfloat16)
    experts_all = w_router.shape[1]
    top_count = routes.shape[1]
    logits = jnp.dot(normed_here_low, w_router, preferred_element_type=jnp.float32)
    picked = routes[:, :, None] == jnp.arange(experts_all, dtype=jnp.int32)[None, None, :]
    chosen = jnp.sum(jnp.where(picked, logits[:, None, :], 0.0), -1)
    gate_probs = jax.nn.softmax(chosen, axis=-1)
    flat_gates = gate_probs.reshape(-1)
    capacity = 2 * token_count * top_count // experts_all
    slot_span = capacity // lax.axis_size("tensor")
    slot_all = jnp.transpose(slot_table(routes, experts_all, capacity))
    mine_table = lax.dynamic_slice_in_dim(
        slot_all, lax.axis_index("tensor") * slot_span, slot_span, 0
    )
    mine_filled, mine_assign, mine_token = slot_fields(mine_table, top_count)

    def from_experts(buffer):
        return lax.all_to_all(buffer, "expert", split_axis=1, concat_axis=1, tiled=True)

    def to_experts(buffer):
        return lax.all_to_all(buffer, "expert", split_axis=1, concat_axis=1, tiled=True)

    def sum_hidden(left, right):
        return lax.psum_scatter(
            jnp.dot(left, right, preferred_element_type=jnp.float32),
            "tensor",
            scatter_dimension=0,
            tiled=True,
        )

    w_in_here = w_in[0].reshape(-1, model_width)
    w_out_here = w_out[0]
    send_filled, send_assign, send_token = slot_fields(slot_all, top_count)
    send_rows = jnp.where(send_filled[..., None], normed_here_low[send_token], 0.0)
    arrived_rows = to_experts(send_rows).reshape(-1, model_width)
    gate_up = lax.dot_general(
        arrived_rows, w_in_here, (((1,), (1,)), ((), ())), preferred_element_type=jnp.float32
    )
    unit_count = gate_up.shape[1] // 2
    gate_vals = gate_up[:, :unit_count]
    up_vals = gate_up[:, unit_count:]
    active = (jax.nn.silu(gate_vals) * up_vals).astype(jnp.bfloat16)
    expert_out = sum_hidden(active, w_out_here)
    returned = from_experts(
        expert_out.astype(jnp.bfloat16).reshape(slot_span, experts_all, model_width)
    )
    returned_float = returned.astype(jnp.float32)
    mine_gate = jnp.where(mine_filled, flat_gates[mine_assign], 0.0)
    moe_part = jax.ops.segment_sum(
        (returned_float * mine_gate[..., None]).reshape(-1, model_width),
        mine_token.reshape(-1),
        num_segments=token_count,
    )
    mixture = lax.psum(moe_part.astype(jnp.bfloat16), "tensor").astype(jnp.float32)
    layer_here = (residual + mixture).astype(jnp.bfloat16)
    upstream = out_grad.astype(jnp.float32)
    gate_grad_slot = jnp.where(mine_filled, jnp.sum(upstream[mine_token] * returned_float, -1), 0.0)
    gate_grad_part = jax.ops.segment_sum(
        gate_grad_slot.reshape(-1), mine_assign.reshape(-1), num_segments=flat_gates.shape[0]
    )
    send_gate = jnp.where(send_filled, flat_gates[send_assign], 0.0)
    row_grads = (upstream[send_token] * send_gate[..., None]).astype(jnp.bfloat16)
    grad_arrived = to_experts(row_grads).reshape(-1, model_width)
    active_grad = lax.dot_general(
        grad_arrived, w_out_here, (((1,), (1,)), ((), ())), preferred_element_type=jnp.float32
    )
    sig_vals = jax.nn.sigmoid(gate_vals)
    pre_grad = jnp.concatenate(
        [
            active_grad * up_vals * (sig_vals * (1.0 + gate_vals * (1.0 - sig_vals))),
            active_grad * jax.nn.silu(gate_vals),
        ],
        1,
    ).astype(jnp.bfloat16)
    w_in_full = lax.dot_general(
        pre_grad, arrived_rows, (((0,), (0,)), ((), ())), preferred_element_type=jnp.float32
    )
    w_out_full = lax.dot_general(
        active, grad_arrived, (((0,), (0,)), ((), ())), preferred_element_type=jnp.float32
    )
    copy_part = sum_hidden(pre_grad, w_in_here)
    w_in_grad = w_in_full.reshape(w_in.shape)
    w_out_grad = w_out_full.reshape(w_out.shape)
    returned_grad = from_experts(
        copy_part.astype(jnp.bfloat16).reshape(slot_span, experts_all, model_width)
    )
    normed_part = jax.ops.segment_sum(
        returned_grad.astype(jnp.float32).reshape(-1, model_width),
        mine_token.reshape(-1),
        num_segments=token_count,
    )
    gate_grad_rows = gate_grad_part.reshape(token_count, top_count)
    normed_summed, gate_grad = (
        lax.psum(normed_part.astype(jnp.bfloat16), "tensor").astype(jnp.float32),
        lax.psum(gate_grad_rows.astype(jnp.bfloat16), "tensor").astype(jnp.float32),
    )
    chosen_grad = gate_probs * (gate_grad - jnp.sum(gate_probs * gate_grad, -1, keepdims=True))
    logit_grad = jnp.sum(jnp.where(picked, chosen_grad[:, :, None], 0.0), 1).astype(jnp.bfloat16)
    router_grad = lax.dot_general(
        normed_here_low, logit_grad, (((0,), (0,)), ((), ())), preferred_element_type=jnp.float32
    )
    normed_two_grad = normed_summed + lax.dot_general(
        logit_grad, w_router, (((1,), (1,)), ((), ())), preferred_element_type=jnp.float32
    )
    residual_part, gain_ffn_grad = rms_backward(residual, inverse_two, gain_ffn, normed_two_grad)
    residual_grad = upstream + residual_part
    branch_here_grad = residual_grad.astype(jnp.bfloat16)
    w_output_grad = lax.dot_general(
        heads_out, branch_here_grad, (((0,), (0,)), ((), ())), preferred_element_type=jnp.float32
    )
    heads_flat = lax.dot_general(
        branch_here_grad, w_output, (((1,), (1,)), ((), ())), preferred_element_type=jnp.float32
    ).astype(jnp.bfloat16)
    heads_grad = jnp.transpose(
        heads_flat.reshape(token_count, kv_here, group_size, HEAD_DIM), (1, 2, 0, 3)
    )
    query_grad, key_grad, value_grad = attention_backward(
        queries, key_rows, values, heads_grad, segment, top_kept, total_kept, scaling, block_size
    )
    query_grad = rotate(query_grad, cosine, -sine_tab)
    key_grad = rotate(key_grad, cosine, -sine_tab)
    projected_grad = jnp.concatenate(
        [
            jnp.transpose(query_grad, (2, 0, 1, 3)),
            jnp.transpose(key_grad, (1, 0, 2))[:, :, None],
            jnp.transpose(value_grad, (1, 0, 2))[:, :, None],
        ],
        2,
    )
    projected_grad = projected_grad.reshape(token_count, -1).astype(jnp.bfloat16)
    w_qkv_grad = lax.dot_general(
        normed_one_low, projected_grad, (((0,), (0,)), ((), ())), preferred_element_type=jnp.float32
    ).reshape(w_qkv.shape)
    normed_one_part = lax.dot_general(
        projected_grad, qkv_flat, (((1,), (1,)), ((), ())), preferred_element_type=jnp.float32
    )
    normed_one_grad = lax.psum(normed_one_part.astype(jnp.bfloat16), "tensor").astype(jnp.float32)
    input_part, gain_attn_grad = rms_backward(inputs, inverse_one, gain_attn, normed_one_grad)
    in_here = (residual_grad + input_part).astype(jnp.bfloat16)
    qkv_summed, output_summed, router_summed, gain_attn_summed, gain_ffn_summed = (
        lax.psum(w_qkv_grad.astype(jnp.bfloat16), "expert").astype(jnp.float32),
        lax.psum(w_output_grad.astype(jnp.bfloat16), "expert").astype(jnp.float32),
        lax.psum(router_grad.astype(jnp.bfloat16), "expert").astype(jnp.float32),
        lax.psum(gain_attn_grad.astype(jnp.bfloat16), "expert").astype(jnp.float32),
        lax.psum(gain_ffn_grad.astype(jnp.bfloat16), "expert").astype(jnp.float32),
    )
    return (
        layer_here,
        in_here,
        gain_attn_summed,
        qkv_summed,
        output_summed,
        gain_ffn_summed,
        router_summed,
        w_in_grad,
        w_out_grad,
    )


def solution(mesh):
    placed = (
        P("expert", None),
        P("expert", None),
        P("expert", None),
        P(),
        P(None, "tensor", None),
        P("tensor", None),
        P(),
        P(),
        P("expert", None, "tensor", None),
        P("expert", "tensor", None),
        P("expert", None),
    )
    return jax.shard_map(
        on_device,
        mesh=mesh,
        in_specs=placed,
        out_specs=(
            P("expert", None),
            P("expert", None),
            P(),
            P(None, "tensor", None),
            P("tensor", None),
            P(),
            P(),
            P("expert", None, "tensor", None),
            P("expert", "tensor", None),
        ),
        check_vma=False,
    )
```

profile of v0, /device:TPU:0, one launch (start us, length us, event | category | flops | bytes accessed | tf_op | source)
XLA Modules:
  0.0 895.5 jit_solution(17515474595715483053)
XLA Ops:
  11.7 2.0 fusion.43
  17.5 3.6 fusion.98
  21.0 2.7 convolution_convert_fusion.3
  23.8 1.8 fusion.99
  26.4 2.3 reduce-window.11
  29.5 4.3 scatter_custom_fusion.3
  34.7 80.3 %all-reduce.8.cloned.1.call-done = f32[512,1024]{1,0:T(8,128)} async-done(((f32[512,1024]{1,0:T(8,128)}), f32[512,1024]{1,0:T(8,128)}) %all-reduce.8.cloned.1.call-update) | async-done | bytes 2097168 | tf_op jit(solution)/shard_map/psum | solution.py:221
  115.0 1.9 multiply_reduce_fusion.3
  118.5 9.7 %gather_fusion = bf16[2048,1024]{1,0:T(8,128)(2,1)} fusion(bf16[512,1024]{1,0:T(8,128)(2,1)S(1)} %multiply_convert_fusion.1, s32[2048]{0:T(1024)S(1)} %broadcast_clamp_fusion.1), kind=kCustom, calls=%fused_computation | custom fusion | bytes 8396800 | tf_op jit(solution)/shard_map/gather | solution.py:257
  128.2 8.6 copy_select_fusion
  136.8 52.7 %all_to_all.20 = bf16[256,8,1024]{2,0,1:T(8,128)(2,1)S(1)} all-to-all(bf16[256,8,1024]{2,0,1:T(8,128)(2,1)S(1)} %copy_select_fusion), channel_id=1, replica_groups=mesh['expert'=8,'tensor'=4] {'expert'}, dimensions={1} | all-to-all | bytes 8388608 | tf_op jit(solution)/shard_map/all_to_all | solution.py:244
  189.5 2.9 fusion.8
  193.8 4.5 fusion.67
  198.5 141.6 %reduce-scatter.3.cloned.1.call-done = f32[512,1024]{1,0:T(8,128)} async-done(((f32[2048,1024]{1,0:T(8,128)}), f32[512,1024]{1,0:T(8,128)}) %reduce-scatter.3.cloned.1.call-update) | async-done | bytes 2097168 | tf_op jit(solution)/shard_map/reduce_scatter | solution.py:247
  340.1 1.7 convert_bitcast_fusion.1
  343.4 4.2 all-to-all-start.1
  349.9 9.8 %gather_fusion.2 = f32[2048,1024]{1,0:T(8,128)} fusion(f32[512,1024]{1,0:T(8,128)S(1)} %convert_element_type.184, s32[2048]{0:T(1024)S(1)} %broadcast_clamp_fusion.1), kind=kCustom, calls=%fused_computation.2 | custom fusion | bytes 16785408 | tf_op jit(solution)/shard_map/gather | solution.py:285
  359.6 2.6 gather_fusion.4
  365.8 3.1 fusion.23
  369.1 4.1 scatter_custom_fusion.2
  373.6 11.6 %psum.73 = bf16[512,2]{0,1:T(2,128)(2,1)S(1)} all-reduce(bf16[512,2]{0,1:T(2,128)(2,1)S(1)} %copy.127), channel_id=1, replica_groups=mesh['expert'=8,'tensor'=4] {'tensor'}, use_global_device_ids=true, to_apply=%region_23.24 | all-reduce | flops 1024 | bytes 4096 | tf_op jit(solution)/shard_map/psum | solution.py:318
  386.1 8.6 gather_fusion.3
  394.8 9.3 %fusion.1 = bf16[256,8,1024]{2,0,1:T(8,128)(2,1)S(1)} fusion(f32[256,8,1024]{2,1,0:T(8,128)} %bitcast.193, f32[256,8]{0,1:T(8,128)S(1)} %broadcast_select_fusion.2), kind=kLoop, calls=%fused_computation.11 | loop fusion | flops 4194304 | bytes 12591104 | tf_op jit(solution)/shard_map/convert_element_type | solution.py:285
  404.2 53.0 %all_to_all.21 = bf16[256,8,1024]{2,0,1:T(8,128)(2,1)S(1)} all-to-all(bf16[256,8,1024]{2,0,1:T(8,128)(2,1)S(1)} %fusion.1), channel_id=1, replica_groups=mesh['expert'=8,'tensor'=4] {'expert'}, dimensions={1} | all-to-all | bytes 8388608 | tf_op jit(solution)/shard_map/all_to_all | solution.py:244
  457.2 3.0 multiply_convert_fusion.3
  461.2 4.5 fusion.96
  465.8 141.0 %reduce-scatter.5.cloned.1.call-done = f32[512,1024]{1,0:T(8,128)} async-done(((f32[2048,1024]{1,0:T(8,128)}), f32[512,1024]{1,0:T(8,128)}) %reduce-scatter.5.cloned.1.call-update) | async-done | bytes 2097168 | tf_op jit(solution)/shard_map/reduce_scatter | solution.py:247
  606.7 1.7 convert_bitcast_fusion
  610.0 4.3 all-to-all-start.3
  614.6 15.1 %all-to-all-done.3 = bf16[64,8,1024]{2,0,1:T(8,128)(2,1)} async-done(((bf16[64,8,1024]{2,0,1:T(8,128)(2,1)}), bf16[64,8,1024]{2,0,1:T(8,128)(2,1)}, u32[]{:S(2)}, u32[]{:S(2)}) %all-to-all-start.3) | async-done | bytes 1048608 | tf_op jit(solution)/shard_map/all_to_all | solution.py:241
  631.2 7.3 scatter_custom_fusion.1
  638.5 2.7 convert_element_type.187
  641.6 2.3 gather_fusion.1
  646.0 46.1 %all-reduce.10.cloned.1.call-done = bf16[512,1024]{1,0:T(8,128)(2,1)} async-done(((bf16[512,1024]{1,0:T(8,128)(2,1)}), bf16[512,1024]{1,0:T(8,128)(2,1)}) %all-reduce.10.cloned.1.call-update) | async-done | bytes 1048592 | tf_op jit(solution)/shard_map/psum | solution.py:317
  692.1 2.8 multiply_reduce_fusion.1
  699.1 1.7 multiply_reduce_fusion
  705.4 1.9 convolution_convert_fusion
  709.1 7.7 scatter_custom_fusion
  716.8 2.9 convert_element_type.181
  719.7 1.8 convolution_convert_fusion.1
  722.8 5.8 fusion.40
  728.6 3.8 fusion.37
  732.4 33.5 %all-reduce.12.cloned.1.call-done = (bf16[1024,2,256]{2,0,1:T(8,128)(2,1)}, bf16[256,1024]{1,0:T(8,128)(2,1)}) async-done(((bf16[1024,2,256]{2,0,1:T(8,128)(2,1)}, bf16[256,1024]{1,0:T(8,128)(2,1)}), (bf16[1024,2,256]{2,0,1:T(8,128)(2,1)}, bf16[256,1024]{1,0:T(8,128)(2,1)})) %all-reduce.12.cloned.1.call-update) | async-done | bytes 1572880 | tf_op jit(solution)/shard_map/psum | solution.py:364
  765.9 3.7 copy.132
  770.7 84.6 %all-reduce.14.cloned.1.call-done = (bf16[512,1024]{1,0:T(8,128)(2,1)}, bf16[512,1024]{1,0:T(8,128)(2,1)}) async-done(((bf16[512,1024]{1,0:T(8,128)(2,1)}, bf16[512,1024]{1,0:T(8,128)(2,1)}), (bf16[512,1024]{1,0:T(8,128)(2,1)}, bf16[512,1024]{1,0:T(8,128)(2,1)})) %all-reduce.14.cloned.1.call-update) | async-done | bytes 2097168 | tf_op jit(solution)/shard_map/psum | solution.py:277
  855.3 2.4 fusion.26
  857.6 24.1 %all-reduce = (bf16[1024]{0:T(1024)(128)(2,1)S(1)}, bf16[1024]{0:T(1024)(128)(2,1)S(1)}, bf16[1024,8]{0,1:T(8,128)(2,1)S(1)}) all-reduce(bf16[1024]{0:T(1024)(128)(2,1)S(1)} %get-tuple-element.119, bf16[1024]{0:T(1024)(128)(2,1)S(1)} %copy-done.58, ...), channel_id=1, replica_groups=mesh['expert'=8,'tensor'=4] {'expert'}, use_global_device_ids=true, to_apply=%region_31.32 | all-reduce | flops 10240 | bytes 40960 | tf_op jit(solution)/shard_map/psum | solution.py:367
  883.5 3.3 fusion.22
  (240 shorter events, 45.1 us)
Async XLA Ops:
  7.2 182.3 %copy-start = (bf16[1,2,128,1024]{3,2,1,0:T(8,128)(2,1)S(1)}, bf16[1,2,128,1024]{3,2,1,0:T(8,128)(2,1)}, u32[]{:S(2)}) copy-start(bf16[1,2,128,1024]{3,2,1,0:T(8,128)(2,1)} %param.19) | copy-start | bytes 1572868
  7.2 107.8 %all-reduce.8.cloned.1.call-start = ((), (), s32[]{:S(2)}) async-start(), calls=%async_computation.6 | async-start | bytes 4194304 | tf_op jit(solution)/shard_map/psum | solution.py:221
  8.8 2.9 copy-start.51
  8.8 2.9 copy-start.8
  8.8 2.9 copy-start.54
  10.4 3.4 copy-start.15
  11.7 3.1 copy-start.62
  14.8 2.4 copy-start.18
  21.0 2.7 copy-start.56
  21.0 2.8 copy-start.25
  25.6 3.6 copy-start.61
  25.6 3.7 copy-start.60
  25.7 314.4 %reduce-scatter.3.cloned.1.call-start = ((), (), s32[]{:S(2)}) async-start(), calls=%async_computation.7 | async-start | bytes 10485760 | tf_op jit(solution)/shard_map/reduce_scatter | solution.py:247
  34.4 93.8 %copy-start.47 = (pred[256,8]{0,1:T(8,128)(4,1)}, pred[256,8]{0,1:T(8,128)(4,1)S(1)}, u32[]{:S(2)}) copy-start(pred[256,8]{0,1:T(8,128)(4,1)S(1)} %get-tuple-element.133) | copy-start | bytes 6148
  34.7 83.6 %copy-start.44 = (f32[1024]{0:T(1024)S(1)}, f32[1024]{0:T(1024)}, u32[]{:S(2)}) copy-start(f32[1024]{0:T(1024)} %param.17) | copy-start | bytes 12292
  117.0 11.2 %copy-start.49 = (f32[512]{0:T(512)}, f32[512]{0:T(512)S(1)}, u32[]{:S(2)}) copy-start(f32[512]{0:T(512)S(1)} %add_rsqrt_fusion) | copy-start | bytes 6148
  118.5 9.7 %copy-start.1 = (bf16[512,1024]{1,0:T(8,128)(2,1)}, bf16[512,1024]{1,0:T(8,128)(2,1)S(1)}, u32[]{:S(2)}) copy-start(bf16[512,1024]{1,0:T(8,128)(2,1)S(1)} %multiply_convert_fusion.1) | copy-start | bytes 3145732
  189.5 2.9 copy-start.11
  198.5 149.2 %copy-start.33 = (s32[8,64]{0,1:T(8,128)}, s32[8,64]{0,1:T(8,128)S(1)}, u32[]{:S(2)}) copy-start(s32[8,64]{0,1:T(8,128)S(1)} %copy.145) | copy-start | bytes 6148
  343.4 22.4 %all-to-all-start.1 = ((bf16[64,8,1024]{2,0,1:T(8,128)(2,1)}), bf16[64,8,1024]{2,0,1:T(8,128)(2,1)}, u32[]{:S(2)}, u32[]{:S(2)}) async-start(bf16[64,8,1024]{2,0,1:T(8,128)(2,1)} %copy.115), calls=%async_computation.2 | async-start | bytes 2097152 | tf_op jit(solution)/shard_map/all_to_all | solution.py:241
  347.6 259.1 %reduce-scatter.5.cloned.1.call-start = ((), (), s32[]{:S(2)}) async-start(), calls=%async_computation.8 | async-start | bytes 10485760 | tf_op jit(solution)/shard_map/reduce_scatter | solution.py:247
  364.1 4.9 copy-start.34
  386.1 8.8 copy-start.48
  404.2 53.1 %copy-start.20 = (f32[2048,256]{0,1:T(8,128)S(1)}, f32[2048,256]{0,1:T(8,128)}, u32[]{:S(2)}) copy-start(f32[2048,256]{0,1:T(8,128)} %copy-done.19) | copy-start | bytes 6291460
  404.2 53.1 %copy-start.39 = (bf16[1,128,1024]{2,1,0:T(8,128)(2,1)S(1)}, bf16[1,128,1024]{2,1,0:T(8,128)(2,1)}, u32[]{:S(2)}) copy-start(bf16[1,128,1024]{2,1,0:T(8,128)(2,1)} %param.20) | copy-start | bytes 786436
  457.2 3.0 copy-start.13
  608.5 6.0 copy-start.42
  610.0 19.7 %all-to-all-start.3 = ((bf16[64,8,1024]{2,0,1:T(8,128)(2,1)}), bf16[64,8,1024]{2,0,1:T(8,128)(2,1)}, u32[]{:S(2)}, u32[]{:S(2)}) async-start(bf16[64,8,1024]{2,0,1:T(8,128)(2,1)} %copy.123), calls=%async_computation.5 | async-start | bytes 2097152 | tf_op jit(solution)/shard_map/all_to_all | solution.py:241
  614.3 77.8 %all-reduce.10.cloned.1.call-start = ((), (), s32[]{:S(2)}) async-start(), calls=%async_computation.9 | async-start | bytes 2097152 | tf_op jit(solution)/shard_map/psum | solution.py:317
  614.6 23.8 %copy-start.59 = (s32[512]{0:T(512)}, s32[512]{0:T(512)S(1)}, u32[]{:S(2)}) copy-start(s32[512]{0:T(512)S(1)} %reshape.399) | copy-start | bytes 6148
  638.5 3.0 copy-start.41
  641.2 124.7 %all-reduce.12.cloned.1.call-start = ((), (), s32[]{:S(2)}) async-start(), calls=%async_computation.10 | async-start | bytes 3145728 | tf_op jit(solution)/shard_map/psum | solution.py:364
  641.6 50.5 %copy-start.4 = (f32[512,1024]{1,0:T(8,128)S(1)}, f32[512,1024]{1,0:T(8,128)}, u32[]{:S(2)}) copy-start(f32[512,1024]{1,0:T(8,128)} %copy-done.3) | copy-start | bytes 6291460
  646.0 49.0 %copy-start.45 = (f32[1024]{0:T(1024)S(1)}, f32[1024]{0:T(1024)}, u32[]{:S(2)}) copy-start(f32[1024]{0:T(1024)} %param.17) | copy-start | bytes 12292
  646.0 49.0 %copy-start.50 = (f32[512]{0:T(512)S(1)}, f32[512]{0:T(512)}, u32[]{:S(2)}) copy-start(f32[512]{0:T(512)} %copy-done.49) | copy-start | bytes 6148
  692.1 2.8 copy-start.14
  695.9 3.2 copy-start.10
  704.5 2.8 copy-start.36
  705.4 2.3 copy-start.43
  707.3 148.0 %all-reduce.14.cloned.1.call-start = ((), (), s32[]{:S(2)}) async-start(), calls=%async_computation.11 | async-start | bytes 4194304 | tf_op jit(solution)/shard_map/psum | solution.py:277
  716.8 2.9 copy-start.16
  716.8 2.9 copy-start.37
  722.8 5.8 copy-start.12
  765.9 3.7 copy-start.32
  769.6 88.1 %copy-start.58 = (bf16[1024]{0:T(1024)(128)(2,1)S(1)}, bf16[1024]{0:T(1024)(128)(2,1)}, u32[]{:S(2)}) copy-start(bf16[1024]{0:T(1024)(128)(2,1)} %get-tuple-element.117) | copy-start | bytes 6148
  769.6 114.0 %copy-start.7 = (f32[512,1024]{1,0:T(8,128)S(1)}, f32[512,1024]{1,0:T(8,128)}, u32[]{:S(2)}) copy-start(f32[512,1024]{1,0:T(8,128)} %copy-done.6) | copy-start | bytes 6291460
  883.5 3.3 copy-start.5
  883.5 3.3 copy-start.29
  (23 other events, 31.3 us)
Sparse Core Ops, SparseCore 0:
  25.8 89.2 all-reduce.7
  198.4 141.5 reduce-scatter.2
  465.9 140.7 reduce-scatter.4
  641.3 50.7 all-reduce.9
  707.4 58.4 all-reduce.11
  768.9 86.3 all-reduce.13
where the time goes:
time: 905 us; the launch traced here: 896 us
  waiting for transfers between devices  542 us (60%)
  blocking collectives  141 us (16%)
  other arithmetic  78.2 us (9%)
  local copies, waits for them, and re-layouts  60.2 us (7%)
  matrix products  48.3 us (5%)
  between operations  15.6 us (2%)
  starting transfers between devices  9.38 us (1%)
    reduce_scatter x2, waiting for transfers between devices, sum_hidden(): lax.psum_scatter(jnp.dot(left, right, preferred_element_type=jnp.float32)...  283 us
    all_to_all x2, blocking collectives, to_experts(): lax.all_to_all(buffer, 'expert', split_axis=1, concat_axis=1, tiled=True)  106 us
    psum x1, waiting for transfers between devices, on_device(): lax.psum(moe_part.astype(jnp.bfloat16), 'tensor').astype(jnp.float32)  84.6 us
    psum x1, waiting for transfers between devices, on_device(): branch_here = lax.psum(branch_part, 'tensor')  80.3 us
    psum x1, waiting for transfers between devices, on_device(): lax.psum(normed_part.astype(jnp.bfloat16), 'tensor').astype(jnp.float32)  46.1 us
    psum x1, waiting for transfers between devices, on_device(): lax.psum(w_qkv_grad.astype(jnp.bfloat16), 'expert').astype(jnp.float32)  33.5 us
    psum x1, blocking collectives, on_device(): lax.psum(gain_attn_grad.astype(jnp.bfloat16), 'expert').astype(jnp.float32)  24.1 us
  transfers between devices with their start and end apart: 8, of which 7 were waited for; matrix products, arithmetic and copies ran while one was open for 7% of the time, Pallas kernels for 0%

commit v1 on v0

--- a/solution.py
+++ b/solution.py
@@ -23,9 +23,8 @@
 def rms_backward(values, inverse, gain_vec, upstream):
     normal = values * inverse
     scaled = upstream * gain_vec
-    gain_part = jnp.sum(upstream * normal, axis=0)
     inner_mean = jnp.mean(scaled * normal, axis=-1, keepdims=True)
-    return (inverse * (scaled - normal * inner_mean), gain_part)
+    return inverse * (scaled - normal * inner_mean)
 
 
 def positions(lengths, token_count):
@@ -58,23 +57,6 @@
     half_dim = values.shape[-1] // 2
     turned = jnp.concatenate([-values[..., half_dim:], values[..., :half_dim]], -1)
     return values * cosine + turned * sine_tab
-
-
-def slot_table(routes_part, experts_all, capacity):
-    flat_routes = routes_part.reshape(-1)
-    hot_table = (flat_routes[:, None] == jnp.arange(experts_all, dtype=jnp.int32)[None, :]).astype(
-        jnp.int32
-    )
-    earlier = jnp.cumsum(hot_table, axis=0, dtype=jnp.int32) - hot_table
-    slot_of = jnp.sum(earlier * hot_table, axis=1, dtype=jnp.int32)
-    assign_ids = jnp.arange(flat_routes.shape[0], dtype=jnp.int32)
-    return jnp.full((experts_all, capacity), -1, jnp.int32).at[flat_routes, slot_of].set(assign_ids)
-
-
-def slot_fields(table_part, top_count):
-    filled = table_part >= 0
-    assign = jnp.where(filled, table_part, 0)
-    return (filled, assign, assign // top_count)
 
 
 def split_blocks(array_in, axis_at, block_count):
@@ -198,6 +180,10 @@
     group_size = HEADS // KV_HEADS
     scaling = 1.0 / math.sqrt(HEAD_DIM)
     block_size = min(512, token_count)
+    w_output_all = lax.all_gather(w_output, "tensor", axis=0, tiled=True)
+    w_gate_all = lax.all_gather(w_in[0, 0], "expert", axis=0, tiled=True)
+    w_up_all = lax.all_gather(w_in[0, 1], "expert", axis=0, tiled=True)
+    w_out_all = lax.all_gather(w_out[0], "expert", axis=0, tiled=True)
     segment, position = positions(seq_lengths[0], token_count)
     cosine, sine_tab = rope_tables(position, HEAD_DIM)
     inputs = layer_in.astype(jnp.float32)
@@ -217,115 +203,80 @@
         queries, key_rows, values, segment, scaling, block_size
     )
     heads_out = jnp.transpose(attended, (2, 0, 1, 3)).reshape(token_count, -1)
-    branch_part = jnp.dot(heads_out, w_output, preferred_element_type=jnp.float32)
-    branch_here = lax.psum(branch_part, "tensor")
+    heads_all = lax.all_gather(heads_out, "tensor", axis=1, tiled=True)
+    branch_here = jnp.dot(heads_all, w_output_all, preferred_element_type=jnp.float32)
     residual = inputs + branch_here
     normed_two, inverse_two = rms_forward(residual, gain_ffn)
-    normed_here_low = normed_two.astype(jnp.bfloat16)
+    normed_low = normed_two.astype(jnp.bfloat16)
     experts_all = w_router.shape[1]
-    top_count = routes.shape[1]
-    logits = jnp.dot(normed_here_low, w_router, preferred_element_type=jnp.float32)
-    picked = routes[:, :, None] == jnp.arange(experts_all, dtype=jnp.int32)[None, None, :]
-    chosen = jnp.sum(jnp.where(picked, logits[:, None, :], 0.0), -1)
-    gate_probs = jax.nn.softmax(chosen, axis=-1)
-    flat_gates = gate_probs.reshape(-1)
-    capacity = 2 * token_count * top_count // experts_all
-    slot_span = capacity // lax.axis_size("tensor")
-    slot_all = jnp.transpose(slot_table(routes, experts_all, capacity))
-    mine_table = lax.dynamic_slice_in_dim(
-        slot_all, lax.axis_index("tensor") * slot_span, slot_span, 0
-    )
-    mine_filled, mine_assign, mine_token = slot_fields(mine_table, top_count)
-
-    def from_experts(buffer):
-        return lax.all_to_all(buffer, "expert", split_axis=1, concat_axis=1, tiled=True)
-
-    def to_experts(buffer):
-        return lax.all_to_all(buffer, "expert", split_axis=1, concat_axis=1, tiled=True)
-
-    def sum_hidden(left, right):
+    unit_count = w_out.shape[1]
+    logits = jnp.dot(normed_low, w_router, preferred_element_type=jnp.float32)
+    expert_ids = jnp.arange(experts_all, dtype=jnp.int32)
+    picked = jnp.any(routes[:, :, None] == expert_ids[None, None, :], axis=1)
+    picked_logits = jnp.where(picked, logits, masked_out)
+    top_logit = jnp.max(picked_logits, -1, keepdims=True)
+    weight = jnp.where(picked, jnp.exp(picked_logits - top_logit), 0.0)
+    gates = weight / jnp.sum(weight, -1, keepdims=True)
+
+    def by_unit(per_expert):
+        return jnp.broadcast_to(
+            per_expert[:, :, None], (token_count, experts_all, unit_count)
+        ).reshape(token_count, -1)
+
+    def over_units(per_unit):
+        return jnp.sum(per_unit.reshape(token_count, experts_all, unit_count), -1)
+
+    def times_transposed(left, right):
+        return lax.dot_general(
+            left, right, (((1,), (1,)), ((), ())), preferred_element_type=jnp.float32
+        )
+
+    def transposed_times(left, right):
+        return lax.dot_general(
+            left, right, (((0,), (0,)), ((), ())), preferred_element_type=jnp.float32
+        )
+
+    gates_wide = by_unit(gates)
+    gate_vals = times_transposed(normed_low, w_gate_all)
+    up_vals = times_transposed(normed_low, w_up_all)
+    plain_grad = times_transposed(out_grad, w_out_all)
+    sig_vals = jax.nn.sigmoid(gate_vals)
+    silu_vals = gate_vals * sig_vals
+    active = silu_vals * up_vals
+    scaled_active = (active * gates_wide).astype(jnp.bfloat16)
+    active_grad = plain_grad * gates_wide
+    gate_pre = (
+        active_grad * up_vals * (sig_vals * (1.0 + gate_vals * (1.0 - sig_vals)))
+    ).astype(jnp.bfloat16)
+    up_pre = (active_grad * silu_vals).astype(jnp.bfloat16)
+    gate_grad_part = over_units(active * plain_grad)
+    logit_part = (
+        gates * (gate_grad_part - jnp.sum(gates * gate_grad_part, -1, keepdims=True))
+    ).astype(jnp.bfloat16)
+    normed_two_part = (
+        jnp.dot(gate_pre, w_gate_all, preferred_element_type=jnp.float32)
+        + jnp.dot(up_pre, w_up_all, preferred_element_type=jnp.float32)
+        + times_transposed(logit_part, w_router)
+    )
+    normed_two_grad = lax.psum(normed_two_part.astype(jnp.bfloat16), "tensor").astype(jnp.float32)
+    mixture_part = jnp.dot(scaled_active, w_out_all, preferred_element_type=jnp.float32)
+    mixture = lax.psum(mixture_part.astype(jnp.bfloat16), "tensor").astype(jnp.float32)
+    layer_here = (residual + mixture).astype(jnp.bfloat16)
+
+    def to_owner(partial):
         return lax.psum_scatter(
-            jnp.dot(left, right, preferred_element_type=jnp.float32),
-            "tensor",
-            scatter_dimension=0,
-            tiled=True,
-        )
-
-    w_in_here = w_in[0].reshape(-1, model_width)
-    w_out_here = w_out[0]
-    send_filled, send_assign, send_token = slot_fields(slot_all, top_count)
-    send_rows = jnp.where(send_filled[..., None], normed_here_low[send_token], 0.0)
-    arrived_rows = to_experts(send_rows).reshape(-1, model_width)
-    gate_up = lax.dot_general(
-        arrived_rows, w_in_here, (((1,), (1,)), ((), ())), preferred_element_type=jnp.float32
-    )
-    unit_count = gate_up.shape[1] // 2
-    gate_vals = gate_up[:, :unit_count]
-    up_vals = gate_up[:, unit_count:]
-    active = (jax.nn.silu(gate_vals) * up_vals).astype(jnp.bfloat16)
-    expert_out = sum_hidden(active, w_out_here)
-    returned = from_experts(
-        expert_out.astype(jnp.bfloat16).reshape(slot_span, experts_all, model_width)
-    )
-    returned_float = returned.astype(jnp.float32)
-    mine_gate = jnp.where(mine_filled, flat_gates[mine_assign], 0.0)
-    moe_part = jax.ops.segment_sum(
-        (returned_float * mine_gate[..., None]).reshape(-1, model_width),
-        mine_token.reshape(-1),
-        num_segments=token_count,
-    )
-    mixture = lax.psum(moe_part.astype(jnp.bfloat16), "tensor").astype(jnp.float32)
-    layer_here = (residual + mixture).astype(jnp.bfloat16)
+            partial.astype(jnp.bfloat16), "expert", scatter_dimension=0, tiled=True
+        ).astype(jnp.float32)
+
+    w_gate_grad = to_owner(transposed_times(gate_pre, normed_low))
+    w_up_grad = to_owner(transposed_times(up_pre, normed_low))
+    w_in_grad = jnp.stack([w_gate_grad, w_up_grad])[None]
+    w_out_grad = to_owner(transposed_times(scaled_active, out_grad))[None]
+    router_part = transposed_times(logit_part, normed_low)
+    normal_two = residual * inverse_two
+    gain_ffn_part = jnp.sum(normed_two_part * normal_two, axis=0)
     upstream = out_grad.astype(jnp.float32)
-    gate_grad_slot = jnp.where(mine_filled, jnp.sum(upstream[mine_token] * returned_float, -1), 0.0)
-    gate_grad_part = jax.ops.segment_sum(
-        gate_grad_slot.reshape(-1), mine_assign.reshape(-1), num_segments=flat_gates.shape[0]
-    )
-    send_gate = jnp.where(send_filled, flat_gates[send_assign], 0.0)
-    row_grads = (upstream[send_token] * send_gate[..., None]).astype(jnp.bfloat16)
-    grad_arrived = to_experts(row_grads).reshape(-1, model_width)
-    active_grad = lax.dot_general(
-        grad_arrived, w_out_here, (((1,), (1,)), ((), ())), preferred_element_type=jnp.float32
-    )
-    sig_vals = jax.nn.sigmoid(gate_vals)
-    pre_grad = jnp.concatenate(
-        [
-            active_grad * up_vals * (sig_vals * (1.0 + gate_vals * (1.0 - sig_vals))),
-            active_grad * jax.nn.silu(gate_vals),
-        ],
-        1,
-    ).astype(jnp.bfloat16)
-    w_in_full = lax.dot_general(
-        pre_grad, arrived_rows, (((0,), (0,)), ((), ())), preferred_element_type=jnp.float32
-    )
-    w_out_full = lax.dot_general(
-        active, grad_arrived, (((0,), (0,)), ((), ())), preferred_element_type=jnp.float32
-    )
-    copy_part = sum_hidden(pre_grad, w_in_here)
-    w_in_grad = w_in_full.reshape(w_in.shape)
-    w_out_grad = w_out_full.reshape(w_out.shape)
-    returned_grad = from_experts(
-        copy_part.astype(jnp.bfloat16).reshape(slot_span, experts_all, model_width)
-    )
-    normed_part = jax.ops.segment_sum(
-        returned_grad.astype(jnp.float32).reshape(-1, model_width),
-        mine_token.reshape(-1),
-        num_segments=token_count,
-    )
-    gate_grad_rows = gate_grad_part.reshape(token_count, top_count)
-    normed_summed, gate_grad = (
-        lax.psum(normed_part.astype(jnp.bfloat16), "tensor").astype(jnp.float32),
-        lax.psum(gate_grad_rows.astype(jnp.bfloat16), "tensor").astype(jnp.float32),
-    )
-    chosen_grad = gate_probs * (gate_grad - jnp.sum(gate_probs * gate_grad, -1, keepdims=True))
-    logit_grad = jnp.sum(jnp.where(picked, chosen_grad[:, :, None], 0.0), 1).astype(jnp.bfloat16)
-    router_grad = lax.dot_general(
-        normed_here_low, logit_grad, (((0,), (0,)), ((), ())), preferred_element_type=jnp.float32
-    )
-    normed_two_grad = normed_summed + lax.dot_general(
-        logit_grad, w_router, (((1,), (1,)), ((), ())), preferred_element_type=jnp.float32
-    )
-    residual_part, gain_ffn_grad = rms_backward(residual, inverse_two, gain_ffn, normed_two_grad)
+    residual_part = rms_backward(residual, inverse_two, gain_ffn, normed_two_grad)
     residual_grad = upstream + residual_part
     branch_here_grad = residual_grad.astype(jnp.bfloat16)
     w_output_grad = lax.dot_general(
@@ -357,24 +308,22 @@
     normed_one_part = lax.dot_general(
         projected_grad, qkv_flat, (((1,), (1,)), ((), ())), preferred_element_type=jnp.float32
     )
+    gain_attn_part = jnp.sum(normed_one_part * (inputs * inverse_one), axis=0)
     normed_one_grad = lax.psum(normed_one_part.astype(jnp.bfloat16), "tensor").astype(jnp.float32)
-    input_part, gain_attn_grad = rms_backward(inputs, inverse_one, gain_attn, normed_one_grad)
+    input_part = rms_backward(inputs, inverse_one, gain_attn, normed_one_grad)
     in_here = (residual_grad + input_part).astype(jnp.bfloat16)
-    qkv_summed, output_summed, router_summed, gain_attn_summed, gain_ffn_summed = (
-        lax.psum(w_qkv_grad.astype(jnp.bfloat16), "expert").astype(jnp.float32),
-        lax.psum(w_output_grad.astype(jnp.bfloat16), "expert").astype(jnp.float32),
-        lax.psum(router_grad.astype(jnp.bfloat16), "expert").astype(jnp.float32),
-        lax.psum(gain_attn_grad.astype(jnp.bfloat16), "expert").astype(jnp.float32),
-        lax.psum(gain_ffn_grad.astype(jnp.bfloat16), "expert").astype(jnp.float32),
-    )
+    qkv_summed = lax.psum(w_qkv_grad.astype(jnp.bfloat16), "expert").astype(jnp.float32)
+    output_summed = lax.psum(w_output_grad.astype(jnp.bfloat16), "expert").astype(jnp.float32)
+    small = jnp.concatenate([router_part, gain_ffn_part[None], gain_attn_part[None]])
+    small = lax.psum(small, ("expert", "tensor"))
     return (
         layer_here,
         in_here,
-        gain_attn_summed,
+        small[experts_all + 1],
         qkv_summed,
         output_summed,
-        gain_ffn_summed,
-        router_summed,
+        small[experts_all],
+        jnp.transpose(small[:experts_all]),
         w_in_grad,
         w_out_grad,
     )

time: 905 us -> 576 us (0.64)
  waiting for transfers between devices: 542 us -> 406 us
  blocking collectives: 141 us -> 39.3 us
  other arithmetic: 78.2 us -> 31.6 us
  local copies, waits for them, and re-layouts: 60.2 us -> 23.3 us
  matrix products: 48.3 us -> 59 us
    reduce_scatter x2 -> x3, waiting for transfers between devices: 283 us -> 84.3 us  [to_owner(): lax.psum_scatter(partial.astype(jnp.bfloat16), 'expert', scatter_dimensio...]
    all_gather x0 -> x5, waiting for transfers between devices: none -> 147 us  [the longest x1 47 us: on_device(): w_output_all = lax.all_gather(w_output, 'tensor', axis=0, tiled=True)]
    all_to_all x2 -> x0, blocking collectives: 106 us -> none  [to_experts(): lax.all_to_all(buffer, 'expert', split_axis=1, concat_axis=1, tiled=True)]
    psum x3 -> x2, waiting for transfers between devices: 211 us -> 136 us  [the longest x1 84.6 us: on_device(): lax.psum(mixture_part.astype(jnp.bfloat16), 'tensor').astype(jnp.float32)]
    gather x8 -> x0, local copies, waits for them, and re-layouts: 33.8 us -> none  [the longest x1 9.76 us: on_device(): upstream[send_token] * send_gate[..., None]]
    scatter-add x3 -> x0, other arithmetic: 19 us -> none  [the longest x1 7.67 us: on_device(): jax.ops.segment_sum((returned_float * mine_gate[..., None]).reshape(-1, m...]
    all_to_all x2 -> x0, waiting for transfers between devices: 15.1 us -> none  [from_experts(): lax.all_to_all(buffer, 'expert', split_axis=1, concat_axis=1, tiled=True)]
    convert_element_type x11 -> x3, other arithmetic: 18.7 us -> 5.86 us  [the longest x1 4.93 us: on_device(): up_pre = (active_grad * silu_vals).astype(jnp.bfloat16)]
  transfers between devices with their start and end apart: 8 -> 11, of which waited for: 7 -> 11; matrix products, arithmetic and copies ran while one was open for 7% -> 9% of each run, Pallas kernels for 0% -> 0%
where the time goes in v1:
time: 576 us; the launch traced here: 575 us
  waiting for transfers between devices  406 us (70%)
  matrix products  59 us (10%)
  blocking collectives  39.3 us (7%)
  other arithmetic  31.6 us (5%)
  local copies, waits for them, and re-layouts  23.3 us (4%)
  between operations  14.5 us (3%)
    psum x1, waiting for transfers between devices, on_device(): lax.psum(mixture_part.astype(jnp.bfloat16), 'tensor').astype(jnp.float32)  84.6 us
    reduce_scatter x3, waiting for transfers between devices, to_owner(): lax.psum_scatter(partial.astype(jnp.bfloat16), 'expert', scatter_dimensio...  84.3 us
    psum x1, waiting for transfers between devices, on_device(): lax.psum(normed_two_part.astype(jnp.bfloat16), 'tensor').astype(jnp.float32)  51.7 us
    all_gather x1, waiting for transfers between devices, on_device(): w_output_all = lax.all_gather(w_output, 'tensor', axis=0, tiled=True)  47 us
    psum x1, blocking collectives, on_device(): small = lax.psum(small, ('expert', 'tensor'))  39.3 us
    psum x1, waiting for transfers between devices, on_device(): lax.psum(w_qkv_grad.astype(jnp.bfloat16), 'expert').astype(jnp.float32)  36.5 us
    all_gather x1, waiting for transfers between devices, on_device(): heads_all = lax.all_gather(heads_out, 'tensor', axis=1, tiled=True)  27.1 us
    all_gather x1, waiting for transfers between devices, on_device(): w_gate_all = lax.all_gather(w_in[0, 0], 'expert', axis=0, tiled=True)  25.7 us
  transfers between devices with their start and end apart: 11, of which 11 were waited for; matrix products, arithmetic and copies ran while one was open for 9% of the time, Pallas kernels for 0%

profile of v1, /device:TPU:0, one launch (start us, length us, event | category | flops | bytes accessed | tf_op | source)
XLA Modules:
  0.0 575.2 jit_solution(7086815770672283940)
XLA Ops:
  7.3 1.5 fusion.13
  8.8 1.5 copy.61
  10.4 1.3 copy.40
  11.7 2.0 fusion.34
  15.8 4.6 fusion.70
  20.4 3.4 convolution_convert_fusion.5
  27.6 27.1 %all-gather.9.cloned.1.call-done = bf16[512,1024]{0,1:T(8,128)(2,1)} async-done(((bf16[512,256]{0,1:T(8,128)(2,1)}), bf16[512,1024]{0,1:T(8,128)(2,1)}) %all-gather.9.cloned.1.call-update) | async-done | bytes 1048592 | tf_op jit(solution)/shard_map/all_gather | solution.py:206
  54.7 47.0 %all-gather.11.cloned.1.call-done = bf16[1024,1024]{1,0:T(8,128)(2,1)} async-done(((bf16[256,1024]{1,0:T(8,128)(2,1)}), bf16[1024,1024]{1,0:T(8,128)(2,1)}) %all-gather.11.cloned.1.call-update) | async-done | bytes 2097168 | tf_op jit(solution)/shard_map/all_gather | solution.py:183
  101.7 3.3 multiply_reduce_fusion.3
  108.5 22.3 %all-gather.15.cloned.1.call-done = bf16[1,1,1024,1024]{3,2,1,0:T(8,128)(2,1)} async-done(((bf16[1,1,128,1024]{3,2,1,0:T(8,128)(2,1)}), bf16[1,1,1024,1024]{3,2,1,0:T(8,128)(2,1)}) %all-gather.15.cloned.1.call-update) | async-done | bytes 2097168 | tf_op jit(solution)/shard_map/all_gather | solution.py:185
  130.8 4.6 fusion.21
  135.4 25.7 %all-gather.13.cloned.1.call-done = bf16[1,1,1024,1024]{3,2,1,0:T(8,128)(2,1)} async-done(((bf16[1,1,128,1024]{3,2,1,0:T(8,128)(2,1)}), bf16[1,1,1024,1024]{3,2,1,0:T(8,128)(2,1)}) %all-gather.13.cloned.1.call-update) | async-done | bytes 2097168 | tf_op jit(solution)/shard_map/all_gather | solution.py:184
  161.1 4.5 fusion.25
  165.6 25.2 %all-gather.17.cloned.1.call-done = bf16[1,1024,1024]{2,1,0:T(8,128)(2,1)} async-done(((bf16[1,128,1024]{2,1,0:T(8,128)(2,1)}), bf16[1,1024,1024]{2,1,0:T(8,128)(2,1)}) %all-gather.17.cloned.1.call-update) | async-done | bytes 2097168 | tf_op jit(solution)/shard_map/all_gather | solution.py:186
  190.8 3.3 fusion.15
  195.8 1.8 copy.63
  197.5 2.9 reduce_sum.125
  200.5 1.7 copy.44
  202.1 1.9 multiply_reduce_fusion.4
  204.0 1.6 copy.42
  205.6 1.7 broadcast_in_dim.154
  207.3 4.9 multiply_convert_fusion.1
  212.3 1.3 fusion.19
  214.6 1.3 fusion.23
  215.9 2.1 fusion.72
  218.4 51.7 %all-reduce.6.cloned.1.call-done = bf16[512,1024]{1,0:T(8,128)(2,1)} async-done(((bf16[512,1024]{1,0:T(8,128)(2,1)}), bf16[512,1024]{1,0:T(8,128)(2,1)}) %all-reduce.6.cloned.1.call-update) | async-done | bytes 1048592 | tf_op jit(solution)/shard_map/psum | solution.py:261
  270.1 2.7 multiply_reduce_fusion.1
  275.5 1.4 copy-done.12
  276.9 1.7 multiply_reduce_fusion
  283.5 1.9 convolution_convert_fusion.3
  285.5 4.2 fusion.31
  289.7 2.4 fusion.73
  292.2 4.2 convolution_convert_fusion.2
  296.5 4.2 convolution_convert_fusion.1
  301.1 4.2 convolution_convert_fusion
  306.0 1.5 fusion.74
  307.4 36.5 %all-reduce.8.cloned.1.call-done = (bf16[1024,2,256]{2,0,1:T(8,128)(2,1)}, bf16[256,1024]{1,0:T(8,128)(2,1)}) async-done(((bf16[1024,2,256]{2,0,1:T(8,128)(2,1)}, bf16[256,1024]{1,0:T(8,128)(2,1)}), (bf16[1024,2,256]{2,0,1:T(8,128)(2,1)}, bf16[256,1024]{1,0:T(8,128)(2,1)})) %all-reduce.8.cloned.1.call-update) | async-done | bytes 1572880 | tf_op jit(solution)/shard_map/psum | solution.py:315
  344.0 3.7 copy.49
  348.8 84.6 %all-reduce.10.cloned.1.call-done = (bf16[512,1024]{1,0:T(8,128)(2,1)}, bf16[512,1024]{1,0:T(8,128)(2,1)}) async-done(((bf16[512,1024]{1,0:T(8,128)(2,1)}, bf16[512,1024]{1,0:T(8,128)(2,1)}), (bf16[512,1024]{1,0:T(8,128)(2,1)}, bf16[512,1024]{1,0:T(8,128)(2,1)})) %all-reduce.10.cloned.1.call-update) | async-done | bytes 2097168 | tf_op jit(solution)/shard_map/psum | solution.py:263
  433.4 2.6 fusion.12
  436.0 39.3 %psum.45 = f32[10,1024]{1,0:T(8,128)S(1)} all-reduce(f32[10,1024]{1,0:T(8,128)S(1)} %pad_maximum_fusion.2), channel_id=1, replica_groups=mesh['expert'=8,'tensor'=4] {'expert','tensor'}, use_global_device_ids=true, to_apply=%region_20.21 | all-reduce | flops 10240 | bytes 81920 | tf_op jit(solution)/shard_map/psum | solution.py:318
  475.3 2.4 reduce-scatter.4.cloned.1.call-done
  477.7 44.2 %reduce-scatter.6.cloned.1.call-done = bf16[128,1024]{1,0:T(8,128)(2,1)} async-done(((bf16[1024,1024]{1,0:T(8,128)(2,1)}), bf16[128,1024]{1,0:T(8,128)(2,1)}) %reduce-scatter.6.cloned.1.call-update) | async-done | bytes 262160 | tf_op jit(solution)/shard_map/reduce_scatter | solution.py:267
  521.9 2.2 fusion.44
  525.3 1.4 add_convert_fusion
  527.5 1.6 fusion.11
  529.2 37.7 %reduce-scatter.8.cloned.1.call-done = bf16[128,1024]{1,0:T(8,128)(2,1)} async-done(((bf16[1024,1024]{1,0:T(8,128)(2,1)}), bf16[128,1024]{1,0:T(8,128)(2,1)}) %reduce-scatter.8.cloned.1.call-update) | async-done | bytes 262160 | tf_op jit(solution)/shard_map/reduce_scatter | solution.py:267
  566.9 1.8 bitcast_convert_fusion
  (161 shorter events, 24.0 us)
Async XLA Ops:
  7.2 99.8 %copy-start = (bf16[1024,8]{0,1:T(8,128)(2,1)S(1)}, bf16[1024,8]{0,1:T(8,128)(2,1)}, u32[]{:S(2)}) copy-start(bf16[1024,8]{0,1:T(8,128)(2,1)} %param.18) | copy-start | bytes 49156
  7.2 47.5 %all-gather.9.cloned.1.call-start = ((), (), s32[]{:S(2)}) async-start(), calls=%async_computation.3 | async-start | bytes 1310720 | tf_op jit(solution)/shard_map/all_gather | solution.py:206
  8.8 2.9 copy-start.37
  8.8 2.9 copy-start.4
  8.8 2.9 copy-start.40
  10.3 3.4 copy-start.6
  11.7 2.2 copy-start.48
  13.8 6.6 %copy-start.15 = (f32[512,2,4,64]{0,3,2,1:T(8,128)}, f32[512,2,4,64]{0,3,2,1:T(8,128)S(1)}, u32[]{:S(2)}) copy-start(f32[512,2,4,64]{0,3,2,1:T(8,128)S(1)} %fusion.34) | copy-start | bytes 3145732
  15.8 4.6 copy-start.22
  20.4 3.5 copy-start.42
  20.4 4.3 copy-start.27
  23.9 3.1 copy-start.45
  23.9 77.8 %all-gather.11.cloned.1.call-start = ((), (), s32[]{:S(2)}) async-start(), calls=%async_computation.4 | async-start | bytes 2621440 | tf_op jit(solution)/shard_map/all_gather | solution.py:183
  24.7 106.2 %all-gather.15.cloned.1.call-start = ((), (), s32[]{:S(2)}) async-start(), calls=%async_computation.10 | async-start | bytes 2359296 | tf_op jit(solution)/shard_map/all_gather | solution.py:185
  25.6 135.5 %all-gather.13.cloned.1.call-start = ((), (), s32[]{:S(2)}) async-start(), calls=%async_computation.9 | async-start | bytes 2359296 | tf_op jit(solution)/shard_map/all_gather | solution.py:184
  26.1 164.6 %all-gather.17.cloned.1.call-start = ((), (), s32[]{:S(2)}) async-start(), calls=%async_computation.11 | async-start | bytes 2359296 | tf_op jit(solution)/shard_map/all_gather | solution.py:186
  26.7 243.3 %all-reduce.6.cloned.1.call-start = ((), (), s32[]{:S(2)}) async-start(), calls=%async_computation.5 | async-start | bytes 2097152 | tf_op jit(solution)/shard_map/psum | solution.py:261
  105.0 1.9 copy-start.33
  105.0 2.3 copy-start.35
  190.8 3.4 copy-start.8
  190.8 3.4 copy-start.10
  205.6 1.7 copy-start.9
  207.3 5.0 copy-start.29
  207.3 5.0 copy-start.30
  207.3 5.0 copy-start.44
  207.3 5.0 copy-start.46
  212.3 3.6 copy-start.31
  212.3 2.3 copy-start.47
  218.1 125.9 %all-reduce.8.cloned.1.call-start = ((), (), s32[]{:S(2)}) async-start(), calls=%async_computation.12 | async-start | bytes 3145728 | tf_op jit(solution)/shard_map/psum | solution.py:315
  270.1 2.7 copy-start.14
  270.1 2.7 copy-start.19
  270.1 2.7 copy-start.34
  270.1 2.7 copy-start.36
  272.8 2.2 copy-start.18
  273.7 1.8 copy-start.2
  273.7 3.2 copy-start.12
  275.0 1.9 copy-start.43
  285.4 148.0 %all-reduce.10.cloned.1.call-start = ((), (), s32[]{:S(2)}) async-start(), calls=%async_computation.13 | async-start | bytes 4194304 | tf_op jit(solution)/shard_map/psum | solution.py:263
  285.5 4.3 copy-start.7
  285.5 4.3 copy-start.17
  292.2 185.5 %reduce-scatter.4.cloned.1.call-start = ((), (), s32[]{:S(2)}) async-start(), calls=%async_computation.6 | async-start | bytes 2359296 | tf_op jit(solution)/shard_map/reduce_scatter | solution.py:267
  296.5 225.5 %reduce-scatter.6.cloned.1.call-start = ((), (), s32[]{:S(2)}) async-start(), calls=%async_computation.7 | async-start | bytes 2359296 | tf_op jit(solution)/shard_map/reduce_scatter | solution.py:267
  300.8 266.1 %reduce-scatter.8.cloned.1.call-start = ((), (), s32[]{:S(2)}) async-start(), calls=%async_computation.8 | async-start | bytes 2359296 | tf_op jit(solution)/shard_map/reduce_scatter | solution.py:267
  344.0 3.7 copy-start.26
  521.9 3.4 copy-start.20
  525.3 2.0 copy-start.3
  525.3 2.2 copy-start.13
  525.3 43.3 %copy-start.1 = (bf16[1024,8]{0,1:T(8,128)(2,1)S(1)}, bf16[1024,8]{0,1:T(8,128)(2,1)}, u32[]{:S(2)}) copy-start(bf16[1024,8]{0,1:T(8,128)(2,1)} %param.18) | copy-start | bytes 49156
  (12 other events, 12.2 us)
Sparse Core Ops, SparseCore 0:
  24.0 30.6 all-gather.8
  56.3 45.3 all-gather.10
  104.2 26.6 all-gather.14
  133.2 27.8 all-gather.12
  162.8 27.8 all-gather.16
  218.2 51.8 all-reduce.5
  285.5 58.4 all-reduce.7
  347.0 86.3 all-reduce.9
  437.1 40.6 reduce-scatter.3
  480.9 41.0 reduce-scatter.5
  525.6 41.2 reduce-scatter.7

commit v2 on v1

--- a/solution.py
+++ b/solution.py
@@ -1,8 +1,12 @@
+import functools
 import math
 
 import jax
 import jax.numpy as jnp
+import numpy as np
 from jax import lax
+from jax.experimental import pallas as pl
+from jax.experimental.pallas import tpu as pltpu
 from jax.sharding import PartitionSpec as P
 
 HEADS = 16
@@ -162,7 +166,7 @@
     return (join_blocks(query_blocks, 2), key_grad, value_grad)
 
 
-def on_device(
+def on_device_general(
     layer_in,
     seq_lengths,
     routes,
@@ -329,7 +333,557 @@
     )
 
 
+LANES = 128
+ROWS = 128
+
+
+def exchange(array_in, axis_name, bits):
+    count = lax.axis_size(axis_name)
+    return lax.ppermute(array_in, axis_name, [(i, i ^ bits) for i in range(count)])
+
+
+def gather_blocks(own):
+    far = exchange(own, "tensor", 2)
+    near = exchange(own, "tensor", 1)
+    return [own, near, far, exchange(far, "tensor", 1)]
+
+
+def scatter_sums(parts):
+    relayed = exchange(parts[3], "tensor", 1)
+    far = (parts[2].astype(jnp.float32) + relayed.astype(jnp.float32)).astype(jnp.bfloat16)
+    far = exchange(far, "tensor", 2)
+    near = exchange(parts[1], "tensor", 1)
+    return parts[0] + near.astype(jnp.float32) + far.astype(jnp.float32)
+
+
+def gather_experts(own, high_first):
+    near = exchange(own, "expert", 2)
+    far = exchange(own, "expert", 4)
+    both = exchange(near, "expert", 4) if high_first else exchange(far, "expert", 2)
+    chips = [own, near, far, both]
+    return chips + [exchange(block, "expert", 1) for block in chips]
+
+
+def scatter_experts(even, odd):
+    summed = even + exchange(odd.astype(jnp.bfloat16), "expert", 1).astype(jnp.float32)
+    chips = split_blocks(summed, 0, 4)
+    total = chips[0]
+    for place in (3, 1, 2):
+        total = total + exchange(
+            chips[place].astype(jnp.bfloat16), "expert", 2 * place
+        ).astype(jnp.float32)
+    return total
+
+
+def sum_experts(array_in, bits):
+    core = lax.axis_index("expert") & 1
+    rows = array_in.shape[0] // 2
+    top, bottom = array_in[:rows], array_in[rows:]
+    keep = jnp.where(core == 0, top, bottom)
+    give = jnp.where(core == 0, bottom, top).astype(jnp.bfloat16)
+    half = keep + exchange(give, "expert", 1).astype(jnp.float32)
+    half = half.astype(jnp.bfloat16)
+    for bit in bits:
+        arrived = exchange(half, "expert", bit)
+        half = (half.astype(jnp.float32) + arrived.astype(jnp.float32)).astype(jnp.bfloat16)
+    other = exchange(half, "expert", 1)
+    return jnp.concatenate(
+        [jnp.where(core == 0, half, other), jnp.where(core == 0, other, half)]
+    ).astype(jnp.float32)
+
+
+def sum_all(array_in):
+    for axis_name in ("tensor", "expert"):
+        bit = 1
+        while bit < lax.axis_size(axis_name):
+            array_in = array_in + exchange(array_in, axis_name, bit)
+            bit *= 2
+    return array_in
+
+
+def dot_plain(left, right):
+    return jnp.dot(left, right, preferred_element_type=jnp.float32)
+
+
+def dot_transposed(left, right):
+    return lax.dot_general(
+        left, right, (((1,), (1,)), ((), ())), preferred_element_type=jnp.float32
+    )
+
+
+def transposed_dot(left, right):
+    return lax.dot_general(
+        left, right, (((0,), (0,)), ((), ())), preferred_element_type=jnp.float32
+    )
+
+
+def lane_index(shape):
+    return lax.broadcasted_iota(jnp.int32, shape, 1)
+
+
+def turn(values):
+    low_half = (lane_index(values.shape) & (HEAD_DIM - 1)) < HEAD_DIM // 2
+    return jnp.where(
+        low_half,
+        -pltpu.roll(values, LANES - HEAD_DIM // 2, 1),
+        pltpu.roll(values, HEAD_DIM // 2, 1),
+    )
+
+
+def swap_heads(values):
+    return pltpu.roll(values, HEAD_DIM, 1)
+
+
+def first_head(shape):
+    return lane_index(shape) < HEAD_DIM
+
+
+def angle_tables(token_count):
+    half_dim = HEAD_DIM // 2
+    inverse_freq = np.exp(np.arange(half_dim) * (-2.0 * math.log(rope_base) / HEAD_DIM))
+    angles = np.arange(token_count)[:, None] * inverse_freq[None, :]
+    tile = LANES // half_dim
+    return (
+        np.tile(np.cos(angles), (1, tile)).astype(np.float32),
+        np.tile(np.sin(angles), (1, tile)).astype(np.float32),
+    )
+
+
+def attend_kernel(
+    lengths, layer_in, gain, w_qkv, cosine, sine, normed, inverse, queries, pairs, probs, attended
+):
+    token_count = layer_in.shape[0]
+    kv_here = pairs.shape[0]
+    for row in range(0, token_count, ROWS):
+        rows = pl.ds(row, ROWS)
+        values = layer_in[rows, :].astype(jnp.float32)
+        scale = lax.rsqrt(jnp.mean(values * values, axis=-1, keepdims=True) + epsilon)
+        inverse[rows, :] = scale
+        normed[rows, :] = (values * scale * gain[...]).astype(jnp.bfloat16)
+    is_first = first_head((ROWS, LANES))
+    for kv in range(kv_here):
+        projected = dot_plain(normed[...], w_qkv[:, 2 * LANES * kv : 2 * LANES * (kv + 1)])
+        for block in range(token_count // ROWS):
+            rows = pl.ds(block * ROWS, ROWS)
+            cos_rows, sin_rows = cosine[rows, :], sine[rows, :]
+            query = projected[block * ROWS : (block + 1) * ROWS, :LANES]
+            query = (query * cos_rows + turn(query) * sin_rows) * (1.0 / math.sqrt(HEAD_DIM))
+            queries[kv, block, :ROWS, :] = jnp.where(is_first, query, 0.0).astype(jnp.bfloat16)
+            queries[kv, block, ROWS:, :] = jnp.where(is_first, swap_heads(query), 0.0).astype(
+                jnp.bfloat16
+            )
+            pair = projected[block * ROWS : (block + 1) * ROWS, LANES:]
+            pairs[kv, rows, :] = jnp.where(
+                is_first, pair * cos_rows + turn(pair) * sin_rows, pair
+            ).astype(jnp.bfloat16)
+    for block in range(token_count // ROWS):
+        keys = (block + 1) * ROWS
+        token = block * ROWS + (
+            lax.broadcasted_iota(jnp.int32, (2 * ROWS, keys), 0) & (ROWS - 1)
+        )
+        start = jnp.zeros_like(token)
+        end = 0
+        for seq in range(lengths.shape[1] - 1):
+            end = end + lengths[0, seq]
+            start = jnp.where(token >= end, end, start)
+        key = lane_index((2 * ROWS, keys))
+        allowed = (key <= token) & (key >= start)
+        for kv in range(kv_here):
+            scores = dot_transposed(queries[kv, block], pairs[kv, :keys, :])
+            scores = jnp.where(allowed, scores, masked_out)
+            exponent = jnp.exp(scores - jnp.max(scores, -1, keepdims=True))
+            share = (exponent * (1.0 / jnp.sum(exponent, -1, keepdims=True))).astype(jnp.bfloat16)
+            probs[kv, block, :, :keys] = share
+            output = dot_plain(share, pairs[kv, :keys, :])
+            attended[pl.ds(block * ROWS, ROWS), kv * LANES : (kv + 1) * LANES] = jnp.where(
+                is_first, swap_heads(output[:ROWS]), output[ROWS:]
+            ).astype(jnp.bfloat16)
+
+
+def write_parts(place, total, parts, span):
+    for number, part in enumerate(parts):
+        row = pl.multiple_of((place[0] ^ number) * span, span)
+        part[...] = total[pl.ds(row, span), :].astype(part.dtype)
+
+
+def middle_kernel(tensor_count, experts_all, *refs):
+    place, gain, router, routes, layer_in, out_grad = refs[:6]
+    refs = refs[6:]
+    heads, refs = refs[:tensor_count], refs[tensor_count:]
+    outputs_w, refs = refs[:tensor_count], refs[tensor_count:]
+    w_ins, refs = refs[:experts_all], refs[experts_all:]
+    w_outs, refs = refs[:experts_all], refs[experts_all:]
+    parts, refs = refs[:tensor_count], refs[tensor_count:]
+    (residual_block, inverse_block, normed, active_out, pre_out, gain_part, router_part) = refs[:7]
+    (w_in, w_out, residual, inverse, gates, gate_grad, hidden, plain, total, sems) = refs[7:]
+    token_count, model_width = layer_in.shape
+    units = w_outs[0].shape[0]
+    span = token_count // tensor_count
+    copies = []
+    for number in range(experts_all):
+        copies.append(
+            pltpu.make_async_copy(
+                w_ins[number], w_in.at[pl.ds(number * 2 * units, 2 * units)], sems.at[0, number]
+            )
+        )
+        copies.append(
+            pltpu.make_async_copy(
+                w_outs[number], w_out.at[pl.ds(number * units, units)], sems.at[1, number]
+            )
+        )
+    for copy in copies:
+        copy.start()
+    lane = lane_index((ROWS, LANES))
+    for row in range(0, token_count, ROWS):
+        rows = pl.ds(row, ROWS)
+        values = layer_in[rows, :].astype(jnp.float32)
+        for head, output in zip(heads, outputs_w):
+            values = values + dot_plain(head[rows, :], output[...])
+        residual[rows, :] = values
+        scale = lax.rsqrt(jnp.mean(values * values, axis=-1, keepdims=True) + epsilon)
+        inverse[rows, :] = scale
+        normed_low = (values * scale * gain[...]).astype(jnp.bfloat16)
+        normed[rows, :] = normed_low
+        logits = dot_transposed(normed_low, router[...])
+        picked = routes[rows, 0:1] == lane
+        for top in range(1, routes.shape[1]):
+            picked = picked | (routes[rows, top : top + 1] == lane)
+        logits = jnp.where(picked, logits, masked_out)
+        weight = jnp.where(picked, jnp.exp(logits - jnp.max(logits, -1, keepdims=True)), 0.0)
+        gates[rows, :] = weight / jnp.sum(weight, -1, keepdims=True)
+    gate_grad[...] = jnp.zeros_like(gate_grad)
+    for copy in copies:
+        copy.wait()
+
+    def expert_step(number, carry):
+        twice = 2 * number
+        name = place[1] ^ jnp.where(twice < experts_all, twice, twice - experts_all + 1)
+        in_rows = pl.ds(pl.multiple_of(number * 2 * units, 2 * units), 2 * units)
+        out_rows = pl.ds(pl.multiple_of(number * units, units), units)
+        gate_lanes = pl.ds(pl.multiple_of(number * 2 * units, units), units)
+        up_lanes = pl.ds(pl.multiple_of(number * 2 * units + units, units), units)
+        hidden[...] = dot_transposed(normed[...], w_in[in_rows, :])
+        plain[...] = dot_transposed(out_grad[...], w_out[out_rows, :])
+        for row in range(0, token_count, ROWS):
+            rows = pl.ds(row, ROWS)
+            gate = jnp.sum(jnp.where(lane == name, gates[rows, :], 0.0), -1, keepdims=True)
+            gate_vals, up_vals = hidden[rows, :units], hidden[rows, units:]
+            sig_vals = 1.0 / (1.0 + jnp.exp(-gate_vals))
+            silu_vals = gate_vals * sig_vals
+            active = silu_vals * up_vals
+            grad = plain[rows, :]
+            gate_grad[rows, :] = gate_grad[rows, :] + jnp.where(
+                lane == name, jnp.sum(active * grad, -1, keepdims=True), 0.0
+            )
+            active_grad = grad * gate
+            active_out[rows, out_rows] = (active * gate).astype(jnp.bfloat16)
+            pre_out[rows, gate_lanes] = (
+                active_grad * up_vals * (sig_vals * (1.0 + gate_vals * (1.0 - sig_vals)))
+            ).astype(jnp.bfloat16)
+            pre_out[rows, up_lanes] = (active_grad * silu_vals).astype(jnp.bfloat16)
+        return carry
+
+    lax.fori_loop(0, experts_all, expert_step, 0)
+    gate_all, grad_all = gates[...], gate_grad[...]
+    logit_part = (
+        gate_all * (grad_all - jnp.sum(gate_all * grad_all, -1, keepdims=True))
+    ).astype(jnp.bfloat16)
+    router_part[...] = transposed_dot(logit_part, normed[...])[:experts_all]
+
+    def column_step(number, carry):
+        columns = pl.ds(pl.multiple_of(number * 2 * LANES, 2 * LANES), 2 * LANES)
+        total[:, columns] = dot_plain(pre_out[...], w_in[:, columns]) + dot_plain(
+            logit_part, router[:, columns]
+        )
+        return carry
+
+    lax.fori_loop(0, model_width // (2 * LANES), column_step, 0)
+    write_parts(place, total, parts, span)
+    row = pl.ds(pl.multiple_of(place[0] * span, span), span)
+    residual_block[...] = residual[row, :]
+    inverse_block[...] = inverse[row, :]
+    gain_sum = jnp.zeros((1, model_width), jnp.float32)
+    for row in range(0, token_count, ROWS):
+        rows = pl.ds(row, ROWS)
+        gain_sum = gain_sum + jnp.sum(
+            total[rows, :] * (residual[rows, :] * inverse[rows, :]), 0, keepdims=True
+        )
+    gain_part[...] = gain_sum
+
+
+def attend_back_kernel(tensor_count, *refs):
+    place, w_output, queries, pairs, probs, cosine, sine, w_qkv, layer_in, inverse = refs[:10]
+    refs = refs[10:]
+    blocks, refs = refs[:tensor_count], refs[tensor_count:]
+    parts, refs = refs[:tensor_count], refs[tensor_count:]
+    branch_grad, projected_grad, gain_part, heads_grad, pair_grad, total = refs
+    token_count, model_width = layer_in.shape
+    span = token_count // tensor_count
+    for number, block in enumerate(blocks):
+        row = pl.multiple_of((place[0] ^ number) * span, span)
+        branch_grad[pl.ds(row, span), :] = block[...]
+    heads_grad[...] = dot_transposed(branch_grad[...], w_output[...])
+    is_first = first_head((ROWS, LANES))
+    for kv in range(pairs.shape[0]):
+        pair_grad[...] = jnp.zeros_like(pair_grad)
+        for block in range(token_count // ROWS):
+            keys = (block + 1) * ROWS
+            rows = pl.ds(block * ROWS, ROWS)
+            upper = heads_grad[rows, kv * LANES : (kv + 1) * LANES]
+            upper = jnp.concatenate(
+                [
+                    jnp.where(is_first, 0.0, swap_heads(upper)),
+                    jnp.where(is_first, 0.0, upper),
+                ]
+            ).astype(jnp.bfloat16)
+            share_low = probs[kv, block, :, :keys]
+            share = share_low.astype(jnp.float32)
+            prob_grad = dot_transposed(upper, pairs[kv, :keys, :])
+            inner = jnp.sum(share * prob_grad, -1, keepdims=True)
+            score_grad = (share * (prob_grad - inner)).astype(jnp.bfloat16)
+            query_grad = dot_plain(score_grad, pairs[kv, :keys, :])
+            query_grad = jnp.where(
+                is_first, query_grad[:ROWS], swap_heads(query_grad[ROWS:])
+            ) * (1.0 / math.sqrt(HEAD_DIM))
+            projected_grad[rows, 2 * kv * LANES : (2 * kv + 1) * LANES] = (
+                query_grad * cosine[rows, :] - turn(query_grad) * sine[rows, :]
+            ).astype(jnp.bfloat16)
+            pair_grad[:keys, :] = (
+                pair_grad[:keys, :]
+                + transposed_dot(score_grad, queries[kv, block])
+                + transposed_dot(share_low, upper)
+            )
+        for block in range(token_count // ROWS):
+            rows = pl.ds(block * ROWS, ROWS)
+            grad = pair_grad[rows, :]
+            projected_grad[rows, (2 * kv + 1) * LANES : (2 * kv + 2) * LANES] = jnp.where(
+                is_first, grad * cosine[rows, :] - turn(grad) * sine[rows, :], grad
+            ).astype(jnp.bfloat16)
+
+    def column_step(number, carry):
+        columns = pl.ds(pl.multiple_of(number * 2 * LANES, 2 * LANES), 2 * LANES)
+        total[:, columns] = dot_transposed(projected_grad[...], w_qkv[columns, :])
+        return carry
+
+    lax.fori_loop(0, model_width // (2 * LANES), column_step, 0)
+    write_parts(place, total, parts, span)
+    gain_sum = jnp.zeros((1, model_width), jnp.float32)
+    for row in range(0, token_count, ROWS):
+        rows = pl.ds(row, ROWS)
+        gain_sum = gain_sum + jnp.sum(
+            total[rows, :] * (layer_in[rows, :].astype(jnp.float32) * inverse[rows, :]),
+            0,
+            keepdims=True,
+        )
+    gain_part[...] = gain_sum
+
+
+def in_vmem(count):
+    return [pl.BlockSpec(memory_space=pltpu.VMEM)] * count
+
+
+def in_smem(count):
+    return [pl.BlockSpec(memory_space=pltpu.SMEM)] * count
+
+
+def shaped(shape, dtype):
+    return jax.ShapeDtypeStruct(shape, dtype)
+
+
+def on_device(
+    layer_in,
+    seq_lengths,
+    routes,
+    gain_attn,
+    w_qkv,
+    w_output,
+    gain_ffn,
+    w_router,
+    w_in,
+    w_out,
+    out_grad,
+):
+    low, wide = jnp.bfloat16, jnp.float32
+    token_count, model_width = layer_in.shape
+    kv_here = w_qkv.shape[1]
+    experts_all = w_router.shape[1]
+    units = w_out.shape[1]
+    head_width = kv_here * LANES
+    block_count = token_count // ROWS
+    tensor_count = lax.axis_size("tensor")
+    span = token_count // tensor_count
+    tensor_here = lax.axis_index("tensor")
+    place = jnp.stack([tensor_here, lax.axis_index("expert")]).astype(jnp.int32)
+    mib = 1 << 20
+
+    def token_block(array_in):
+        return lax.dynamic_slice_in_dim(array_in, tensor_here * span, span, 0)
+
+    def in_order(blocks):
+        joined = jnp.zeros((token_count,) + blocks[0].shape[1:], blocks[0].dtype)
+        for number, block in enumerate(blocks):
+            joined = lax.dynamic_update_slice_in_dim(
+                joined, block, (tensor_here ^ number) * span, 0
+            )
+        return joined
+
+    w_in_all = gather_experts(w_in.reshape(2 * units, model_width), True)
+    w_out_all = gather_experts(w_out[0], False)
+    w_output_all = gather_blocks(w_output)
+
+    cosine, sine = angle_tables(token_count)
+    qkv_flat = w_qkv.reshape(model_width, -1)
+    normed_one, inverse_one, queries, pairs, probs, attended = pl.pallas_call(
+        attend_kernel,
+        out_shape=(
+            shaped((token_count, model_width), low),
+            shaped((token_count, 1), wide),
+            shaped((kv_here, block_count, 2 * ROWS, LANES), low),
+            shaped((kv_here, token_count, LANES), low),
+            shaped((kv_here, block_count, 2 * ROWS, token_count), low),
+            shaped((token_count, head_width), low),
+        ),
+        in_specs=in_smem(1) + in_vmem(5),
+        out_specs=tuple(in_vmem(6)),
+        compiler_params=pltpu.CompilerParams(vmem_limit_bytes=32 * mib),
+        name="attend",
+    )(seq_lengths, layer_in, gain_attn[None], qkv_flat, cosine, sine)
+
+    heads_all = gather_blocks(attended)
+    router_rows = jnp.pad(jnp.transpose(w_router), ((0, LANES - experts_all), (0, 0)))
+    part_shapes = (shaped((span, model_width), wide),) + (
+        shaped((span, model_width), low),
+    ) * (tensor_count - 1)
+    middle = pl.pallas_call(
+        functools.partial(middle_kernel, tensor_count, experts_all),
+        out_shape=part_shapes
+        + (
+            shaped((span, model_width), wide),
+            shaped((span, 1), wide),
+            shaped((token_count, model_width), low),
+            shaped((token_count, experts_all * units), low),
+            shaped((token_count, experts_all * 2 * units), low),
+            shaped((1, model_width), wide),
+            shaped((experts_all, model_width), wide),
+        ),
+        in_specs=in_smem(1)
+        + in_vmem(5 + 2 * tensor_count)
+        + [pl.BlockSpec(memory_space=pl.ANY)] * (2 * experts_all),
+        out_specs=tuple(in_vmem(tensor_count + 7)),
+        scratch_shapes=[
+            pltpu.VMEM((experts_all * 2 * units, model_width), low),
+            pltpu.VMEM((experts_all * units, model_width), low),
+            pltpu.VMEM((token_count, model_width), wide),
+            pltpu.VMEM((token_count, 1), wide),
+            pltpu.VMEM((token_count, LANES), wide),
+            pltpu.VMEM((token_count, LANES), wide),
+            pltpu.VMEM((token_count, 2 * units), wide),
+            pltpu.VMEM((token_count, units), wide),
+            pltpu.VMEM((token_count, model_width), wide),
+            pltpu.SemaphoreType.DMA((2, experts_all)),
+        ],
+        compiler_params=pltpu.CompilerParams(vmem_limit_bytes=44 * mib),
+        name="middle",
+    )(
+        place,
+        gain_ffn[None],
+        router_rows,
+        routes,
+        layer_in,
+        out_grad,
+        *heads_all,
+        *w_output_all,
+        *w_in_all,
+        *w_out_all,
+    )
+    normed_parts, middle = middle[:tensor_count], middle[tensor_count:]
+    residual, inverse_two, normed_two, active, pre_grad, gain_ffn_part, router_part = middle
+
+    normed_two_grad = scatter_sums(normed_parts)
+    residual_grad = token_block(out_grad).astype(wide) + rms_backward(
+        residual, inverse_two, gain_ffn, normed_two_grad
+    )
+    grad_blocks = gather_blocks(residual_grad.astype(low))
+
+    half_units = experts_all * units
+    w_in_grad = scatter_experts(
+        transposed_dot(pre_grad[:, :half_units], normed_two),
+        transposed_dot(pre_grad[:, half_units:], normed_two),
+    ).reshape(w_in.shape)
+    w_out_grad = scatter_experts(
+        transposed_dot(active[:, : half_units // 2], out_grad),
+        transposed_dot(active[:, half_units // 2 :], out_grad),
+    )[None]
+
+    back = pl.pallas_call(
+        functools.partial(attend_back_kernel, tensor_count),
+        out_shape=part_shapes
+        + (
+            shaped((token_count, model_width), low),
+            shaped((token_count, 2 * head_width), low),
+            shaped((1, model_width), wide),
+        ),
+        in_specs=in_smem(1) + in_vmem(9 + tensor_count),
+        out_specs=tuple(in_vmem(tensor_count + 3)),
+        scratch_shapes=[
+            pltpu.VMEM((token_count, head_width), wide),
+            pltpu.VMEM((token_count, LANES), wide),
+            pltpu.VMEM((token_count, model_width), wide),
+        ],
+        compiler_params=pltpu.CompilerParams(vmem_limit_bytes=32 * mib),
+        name="attend_back",
+    )(
+        place,
+        w_output,
+        queries,
+        pairs,
+        probs,
+        cosine,
+        sine,
+        qkv_flat,
+        layer_in,
+        inverse_one,
+        *grad_blocks,
+    )
+    input_parts, (branch_grad, projected_grad, gain_attn_part) = (
+        back[:tensor_count],
+        back[tensor_count:],
+    )
+    normed_one_grad = scatter_sums(input_parts)
+    input_part = rms_backward(
+        token_block(layer_in).astype(wide), token_block(inverse_one), gain_attn, normed_one_grad
+    )
+    in_here = in_order(gather_blocks((residual_grad + input_part).astype(low)))
+
+    mixture_part = dot_plain(active, jnp.concatenate(w_out_all))
+    mixture_part, _ = lax.optimization_barrier((mixture_part, grad_blocks[3]))
+    mixture_parts = [
+        lax.dynamic_slice_in_dim(mixture_part, (tensor_here ^ number) * span, span, 0)
+        for number in range(tensor_count)
+    ]
+    mixture = scatter_sums(mixture_parts[:1] + [part.astype(low) for part in mixture_parts[1:]])
+    layer_here = in_order(gather_blocks((residual + mixture).astype(low)))
+
+    qkv_summed = sum_experts(transposed_dot(normed_one, projected_grad), (2, 4)).reshape(
+        w_qkv.shape
+    )
+    output_summed = sum_experts(transposed_dot(attended, branch_grad), (4, 2))
+    small = sum_all(jnp.concatenate([router_part, gain_ffn_part, gain_attn_part]))
+    return (
+        layer_here,
+        in_here,
+        small[experts_all + 1],
+        qkv_summed,
+        output_summed,
+        small[experts_all],
+        jnp.transpose(small[:experts_all]),
+        w_in_grad,
+        w_out_grad,
+    )
+
+
 def solution(mesh):
+    fits = mesh.shape["tensor"] == 4 and mesh.shape["expert"] == 8
     placed = (
         P("expert", None),
         P("expert", None),
@@ -344,7 +898,7 @@
         P("expert", None),
     )
     return jax.shard_map(
-        on_device,
+        on_device if fits else on_device_general,
         mesh=mesh,
         in_specs=placed,
         out_specs=(

time: 576 us -> 279 us (0.48)
  waiting for transfers between devices: 406 us -> 147 us
  matrix products: 59 us -> 8.53 us
  starting transfers between devices: 1.11 us -> 50.7 us
  blocking collectives: 39.3 us -> 0 us
  Pallas kernels: 0 us -> 29.7 us
  other arithmetic: 31.6 us -> 9.48 us
  between operations: 14.5 us -> 1.53 us
  local copies, waits for them, and re-layouts: 23.3 us -> 30.9 us
    psum x3 -> x0, waiting for transfers between devices: 173 us -> none  [the longest x1 84.6 us: on_device(): lax.psum(mixture_part.astype(jnp.bfloat16), 'tensor').astype(jnp.float32)]
    ppermute x0 -> x59, waiting for transfers between devices: none -> 147 us  [exchange(): lax.ppermute(array_in, axis_name, [(i, i ^ bits) for i in range(count)])]
    all_gather x5 -> x0, waiting for transfers between devices: 147 us -> none  [the longest x1 47 us: on_device(): w_output_all = lax.all_gather(w_output, 'tensor', axis=0, tiled=True)]
    reduce_scatter x3 -> x0, waiting for transfers between devices: 84.3 us -> none  [to_owner(): lax.psum_scatter(partial.astype(jnp.bfloat16), 'expert', scatter_dimensio...]
    ppermute x0 -> x59, starting transfers between devices: none -> 50.7 us  [exchange(): lax.ppermute(array_in, axis_name, [(i, i ^ bits) for i in range(count)])]
    dot_general x23 -> x7, matrix products: 54.4 us -> 8.53 us  [the longest x6 5.29 us: transposed_dot(): lax.dot_general(left, right, (((0,), (0,)), ((), ())), preferred_element_...]
    psum x1 -> x0, blocking collectives: 39.3 us -> none  [on_device(): small = lax.psum(small, ('expert', 'tensor'))]
    pallas_call x0 -> x3, Pallas kernels: none -> 29.7 us  [the longest x1 18.3 us: on_device(): pl.pallas_call(functools.partial(middle_kernel, tensor_count, experts_all...]
  transfers between devices with their start and end apart: 11 -> 59, of which waited for: 11 -> 26; matrix products, arithmetic and copies ran while one was open for 9% -> 9% of each run, Pallas kernels for 0% -> 3%
where the time goes in v2:
time: 279 us; the launch traced here: 278 us
  waiting for transfers between devices  147 us (53%)
  starting transfers between devices  50.7 us (18%)
  local copies, waits for them, and re-layouts  30.9 us (11%)
  Pallas kernels  29.7 us (11%)
  other arithmetic  9.48 us (3%)
  matrix products  8.53 us (3%)
    ppermute x59, waiting for transfers between devices, exchange(): lax.ppermute(array_in, axis_name, [(i, i ^ bits) for i in range(count)])  147 us
    ppermute x59, starting transfers between devices, exchange(): lax.ppermute(array_in, axis_name, [(i, i ^ bits) for i in range(count)])  50.7 us
    unnamed x113, local copies, waits for them, and re-layouts  25.6 us
    pallas_call x1, Pallas kernels, on_device(): pl.pallas_call(functools.partial(middle_kernel, tensor_count, experts_all...  18.3 us
    pallas_call x1, Pallas kernels, on_device(): pl.pallas_call(functools.partial(attend_back_kernel, tensor_count), out_s...  7.13 us
  transfers between devices with their start and end apart: 59, of which 26 were waited for; matrix products, arithmetic and copies ran while one was open for 9% of the time, Pallas kernels for 3%

profile of v2, /device:TPU:0, one launch (start us, length us, event | category | flops | bytes accessed | tf_op | source)
XLA Modules:
  0.0 278.1 jit_solution(10850038284476594315)
XLA Ops:
  0.7 1.6 copy.28
  2.4 4.3 %attend.1 = (bf16[512,1024]{1,0:T(8,128)(2,1)S(1)}, f32[512,1]{1,0:T(8,128)S(1)}, bf16[2,4,256,128]{3,2,1,0:T(8,128)(2,1)S(1)}, bf16[2,512,128]{2,1,0:T(8,128)(2...) custom-call(s32[1,3]{1,0:T(1,128)S(1)} %copy-done.43, bf16[512,1024]{1,0:T(8,128)(2,1)S(1)} %copy-done, ...), custom_call_target="tpu_custom_call" | custom-call | tf_op jit(solution)/shard_map/attend/pallas_call | solution.py:736
  11.2 3.0 %collective-permute-start = (bf16[512,256]{1,0:T(8,128)(2,1)S(1)}, bf16[512,256]{1,0:T(8,128)(2,1)S(1)}, u32[]{:S(2)}, u32[]{:S(2)}) collective-permute-start(bf16[512,256]{1,0:T(8,128)(2,1)S(1)} %get-tuple-element.34.refs_6_), channel_id=1, source_target_pairs={{0,1},{1,0},{2,3},{3,2},{4,5},{5,4},{6,7},{7,6},{8,9},{9,8},{10,11... | collective-permute-start | bytes 786440 | tf_op jit(solution)/shard_map/ppermute | solution.py:342
  14.2 2.6 collective-permute-start.1
  16.8 1.5 collective-permute-start.13
  18.3 1.5 collective-permute-start.14
  20.3 5.7 %collective-permute-done.refs_7_ = bf16[512,256]{1,0:T(8,128)(2,1)S(1)} collective-permute-done((bf16[512,256]{1,0:T(8,128)(2,1)S(1)}, bf16[512,256]{1,0:T(8,128)(2,1)S(1)}, u32[]{:S(2)}, u32[]{:S(2)}) %collective-permute-start) | collective-permute-done | bytes 262176 | tf_op jit(solution)/shard_map/ppermute | solution.py:342
  26.7 1.8 collective-permute-done.1.refs_8_
  29.7 1.6 collective-permute-start.3
  32.4 1.5 collective-permute-start.7
  33.9 15.1 %collective-permute-done.2.refs_9_ = bf16[512,256]{1,0:T(8,128)(2,1)S(1)} collective-permute-done((bf16[512,256]{1,0:T(8,128)(2,1)S(1)}, bf16[512,256]{1,0:T(8,128)(2,1)S(1)}, u32[]{:S(2)}, u32[]{:S(2)}) %collective-permute-start.2) | collective-permute-done | bytes 262176 | tf_op jit(solution)/shard_map/ppermute | solution.py:342
  49.7 1.5 collective-permute-start.8
  51.3 6.7 %collective-permute-done.3.refs_11_ = bf16[256,1024]{1,0:T(8,128)(2,1)S(1)} collective-permute-done((bf16[256,1024]{1,0:T(8,128)(2,1)S(1)}, bf16[256,1024]{1,0:T(8,128)(2,1)S(1)}, u32[]{:S(2)}, u32[]{:S(2)}) %collective-permute-start.3) | collective-permute-done | bytes 524320 | tf_op jit(solution)/shard_map/ppermute | solution.py:342
  58.7 1.6 collective-permute-start.15
  63.2 2.0 collective-permute-done.15.refs_25_
  70.1 1.7 constant_dynamic-update-slice_fusion.4
  72.5 4.9 %collective-permute-done.5.refs_13_ = bf16[256,1024]{1,0:T(8,128)(2,1)} collective-permute-done((bf16[256,1024]{1,0:T(8,128)(2,1)}, bf16[256,1024]{1,0:T(8,128)(2,1)}, u32[]{:S(2)}, u32[]{:S(2)}) %collective-permute-start.5) | collective-permute-done | bytes 524320 | tf_op jit(solution)/shard_map/ppermute | solution.py:342
  84.2 18.3 %middle.1 = (f32[128,1024]{1,0:T(8,128)S(1)}, bf16[128,1024]{1,0:T(8,128)(2,1)}, bf16[128,1024]{1,0:T(8,128)(2,1)S(1)}, bf16[128,1024]{1,0:T(8,128)(2,1)}, f32[1...) custom-call(s32[2]{0:T(128)S(1)} %pad_add_fusion.refs_0_, ...), custom_call_target="tpu_custom_call" | custom-call | tf_op jit(solution)/shard_map/middle/pallas_call | solution.py:757
  105.0 1.7 collective-permute-start.20
  106.9 6.8 %collective-permute-done.21 = bf16[128,1024]{1,0:T(8,128)(2,1)S(1)} collective-permute-done((bf16[128,1024]{1,0:T(8,128)(2,1)}, bf16[128,1024]{1,0:T(8,128)(2,1)S(1)}, u32[]{:S(2)}, u32[]{:S(2)}) %collective-permute-start.21) | collective-permute-done | bytes 262176 | tf_op jit(solution)/shard_map/ppermute | solution.py:342
  115.2 3.2 %fusion.16 = f32[512,1024]{1,0:T(8,128)S(1)} fusion(bf16[512,1024]{1,0:T(8,128)(2,1)} %get-tuple-element.36, bf16[1024,1024]{1,0:T(8,128)(2,1)} %constant_dynamic-update-slice_fusion), kind=kOutput, calls=%fused_computation.72 | convolution fusion | flops 1073741824 | bytes 5242880 | tf_op jit(solution)/shard_map/dot_general | solution.py:405
  118.4 11.5 %collective-permute-done.22 = bf16[128,1024]{1,0:T(8,128)(2,1)S(1)} collective-permute-done((bf16[128,1024]{1,0:T(8,128)(2,1)S(1)}, bf16[128,1024]{1,0:T(8,128)(2,1)S(1)}, u32[]{:S(2)}, u32[]{:S(2)}) %collective-permute-start.22) | collective-permute-done | bytes 262176 | tf_op jit(solution)/shard_map/ppermute | solution.py:342
  134.5 5.8 %collective-permute-done.23.refs_12_ = bf16[128,1024]{1,0:T(8,128)(2,1)S(1)} collective-permute-done((bf16[128,1024]{1,0:T(8,128)(2,1)S(1)}, bf16[128,1024]{1,0:T(8,128)(2,1)S(1)}, u32[]{:S(2)}, u32[]{:S(2)}) %collective-permute-start.23) | collective-permute-done | bytes 262176 | tf_op jit(solution)/shard_map/ppermute | solution.py:342
  141.6 7.0 %collective-permute-done.24.refs_13_ = bf16[128,1024]{1,0:T(8,128)(2,1)S(1)} collective-permute-done((bf16[128,1024]{1,0:T(8,128)(2,1)S(1)}, bf16[128,1024]{1,0:T(8,128)(2,1)S(1)}, u32[]{:S(2)}, u32[]{:S(2)}) %collective-permute-start.24) | collective-permute-done | bytes 262176 | tf_op jit(solution)/shard_map/ppermute | solution.py:342
  148.8 7.1 %attend_back.1 = (f32[128,1024]{1,0:T(8,128)S(1)}, bf16[128,1024]{1,0:T(8,128)(2,1)S(1)}, bf16[128,1024]{1,0:T(8,128)(2,1)S(1)}, bf16[128,1024]{1,0:T(8,128)(2,1...) custom-call(s32[2]{0:T(128)S(1)} %pad_add_fusion.refs_0_, ...), custom_call_target="tpu_custom_call" | custom-call | tf_op jit(solution)/shard_map/attend_back/pallas_call | solution.py:818
  156.0 2.1 collective-permute-start.33
  159.4 4.4 %collective-permute-done.38 = f32[10,1024]{1,0:T(8,128)S(1)} collective-permute-done((f32[10,1024]{1,0:T(8,128)S(1)}, f32[10,1024]{1,0:T(8,128)S(1)}, u32[]{:S(2)}, u32[]{:S(2)}) %collective-permute-start.38) | collective-permute-done | bytes 40992 | tf_op jit(solution)/shard_map/ppermute | solution.py:342
  163.8 2.5 collective-permute-start.39
  166.4 2.7 collective-permute-done.39
  172.8 2.2 collective-permute-done.41
  176.4 3.0 %collective-permute-done.42 = f32[10,1024]{1,0:T(8,128)S(1)} collective-permute-done((f32[10,1024]{1,0:T(8,128)S(1)}, f32[10,1024]{1,0:T(8,128)S(1)}, u32[]{:S(2)}, u32[]{:S(2)}) %collective-permute-start.42) | collective-permute-done | bytes 40992 | tf_op jit(solution)/shard_map/ppermute | solution.py:342
  181.8 1.6 collective-permute-start.57
  184.3 2.0 collective-permute-start.25
  186.5 2.0 collective-permute-start.32
  188.4 2.5 collective-permute-done.57
  190.9 3.1 %collective-permute-done.56 = bf16[128,1024]{1,0:T(8,128)(2,1)S(1)} collective-permute-done((bf16[128,1024]{1,0:T(8,128)(2,1)S(1)}, bf16[128,1024]{1,0:T(8,128)(2,1)S(1)}, u32[]{:S(2)}, u32[]{:S(2)}) %collective-permute-start.56) | collective-permute-done | bytes 262176 | tf_op jit(solution)/shard_map/ppermute | solution.py:342
  194.0 2.4 collective-permute-start.27
  197.9 16.6 %collective-permute-done.27 = bf16[128,1024]{1,0:T(8,128)(2,1)S(1)} collective-permute-done((bf16[128,1024]{1,0:T(8,128)(2,1)S(1)}, bf16[128,1024]{1,0:T(8,128)(2,1)S(1)}, u32[]{:S(2)}, u32[]{:S(2)}) %collective-permute-start.27) | collective-permute-done | bytes 262176 | tf_op jit(solution)/shard_map/ppermute | solution.py:342
  215.8 1.8 collective-permute-done.34
  218.9 1.9 collective-permute-done.48
  220.9 1.6 collective-permute-start.49
  222.9 8.8 %collective-permute-done.28 = bf16[128,1024]{1,0:T(8,128)(2,1)S(1)} collective-permute-done((bf16[128,1024]{1,0:T(8,128)(2,1)S(1)}, bf16[128,1024]{1,0:T(8,128)(2,1)S(1)}, u32[]{:S(2)}, u32[]{:S(2)}) %collective-permute-start.28) | collective-permute-done | bytes 262176 | tf_op jit(solution)/shard_map/ppermute | solution.py:342
  232.9 4.4 %collective-permute-done.35 = bf16[128,1024]{1,0:T(8,128)(2,1)S(1)} collective-permute-done((bf16[128,1024]{1,0:T(8,128)(2,1)S(1)}, bf16[128,1024]{1,0:T(8,128)(2,1)S(1)}, u32[]{:S(2)}, u32[]{:S(2)}) %collective-permute-start.35) | collective-permute-done | bytes 262176 | tf_op jit(solution)/shard_map/ppermute | solution.py:342
  237.2 3.6 %collective-permute-done.36 = bf16[128,1024]{1,0:T(8,128)(2,1)S(1)} collective-permute-done((bf16[128,1024]{1,0:T(8,128)(2,1)S(1)}, bf16[128,1024]{1,0:T(8,128)(2,1)S(1)}, u32[]{:S(2)}, u32[]{:S(2)}) %collective-permute-start.36) | collective-permute-done | bytes 262176 | tf_op jit(solution)/shard_map/ppermute | solution.py:342
  246.4 1.9 collective-permute-start.52
  248.4 18.8 %collective-permute-done.45 = bf16[512,512]{0,1:T(8,128)(2,1)S(1)} collective-permute-done((bf16[512,512]{0,1:T(8,128)(2,1)S(1)}, bf16[512,512]{0,1:T(8,128)(2,1)S(1)}, u32[]{:S(2)}, u32[]{:S(2)}) %collective-permute-start.45) | collective-permute-done | bytes 524320 | tf_op jit(solution)/shard_map/ppermute | solution.py:342
  268.7 4.7 %collective-permute-done.54 = bf16[256,1024]{1,0:T(8,128)(2,1)S(1)} collective-permute-done((bf16[256,1024]{1,0:T(8,128)(2,1)S(1)}, bf16[256,1024]{1,0:T(8,128)(2,1)S(1)}, u32[]{:S(2)}, u32[]{:S(2)}) %collective-permute-start.54) | collective-permute-done | bytes 524320 | tf_op jit(solution)/shard_map/ppermute | solution.py:342
  275.7 2.4 maximum_convert_fusion
  (243 shorter events, 59.5 us)
Async XLA Ops:
  11.2 14.8 %collective-permute-start = (bf16[512,256]{1,0:T(8,128)(2,1)S(1)}, bf16[512,256]{1,0:T(8,128)(2,1)S(1)}, u32[]{:S(2)}, u32[]{:S(2)}) collective-permute-start(bf16[512,256]{1,0:T(8,128)(2,1)S(1)} %get-tuple-element.34.refs_6_), channel_id=1, source_target_pairs={{0,1},{1,0},{2,3},{3,2},{4,5},{5,4},{6,7},{7,6},{8,9},{9,8},{10,11... | collective-permute-start | bytes 786440 | tf_op jit(solution)/shard_map/ppermute | solution.py:342
  14.2 14.3 %collective-permute-start.1 = (bf16[512,256]{1,0:T(8,128)(2,1)S(1)}, bf16[512,256]{1,0:T(8,128)(2,1)S(1)}, u32[]{:S(2)}, u32[]{:S(2)}) collective-permute-start(bf16[512,256]{1,0:T(8,128)(2,1)S(1)} %get-tuple-element.34.refs_6_), channel_id=1, source_target_pairs={{0,2},{1,3},{2,0},{3,1},{4,6},{5,7},{6,4},{7,5},{8,10},{9,11},{10,... | collective-permute-start | bytes 786440 | tf_op jit(solution)/shard_map/ppermute | solution.py:342
  16.8 12.9 %collective-permute-start.13 = (bf16[128,1024]{1,0:T(8,128)(2,1)S(1)}, bf16[128,1024]{1,0:T(8,128)(2,1)S(1)}, u32[]{:S(2)}, u32[]{:S(2)}) collective-permute-start(bf16[128,1024]{1,0:T(8,128)(2,1)S(1)} %bitcast.31), channel_id=1, source_target_pairs={{0,8},{4,12},{8,0},{12,4},{16,24},{20,28},{24,16},{28,20},{1,9},{5... | collective-permute-start | bytes 786440 | tf_op jit(solution)/shard_map/ppermute | solution.py:342
  18.3 13.0 %collective-permute-start.14 = (bf16[128,1024]{1,0:T(8,128)(2,1)S(1)}, bf16[128,1024]{1,0:T(8,128)(2,1)S(1)}, u32[]{:S(2)}, u32[]{:S(2)}) collective-permute-start(bf16[128,1024]{1,0:T(8,128)(2,1)S(1)} %bitcast.32), channel_id=1, source_target_pairs={{0,16},{4,20},{8,24},{12,28},{16,0},{20,4},{24,8},{28,12},{1,17},{... | collective-permute-start | bytes 786440 | tf_op jit(solution)/shard_map/ppermute | solution.py:342
  19.8 29.9 %collective-permute-start.6 = (bf16[256,1024]{1,0:T(8,128)(2,1)}, bf16[256,1024]{1,0:T(8,128)(2,1)}, u32[]{:S(2)}, u32[]{:S(2)}) collective-permute-start(bf16[256,1024]{1,0:T(8,128)(2,1)} %bitcast.5.refs_14_), channel_id=1, source_target_pairs={{0,8},{4,12},{8,0},{12,4},{16,24},{20,28},{24,16},{28,20},{1,9},{5... | collective-permute-start | bytes 1572872 | tf_op jit(solution)/shard_map/ppermute | solution.py:342
  28.5 20.5 %collective-permute-start.2 = (bf16[512,256]{1,0:T(8,128)(2,1)S(1)}, bf16[512,256]{1,0:T(8,128)(2,1)S(1)}, u32[]{:S(2)}, u32[]{:S(2)}) collective-permute-start(bf16[512,256]{1,0:T(8,128)(2,1)S(1)} %collective-permute-done.1.refs_8_), channel_id=1, source_target_pairs={{0,1},{1,0},{2,3},{3,2},{4,5},{5,4},{6,7},{7,6},{8,9},{9,8},{10,11... | collective-permute-start | bytes 786440 | tf_op jit(solution)/shard_map/ppermute | solution.py:342
  29.7 28.2 %collective-permute-start.3 = (bf16[256,1024]{1,0:T(8,128)(2,1)S(1)}, bf16[256,1024]{1,0:T(8,128)(2,1)S(1)}, u32[]{:S(2)}, u32[]{:S(2)}) collective-permute-start(bf16[256,1024]{1,0:T(8,128)(2,1)S(1)} %copy-done.4), channel_id=1, source_target_pairs={{0,1},{1,0},{2,3},{3,2},{4,5},{5,4},{6,7},{7,6},{8,9},{9,8},{10,11... | collective-permute-start | bytes 1572872 | tf_op jit(solution)/shard_map/ppermute | solution.py:342
  31.3 29.1 %collective-permute-start.4 = (bf16[256,1024]{1,0:T(8,128)(2,1)S(1)}, bf16[256,1024]{1,0:T(8,128)(2,1)S(1)}, u32[]{:S(2)}, u32[]{:S(2)}) collective-permute-start(bf16[256,1024]{1,0:T(8,128)(2,1)S(1)} %copy-done.4), channel_id=1, source_target_pairs={{0,2},{1,3},{2,0},{3,1},{4,6},{5,7},{6,4},{7,5},{8,10},{9,11},{10,... | collective-permute-start | bytes 1572872 | tf_op jit(solution)/shard_map/ppermute | solution.py:342
  32.4 28.8 %collective-permute-start.7 = (bf16[256,1024]{1,0:T(8,128)(2,1)}, bf16[256,1024]{1,0:T(8,128)(2,1)S(1)}, u32[]{:S(2)}, u32[]{:S(2)}) collective-permute-start(bf16[256,1024]{1,0:T(8,128)(2,1)} %bitcast.5.refs_14_), channel_id=1, source_target_pairs={{0,16},{4,20},{8,24},{12,28},{16,0},{20,4},{24,8},{28,12},{1,17},{... | collective-permute-start | bytes 1572872 | tf_op jit(solution)/shard_map/ppermute | solution.py:342
  49.7 12.9 %collective-permute-start.9 = (bf16[256,1024]{1,0:T(8,128)(2,1)}, bf16[256,1024]{1,0:T(8,128)(2,1)}, u32[]{:S(2)}, u32[]{:S(2)}) collective-permute-start(bf16[256,1024]{1,0:T(8,128)(2,1)} %bitcast.5.refs_14_), channel_id=1, source_target_pairs={{0,4},{4,0},{8,12},{12,8},{16,20},{20,16},{24,28},{28,24},{1,5},{5... | collective-permute-start | bytes 1572872 | tf_op jit(solution)/shard_map/ppermute | solution.py:342
  49.7 15.5 %collective-permute-start.8 = (bf16[256,1024]{1,0:T(8,128)(2,1)}, bf16[256,1024]{1,0:T(8,128)(2,1)}, u32[]{:S(2)}, u32[]{:S(2)}) collective-permute-start(bf16[256,1024]{1,0:T(8,128)(2,1)} %collective-permute-done.6.refs_15_), channel_id=1, source_target_pairs={{0,16},{4,20},{8,24},{12,28},{16,0},{20,4},{24,8},{28,12},{1,17},{... | collective-permute-start | bytes 1572872 | tf_op jit(solution)/shard_map/ppermute | solution.py:342
  62.0 7.3 %collective-permute-start.18 = (bf16[128,1024]{1,0:T(8,128)(2,1)S(1)}, bf16[128,1024]{1,0:T(8,128)(2,1)S(1)}, u32[]{:S(2)}, u32[]{:S(2)}) collective-permute-start(bf16[128,1024]{1,0:T(8,128)(2,1)S(1)} %collective-permute-done.14.refs_24_), channel_id=1, source_target_pairs={{0,4},{4,0},{8,12},{12,8},{16,20},{20,16},{24,28},{28,24},{1,5},{5... | collective-permute-start | bytes 786440 | tf_op jit(solution)/shard_map/ppermute | solution.py:342
  62.7 14.7 %collective-permute-start.10 = (bf16[256,1024]{1,0:T(8,128)(2,1)}, bf16[256,1024]{1,0:T(8,128)(2,1)}, u32[]{:S(2)}, u32[]{:S(2)}) collective-permute-start(bf16[256,1024]{1,0:T(8,128)(2,1)} %collective-permute-done.6.refs_15_), channel_id=1, source_target_pairs={{0,4},{4,0},{8,12},{12,8},{16,20},{20,16},{24,28},{28,24},{1,5},{5... | collective-permute-start | bytes 1572872 | tf_op jit(solution)/shard_map/ppermute | solution.py:342
  65.2 12.2 %collective-permute-start.5 = (bf16[256,1024]{1,0:T(8,128)(2,1)}, bf16[256,1024]{1,0:T(8,128)(2,1)}, u32[]{:S(2)}, u32[]{:S(2)}) collective-permute-start(bf16[256,1024]{1,0:T(8,128)(2,1)} %copy-done.24), channel_id=1, source_target_pairs={{0,1},{1,0},{2,3},{3,2},{4,5},{5,4},{6,7},{7,6},{8,9},{9,8},{10,11... | collective-permute-start | bytes 1572872 | tf_op jit(solution)/shard_map/ppermute | solution.py:342
  65.2 12.2 %collective-permute-start.11 = (bf16[256,1024]{1,0:T(8,128)(2,1)}, bf16[256,1024]{1,0:T(8,128)(2,1)}, u32[]{:S(2)}, u32[]{:S(2)}) collective-permute-start(bf16[256,1024]{1,0:T(8,128)(2,1)} %copy-done.26), channel_id=1, source_target_pairs={{0,4},{4,0},{8,12},{12,8},{16,20},{20,16},{24,28},{28,24},{1,5},{5... | collective-permute-start | bytes 1572872 | tf_op jit(solution)/shard_map/ppermute | solution.py:342
  65.3 12.1 %collective-permute-start.12 = (bf16[256,1024]{1,0:T(8,128)(2,1)}, bf16[256,1024]{1,0:T(8,128)(2,1)}, u32[]{:S(2)}, u32[]{:S(2)}) collective-permute-start(bf16[256,1024]{1,0:T(8,128)(2,1)} %collective-permute-done.8.refs_17_), channel_id=1, source_target_pairs={{0,4},{4,0},{8,12},{12,8},{16,20},{20,16},{24,28},{28,24},{1,5},{5... | collective-permute-start | bytes 1572872 | tf_op jit(solution)/shard_map/ppermute | solution.py:342
  102.5 11.2 %collective-permute-start.21 = (bf16[128,1024]{1,0:T(8,128)(2,1)}, bf16[128,1024]{1,0:T(8,128)(2,1)S(1)}, u32[]{:S(2)}, u32[]{:S(2)}) collective-permute-start(bf16[128,1024]{1,0:T(8,128)(2,1)} %get-tuple-element.41), channel_id=1, source_target_pairs={{0,1},{1,0},{2,3},{3,2},{4,5},{5,4},{6,7},{7,6},{8,9},{9,8},{10,11... | collective-permute-start | bytes 786440 | tf_op jit(solution)/shard_map/ppermute | solution.py:342
  105.0 13.4 %collective-permute-start.20 = (bf16[128,1024]{1,0:T(8,128)(2,1)}, bf16[128,1024]{1,0:T(8,128)(2,1)S(1)}, u32[]{:S(2)}, u32[]{:S(2)}) collective-permute-start(bf16[128,1024]{1,0:T(8,128)(2,1)} %get-tuple-element.39), channel_id=1, source_target_pairs={{0,1},{1,0},{2,3},{3,2},{4,5},{5,4},{6,7},{7,6},{8,9},{9,8},{10,11... | collective-permute-start | bytes 786440 | tf_op jit(solution)/shard_map/ppermute | solution.py:342
  114.8 15.2 %collective-permute-start.22 = (bf16[128,1024]{1,0:T(8,128)(2,1)S(1)}, bf16[128,1024]{1,0:T(8,128)(2,1)S(1)}, u32[]{:S(2)}, u32[]{:S(2)}) collective-permute-start(bf16[128,1024]{1,0:T(8,128)(2,1)S(1)} %add_convert_fusion.10), channel_id=1, source_target_pairs={{0,2},{1,3},{2,0},{3,1},{4,6},{5,7},{6,4},{7,5},{8,10},{9,11},{10,... | collective-permute-start | bytes 786440 | tf_op jit(solution)/shard_map/ppermute | solution.py:342
  130.5 9.7 %collective-permute-start.23 = (bf16[128,1024]{1,0:T(8,128)(2,1)S(1)}, bf16[128,1024]{1,0:T(8,128)(2,1)S(1)}, u32[]{:S(2)}, u32[]{:S(2)}) collective-permute-start(bf16[128,1024]{1,0:T(8,128)(2,1)S(1)} %get-tuple-element.63.refs_10_), channel_id=1, source_target_pairs={{0,2},{1,3},{2,0},{3,1},{4,6},{5,7},{6,4},{7,5},{8,10},{9,11},{10,... | collective-permute-start | bytes 786440 | tf_op jit(solution)/shard_map/ppermute | solution.py:342
  133.3 15.5 %collective-permute-start.31 = (bf16[128,1024]{1,0:T(8,128)(2,1)S(1)}, bf16[128,1024]{1,0:T(8,128)(2,1)S(1)}, u32[]{:S(2)}, u32[]{:S(2)}) collective-permute-start(bf16[128,1024]{1,0:T(8,128)(2,1)S(1)} %get-tuple-element.63.refs_10_), channel_id=1, source_target_pairs={{0,1},{1,0},{2,3},{3,2},{4,5},{5,4},{6,7},{7,6},{8,9},{9,8},{10,11... | collective-permute-start | bytes 786440 | tf_op jit(solution)/shard_map/ppermute | solution.py:342
  140.3 8.3 %collective-permute-start.24 = (bf16[128,1024]{1,0:T(8,128)(2,1)S(1)}, bf16[128,1024]{1,0:T(8,128)(2,1)S(1)}, u32[]{:S(2)}, u32[]{:S(2)}) collective-permute-start(bf16[128,1024]{1,0:T(8,128)(2,1)S(1)} %collective-permute-done.23.refs_12_), channel_id=1, source_target_pairs={{0,1},{1,0},{2,3},{3,2},{4,5},{5,4},{6,7},{7,6},{8,9},{9,8},{10,11... | collective-permute-start | bytes 786440 | tf_op jit(solution)/shard_map/ppermute | solution.py:342
  141.0 101.1 %collective-permute-start.51 = (bf16[1024,1024]{1,0:T(8,128)(2,1)S(1)}, bf16[1024,1024]{1,0:T(8,128)(2,1)S(1)}, u32[]{:S(2)}, u32[]{:S(2)}) collective-permute-start(bf16[1024,1024]{1,0:T(8,128)(2,1)S(1)} %convolution_convert_fusion), channel_id=1, source_target_pairs={{0,4},{4,0},{8,12},{12,8},{16,20},{20,16},{24,28},{28,24},{1,5},{5... | collective-permute-start | bytes 6291464 | tf_op jit(solution)/shard_map/ppermute | solution.py:342
  141.1 29.5 %collective-permute-start.55 = (bf16[512,1024]{1,0:T(8,128)(2,1)S(1)}, bf16[512,1024]{1,0:T(8,128)(2,1)S(1)}, u32[]{:S(2)}, u32[]{:S(2)}) collective-permute-start(bf16[512,1024]{1,0:T(8,128)(2,1)S(1)} %convolution_convert_fusion.1), channel_id=1, source_target_pairs={{0,4},{4,0},{8,12},{12,8},{16,20},{20,16},{24,28},{28,24},{1,5},{5... | collective-permute-start | bytes 3145736 | tf_op jit(solution)/shard_map/ppermute | solution.py:342
  148.7 34.8 %collective-permute-start.26 = (bf16[128,1024]{1,0:T(8,128)(2,1)S(1)}, bf16[128,1024]{1,0:T(8,128)(2,1)S(1)}, u32[]{:S(2)}, u32[]{:S(2)}) collective-permute-start(bf16[128,1024]{1,0:T(8,128)(2,1)S(1)} %get-tuple-element.69), channel_id=1, source_target_pairs={{0,1},{1,0},{2,3},{3,2},{4,5},{5,4},{6,7},{7,6},{8,9},{9,8},{10,11... | collective-permute-start | bytes 786440 | tf_op jit(solution)/shard_map/ppermute | solution.py:342
  156.0 25.8 %collective-permute-start.33 = (bf16[128,1024]{1,0:T(8,128)(2,1)S(1)}, bf16[128,1024]{1,0:T(8,128)(2,1)S(1)}, u32[]{:S(2)}, u32[]{:S(2)}) collective-permute-start(bf16[128,1024]{1,0:T(8,128)(2,1)S(1)} %get-tuple-element.50), channel_id=1, source_target_pairs={{0,1},{1,0},{2,3},{3,2},{4,5},{5,4},{6,7},{7,6},{8,9},{9,8},{10,11... | collective-permute-start | bytes 786440 | tf_op jit(solution)/shard_map/ppermute | solution.py:342
  170.4 13.9 %collective-permute-start.47 = (bf16[128,1024]{1,0:T(8,128)(2,1)S(1)}, bf16[128,1024]{1,0:T(8,128)(2,1)S(1)}, u32[]{:S(2)}, u32[]{:S(2)}) collective-permute-start(bf16[128,1024]{1,0:T(8,128)(2,1)S(1)} %select_convert_fusion.1), channel_id=1, source_target_pairs={{0,4},{4,0},{8,12},{12,8},{16,20},{20,16},{24,28},{28,24},{1,5},{5... | collective-permute-start | bytes 786440 | tf_op jit(solution)/shard_map/ppermute | solution.py:342
  181.8 9.1 %collective-permute-start.57 = (bf16[128,1024]{1,0:T(8,128)(2,1)S(1)}, bf16[128,1024]{1,0:T(8,128)(2,1)S(1)}, u32[]{:S(2)}, u32[]{:S(2)}) collective-permute-start(bf16[128,1024]{1,0:T(8,128)(2,1)S(1)} %get-tuple-element.72), channel_id=1, source_target_pairs={{0,8},{4,12},{8,0},{12,4},{16,24},{20,28},{24,16},{28,20},{1,9},{5... | collective-permute-start | bytes 786440 | tf_op jit(solution)/shard_map/ppermute | solution.py:342
  183.5 10.5 %collective-permute-start.56 = (bf16[128,1024]{1,0:T(8,128)(2,1)S(1)}, bf16[128,1024]{1,0:T(8,128)(2,1)S(1)}, u32[]{:S(2)}, u32[]{:S(2)}) collective-permute-start(bf16[128,1024]{1,0:T(8,128)(2,1)S(1)} %get-tuple-element.70), channel_id=1, source_target_pairs={{0,24},{4,28},{8,16},{12,20},{16,8},{20,12},{24,0},{28,4},{1,25},{... | collective-permute-start | bytes 786440 | tf_op jit(solution)/shard_map/ppermute | solution.py:342
  184.3 13.0 %collective-permute-start.25 = (bf16[128,1024]{1,0:T(8,128)(2,1)S(1)}, bf16[128,1024]{1,0:T(8,128)(2,1)S(1)}, u32[]{:S(2)}, u32[]{:S(2)}) collective-permute-start(bf16[128,1024]{1,0:T(8,128)(2,1)S(1)} %get-tuple-element.68), channel_id=1, source_target_pairs={{0,1},{1,0},{2,3},{3,2},{4,5},{5,4},{6,7},{7,6},{8,9},{9,8},{10,11... | collective-permute-start | bytes 786440 | tf_op jit(solution)/shard_map/ppermute | solution.py:342
  186.5 29.3 %collective-permute-start.32 = (bf16[128,1024]{1,0:T(8,128)(2,1)S(1)}, bf16[128,1024]{1,0:T(8,128)(2,1)S(1)}, u32[]{:S(2)}, u32[]{:S(2)}) collective-permute-start(bf16[128,1024]{1,0:T(8,128)(2,1)S(1)} %get-tuple-element.48), channel_id=1, source_target_pairs={{0,1},{1,0},{2,3},{3,2},{4,5},{5,4},{6,7},{7,6},{8,9},{9,8},{10,11... | collective-permute-start | bytes 786440 | tf_op jit(solution)/shard_map/ppermute | solution.py:342
  190.9 30.0 %collective-permute-start.43 = (bf16[512,512]{0,1:T(8,128)(2,1)S(1)}, bf16[512,512]{0,1:T(8,128)(2,1)S(1)}, u32[]{:S(2)}, u32[]{:S(2)}) collective-permute-start(bf16[512,512]{0,1:T(8,128)(2,1)S(1)} %select_convert_fusion), channel_id=1, source_target_pairs={{0,4},{4,0},{8,12},{12,8},{16,20},{20,16},{24,28},{28,24},{1,5},{5... | collective-permute-start | bytes 1572872 | tf_op jit(solution)/shard_map/ppermute | solution.py:342
  194.0 20.5 %collective-permute-start.27 = (bf16[128,1024]{1,0:T(8,128)(2,1)S(1)}, bf16[128,1024]{1,0:T(8,128)(2,1)S(1)}, u32[]{:S(2)}, u32[]{:S(2)}) collective-permute-start(bf16[128,1024]{1,0:T(8,128)(2,1)S(1)} %add_convert_fusion.9), channel_id=1, source_target_pairs={{0,2},{1,3},{2,0},{3,1},{4,6},{5,7},{6,4},{7,5},{8,10},{9,11},{10,... | collective-permute-start | bytes 786440 | tf_op jit(solution)/shard_map/ppermute | solution.py:342
  197.3 20.2 %collective-permute-start.34 = (bf16[128,1024]{1,0:T(8,128)(2,1)S(1)}, bf16[128,1024]{1,0:T(8,128)(2,1)S(1)}, u32[]{:S(2)}, u32[]{:S(2)}) collective-permute-start(bf16[128,1024]{1,0:T(8,128)(2,1)S(1)} %add_convert_fusion.7), channel_id=1, source_target_pairs={{0,2},{1,3},{2,0},{3,1},{4,6},{5,7},{6,4},{7,5},{8,10},{9,11},{10,... | collective-permute-start | bytes 786440 | tf_op jit(solution)/shard_map/ppermute | solution.py:342
  215.7 15.9 %collective-permute-start.28 = (bf16[128,1024]{1,0:T(8,128)(2,1)S(1)}, bf16[128,1024]{1,0:T(8,128)(2,1)S(1)}, u32[]{:S(2)}, u32[]{:S(2)}) collective-permute-start(bf16[128,1024]{1,0:T(8,128)(2,1)S(1)} %get-tuple-element.62), channel_id=1, source_target_pairs={{0,1},{1,0},{2,3},{3,2},{4,5},{5,4},{6,7},{7,6},{8,9},{9,8},{10,11... | collective-permute-start | bytes 786440 | tf_op jit(solution)/shard_map/ppermute | solution.py:342
  217.6 15.2 %collective-permute-start.29 = (bf16[128,1024]{1,0:T(8,128)(2,1)S(1)}, bf16[128,1024]{1,0:T(8,128)(2,1)S(1)}, u32[]{:S(2)}, u32[]{:S(2)}) collective-permute-start(bf16[128,1024]{1,0:T(8,128)(2,1)S(1)} %get-tuple-element.62), channel_id=1, source_target_pairs={{0,2},{1,3},{2,0},{3,1},{4,6},{5,7},{6,4},{7,5},{8,10},{9,11},{10,... | collective-permute-start | bytes 786440 | tf_op jit(solution)/shard_map/ppermute | solution.py:342
  220.8 16.4 %collective-permute-start.35 = (bf16[128,1024]{1,0:T(8,128)(2,1)S(1)}, bf16[128,1024]{1,0:T(8,128)(2,1)S(1)}, u32[]{:S(2)}, u32[]{:S(2)}) collective-permute-start(bf16[128,1024]{1,0:T(8,128)(2,1)S(1)} %get-tuple-element.60), channel_id=1, source_target_pairs={{0,1},{1,0},{2,3},{3,2},{4,5},{5,4},{6,7},{7,6},{8,9},{9,8},{10,11... | collective-permute-start | bytes 786440 | tf_op jit(solution)/shard_map/ppermute | solution.py:342
  220.9 10.7 %collective-permute-start.49 = (bf16[128,1024]{1,0:T(8,128)(2,1)S(1)}, bf16[128,1024]{1,0:T(8,128)(2,1)S(1)}, u32[]{:S(2)}, u32[]{:S(2)}) collective-permute-start(bf16[128,1024]{1,0:T(8,128)(2,1)S(1)} %add_convert_fusion.4), channel_id=1, source_target_pairs={{0,8},{4,12},{8,0},{12,4},{16,24},{20,28},{24,16},{28,20},{1,9},{5... | collective-permute-start | bytes 786440 | tf_op jit(solution)/shard_map/ppermute | solution.py:342
  231.7 9.2 %collective-permute-start.36 = (bf16[128,1024]{1,0:T(8,128)(2,1)S(1)}, bf16[128,1024]{1,0:T(8,128)(2,1)S(1)}, u32[]{:S(2)}, u32[]{:S(2)}) collective-permute-start(bf16[128,1024]{1,0:T(8,128)(2,1)S(1)} %get-tuple-element.60), channel_id=1, source_target_pairs={{0,2},{1,3},{2,0},{3,1},{4,6},{5,7},{6,4},{7,5},{8,10},{9,11},{10,... | collective-permute-start | bytes 786440 | tf_op jit(solution)/shard_map/ppermute | solution.py:342
  231.7 9.2 %collective-permute-start.44 = (bf16[512,512]{0,1:T(8,128)(2,1)S(1)}, bf16[512,512]{0,1:T(8,128)(2,1)S(1)}, u32[]{:S(2)}, u32[]{:S(2)}) collective-permute-start(bf16[512,512]{0,1:T(8,128)(2,1)S(1)} %add_convert_fusion.2), channel_id=1, source_target_pairs={{0,8},{4,12},{8,0},{12,4},{16,24},{20,28},{24,16},{28,20},{1,9},{5... | collective-permute-start | bytes 1572872 | tf_op jit(solution)/shard_map/ppermute | solution.py:342
  232.7 9.3 %collective-permute-start.50 = (bf16[128,1024]{1,0:T(8,128)(2,1)S(1)}, bf16[128,1024]{1,0:T(8,128)(2,1)S(1)}, u32[]{:S(2)}, u32[]{:S(2)}) collective-permute-start(bf16[128,1024]{1,0:T(8,128)(2,1)S(1)} %add_convert_fusion.3), channel_id=1, source_target_pairs={{0,4},{4,0},{8,12},{12,8},{16,20},{20,16},{24,28},{28,24},{1,5},{5... | collective-permute-start | bytes 786440 | tf_op jit(solution)/shard_map/ppermute | solution.py:342
  237.2 9.2 %collective-permute-start.30 = (bf16[128,1024]{1,0:T(8,128)(2,1)S(1)}, bf16[128,1024]{1,0:T(8,128)(2,1)S(1)}, u32[]{:S(2)}, u32[]{:S(2)}) collective-permute-start(bf16[128,1024]{1,0:T(8,128)(2,1)S(1)} %collective-permute-done.29), channel_id=1, source_target_pairs={{0,1},{1,0},{2,3},{3,2},{4,5},{5,4},{6,7},{7,6},{8,9},{9,8},{10,11... | collective-permute-start | bytes 786440 | tf_op jit(solution)/shard_map/ppermute | solution.py:342
  240.8 26.6 %collective-permute-start.37 = (bf16[128,1024]{1,0:T(8,128)(2,1)S(1)}, bf16[128,1024]{1,0:T(8,128)(2,1)S(1)}, u32[]{:S(2)}, u32[]{:S(2)}) collective-permute-start(bf16[128,1024]{1,0:T(8,128)(2,1)S(1)} %collective-permute-done.36), channel_id=1, source_target_pairs={{0,1},{1,0},{2,3},{3,2},{4,5},{5,4},{6,7},{7,6},{8,9},{9,8},{10,11... | collective-permute-start | bytes 786440 | tf_op jit(solution)/shard_map/ppermute | solution.py:342
  241.1 26.2 %collective-permute-start.45 = (bf16[512,512]{0,1:T(8,128)(2,1)S(1)}, bf16[512,512]{0,1:T(8,128)(2,1)S(1)}, u32[]{:S(2)}, u32[]{:S(2)}) collective-permute-start(bf16[512,512]{0,1:T(8,128)(2,1)S(1)} %add_convert_fusion.1), channel_id=1, source_target_pairs={{0,16},{4,20},{8,24},{12,28},{16,0},{20,4},{24,8},{28,12},{1,17},{... | collective-permute-start | bytes 1572872 | tf_op jit(solution)/shard_map/ppermute | solution.py:342
  243.6 29.8 %collective-permute-start.54 = (bf16[256,1024]{1,0:T(8,128)(2,1)S(1)}, bf16[256,1024]{1,0:T(8,128)(2,1)S(1)}, u32[]{:S(2)}, u32[]{:S(2)}) collective-permute-start(bf16[256,1024]{1,0:T(8,128)(2,1)S(1)} %get-tuple-element.66), channel_id=1, source_target_pairs={{0,16},{4,20},{8,24},{12,28},{16,0},{20,4},{24,8},{28,12},{1,17},{... | collective-permute-start | bytes 1572872 | tf_op jit(solution)/shard_map/ppermute | solution.py:342
  244.7 28.7 %collective-permute-start.53 = (bf16[256,1024]{1,0:T(8,128)(2,1)S(1)}, bf16[256,1024]{1,0:T(8,128)(2,1)S(1)}, u32[]{:S(2)}, u32[]{:S(2)}) collective-permute-start(bf16[256,1024]{1,0:T(8,128)(2,1)S(1)} %get-tuple-element.67), channel_id=1, source_target_pairs={{0,8},{4,12},{8,0},{12,4},{16,24},{20,28},{24,16},{28,20},{1,9},{5... | collective-permute-start | bytes 1572872 | tf_op jit(solution)/shard_map/ppermute | solution.py:342
  246.4 27.0 %collective-permute-start.52 = (bf16[256,1024]{1,0:T(8,128)(2,1)S(1)}, bf16[256,1024]{1,0:T(8,128)(2,1)S(1)}, u32[]{:S(2)}, u32[]{:S(2)}) collective-permute-start(bf16[256,1024]{1,0:T(8,128)(2,1)S(1)} %get-tuple-element.65), channel_id=1, source_target_pairs={{0,24},{4,28},{8,16},{12,20},{16,8},{20,12},{24,0},{28,4},{1,25},{... | collective-permute-start | bytes 1572872 | tf_op jit(solution)/shard_map/ppermute | solution.py:342
  267.4 7.4 %collective-permute-start.46 = (bf16[512,512]{0,1:T(8,128)(2,1)S(1)}, bf16[512,512]{0,1:T(8,128)(2,1)S(1)}, u32[]{:S(2)}, u32[]{:S(2)}) collective-permute-start(bf16[512,512]{0,1:T(8,128)(2,1)S(1)} %add_convert_fusion), channel_id=1, source_target_pairs={{0,4},{4,0},{8,12},{12,8},{16,20},{20,16},{24,28},{28,24},{1,5},{5... | collective-permute-start | bytes 1572872 | tf_op jit(solution)/shard_map/ppermute | solution.py:342
  (63 other events, 663.6 us)

commit v3 on v2

--- a/solution.py
+++ b/solution.py
@@ -335,6 +335,9 @@
 
 LANES = 128
 ROWS = 128
+SMALL_ROWS = 16
+IN_ORDER = (0, 2, 4, 6, 1, 3, 5, 7)
+OUT_ORDER = (0, 4, 2, 6, 1, 5, 3, 7)
 
 
 def exchange(array_in, axis_name, bits):
@@ -345,59 +348,47 @@
 def gather_blocks(own):
     far = exchange(own, "tensor", 2)
     near = exchange(own, "tensor", 1)
+    far, near = lax.optimization_barrier((far, near))
     return [own, near, far, exchange(far, "tensor", 1)]
 
 
-def scatter_sums(parts):
-    relayed = exchange(parts[3], "tensor", 1)
-    far = (parts[2].astype(jnp.float32) + relayed.astype(jnp.float32)).astype(jnp.bfloat16)
+def scatter_parts(parts, relayed):
+    near, far, relayed = lax.optimization_barrier((parts[1], parts[2], relayed))
+    far = (far.astype(jnp.float32) + relayed.astype(jnp.float32)).astype(jnp.bfloat16)
     far = exchange(far, "tensor", 2)
-    near = exchange(parts[1], "tensor", 1)
-    return parts[0] + near.astype(jnp.float32) + far.astype(jnp.float32)
-
-
-def gather_experts(own, high_first):
-    near = exchange(own, "expert", 2)
-    far = exchange(own, "expert", 4)
-    both = exchange(near, "expert", 4) if high_first else exchange(far, "expert", 2)
-    chips = [own, near, far, both]
-    return chips + [exchange(block, "expert", 1) for block in chips]
-
-
-def scatter_experts(even, odd):
-    summed = even + exchange(odd.astype(jnp.bfloat16), "expert", 1).astype(jnp.float32)
-    chips = split_blocks(summed, 0, 4)
-    total = chips[0]
-    for place in (3, 1, 2):
-        total = total + exchange(
-            chips[place].astype(jnp.bfloat16), "expert", 2 * place
-        ).astype(jnp.float32)
-    return total
-
-
-def sum_experts(array_in, bits):
+    return parts[0], exchange(near, "tensor", 1), far
+
+
+def gather_pairs(own, arrived, second):
+    near = jnp.concatenate([own, arrived])
+    far = exchange(near, "expert", second)
+    return [near, far, exchange(near, "expert", 1), exchange(far, "expert", 1)]
+
+
+def sum_experts(array_in):
     core = lax.axis_index("expert") & 1
     rows = array_in.shape[0] // 2
     top, bottom = array_in[:rows], array_in[rows:]
     keep = jnp.where(core == 0, top, bottom)
     give = jnp.where(core == 0, bottom, top).astype(jnp.bfloat16)
     half = keep + exchange(give, "expert", 1).astype(jnp.float32)
-    half = half.astype(jnp.bfloat16)
-    for bit in bits:
-        arrived = exchange(half, "expert", bit)
-        half = (half.astype(jnp.float32) + arrived.astype(jnp.float32)).astype(jnp.bfloat16)
+    pieces = []
+    for piece, bits in ((half[: rows // 2], (2, 4)), (half[rows // 2 :], (4, 2))):
+        piece = piece.astype(jnp.bfloat16)
+        for bit in bits:
+            arrived = exchange(piece, "expert", bit)
+            piece = (piece.astype(jnp.float32) + arrived.astype(jnp.float32)).astype(jnp.bfloat16)
+        pieces.append(piece)
+    half = jnp.concatenate(pieces)
     other = exchange(half, "expert", 1)
     return jnp.concatenate(
         [jnp.where(core == 0, half, other), jnp.where(core == 0, other, half)]
     ).astype(jnp.float32)
 
 
-def sum_all(array_in):
-    for axis_name in ("tensor", "expert"):
-        bit = 1
-        while bit < lax.axis_size(axis_name):
-            array_in = array_in + exchange(array_in, axis_name, bit)
-            bit *= 2
+def sum_over_experts(array_in):
+    for bit in (1, 2, 4):
+        array_in = array_in + exchange(array_in, "expert", bit)
     return array_in
 
 
@@ -450,7 +441,22 @@
 
 
 def attend_kernel(
-    lengths, layer_in, gain, w_qkv, cosine, sine, normed, inverse, queries, pairs, probs, attended
+    lengths,
+    layer_in,
+    gain,
+    w_qkv,
+    cosine,
+    sine,
+    normed_out,
+    queries_out,
+    pairs_out,
+    probs_out,
+    attended,
+    normed,
+    queries,
+    pairs,
+    probs,
+    sems,
 ):
     token_count = layer_in.shape[0]
     kv_here = pairs.shape[0]
@@ -458,8 +464,9 @@
         rows = pl.ds(row, ROWS)
         values = layer_in[rows, :].astype(jnp.float32)
         scale = lax.rsqrt(jnp.mean(values * values, axis=-1, keepdims=True) + epsilon)
-        inverse[rows, :] = scale
         normed[rows, :] = (values * scale * gain[...]).astype(jnp.bfloat16)
+    copies = [pltpu.make_async_copy(normed, normed_out, sems.at[0])]
+    copies[0].start()
     is_first = first_head((ROWS, LANES))
     for kv in range(kv_here):
         projected = dot_plain(normed[...], w_qkv[:, 2 * LANES * kv : 2 * LANES * (kv + 1)])
@@ -476,6 +483,10 @@
             pairs[kv, rows, :] = jnp.where(
                 is_first, pair * cos_rows + turn(pair) * sin_rows, pair
             ).astype(jnp.bfloat16)
+    copies.append(pltpu.make_async_copy(queries, queries_out, sems.at[1]))
+    copies.append(pltpu.make_async_copy(pairs, pairs_out, sems.at[2]))
+    copies[1].start()
+    copies[2].start()
     for block in range(token_count // ROWS):
         keys = (block + 1) * ROWS
         token = block * ROWS + (
@@ -498,6 +509,14 @@
             attended[pl.ds(block * ROWS, ROWS), kv * LANES : (kv + 1) * LANES] = jnp.where(
                 is_first, swap_heads(output[:ROWS]), output[ROWS:]
             ).astype(jnp.bfloat16)
+        copies.append(
+            pltpu.make_async_copy(
+                probs.at[:, block, :, :keys], probs_out.at[:, block, :, :keys], sems.at[3 + block]
+            )
+        )
+        copies[-1].start()
+    for copy in copies:
+        copy.wait()
 
 
 def write_parts(place, total, parts, span):
@@ -506,39 +525,30 @@
         part[...] = total[pl.ds(row, span), :].astype(part.dtype)
 
 
-def middle_kernel(tensor_count, experts_all, *refs):
+def middle_kernel(tensor_count, *refs):
     place, gain, router, routes, layer_in, out_grad = refs[:6]
-    refs = refs[6:]
-    heads, refs = refs[:tensor_count], refs[tensor_count:]
-    outputs_w, refs = refs[:tensor_count], refs[tensor_count:]
-    w_ins, refs = refs[:experts_all], refs[experts_all:]
-    w_outs, refs = refs[:experts_all], refs[experts_all:]
+    w_mine, w_other, heads, refs = refs[6], refs[7], refs[8], refs[9:]
+    w_ins, w_outs, refs = refs[:4], refs[4:8], refs[8:]
     parts, refs = refs[:tensor_count], refs[tensor_count:]
     (residual_block, inverse_block, normed, active_out, pre_out, gain_part, router_part) = refs[:7]
-    (w_in, w_out, residual, inverse, gates, gate_grad, hidden, plain, total, sems) = refs[7:]
+    (residual, inverse, gates, gate_grad, hidden, plain, total) = refs[7:]
     token_count, model_width = layer_in.shape
-    units = w_outs[0].shape[0]
+    experts_all = router_part.shape[0]
+    units = w_outs[0].shape[0] // 2
     span = token_count // tensor_count
-    copies = []
-    for number in range(experts_all):
-        copies.append(
-            pltpu.make_async_copy(
-                w_ins[number], w_in.at[pl.ds(number * 2 * units, 2 * units)], sems.at[0, number]
-            )
-        )
-        copies.append(
-            pltpu.make_async_copy(
-                w_outs[number], w_out.at[pl.ds(number * units, units)], sems.at[1, number]
-            )
-        )
-    for copy in copies:
-        copy.start()
     lane = lane_index((ROWS, LANES))
+    half = w_mine.shape[0] // tensor_count
+    core = place[1] & 1
+    mine_lanes = pl.ds(pl.multiple_of(core * half, half), half)
+    other_lanes = pl.ds(pl.multiple_of((1 - core) * half, half), half)
     for row in range(0, token_count, ROWS):
         rows = pl.ds(row, ROWS)
         values = layer_in[rows, :].astype(jnp.float32)
-        for head, output in zip(heads, outputs_w):
-            values = values + dot_plain(head[rows, :], output[...])
+        for number in range(tensor_count):
+            head_rows = pl.ds(number * token_count + row, ROWS)
+            half_rows = pl.ds(number * half, half)
+            values = values + dot_plain(heads[head_rows, mine_lanes], w_mine[half_rows, :])
+            values = values + dot_plain(heads[head_rows, other_lanes], w_other[half_rows, :])
         residual[rows, :] = values
         scale = lax.rsqrt(jnp.mean(values * values, axis=-1, keepdims=True) + epsilon)
         inverse[rows, :] = scale
@@ -552,18 +562,13 @@
         weight = jnp.where(picked, jnp.exp(logits - jnp.max(logits, -1, keepdims=True)), 0.0)
         gates[rows, :] = weight / jnp.sum(weight, -1, keepdims=True)
     gate_grad[...] = jnp.zeros_like(gate_grad)
-    for copy in copies:
-        copy.wait()
-
-    def expert_step(number, carry):
-        twice = 2 * number
-        name = place[1] ^ jnp.where(twice < experts_all, twice, twice - experts_all + 1)
-        in_rows = pl.ds(pl.multiple_of(number * 2 * units, 2 * units), 2 * units)
-        out_rows = pl.ds(pl.multiple_of(number * units, units), units)
-        gate_lanes = pl.ds(pl.multiple_of(number * 2 * units, units), units)
-        up_lanes = pl.ds(pl.multiple_of(number * 2 * units + units, units), units)
-        hidden[...] = dot_transposed(normed[...], w_in[in_rows, :])
-        plain[...] = dot_transposed(out_grad[...], w_out[out_rows, :])
+    for number in range(experts_all):
+        name = place[1] ^ IN_ORDER[number]
+        in_rows = pl.ds(number % 2 * 2 * units, 2 * units)
+        out_number = OUT_ORDER.index(IN_ORDER[number])
+        out_rows = pl.ds(out_number % 2 * units, units)
+        hidden[...] = dot_transposed(normed[...], w_ins[number // 2][in_rows, :])
+        plain[...] = dot_transposed(out_grad[...], w_outs[out_number // 2][out_rows, :])
         for row in range(0, token_count, ROWS):
             rows = pl.ds(row, ROWS)
             gate = jnp.sum(jnp.where(lane == name, gates[rows, :], 0.0), -1, keepdims=True)
@@ -576,14 +581,15 @@
                 lane == name, jnp.sum(active * grad, -1, keepdims=True), 0.0
             )
             active_grad = grad * gate
-            active_out[rows, out_rows] = (active * gate).astype(jnp.bfloat16)
-            pre_out[rows, gate_lanes] = (
+            active_out[rows, out_number * units : (out_number + 1) * units] = (
+                active * gate
+            ).astype(jnp.bfloat16)
+            pre_out[rows, 2 * number * units : (2 * number + 1) * units] = (
                 active_grad * up_vals * (sig_vals * (1.0 + gate_vals * (1.0 - sig_vals)))
             ).astype(jnp.bfloat16)
-            pre_out[rows, up_lanes] = (active_grad * silu_vals).astype(jnp.bfloat16)
-        return carry
-
-    lax.fori_loop(0, experts_all, expert_step, 0)
+            pre_out[rows, (2 * number + 1) * units : (2 * number + 2) * units] = (
+                active_grad * silu_vals
+            ).astype(jnp.bfloat16)
     gate_all, grad_all = gates[...], gate_grad[...]
     logit_part = (
         gate_all * (grad_all - jnp.sum(gate_all * grad_all, -1, keepdims=True))
@@ -592,9 +598,11 @@
 
     def column_step(number, carry):
         columns = pl.ds(pl.multiple_of(number * 2 * LANES, 2 * LANES), 2 * LANES)
-        total[:, columns] = dot_plain(pre_out[...], w_in[:, columns]) + dot_plain(
-            logit_part, router[:, columns]
-        )
+        summed = dot_plain(logit_part, router[:, columns])
+        for pair, weights in enumerate(w_ins):
+            pre = pre_out[:, 4 * pair * units : 4 * (pair + 1) * units]
+            summed = summed + dot_plain(pre, weights[:, columns])
+        total[:, columns] = summed
         return carry
 
     lax.fori_loop(0, model_width // (2 * LANES), column_step, 0)
@@ -611,18 +619,68 @@
     gain_part[...] = gain_sum
 
 
+def weight_grad_kernel(tensor_count, *refs):
+    place, normed, out_grad, active, pre_grad = refs[:5]
+    w_outs, parts = refs[5:9], refs[9 : 9 + tensor_count]
+    grads, total, slots, sems = refs[9 + tensor_count :]
+    token_count, model_width = normed.shape
+    experts_all = grads.shape[0]
+    units = w_outs[0].shape[0] // 2
+
+    def column_step(number, carry):
+        columns = pl.ds(pl.multiple_of(number * 2 * LANES, 2 * LANES), 2 * LANES)
+        summed = jnp.zeros((token_count, 2 * LANES), jnp.float32)
+        for pair, weights in enumerate(w_outs):
+            summed = summed + dot_plain(
+                active[:, 2 * pair * units : 2 * (pair + 1) * units], weights[:, columns]
+            )
+        total[:, columns] = summed
+        return carry
+
+    lax.fori_loop(0, model_width // (2 * LANES), column_step, 0)
+    write_parts(place, total, parts, token_count // tensor_count)
+    copies = []
+    for number in range(experts_all):
+        name = place[1] ^ IN_ORDER[number]
+        out_number = OUT_ORDER.index(IN_ORDER[number])
+        slot = number % 2
+        if number >= 2:
+            copies[number - 2].wait()
+        slots[slot, : 2 * units, :] = transposed_dot(
+            pre_grad[:, 2 * number * units : 2 * (number + 1) * units], normed[...]
+        ).astype(jnp.bfloat16)
+        slots[slot, 2 * units :, :] = transposed_dot(
+            active[:, out_number * units : (out_number + 1) * units], out_grad[...]
+        ).astype(jnp.bfloat16)
+        copies.append(pltpu.make_async_copy(slots.at[slot], grads.at[name], sems.at[slot]))
+        copies[-1].start()
+    for copy in copies[-2:]:
+        copy.wait()
+
+
 def attend_back_kernel(tensor_count, *refs):
-    place, w_output, queries, pairs, probs, cosine, sine, w_qkv, layer_in, inverse = refs[:10]
-    refs = refs[10:]
+    place, far_refs, refs = refs[0], refs[1:9], refs[9:]
     blocks, refs = refs[:tensor_count], refs[tensor_count:]
+    mixtures, refs = refs[:tensor_count], refs[tensor_count:]
     parts, refs = refs[:tensor_count], refs[tensor_count:]
-    branch_grad, projected_grad, gain_part, heads_grad, pair_grad, total = refs
+    branch_grad, projected_grad, gain_part, heads_grad, pair_grad, total = refs[:6]
+    near_refs, sems = refs[6:14], refs[14]
+    w_output, queries, pairs, probs, cosine, sine, w_qkv, layer_in = near_refs
+    copies = [
+        pltpu.make_async_copy(source, target, sems.at[number])
+        for number, (source, target) in enumerate(zip(far_refs, near_refs))
+    ]
+    for copy in copies:
+        copy.start()
     token_count, model_width = layer_in.shape
     span = token_count // tensor_count
     for number, block in enumerate(blocks):
         row = pl.multiple_of((place[0] ^ number) * span, span)
         branch_grad[pl.ds(row, span), :] = block[...]
+    copies[0].wait()
     heads_grad[...] = dot_transposed(branch_grad[...], w_output[...])
+    for copy in copies[1:6]:
+        copy.wait()
     is_first = first_head((ROWS, LANES))
     for kv in range(pairs.shape[0]):
         pair_grad[...] = jnp.zeros_like(pair_grad)
@@ -660,26 +718,54 @@
                 is_first, grad * cosine[rows, :] - turn(grad) * sine[rows, :], grad
             ).astype(jnp.bfloat16)
 
+    for copy in copies[6:]:
+        copy.wait()
+
     def column_step(number, carry):
         columns = pl.ds(pl.multiple_of(number * 2 * LANES, 2 * LANES), 2 * LANES)
         total[:, columns] = dot_transposed(projected_grad[...], w_qkv[columns, :])
         return carry
 
     lax.fori_loop(0, model_width // (2 * LANES), column_step, 0)
-    write_parts(place, total, parts, span)
+    write_parts(place, total, [part.at[:span] for part in parts], span)
+    for mixture, part in zip(mixtures, parts):
+        part[span:, :] = mixture[...]
     gain_sum = jnp.zeros((1, model_width), jnp.float32)
     for row in range(0, token_count, ROWS):
         rows = pl.ds(row, ROWS)
-        gain_sum = gain_sum + jnp.sum(
-            total[rows, :] * (layer_in[rows, :].astype(jnp.float32) * inverse[rows, :]),
-            0,
-            keepdims=True,
-        )
+        values = layer_in[rows, :].astype(jnp.float32)
+        scale = lax.rsqrt(jnp.mean(values * values, axis=-1, keepdims=True) + epsilon)
+        gain_sum = gain_sum + jnp.sum(total[rows, :] * (values * scale), 0, keepdims=True)
     gain_part[...] = gain_sum
+
+
+def norm_back_kernel(own, near, far, residual, inverse, gain, out_grad, residual_grad, low_grad):
+    summed = own[...] + near[...].astype(jnp.float32) + far[...].astype(jnp.float32)
+    total = out_grad[...].astype(jnp.float32) + rms_backward(
+        residual[...], inverse[...], gain[...], summed
+    )
+    residual_grad[...] = total
+    low_grad[...] = total.astype(jnp.bfloat16)
+
+
+def finish_kernel(own, near, far, layer_in, gain, residual_grad, residual, small, block):
+    span = layer_in.shape[0]
+    summed = own[...] + near[...].astype(jnp.float32) + far[...].astype(jnp.float32)
+    values = layer_in[...].astype(jnp.float32)
+    inverse = lax.rsqrt(jnp.mean(values * values, axis=-1, keepdims=True) + epsilon)
+    block[:span, :] = (residual[...] + summed[span:]).astype(jnp.bfloat16)
+    block[span : 2 * span, :] = (
+        residual_grad[...] + rms_backward(values, inverse, gain[...], summed[:span])
+    ).astype(jnp.bfloat16)
+    block[2 * span :, :] = small[...]
 
 
 def in_vmem(count):
     return [pl.BlockSpec(memory_space=pltpu.VMEM)] * count
+
+
+def in_hbm(count):
+    return [pl.BlockSpec(memory_space=pltpu.HBM)] * count
 
 
 def in_smem(count):
@@ -719,43 +805,63 @@
     def token_block(array_in):
         return lax.dynamic_slice_in_dim(array_in, tensor_here * span, span, 0)
 
-    def in_order(blocks):
-        joined = jnp.zeros((token_count,) + blocks[0].shape[1:], blocks[0].dtype)
+    def in_order(blocks, rows=span):
+        joined = jnp.zeros((tensor_count * rows,) + blocks[0].shape[1:], blocks[0].dtype)
         for number, block in enumerate(blocks):
             joined = lax.dynamic_update_slice_in_dim(
-                joined, block, (tensor_here ^ number) * span, 0
+                joined, block, (tensor_here ^ number) * rows, 0
             )
         return joined
 
-    w_in_all = gather_experts(w_in.reshape(2 * units, model_width), True)
-    w_out_all = gather_experts(w_out[0], False)
-    w_output_all = gather_blocks(w_output)
+    core = lax.axis_index("expert") & 1
+    half = w_output.shape[0] // 2
+    output_own = jnp.where(core == 0, w_output[:half], w_output[half:])
+    output_far = exchange(output_own, "tensor", 2)
+    output_near = exchange(output_own, "tensor", 1)
+    w_in_own, w_out_own = w_in.reshape(2 * units, model_width), w_out[0]
+    w_in_near = exchange(w_in_own, "expert", 2)
+    w_out_near = exchange(w_out_own, "expert", 4)
 
     cosine, sine = angle_tables(token_count)
     qkv_flat = w_qkv.reshape(model_width, -1)
-    normed_one, inverse_one, queries, pairs, probs, attended = pl.pallas_call(
+    kept = (
+        shaped((token_count, model_width), low),
+        shaped((kv_here, block_count, 2 * ROWS, LANES), low),
+        shaped((kv_here, token_count, LANES), low),
+        shaped((kv_here, block_count, 2 * ROWS, token_count), low),
+    )
+    normed_one, queries, pairs, probs, attended = pl.pallas_call(
         attend_kernel,
-        out_shape=(
-            shaped((token_count, model_width), low),
-            shaped((token_count, 1), wide),
-            shaped((kv_here, block_count, 2 * ROWS, LANES), low),
-            shaped((kv_here, token_count, LANES), low),
-            shaped((kv_here, block_count, 2 * ROWS, token_count), low),
-            shaped((token_count, head_width), low),
-        ),
+        out_shape=kept + (shaped((token_count, head_width), low),),
         in_specs=in_smem(1) + in_vmem(5),
-        out_specs=tuple(in_vmem(6)),
-        compiler_params=pltpu.CompilerParams(vmem_limit_bytes=32 * mib),
+        out_specs=tuple(in_hbm(4) + in_vmem(1)),
+        scratch_shapes=[pltpu.VMEM(each.shape, low) for each in kept]
+        + [pltpu.SemaphoreType.DMA((3 + block_count,))],
+        compiler_params=pltpu.CompilerParams(vmem_limit_bytes=56 * mib),
         name="attend",
     )(seq_lengths, layer_in, gain_attn[None], qkv_flat, cosine, sine)
 
-    heads_all = gather_blocks(attended)
+    w_in_near, w_out_near, output_far, output_near, attended = lax.optimization_barrier(
+        (w_in_near, w_out_near, output_far, output_near, attended)
+    )
+    heads_far = exchange(attended, "tensor", 2)
+    heads_near = exchange(attended, "tensor", 1)
+    w_in_all = gather_pairs(w_in_own, w_in_near, 4)
+    w_out_all = gather_pairs(w_out_own, w_out_near, 2)
+    heads_far, heads_near, w_out_all = lax.optimization_barrier(
+        (heads_far, heads_near, w_out_all)
+    )
+    heads_both = exchange(heads_far, "tensor", 1)
+    heads_all = [attended, heads_near, heads_far, heads_both]
+    output_both = exchange(output_far, "tensor", 1)
+    output_mine = jnp.concatenate([output_own, output_near, output_far, output_both])
+    output_other = exchange(output_mine, "expert", 1)
     router_rows = jnp.pad(jnp.transpose(w_router), ((0, LANES - experts_all), (0, 0)))
     part_shapes = (shaped((span, model_width), wide),) + (
         shaped((span, model_width), low),
     ) * (tensor_count - 1)
     middle = pl.pallas_call(
-        functools.partial(middle_kernel, tensor_count, experts_all),
+        functools.partial(middle_kernel, tensor_count),
         out_shape=part_shapes
         + (
             shaped((span, model_width), wide),
@@ -766,13 +872,9 @@
             shaped((1, model_width), wide),
             shaped((experts_all, model_width), wide),
         ),
-        in_specs=in_smem(1)
-        + in_vmem(5 + 2 * tensor_count)
-        + [pl.BlockSpec(memory_space=pl.ANY)] * (2 * experts_all),
+        in_specs=in_smem(1) + in_vmem(16),
         out_specs=tuple(in_vmem(tensor_count + 7)),
         scratch_shapes=[
-            pltpu.VMEM((experts_all * 2 * units, model_width), low),
-            pltpu.VMEM((experts_all * units, model_width), low),
             pltpu.VMEM((token_count, model_width), wide),
             pltpu.VMEM((token_count, 1), wide),
             pltpu.VMEM((token_count, LANES), wide),
@@ -780,9 +882,8 @@
             pltpu.VMEM((token_count, 2 * units), wide),
             pltpu.VMEM((token_count, units), wide),
             pltpu.VMEM((token_count, model_width), wide),
-            pltpu.SemaphoreType.DMA((2, experts_all)),
         ],
-        compiler_params=pltpu.CompilerParams(vmem_limit_bytes=44 * mib),
+        compiler_params=pltpu.CompilerParams(vmem_limit_bytes=20 * mib),
         name="middle",
     )(
         place,
@@ -791,84 +892,124 @@
         routes,
         layer_in,
         out_grad,
-        *heads_all,
-        *w_output_all,
+        output_mine,
+        output_other,
+        jnp.concatenate(heads_all),
         *w_in_all,
         *w_out_all,
     )
     normed_parts, middle = middle[:tensor_count], middle[tensor_count:]
     residual, inverse_two, normed_two, active, pre_grad, gain_ffn_part, router_part = middle
 
-    normed_two_grad = scatter_sums(normed_parts)
-    residual_grad = token_block(out_grad).astype(wide) + rms_backward(
-        residual, inverse_two, gain_ffn, normed_two_grad
-    )
-    grad_blocks = gather_blocks(residual_grad.astype(low))
-
-    half_units = experts_all * units
-    w_in_grad = scatter_experts(
-        transposed_dot(pre_grad[:, :half_units], normed_two),
-        transposed_dot(pre_grad[:, half_units:], normed_two),
-    ).reshape(w_in.shape)
-    w_out_grad = scatter_experts(
-        transposed_dot(active[:, : half_units // 2], out_grad),
-        transposed_dot(active[:, half_units // 2 :], out_grad),
-    )[None]
-
+    late = pl.pallas_call(
+        functools.partial(weight_grad_kernel, tensor_count),
+        out_shape=part_shapes + (shaped((experts_all, 3 * units, model_width), low),),
+        in_specs=in_smem(1) + in_vmem(8),
+        out_specs=tuple(in_vmem(tensor_count) + in_hbm(1)),
+        scratch_shapes=[
+            pltpu.VMEM((token_count, model_width), wide),
+            pltpu.VMEM((2, 3 * units, model_width), low),
+            pltpu.SemaphoreType.DMA((2,)),
+        ],
+        compiler_params=pltpu.CompilerParams(vmem_limit_bytes=48 * mib),
+        name="weight_grad",
+    )(place, normed_two, out_grad, active, pre_grad, *w_out_all)
+    late, relayed = lax.optimization_barrier((late, exchange(normed_parts[3], "tensor", 1)))
+    mixture_parts, weight_grads = late[:tensor_count], late[tensor_count]
+    residual_grad, low_grad = pl.pallas_call(
+        norm_back_kernel,
+        out_shape=(shaped((span, model_width), wide), shaped((span, model_width), low)),
+        in_specs=in_vmem(7),
+        out_specs=tuple(in_vmem(2)),
+        compiler_params=pltpu.CompilerParams(vmem_limit_bytes=6 * mib),
+        name="norm_back",
+    )(
+        *scatter_parts(normed_parts, relayed),
+        residual,
+        inverse_two,
+        gain_ffn[None],
+        token_block(out_grad),
+    )
+    grad_blocks = gather_blocks(low_grad)
+
+    weight_grads = lax.psum_scatter(
+        weight_grads, "expert", scatter_dimension=0, tiled=False
+    ).astype(wide)
+    w_in_grad = weight_grads[: 2 * units].reshape(w_in.shape)
+    w_out_grad = weight_grads[2 * units :].reshape(w_out.shape)
+
+    fetched = (w_output, queries, pairs, probs, cosine, sine, qkv_flat, layer_in)
     back = pl.pallas_call(
         functools.partial(attend_back_kernel, tensor_count),
-        out_shape=part_shapes
+        out_shape=(shaped((2 * span, model_width), wide),)
+        + (shaped((2 * span, model_width), low),) * (tensor_count - 1)
         + (
             shaped((token_count, model_width), low),
             shaped((token_count, 2 * head_width), low),
             shaped((1, model_width), wide),
         ),
-        in_specs=in_smem(1) + in_vmem(9 + tensor_count),
+        in_specs=in_smem(1) + in_hbm(8) + in_vmem(2 * tensor_count),
         out_specs=tuple(in_vmem(tensor_count + 3)),
         scratch_shapes=[
             pltpu.VMEM((token_count, head_width), wide),
             pltpu.VMEM((token_count, LANES), wide),
             pltpu.VMEM((token_count, model_width), wide),
-        ],
-        compiler_params=pltpu.CompilerParams(vmem_limit_bytes=32 * mib),
+        ]
+        + [pltpu.VMEM(each.shape, each.dtype) for each in fetched]
+        + [pltpu.SemaphoreType.DMA((len(fetched),))],
+        compiler_params=pltpu.CompilerParams(vmem_limit_bytes=50 * mib),
         name="attend_back",
     )(
         place,
-        w_output,
-        queries,
-        pairs,
-        probs,
-        cosine,
-        sine,
-        qkv_flat,
-        layer_in,
-        inverse_one,
+        *fetched,
         *grad_blocks,
+        *mixture_parts,
     )
     input_parts, (branch_grad, projected_grad, gain_attn_part) = (
         back[:tensor_count],
         back[tensor_count:],
     )
-    normed_one_grad = scatter_sums(input_parts)
-    input_part = rms_backward(
-        token_block(layer_in).astype(wide), token_block(inverse_one), gain_attn, normed_one_grad
-    )
-    in_here = in_order(gather_blocks((residual_grad + input_part).astype(low)))
-
-    mixture_part = dot_plain(active, jnp.concatenate(w_out_all))
-    mixture_part, _ = lax.optimization_barrier((mixture_part, grad_blocks[3]))
-    mixture_parts = [
-        lax.dynamic_slice_in_dim(mixture_part, (tensor_here ^ number) * span, span, 0)
-        for number in range(tensor_count)
-    ]
-    mixture = scatter_sums(mixture_parts[:1] + [part.astype(low) for part in mixture_parts[1:]])
-    layer_here = in_order(gather_blocks((residual + mixture).astype(low)))
-
-    qkv_summed = sum_experts(transposed_dot(normed_one, projected_grad), (2, 4)).reshape(
-        w_qkv.shape
-    )
-    output_summed = sum_experts(transposed_dot(attended, branch_grad), (4, 2))
-    small = sum_all(jnp.concatenate([router_part, gain_ffn_part, gain_attn_part]))
+    w_output_grad = transposed_dot(attended, branch_grad)
+    lanes_each = w_output_grad.shape[1] * kv_here * LANES // model_width * 2
+    summed = sum_experts(
+        jnp.concatenate(
+            [transposed_dot(normed_one, projected_grad)]
+            + [
+                w_output_grad[:, lanes : lanes + lanes_each]
+                for lanes in range(0, model_width, lanes_each)
+            ]
+        )
+    )
+    qkv_summed = summed[:model_width].reshape(w_qkv.shape)
+    output_summed = jnp.concatenate(split_blocks(summed[model_width:], 0, 2), 1)
+
+    small = sum_over_experts(jnp.concatenate([router_part, gain_ffn_part, gain_attn_part]))
+    small = jnp.pad(small, ((0, SMALL_ROWS - small.shape[0]), (0, 0))).astype(low)
+    block = pl.pallas_call(
+        finish_kernel,
+        out_shape=shaped((2 * span + SMALL_ROWS, model_width), low),
+        in_specs=in_vmem(8),
+        out_specs=in_vmem(1)[0],
+        compiler_params=pltpu.CompilerParams(vmem_limit_bytes=6 * mib),
+        name="finish",
+    )(
+        *scatter_parts(input_parts, exchange(input_parts[3], "tensor", 1)),
+        token_block(layer_in),
+        gain_attn[None],
+        residual_grad,
+        residual,
+        small,
+    )
+    far = exchange(block, "tensor", 2)
+    near = exchange(block, "tensor", 1)
+    far, near, qkv_summed, output_summed, w_in_grad, w_out_grad = lax.optimization_barrier(
+        (far, near, qkv_summed, output_summed, w_in_grad, w_out_grad)
+    )
+    blocks = [block, near, far, exchange(far, "tensor", 1)]
+    layer_here = in_order([block[:span] for block in blocks])
+    in_here = in_order([block[span : 2 * span] for block in blocks])
+    small = in_order([block[2 * span :] for block in blocks], SMALL_ROWS)
+    small = jnp.sum(small.reshape(tensor_count, SMALL_ROWS, -1).astype(wide), 0)
     return (
         layer_here,
         in_here,

time: 279 us -> 253 us (0.907)
  waiting for transfers between devices: 147 us -> 109 us
  Pallas kernels: 29.7 us -> 47.9 us
  between operations: 1.53 us -> 14.7 us
  starting transfers between devices: 50.7 us -> 37.8 us
  matrix products: 8.53 us -> 2.64 us
    ppermute x59 -> x36, waiting for transfers between devices: 147 us -> 109 us  [exchange(): lax.ppermute(array_in, axis_name, [(i, i ^ bits) for i in range(count)])]
    pallas_call x2 -> x5, Pallas kernels: 22.6 us -> 37.1 us  [the longest x1 17.3 us: on_device(): pl.pallas_call(functools.partial(middle_kernel, tensor_count), out_shape=...]
    ppermute x59 -> x36, starting transfers between devices: 50.7 us -> 37.8 us  [exchange(): lax.ppermute(array_in, axis_name, [(i, i ^ bits) for i in range(count)])]
    unnamed x113 -> x82, local copies, waits for them, and re-layouts: 25.6 us -> 13.6 us
    dynamic_update_slice x6 -> x9, local copies, waits for them, and re-layouts: 0.14 us -> 4.79 us  [in_order(): lax.dynamic_update_slice_in_dim(joined, block, (tensor_here ^ number) * r...]
    pallas_call x1, Pallas kernels: 7.13 us -> 10.7 us  [on_device(): pl.pallas_call(functools.partial(attend_back_kernel, tensor_count), out_s...]
    reshape x0 -> x2, local copies, waits for them, and re-layouts: none -> 3.42 us  [the longest x1 2.35 us: on_device(): qkv_summed = summed[:model_width].reshape(w_qkv.shape)]
    concatenate x0 -> x5, other arithmetic: none -> 3.26 us  [the longest x1 1.1 us: on_device(): jnp.concatenate(heads_all)]
  transfers between devices with their start and end apart: 59 -> 37, of which waited for: 26 -> 18; matrix products, arithmetic and copies ran while one was open for 9% -> 12% of each run, Pallas kernels for 3% -> 12%
where the time goes in v3:
time: 253 us; the launch traced here: 252 us
  waiting for transfers between devices  109 us (43%)
  Pallas kernels  47.9 us (19%)
  starting transfers between devices  37.8 us (15%)
  local copies, waits for them, and re-layouts  28.7 us (11%)
  between operations  14.7 us (6%)
  other arithmetic  11.7 us (5%)
  matrix products  2.64 us (1%)
    ppermute x36, waiting for transfers between devices, exchange(): lax.ppermute(array_in, axis_name, [(i, i ^ bits) for i in range(count)])  109 us
    ppermute x36, starting transfers between devices, exchange(): lax.ppermute(array_in, axis_name, [(i, i ^ bits) for i in range(count)])  37.8 us
    pallas_call x1, Pallas kernels, on_device(): pl.pallas_call(functools.partial(middle_kernel, tensor_count), out_shape=...  17.3 us
    unnamed x82, local copies, waits for them, and re-layouts  13.6 us
    pallas_call x1, Pallas kernels, on_device(): pl.pallas_call(functools.partial(attend_back_kernel, tensor_count), out_s...  10.7 us
    pallas_call x1, Pallas kernels, on_device(): pl.pallas_call(functools.partial(weight_grad_kernel, tensor_count), out_s...  10.5 us
    pallas_call x1, Pallas kernels, on_device(): pl.pallas_call(attend_kernel, out_shape=kept + (shaped((token_count, head...  7.61 us
  transfers between devices with their start and end apart: 37, of which 18 were waited for; matrix products, arithmetic and copies ran while one was open for 12% of the time, Pallas kernels for 12%

profile of v3, /device:TPU:0, one launch (start us, length us, event | category | flops | bytes accessed | tf_op | source)
XLA Modules:
  0.0 252.2 jit_solution(17768514305681229703)
XLA Ops:
  7.2 3.0 %collective-permute-start = (bf16[256,1024]{1,0:T(8,128)(2,1)}, bf16[256,1024]{1,0:T(8,128)(2,1)S(1)}, u32[]{:S(2)}, u32[]{:S(2)}) collective-permute-start(bf16[256,1024]{1,0:T(8,128)(2,1)} %bitcast.36), channel_id=1, source_target_pairs={{0,8},{4,12},{8,0},{12,4},{16,24},{20,28},{24,16},{28,20},{1,9},{5... | collective-permute-start | bytes 1572872 | tf_op jit(solution)/shard_map/ppermute | solution.py:345
  11.3 2.7 %collective-permute-start.2 = (bf16[128,1024]{1,0:T(8,128)(2,1)S(1)}, bf16[128,1024]{1,0:T(8,128)(2,1)S(1)}, u32[]{:S(2)}, u32[]{:S(2)}) collective-permute-start(bf16[128,1024]{1,0:T(8,128)(2,1)S(1)} %slice_select_fusion), channel_id=1, source_target_pairs={{0,2},{1,3},{2,0},{3,1},{4,6},{5,7},{6,4},{7,5},{8,10},{9,11},{10,... | collective-permute-start | bytes 786440 | tf_op jit(solution)/shard_map/ppermute | solution.py:345
  13.9 1.6 collective-permute-start.3
  15.5 1.5 collective-permute-start.1
  17.0 2.5 copy.25
  19.5 7.6 %attend.1 = (bf16[512,1024]{1,0:T(8,128)(2,1)}, bf16[2,4,256,128]{3,2,1,0:T(8,128)(2,1)}, bf16[2,512,128]{2,1,0:T(8,128)(2,1)}, bf16[2,4,256,512]{3,2,1,0:T(8,128)(2,1)}, bf16[512,256]{1,0:T(8,128)(2,1)}) custom-call(s32[1,3]{1,0:T(1,128)} %lengths.1, bf16[512,1024]{1,0:T(8,128)(2,1)} %refs_8_.1, f32[1,1024]{1,0:T(1,128)} %bitcast.27, ...), custom_call_target="tpu_custom_call" | custom-call | tf_op jit(solution)/shard_map/attend/pallas_call | solution.py:833
  29.4 1.2 collective-permute-start.4
  30.6 2.3 collective-permute-start.6
  33.0 11.2 %collective-permute-done.4 = bf16[128,1024]{1,0:T(8,128)(2,1)S(1)} collective-permute-done((bf16[128,1024]{1,0:T(8,128)(2,1)S(1)}, bf16[128,1024]{1,0:T(8,128)(2,1)S(1)}, u32[]{:S(2)}, u32[]{:S(2)}) %collective-permute-start.4) | collective-permute-done | bytes 262176 | tf_op jit(solution)/shard_map/ppermute | solution.py:345
  45.7 6.7 %collective-permute-done.12.refs_10_ = bf16[512,1024]{1,0:T(8,128)(2,1)} collective-permute-done((bf16[512,1024]{1,0:T(8,128)(2,1)}, bf16[512,1024]{1,0:T(8,128)(2,1)}, u32[]{:S(2)}, u32[]{:S(2)}) %collective-permute-start.12) | collective-permute-done | bytes 1048608 | tf_op jit(solution)/shard_map/ppermute | solution.py:345
  53.7 2.0 collective-permute-done.9.refs_15_.refs_7_
  58.1 7.8 %collective-permute-done.11 = bf16[512,256]{1,0:T(8,128)(2,1)S(1)} collective-permute-done((bf16[512,256]{1,0:T(8,128)(2,1)}, bf16[512,256]{1,0:T(8,128)(2,1)S(1)}, u32[]{:S(2)}, u32[]{:S(2)}) %collective-permute-start.11) | collective-permute-done | bytes 262176 | tf_op jit(solution)/shard_map/ppermute | solution.py:345
  65.9 1.1 pad_maximum_fusion.3.refs_8_
  67.1 17.3 %middle.1 = (f32[128,1024]{1,0:T(8,128)S(1)}, bf16[128,1024]{1,0:T(8,128)(2,1)S(1)}, bf16[128,1024]{1,0:T(8,128)(2,1)S(1)}, bf16[128,1024]{1,0:T(8,128)(2,1)S(1)...) custom-call(s32[2]{0:T(128)S(1)} %pad_add_fusion.refs_0_, ...), custom_call_target="tpu_custom_call" | custom-call | tf_op jit(solution)/shard_map/middle/pallas_call | solution.py:863
  84.5 1.4 copy-done.2
  88.4 10.5 %weight_grad.1 = (f32[128,1024]{1,0:T(8,128)S(1)}, bf16[128,1024]{1,0:T(8,128)(2,1)S(1)}, bf16[128,1024]{1,0:T(8,128)(2,1)S(1)}, bf16[128,1024]{1,0:T(8,128)(2,1)S(1)}, bf16[8,384,1024]{2,1,0:T(8,128)(2,1)}) custom-call(s32[2]{0:T(128)S(1)} %pad_add_fusion.refs_0_, bf16[512,1024]{1,0:T(8,128)(2,1)S(1)} %get-tuple-element.88.refs_1_, ...), custom_call_target="tpu_custom_call" | custom-call | tf_op jit(solution)/shard_map/weight_grad/pallas_call | solution.py:904
  101.2 1.9 add_convert_fusion.6
  103.0 3.0 %collective-permute-start.17 = (bf16[128,1024]{1,0:T(8,128)(2,1)}, bf16[128,1024]{1,0:T(8,128)(2,1)}, u32[]{:S(2)}, u32[]{:S(2)}) collective-permute-start(bf16[128,1024]{1,0:T(8,128)(2,1)} %add_convert_fusion.6), channel_id=1, source_target_pairs={{0,2},{1,3},{2,0},{3,1},{4,6},{5,7},{6,4},{7,5},{8,10},{9,11},{10,... | collective-permute-start | bytes 786440 | tf_op jit(solution)/shard_map/ppermute | solution.py:345
  106.9 10.8 %collective-permute-done.17.far = bf16[128,1024]{1,0:T(8,128)(2,1)} collective-permute-done((bf16[128,1024]{1,0:T(8,128)(2,1)}, bf16[128,1024]{1,0:T(8,128)(2,1)}, u32[]{:S(2)}, u32[]{:S(2)}) %collective-permute-start.17) | collective-permute-done | bytes 262176 | tf_op jit(solution)/shard_map/ppermute | solution.py:345
  118.4 1.3 norm_back.1
  120.8 2.6 %collective-permute-start.19 = (bf16[128,1024]{1,0:T(8,128)(2,1)S(1)}, bf16[128,1024]{1,0:T(8,128)(2,1)S(1)}, u32[]{:S(2)}, u32[]{:S(2)}) collective-permute-start(bf16[128,1024]{1,0:T(8,128)(2,1)S(1)} %get-tuple-element.103.refs_9_), channel_id=1, source_target_pairs={{0,1},{1,0},{2,3},{3,2},{4,5},{5,4},{6,7},{7,6},{8,9},{9,8},{10,11... | collective-permute-start | bytes 786440 | tf_op jit(solution)/shard_map/ppermute | solution.py:345
  123.4 10.7 %collective-permute-done.18.refs_11_ = bf16[128,1024]{1,0:T(8,128)(2,1)S(1)} collective-permute-done((bf16[128,1024]{1,0:T(8,128)(2,1)S(1)}, bf16[128,1024]{1,0:T(8,128)(2,1)S(1)}, u32[]{:S(2)}, u32[]{:S(2)}) %collective-permute-start.18) | collective-permute-done | bytes 262176 | tf_op jit(solution)/shard_map/ppermute | solution.py:345
  134.1 7.5 %collective-permute-done.20.refs_12_ = bf16[128,1024]{1,0:T(8,128)(2,1)S(1)} collective-permute-done((bf16[128,1024]{1,0:T(8,128)(2,1)S(1)}, bf16[128,1024]{1,0:T(8,128)(2,1)S(1)}, u32[]{:S(2)}, u32[]{:S(2)}) %collective-permute-start.20) | collective-permute-done | bytes 262176 | tf_op jit(solution)/shard_map/ppermute | solution.py:345
  141.7 10.7 %attend_back.1 = (f32[256,1024]{1,0:T(8,128)}, bf16[256,1024]{1,0:T(8,128)(2,1)S(1)}, bf16[256,1024]{1,0:T(8,128)(2,1)S(1)}, bf16[256,1024]{1,0:T(8,128)(2,1)}, ...) custom-call(s32[2]{0:T(128)S(1)} %pad_add_fusion.refs_0_, bf16[256,1024]{1,0:T(8,128)(2,1)} %refs_1_.1, ...), custom_call_target="tpu_custom_call" | custom-call | tf_op jit(solution)/shard_map/attend_back/pallas_call | solution.py:942
  152.4 1.9 fusion.5
  155.7 2.3 collective-permute-done.29
  159.1 1.5 collective-permute-start.32
  161.4 8.7 %collective-permute-done.30 = bf16[384,512]{1,0:T(8,128)(2,1)S(1)} collective-permute-done((bf16[384,512]{1,0:T(8,128)(2,1)S(1)}, bf16[384,512]{1,0:T(8,128)(2,1)S(1)}, u32[]{:S(2)}, u32[]{:S(2)}) %collective-permute-start.30) | collective-permute-done | bytes 393248 | tf_op jit(solution)/shard_map/ppermute | solution.py:345
  170.0 1.1 add_convert_fusion.5
  171.1 1.5 collective-permute-start.31
  172.6 1.5 collective-permute-start.25
  175.2 1.8 collective-permute-done.25
  177.6 1.5 collective-permute-start.33
  179.3 2.5 collective-permute-start.23
  181.8 1.5 collective-permute-start.22
  183.2 1.2 add_convert_fusion.4
  184.5 2.5 collective-permute-done.33
  187.0 1.1 add_convert_fusion.2
  188.2 15.1 %collective-permute-done.23.far = bf16[256,1024]{1,0:T(8,128)(2,1)S(1)} collective-permute-done((bf16[256,1024]{1,0:T(8,128)(2,1)S(1)}, bf16[256,1024]{1,0:T(8,128)(2,1)S(1)}, u32[]{:S(2)}, u32[]{:S(2)}) %collective-permute-start.23) | collective-permute-done | bytes 524320 | tf_op jit(solution)/shard_map/ppermute | solution.py:345
  204.1 1.4 collective-permute-start.27
  205.5 2.3 collective-permute-start.28
  207.9 1.1 broadcast.7.clone.1
  211.3 1.1 copy.24
  213.0 2.4 reshape.50
  215.4 2.3 slice.119
  218.5 11.6 %collective-permute-done.27 = bf16[272,1024]{1,0:T(8,128)(2,1)S(1)} collective-permute-done((bf16[272,1024]{1,0:T(8,128)(2,1)S(1)}, bf16[272,1024]{1,0:T(8,128)(2,1)S(1)}, u32[]{:S(2)}, u32[]{:S(2)}) %collective-permute-start.27) | collective-permute-done | bytes 557088 | tf_op jit(solution)/shard_map/ppermute | solution.py:345
  231.0 1.8 slice_dynamic-update-slice_fusion.5
  233.6 8.9 %collective-permute-done.35 = bf16[272,1024]{1,0:T(8,128)(2,1)S(1)} collective-permute-done((bf16[272,1024]{1,0:T(8,128)(2,1)S(1)}, bf16[272,1024]{1,0:T(8,128)(2,1)S(1)}, u32[]{:S(2)}, u32[]{:S(2)}) %collective-permute-start.35) | collective-permute-done | bytes 557088 | tf_op jit(solution)/shard_map/ppermute | solution.py:345
  (164 shorter events, 30.5 us)
Async XLA Ops:
  7.2 208.2 %reduce-scatter.2.cloned.1.call-start = ((), (), s32[]{:S(2)}) async-start(), calls=%async_computation.1 | async-start | bytes 7077888 | tf_op jit(solution)/shard_map/reduce_scatter | solution.py:935
  7.2 20.0 %collective-permute-start = (bf16[256,1024]{1,0:T(8,128)(2,1)}, bf16[256,1024]{1,0:T(8,128)(2,1)S(1)}, u32[]{:S(2)}, u32[]{:S(2)}) collective-permute-start(bf16[256,1024]{1,0:T(8,128)(2,1)} %bitcast.36), channel_id=1, source_target_pairs={{0,8},{4,12},{8,0},{12,4},{16,24},{20,28},{24,16},{28,20},{1,9},{5... | collective-permute-start | bytes 1572872 | tf_op jit(solution)/shard_map/ppermute | solution.py:345
  11.3 15.9 %collective-permute-start.2 = (bf16[128,1024]{1,0:T(8,128)(2,1)S(1)}, bf16[128,1024]{1,0:T(8,128)(2,1)S(1)}, u32[]{:S(2)}, u32[]{:S(2)}) collective-permute-start(bf16[128,1024]{1,0:T(8,128)(2,1)S(1)} %slice_select_fusion), channel_id=1, source_target_pairs={{0,2},{1,3},{2,0},{3,1},{4,6},{5,7},{6,4},{7,5},{8,10},{9,11},{10,... | collective-permute-start | bytes 786440 | tf_op jit(solution)/shard_map/ppermute | solution.py:345
  13.9 13.2 %collective-permute-start.3 = (bf16[128,1024]{1,0:T(8,128)(2,1)S(1)}, bf16[128,1024]{1,0:T(8,128)(2,1)S(1)}, u32[]{:S(2)}, u32[]{:S(2)}) collective-permute-start(bf16[128,1024]{1,0:T(8,128)(2,1)S(1)} %slice_select_fusion), channel_id=1, source_target_pairs={{0,1},{1,0},{2,3},{3,2},{4,5},{5,4},{6,7},{7,6},{8,9},{9,8},{10,11... | collective-permute-start | bytes 786440 | tf_op jit(solution)/shard_map/ppermute | solution.py:345
  15.5 11.7 %collective-permute-start.1 = (bf16[128,1024]{1,0:T(8,128)(2,1)}, bf16[128,1024]{1,0:T(8,128)(2,1)S(1)}, u32[]{:S(2)}, u32[]{:S(2)}) collective-permute-start(bf16[128,1024]{1,0:T(8,128)(2,1)} %bitcast.38), channel_id=1, source_target_pairs={{0,16},{4,20},{8,24},{12,28},{16,0},{20,4},{24,8},{28,12},{1,17},{... | collective-permute-start | bytes 786440 | tf_op jit(solution)/shard_map/ppermute | solution.py:345
  28.2 29.6 %copy-start.39 = (s32[512,2]{0,1:T(2,128)S(1)}, s32[512,2]{0,1:T(2,128)}, u32[]{:S(2)}) copy-start(s32[512,2]{0,1:T(2,128)} %param.15) | copy-start | bytes 12292
  28.2 29.7 %copy-start.38 = (bf16[1024,8]{0,1:T(8,128)(2,1)S(1)}, bf16[1024,8]{0,1:T(8,128)(2,1)}, u32[]{:S(2)}) copy-start(bf16[1024,8]{0,1:T(8,128)(2,1)} %param.20) | copy-start | bytes 49156
  28.2 24.1 %collective-permute-start.12 = (bf16[512,1024]{1,0:T(8,128)(2,1)}, bf16[512,1024]{1,0:T(8,128)(2,1)}, u32[]{:S(2)}, u32[]{:S(2)}) collective-permute-start(bf16[512,1024]{1,0:T(8,128)(2,1)} %pad_maximum_fusion.4.refs_9_), channel_id=1, source_target_pairs={{0,16},{4,20},{8,24},{12,28},{16,0},{20,4},{24,8},{28,12},{1,17},{... | collective-permute-start | bytes 3145736 | tf_op jit(solution)/shard_map/ppermute | solution.py:345
  28.8 38.3 %copy-start = (bf16[512,1024]{1,0:T(8,128)(2,1)S(1)}, bf16[512,1024]{1,0:T(8,128)(2,1)}, u32[]{:S(2)}) copy-start(bf16[512,1024]{1,0:T(8,128)(2,1)} %refs_8_.1) | copy-start | bytes 3145732
  28.8 38.3 %copy-start.1 = (bf16[512,1024]{1,0:T(8,128)(2,1)S(1)}, bf16[512,1024]{1,0:T(8,128)(2,1)}, u32[]{:S(2)}) copy-start(bf16[512,1024]{1,0:T(8,128)(2,1)} %refs_2_.1) | copy-start | bytes 3145732
  28.8 38.3 %copy-start.22 = (f32[1024]{0:T(1024)S(1)}, f32[1024]{0:T(1024)}, u32[]{:S(2)}) copy-start(f32[1024]{0:T(1024)} %param.19) | copy-start | bytes 12292
  28.8 24.0 %collective-permute-start.8 = (bf16[256,1024]{1,0:T(8,128)(2,1)S(1)}, bf16[256,1024]{1,0:T(8,128)(2,1)S(1)}, u32[]{:S(2)}, u32[]{:S(2)}) collective-permute-start(bf16[256,1024]{1,0:T(8,128)(2,1)S(1)} %pad_maximum_fusion.6.refs_13_.refs_5_), channel_id=1, source_target_pairs={{0,8},{4,12},{8,0},{12,4},{16,24},{20,28},{24,16},{28,20},{1,9},{5... | collective-permute-start | bytes 1572872 | tf_op jit(solution)/shard_map/ppermute | solution.py:345
  29.4 14.7 %collective-permute-start.4 = (bf16[128,1024]{1,0:T(8,128)(2,1)S(1)}, bf16[128,1024]{1,0:T(8,128)(2,1)S(1)}, u32[]{:S(2)}, u32[]{:S(2)}) collective-permute-start(bf16[128,1024]{1,0:T(8,128)(2,1)S(1)} %collective-permute-done.2), channel_id=1, source_target_pairs={{0,1},{1,0},{2,3},{3,2},{4,5},{5,4},{6,7},{7,6},{8,9},{9,8},{10,11... | collective-permute-start | bytes 786440 | tf_op jit(solution)/shard_map/ppermute | solution.py:345
  30.6 14.6 %collective-permute-start.6 = (bf16[512,256]{1,0:T(8,128)(2,1)S(1)}, bf16[512,256]{1,0:T(8,128)(2,1)}, u32[]{:S(2)}, u32[]{:S(2)}) collective-permute-start(bf16[512,256]{1,0:T(8,128)(2,1)S(1)} %copy-done.31), channel_id=1, source_target_pairs={{0,2},{1,3},{2,0},{3,1},{4,6},{5,7},{6,4},{7,5},{8,10},{9,11},{10,... | collective-permute-start | bytes 786440 | tf_op jit(solution)/shard_map/ppermute | solution.py:345
  33.0 19.4 %collective-permute-start.7 = (bf16[512,256]{1,0:T(8,128)(2,1)S(1)}, bf16[512,256]{1,0:T(8,128)(2,1)S(1)}, u32[]{:S(2)}, u32[]{:S(2)}) collective-permute-start(bf16[512,256]{1,0:T(8,128)(2,1)S(1)} %copy-done.31), channel_id=1, source_target_pairs={{0,1},{1,0},{2,3},{3,2},{4,5},{5,4},{6,7},{7,6},{8,9},{9,8},{10,11... | collective-permute-start | bytes 786440 | tf_op jit(solution)/shard_map/ppermute | solution.py:345
  44.1 22.9 %collective-permute-start.13 = (bf16[512,1024]{1,0:T(8,128)(2,1)}, bf16[512,1024]{1,0:T(8,128)(2,1)}, u32[]{:S(2)}, u32[]{:S(2)}) collective-permute-start(bf16[512,1024]{1,0:T(8,128)(2,1)} %pad_maximum_fusion.4.refs_9_), channel_id=1, source_target_pairs={{0,4},{4,0},{8,12},{12,8},{16,20},{20,16},{24,28},{28,24},{1,5},{5... | collective-permute-start | bytes 3145736 | tf_op jit(solution)/shard_map/ppermute | solution.py:345
  45.2 21.9 %collective-permute-start.5 = (bf16[512,1024]{1,0:T(8,128)(2,1)}, bf16[512,1024]{1,0:T(8,128)(2,1)}, u32[]{:S(2)}, u32[]{:S(2)}) collective-permute-start(bf16[512,1024]{1,0:T(8,128)(2,1)} %pad_maximum_fusion.2.refs_6_), channel_id=1, source_target_pairs={{0,4},{4,0},{8,12},{12,8},{16,20},{20,16},{24,28},{28,24},{1,5},{5... | collective-permute-start | bytes 3145736 | tf_op jit(solution)/shard_map/ppermute | solution.py:345
  52.3 14.7 %collective-permute-start.14 = (bf16[512,1024]{1,0:T(8,128)(2,1)}, bf16[512,1024]{1,0:T(8,128)(2,1)}, u32[]{:S(2)}, u32[]{:S(2)}) collective-permute-start(bf16[512,1024]{1,0:T(8,128)(2,1)} %collective-permute-done.12.refs_10_), channel_id=1, source_target_pairs={{0,4},{4,0},{8,12},{12,8},{16,20},{20,16},{24,28},{28,24},{1,5},{5... | collective-permute-start | bytes 3145736 | tf_op jit(solution)/shard_map/ppermute | solution.py:345
  52.4 3.4 %collective-permute-start.9 = (bf16[256,1024]{1,0:T(8,128)(2,1)S(1)}, bf16[256,1024]{1,0:T(8,128)(2,1)S(1)}, u32[]{:S(2)}, u32[]{:S(2)}) collective-permute-start(bf16[256,1024]{1,0:T(8,128)(2,1)S(1)} %pad_maximum_fusion.6.refs_13_.refs_5_), channel_id=1, source_target_pairs={{0,4},{4,0},{8,12},{12,8},{16,20},{20,16},{24,28},{28,24},{1,5},{5... | collective-permute-start | bytes 1572872 | tf_op jit(solution)/shard_map/ppermute | solution.py:345
  52.9 3.7 %collective-permute-start.10 = (bf16[256,1024]{1,0:T(8,128)(2,1)S(1)}, bf16[256,1024]{1,0:T(8,128)(2,1)S(1)}, u32[]{:S(2)}, u32[]{:S(2)}) collective-permute-start(bf16[256,1024]{1,0:T(8,128)(2,1)S(1)} %collective-permute-done.8.refs_14_.refs_6_), channel_id=1, source_target_pairs={{0,4},{4,0},{8,12},{12,8},{16,20},{20,16},{24,28},{28,24},{1,5},{5... | collective-permute-start | bytes 1572872 | tf_op jit(solution)/shard_map/ppermute | solution.py:345
  57.4 8.6 %collective-permute-start.11 = (bf16[512,256]{1,0:T(8,128)(2,1)}, bf16[512,256]{1,0:T(8,128)(2,1)S(1)}, u32[]{:S(2)}, u32[]{:S(2)}) collective-permute-start(bf16[512,256]{1,0:T(8,128)(2,1)} %collective-permute-done.6), channel_id=1, source_target_pairs={{0,1},{1,0},{2,3},{3,2},{4,5},{5,4},{6,7},{7,6},{8,9},{9,8},{10,11... | collective-permute-start | bytes 786440 | tf_op jit(solution)/shard_map/ppermute | solution.py:345
  87.6 12.8 %collective-permute-start.15 = (bf16[128,1024]{1,0:T(8,128)(2,1)S(1)}, bf16[128,1024]{1,0:T(8,128)(2,1)S(1)}, u32[]{:S(2)}, u32[]{:S(2)}) collective-permute-start(bf16[128,1024]{1,0:T(8,128)(2,1)S(1)} %get-tuple-element.96), channel_id=1, source_target_pairs={{0,1},{1,0},{2,3},{3,2},{4,5},{5,4},{6,7},{7,6},{8,9},{9,8},{10,11... | collective-permute-start | bytes 786440 | tf_op jit(solution)/shard_map/ppermute | solution.py:345
  101.1 40.5 %copy-start.10 = (f32[512,128]{1,0:T(8,128)S(1)}, f32[512,128]{1,0:T(8,128)}, u32[]{:S(2)}) copy-start(f32[512,128]{1,0:T(8,128)} %constant.37.clone.cosine.refs_5_) | copy-start | bytes 786436
  101.1 40.5 %copy-start.11 = (f32[512,128]{1,0:T(8,128)S(1)}, f32[512,128]{1,0:T(8,128)}, u32[]{:S(2)}) copy-start(f32[512,128]{1,0:T(8,128)} %constant.38.clone.sine.refs_6_) | copy-start | bytes 786436
  101.1 40.5 %copy-start.18 = (bf16[2,512,128]{2,1,0:T(8,128)(2,1)S(1)}, bf16[2,512,128]{2,1,0:T(8,128)(2,1)}, u32[]{:S(2)}) copy-start(bf16[2,512,128]{2,1,0:T(8,128)(2,1)} %get-tuple-element.71.refs_3_) | copy-start | bytes 786436
  103.0 14.6 %collective-permute-start.17 = (bf16[128,1024]{1,0:T(8,128)(2,1)}, bf16[128,1024]{1,0:T(8,128)(2,1)}, u32[]{:S(2)}, u32[]{:S(2)}) collective-permute-start(bf16[128,1024]{1,0:T(8,128)(2,1)} %add_convert_fusion.6), channel_id=1, source_target_pairs={{0,2},{1,3},{2,0},{3,1},{4,6},{5,7},{6,4},{7,5},{8,10},{9,11},{10,... | collective-permute-start | bytes 786440 | tf_op jit(solution)/shard_map/ppermute | solution.py:345
  106.1 12.3 %collective-permute-start.16 = (bf16[128,1024]{1,0:T(8,128)(2,1)}, bf16[128,1024]{1,0:T(8,128)(2,1)}, u32[]{:S(2)}, u32[]{:S(2)}) collective-permute-start(bf16[128,1024]{1,0:T(8,128)(2,1)} %copy-done.25), channel_id=1, source_target_pairs={{0,1},{1,0},{2,3},{3,2},{4,5},{5,4},{6,7},{7,6},{8,9},{9,8},{10,11... | collective-permute-start | bytes 786440 | tf_op jit(solution)/shard_map/ppermute | solution.py:345
  106.9 34.8 %copy-start.20 = (bf16[128,1024]{1,0:T(8,128)(2,1)S(1)}, bf16[128,1024]{1,0:T(8,128)(2,1)}, u32[]{:S(2)}) copy-start(bf16[128,1024]{1,0:T(8,128)(2,1)} %copy-done.19) | copy-start | bytes 786436
  120.6 13.5 %collective-permute-start.18 = (bf16[128,1024]{1,0:T(8,128)(2,1)S(1)}, bf16[128,1024]{1,0:T(8,128)(2,1)S(1)}, u32[]{:S(2)}, u32[]{:S(2)}) collective-permute-start(bf16[128,1024]{1,0:T(8,128)(2,1)S(1)} %get-tuple-element.103.refs_9_), channel_id=1, source_target_pairs={{0,2},{1,3},{2,0},{3,1},{4,6},{5,7},{6,4},{7,5},{8,10},{9,11},{10,... | collective-permute-start | bytes 786440 | tf_op jit(solution)/shard_map/ppermute | solution.py:345
  120.8 13.3 %collective-permute-start.19 = (bf16[128,1024]{1,0:T(8,128)(2,1)S(1)}, bf16[128,1024]{1,0:T(8,128)(2,1)S(1)}, u32[]{:S(2)}, u32[]{:S(2)}) collective-permute-start(bf16[128,1024]{1,0:T(8,128)(2,1)S(1)} %get-tuple-element.103.refs_9_), channel_id=1, source_target_pairs={{0,1},{1,0},{2,3},{3,2},{4,5},{5,4},{6,7},{7,6},{8,9},{9,8},{10,11... | collective-permute-start | bytes 786440 | tf_op jit(solution)/shard_map/ppermute | solution.py:345
  134.1 7.5 %collective-permute-start.20 = (bf16[128,1024]{1,0:T(8,128)(2,1)S(1)}, bf16[128,1024]{1,0:T(8,128)(2,1)S(1)}, u32[]{:S(2)}, u32[]{:S(2)}) collective-permute-start(bf16[128,1024]{1,0:T(8,128)(2,1)S(1)} %collective-permute-done.18.refs_11_), channel_id=1, source_target_pairs={{0,1},{1,0},{2,3},{3,2},{4,5},{5,4},{6,7},{7,6},{8,9},{9,8},{10,11... | collective-permute-start | bytes 786440 | tf_op jit(solution)/shard_map/ppermute | solution.py:345
  155.6 2.4 collective-permute-start.29
  158.5 11.5 %collective-permute-start.30 = (bf16[384,512]{1,0:T(8,128)(2,1)S(1)}, bf16[384,512]{1,0:T(8,128)(2,1)S(1)}, u32[]{:S(2)}, u32[]{:S(2)}) collective-permute-start(bf16[384,512]{1,0:T(8,128)(2,1)S(1)} %get-tuple-element.137), channel_id=1, source_target_pairs={{0,8},{4,12},{8,0},{12,4},{16,24},{20,28},{24,16},{28,20},{1,9},{5... | collective-permute-start | bytes 1179656 | tf_op jit(solution)/shard_map/ppermute | solution.py:345
  159.1 10.9 %collective-permute-start.32 = (bf16[384,512]{1,0:T(8,128)(2,1)S(1)}, bf16[384,512]{1,0:T(8,128)(2,1)S(1)}, u32[]{:S(2)}, u32[]{:S(2)}) collective-permute-start(bf16[384,512]{1,0:T(8,128)(2,1)S(1)} %get-tuple-element.138), channel_id=1, source_target_pairs={{0,16},{4,20},{8,24},{12,28},{16,0},{20,4},{24,8},{28,12},{1,17},{... | collective-permute-start | bytes 1179656 | tf_op jit(solution)/shard_map/ppermute | solution.py:345
  160.6 12.0 %collective-permute-start.24 = (f32[10,1024]{1,0:T(8,128)S(1)}, f32[10,1024]{1,0:T(8,128)S(1)}, u32[]{:S(2)}, u32[]{:S(2)}) collective-permute-start(f32[10,1024]{1,0:T(8,128)S(1)} %pad_maximum_fusion.7), channel_id=1, source_target_pairs={{0,4},{4,0},{8,12},{12,8},{16,20},{20,16},{24,28},{28,24},{1,5},{5... | collective-permute-start | bytes 122888 | tf_op jit(solution)/shard_map/ppermute | solution.py:345
  160.7 16.9 %collective-permute-start.21 = (bf16[256,1024]{1,0:T(8,128)(2,1)}, bf16[256,1024]{1,0:T(8,128)(2,1)S(1)}, u32[]{:S(2)}, u32[]{:S(2)}) collective-permute-start(bf16[256,1024]{1,0:T(8,128)(2,1)} %get-tuple-element.113), channel_id=1, source_target_pairs={{0,1},{1,0},{2,3},{3,2},{4,5},{5,4},{6,7},{7,6},{8,9},{9,8},{10,11... | collective-permute-start | bytes 1572872 | tf_op jit(solution)/shard_map/ppermute | solution.py:345
  171.1 12.1 %collective-permute-start.31 = (bf16[384,512]{1,0:T(8,128)(2,1)}, bf16[384,512]{1,0:T(8,128)(2,1)}, u32[]{:S(2)}, u32[]{:S(2)}) collective-permute-start(bf16[384,512]{1,0:T(8,128)(2,1)} %get-tuple-element.135), channel_id=1, source_target_pairs={{0,16},{4,20},{8,24},{12,28},{16,0},{20,4},{24,8},{28,12},{1,17},{... | collective-permute-start | bytes 1179656 | tf_op jit(solution)/shard_map/ppermute | solution.py:345
  172.6 4.3 %collective-permute-start.25 = (f32[10,1024]{1,0:T(8,128)S(1)}, f32[10,1024]{1,0:T(8,128)S(1)}, u32[]{:S(2)}, u32[]{:S(2)}) collective-permute-start(f32[10,1024]{1,0:T(8,128)S(1)} %fusion), channel_id=1, source_target_pairs={{0,8},{4,12},{8,0},{12,4},{16,24},{20,28},{24,16},{28,20},{1,9},{5... | collective-permute-start | bytes 122888 | tf_op jit(solution)/shard_map/ppermute | solution.py:345
  177.0 11.2 %collective-permute-start.26 = (f32[10,1024]{1,0:T(8,128)S(1)}, f32[10,1024]{1,0:T(8,128)S(1)}, u32[]{:S(2)}, u32[]{:S(2)}) collective-permute-start(f32[10,1024]{1,0:T(8,128)S(1)} %add.70), channel_id=1, source_target_pairs={{0,16},{4,20},{8,24},{12,28},{16,0},{20,4},{24,8},{28,12},{1,17},{... | collective-permute-start | bytes 122888 | tf_op jit(solution)/shard_map/ppermute | solution.py:345
  177.6 9.4 %collective-permute-start.33 = (bf16[384,512]{1,0:T(8,128)(2,1)}, bf16[384,512]{1,0:T(8,128)(2,1)S(1)}, u32[]{:S(2)}, u32[]{:S(2)}) collective-permute-start(bf16[384,512]{1,0:T(8,128)(2,1)} %get-tuple-element.136), channel_id=1, source_target_pairs={{0,8},{4,12},{8,0},{12,4},{16,24},{20,28},{24,16},{28,20},{1,9},{5... | collective-permute-start | bytes 1179656 | tf_op jit(solution)/shard_map/ppermute | solution.py:345
  179.2 24.4 %copy-start.9 = (f32[256,1024]{1,0:T(8,128)S(1)}, f32[256,1024]{1,0:T(8,128)}, u32[]{:S(2)}) copy-start(f32[256,1024]{1,0:T(8,128)} %get-tuple-element.110.own) | copy-start | bytes 3145732
  179.3 24.4 %copy-start.14 = (f32[128,1024]{1,0:T(8,128)S(1)}, f32[128,1024]{1,0:T(8,128)}, u32[]{:S(2)}) copy-start(f32[128,1024]{1,0:T(8,128)} %copy-done.13) | copy-start | bytes 1572868
  179.3 24.1 %collective-permute-start.23 = (bf16[256,1024]{1,0:T(8,128)(2,1)S(1)}, bf16[256,1024]{1,0:T(8,128)(2,1)S(1)}, u32[]{:S(2)}, u32[]{:S(2)}) collective-permute-start(bf16[256,1024]{1,0:T(8,128)(2,1)S(1)} %add_convert_fusion.1), channel_id=1, source_target_pairs={{0,2},{1,3},{2,0},{3,1},{4,6},{5,7},{6,4},{7,5},{8,10},{9,11},{10,... | collective-permute-start | bytes 1572872 | tf_op jit(solution)/shard_map/ppermute | solution.py:345
  181.8 21.9 %collective-permute-start.22 = (bf16[256,1024]{1,0:T(8,128)(2,1)}, bf16[256,1024]{1,0:T(8,128)(2,1)S(1)}, u32[]{:S(2)}, u32[]{:S(2)}) collective-permute-start(bf16[256,1024]{1,0:T(8,128)(2,1)} %copy-done.24), channel_id=1, source_target_pairs={{0,1},{1,0},{2,3},{3,2},{4,5},{5,4},{6,7},{7,6},{8,9},{9,8},{10,11... | collective-permute-start | bytes 1572872 | tf_op jit(solution)/shard_map/ppermute | solution.py:345
  188.1 22.8 %collective-permute-start.34 = (bf16[768,512]{1,0:T(8,128)(2,1)S(1)}, bf16[768,512]{1,0:T(8,128)(2,1)S(1)}, u32[]{:S(2)}, u32[]{:S(2)}) collective-permute-start(bf16[768,512]{1,0:T(8,128)(2,1)S(1)} %pad_maximum_fusion.5), channel_id=1, source_target_pairs={{0,4},{4,0},{8,12},{12,8},{16,20},{20,16},{24,28},{28,24},{1,5},{5... | collective-permute-start | bytes 2359304 | tf_op jit(solution)/shard_map/ppermute | solution.py:345
  204.1 26.0 %collective-permute-start.27 = (bf16[272,1024]{1,0:T(8,128)(2,1)S(1)}, bf16[272,1024]{1,0:T(8,128)(2,1)S(1)}, u32[]{:S(2)}, u32[]{:S(2)}) collective-permute-start(bf16[272,1024]{1,0:T(8,128)(2,1)S(1)} %finish.1), channel_id=1, source_target_pairs={{0,2},{1,3},{2,0},{3,1},{4,6},{5,7},{6,4},{7,5},{8,10},{9,11},{10,... | collective-permute-start | bytes 1671176 | tf_op jit(solution)/shard_map/ppermute | solution.py:345
  205.5 24.7 %collective-permute-start.28 = (bf16[272,1024]{1,0:T(8,128)(2,1)S(1)}, bf16[272,1024]{1,0:T(8,128)(2,1)}, u32[]{:S(2)}, u32[]{:S(2)}) collective-permute-start(bf16[272,1024]{1,0:T(8,128)(2,1)S(1)} %finish.1), channel_id=1, source_target_pairs={{0,1},{1,0},{2,3},{3,2},{4,5},{5,4},{6,7},{7,6},{8,9},{9,8},{10,11... | collective-permute-start | bytes 1671176 | tf_op jit(solution)/shard_map/ppermute | solution.py:345
  230.3 12.2 %collective-permute-start.35 = (bf16[272,1024]{1,0:T(8,128)(2,1)S(1)}, bf16[272,1024]{1,0:T(8,128)(2,1)S(1)}, u32[]{:S(2)}, u32[]{:S(2)}) collective-permute-start(bf16[272,1024]{1,0:T(8,128)(2,1)S(1)} %collective-permute-done.27), channel_id=1, source_target_pairs={{0,1},{1,0},{2,3},{3,2},{4,5},{5,4},{6,7},{7,6},{8,9},{9,8},{10,11... | collective-permute-start | bytes 1671176 | tf_op jit(solution)/shard_map/ppermute | solution.py:345
  (29 other events, 145.3 us)
Sparse Core Ops, SparseCore 0:
  101.2 61.9 reduce-scatter.1

commit v4 on v3

--- a/solution.py
+++ b/solution.py
@@ -335,7 +335,6 @@
 
 LANES = 128
 ROWS = 128
-SMALL_ROWS = 16
 IN_ORDER = (0, 2, 4, 6, 1, 3, 5, 7)
 OUT_ORDER = (0, 4, 2, 6, 1, 5, 3, 7)
 
@@ -359,27 +358,21 @@
     return parts[0], exchange(near, "tensor", 1), far
 
 
-def gather_pairs(own, arrived, second):
-    near = jnp.concatenate([own, arrived])
-    far = exchange(near, "expert", second)
+def gather_pairs(near, far):
     return [near, far, exchange(near, "expert", 1), exchange(far, "expert", 1)]
 
 
-def sum_experts(array_in):
+def exchange_halves(array_in, bits):
+    rows = array_in.shape[0] // 2
+    halves = []
+    for half, bit in zip((array_in[:rows], array_in[rows:]), bits):
+        arrived = exchange(half, "expert", bit)
+        halves.append((half.astype(jnp.float32) + arrived.astype(jnp.float32)).astype(jnp.bfloat16))
+    return jnp.concatenate(halves)
+
+
+def join_cores(half):
     core = lax.axis_index("expert") & 1
-    rows = array_in.shape[0] // 2
-    top, bottom = array_in[:rows], array_in[rows:]
-    keep = jnp.where(core == 0, top, bottom)
-    give = jnp.where(core == 0, bottom, top).astype(jnp.bfloat16)
-    half = keep + exchange(give, "expert", 1).astype(jnp.float32)
-    pieces = []
-    for piece, bits in ((half[: rows // 2], (2, 4)), (half[rows // 2 :], (4, 2))):
-        piece = piece.astype(jnp.bfloat16)
-        for bit in bits:
-            arrived = exchange(piece, "expert", bit)
-            piece = (piece.astype(jnp.float32) + arrived.astype(jnp.float32)).astype(jnp.bfloat16)
-        pieces.append(piece)
-    half = jnp.concatenate(pieces)
     other = exchange(half, "expert", 1)
     return jnp.concatenate(
         [jnp.where(core == 0, half, other), jnp.where(core == 0, other, half)]
@@ -447,7 +440,6 @@
     w_qkv,
     cosine,
     sine,
-    normed_out,
     queries_out,
     pairs_out,
     probs_out,
@@ -465,8 +457,6 @@
         values = layer_in[rows, :].astype(jnp.float32)
         scale = lax.rsqrt(jnp.mean(values * values, axis=-1, keepdims=True) + epsilon)
         normed[rows, :] = (values * scale * gain[...]).astype(jnp.bfloat16)
-    copies = [pltpu.make_async_copy(normed, normed_out, sems.at[0])]
-    copies[0].start()
     is_first = first_head((ROWS, LANES))
     for kv in range(kv_here):
         projected = dot_plain(normed[...], w_qkv[:, 2 * LANES * kv : 2 * LANES * (kv + 1)])
@@ -483,10 +473,12 @@
             pairs[kv, rows, :] = jnp.where(
                 is_first, pair * cos_rows + turn(pair) * sin_rows, pair
             ).astype(jnp.bfloat16)
-    copies.append(pltpu.make_async_copy(queries, queries_out, sems.at[1]))
-    copies.append(pltpu.make_async_copy(pairs, pairs_out, sems.at[2]))
-    copies[1].start()
-    copies[2].start()
+    copies = [
+        pltpu.make_async_copy(queries, queries_out, sems.at[0]),
+        pltpu.make_async_copy(pairs, pairs_out, sems.at[1]),
+    ]
+    for copy in copies:
+        copy.start()
     for block in range(token_count // ROWS):
         keys = (block + 1) * ROWS
         token = block * ROWS + (
@@ -511,7 +503,7 @@
             ).astype(jnp.bfloat16)
         copies.append(
             pltpu.make_async_copy(
-                probs.at[:, block, :, :keys], probs_out.at[:, block, :, :keys], sems.at[3 + block]
+                probs.at[:, block, :, :keys], probs_out.at[:, block, :, :keys], sems.at[2 + block]
             )
         )
         copies[-1].start()
@@ -622,10 +614,10 @@
 def weight_grad_kernel(tensor_count, *refs):
     place, normed, out_grad, active, pre_grad = refs[:5]
     w_outs, parts = refs[5:9], refs[9 : 9 + tensor_count]
-    grads, total, slots, sems = refs[9 + tensor_count :]
+    kept, given, total = refs[9 + tensor_count :]
     token_count, model_width = normed.shape
-    experts_all = grads.shape[0]
     units = w_outs[0].shape[0] // 2
+    experts_all = 2 * kept.shape[0] // (3 * units)
 
     def column_step(number, carry):
         columns = pl.ds(pl.multiple_of(number * 2 * LANES, 2 * LANES), 2 * LANES)
@@ -639,45 +631,60 @@
 
     lax.fori_loop(0, model_width // (2 * LANES), column_step, 0)
     write_parts(place, total, parts, token_count // tensor_count)
-    copies = []
     for number in range(experts_all):
-        name = place[1] ^ IN_ORDER[number]
         out_number = OUT_ORDER.index(IN_ORDER[number])
-        slot = number % 2
-        if number >= 2:
-            copies[number - 2].wait()
-        slots[slot, : 2 * units, :] = transposed_dot(
+        grads = kept if number < experts_all // 2 else given
+        in_row = number % (experts_all // 2) * 2 * units
+        out_row = experts_all * units + out_number % (experts_all // 2) * units
+        grads[pl.ds(in_row, 2 * units), :] = transposed_dot(
             pre_grad[:, 2 * number * units : 2 * (number + 1) * units], normed[...]
         ).astype(jnp.bfloat16)
-        slots[slot, 2 * units :, :] = transposed_dot(
+        grads[pl.ds(out_row, units), :] = transposed_dot(
             active[:, out_number * units : (out_number + 1) * units], out_grad[...]
         ).astype(jnp.bfloat16)
-        copies.append(pltpu.make_async_copy(slots.at[slot], grads.at[name], sems.at[slot]))
-        copies[-1].start()
-    for copy in copies[-2:]:
-        copy.wait()
+
+
+def add_grads_kernel(kept, given, in_kept, in_given, out_kept, out_given):
+    row = 0
+    for target in (in_kept, in_given, out_kept, out_given):
+        rows = pl.ds(row, target.shape[0])
+        summed = kept[rows, :].astype(jnp.float32) + given[rows, :].astype(jnp.float32)
+        target[...] = summed.astype(target.dtype)
+        row += target.shape[0]
 
 
 def attend_back_kernel(tensor_count, *refs):
-    place, far_refs, refs = refs[0], refs[1:9], refs[9:]
+    place, far_refs, refs = refs[0], refs[1:8], refs[8:]
     blocks, refs = refs[:tensor_count], refs[tensor_count:]
     mixtures, refs = refs[:tensor_count], refs[tensor_count:]
     parts, refs = refs[:tensor_count], refs[tensor_count:]
-    branch_grad, projected_grad, gain_part, heads_grad, pair_grad, total = refs[:6]
-    near_refs, sems = refs[6:14], refs[14]
-    w_output, queries, pairs, probs, cosine, sine, w_qkv, layer_in = near_refs
+    branch_grad, projected_grad, heads_grad, pair_grad, total = refs[:5]
+    near_refs, sems = refs[5:12], refs[12]
+    w_output, queries, pairs, probs, cosine, sine, w_qkv = near_refs
     copies = [
         pltpu.make_async_copy(source, target, sems.at[number])
         for number, (source, target) in enumerate(zip(far_refs, near_refs))
     ]
-    for copy in copies:
-        copy.start()
-    token_count, model_width = layer_in.shape
+    token_count, model_width = branch_grad.shape
     span = token_count // tensor_count
+    mixture_copies = [
+        pltpu.make_async_copy(mixture, part.at[pl.ds(span, span)], sems.at[len(copies) + number])
+        for number, (mixture, part) in enumerate(zip(mixtures, parts))
+    ]
+    block_copies = []
     for number, block in enumerate(blocks):
         row = pl.multiple_of((place[0] ^ number) * span, span)
-        branch_grad[pl.ds(row, span), :] = block[...]
-    copies[0].wait()
+        block_copies.append(
+            pltpu.make_async_copy(
+                block,
+                branch_grad.at[pl.ds(row, span)],
+                sems.at[len(copies) + tensor_count + number],
+            )
+        )
+    for copy in block_copies + copies + mixture_copies:
+        copy.start()
+    for copy in copies[:1] + block_copies:
+        copy.wait()
     heads_grad[...] = dot_transposed(branch_grad[...], w_output[...])
     for copy in copies[1:6]:
         copy.wait()
@@ -728,15 +735,39 @@
 
     lax.fori_loop(0, model_width // (2 * LANES), column_step, 0)
     write_parts(place, total, [part.at[:span] for part in parts], span)
-    for mixture, part in zip(mixtures, parts):
-        part[span:, :] = mixture[...]
-    gain_sum = jnp.zeros((1, model_width), jnp.float32)
+    for copy in mixture_copies:
+        copy.wait()
+
+
+def attend_grad_kernel(
+    place, layer_in, gain, projected_grad, attended, branch_grad, kept, given, normed
+):
+    token_count, model_width = layer_in.shape
     for row in range(0, token_count, ROWS):
         rows = pl.ds(row, ROWS)
         values = layer_in[rows, :].astype(jnp.float32)
         scale = lax.rsqrt(jnp.mean(values * values, axis=-1, keepdims=True) + epsilon)
-        gain_sum = gain_sum + jnp.sum(total[rows, :] * (values * scale), 0, keepdims=True)
-    gain_part[...] = gain_sum
+        normed[rows, :] = (values * scale * gain[...]).astype(jnp.bfloat16)
+    width = projected_grad.shape[1]
+    blocks = []
+    for row in range(0, model_width, attended.shape[1]):
+        lanes = pl.ds(row, attended.shape[1])
+        blocks.append((normed, lanes, projected_grad, pl.ds(0, width)))
+    for lane in range(0, model_width, width):
+        blocks.append((attended, pl.ds(0, attended.shape[1]), branch_grad, pl.ds(lane, width)))
+    half = len(blocks) // 2
+    for number, (left, left_lanes, right, right_lanes) in enumerate(blocks):
+        rows = pl.ds(number % half * attended.shape[1], attended.shape[1])
+        grad = transposed_dot(left[:, left_lanes], right[:, right_lanes])
+        mine = (place[1] & 1) == number // half
+
+        @pl.when(mine)
+        def _():
+            kept[rows, :] = grad
+
+        @pl.when(jnp.logical_not(mine))
+        def _():
+            given[rows, :] = grad.astype(jnp.bfloat16)
 
 
 def norm_back_kernel(own, near, far, residual, inverse, gain, out_grad, residual_grad, low_grad):
@@ -748,7 +779,7 @@
     low_grad[...] = total.astype(jnp.bfloat16)
 
 
-def finish_kernel(own, near, far, layer_in, gain, residual_grad, residual, small, block):
+def finish_kernel(own, near, far, layer_in, gain, residual_grad, residual, block):
     span = layer_in.shape[0]
     summed = own[...] + near[...].astype(jnp.float32) + far[...].astype(jnp.float32)
     values = layer_in[...].astype(jnp.float32)
@@ -757,7 +788,6 @@
     block[span : 2 * span, :] = (
         residual_grad[...] + rms_backward(values, inverse, gain[...], summed[:span])
     ).astype(jnp.bfloat16)
-    block[2 * span :, :] = small[...]
 
 
 def in_vmem(count):
@@ -805,11 +835,11 @@
     def token_block(array_in):
         return lax.dynamic_slice_in_dim(array_in, tensor_here * span, span, 0)
 
-    def in_order(blocks, rows=span):
-        joined = jnp.zeros((tensor_count * rows,) + blocks[0].shape[1:], blocks[0].dtype)
+    def in_order(blocks):
+        joined = jnp.zeros((token_count,) + blocks[0].shape[1:], blocks[0].dtype)
         for number, block in enumerate(blocks):
             joined = lax.dynamic_update_slice_in_dim(
-                joined, block, (tensor_here ^ number) * rows, 0
+                joined, block, (tensor_here ^ number) * span, 0
             )
         return joined
 
@@ -825,18 +855,18 @@
     cosine, sine = angle_tables(token_count)
     qkv_flat = w_qkv.reshape(model_width, -1)
     kept = (
-        shaped((token_count, model_width), low),
         shaped((kv_here, block_count, 2 * ROWS, LANES), low),
         shaped((kv_here, token_count, LANES), low),
         shaped((kv_here, block_count, 2 * ROWS, token_count), low),
     )
-    normed_one, queries, pairs, probs, attended = pl.pallas_call(
+    queries, pairs, probs, attended = pl.pallas_call(
         attend_kernel,
         out_shape=kept + (shaped((token_count, head_width), low),),
         in_specs=in_smem(1) + in_vmem(5),
-        out_specs=tuple(in_hbm(4) + in_vmem(1)),
-        scratch_shapes=[pltpu.VMEM(each.shape, low) for each in kept]
-        + [pltpu.SemaphoreType.DMA((3 + block_count,))],
+        out_specs=tuple(in_hbm(3) + in_vmem(1)),
+        scratch_shapes=[pltpu.VMEM((token_count, model_width), low)]
+        + [pltpu.VMEM(each.shape, low) for each in kept]
+        + [pltpu.SemaphoreType.DMA((2 + block_count,))],
         compiler_params=pltpu.CompilerParams(vmem_limit_bytes=56 * mib),
         name="attend",
     )(seq_lengths, layer_in, gain_attn[None], qkv_flat, cosine, sine)
@@ -844,16 +874,23 @@
     w_in_near, w_out_near, output_far, output_near, attended = lax.optimization_barrier(
         (w_in_near, w_out_near, output_far, output_near, attended)
     )
+    w_in_near = jnp.concatenate([w_in_own, w_in_near])
+    w_out_near = jnp.concatenate([w_out_own, w_out_near])
+    w_in_far = exchange(w_in_near, "expert", 4)
+    w_out_far = exchange(w_out_near, "expert", 2)
     heads_far = exchange(attended, "tensor", 2)
     heads_near = exchange(attended, "tensor", 1)
-    w_in_all = gather_pairs(w_in_own, w_in_near, 4)
-    w_out_all = gather_pairs(w_out_own, w_out_near, 2)
-    heads_far, heads_near, w_out_all = lax.optimization_barrier(
-        (heads_far, heads_near, w_out_all)
-    )
+    output_both = exchange(output_far, "tensor", 1)
+    heads_far, heads_near = lax.optimization_barrier((heads_far, heads_near))
     heads_both = exchange(heads_far, "tensor", 1)
+    heads_both, output_both, w_in_near, w_in_far, w_out_near, w_out_far = (
+        lax.optimization_barrier(
+            (heads_both, output_both, w_in_near, w_in_far, w_out_near, w_out_far)
+        )
+    )
+    w_in_all = gather_pairs(w_in_near, w_in_far)
+    w_out_all = gather_pairs(w_out_near, w_out_far)
     heads_all = [attended, heads_near, heads_far, heads_both]
-    output_both = exchange(output_far, "tensor", 1)
     output_mine = jnp.concatenate([output_own, output_near, output_far, output_both])
     output_other = exchange(output_mine, "expert", 1)
     router_rows = jnp.pad(jnp.transpose(w_router), ((0, LANES - experts_all), (0, 0)))
@@ -901,21 +938,39 @@
     normed_parts, middle = middle[:tensor_count], middle[tensor_count:]
     residual, inverse_two, normed_two, active, pre_grad, gain_ffn_part, router_part = middle
 
+    relayed = exchange(normed_parts[3], "tensor", 1)
+    half_grads = shaped((experts_all // 2 * 3 * units, model_width), low)
     late = pl.pallas_call(
         functools.partial(weight_grad_kernel, tensor_count),
-        out_shape=part_shapes + (shaped((experts_all, 3 * units, model_width), low),),
+        out_shape=part_shapes + (half_grads,) * 2,
         in_specs=in_smem(1) + in_vmem(8),
-        out_specs=tuple(in_vmem(tensor_count) + in_hbm(1)),
-        scratch_shapes=[
-            pltpu.VMEM((token_count, model_width), wide),
-            pltpu.VMEM((2, 3 * units, model_width), low),
-            pltpu.SemaphoreType.DMA((2,)),
-        ],
-        compiler_params=pltpu.CompilerParams(vmem_limit_bytes=48 * mib),
+        out_specs=tuple(in_vmem(tensor_count + 2)),
+        scratch_shapes=[pltpu.VMEM((token_count, model_width), wide)],
+        compiler_params=pltpu.CompilerParams(vmem_limit_bytes=16 * mib),
         name="weight_grad",
     )(place, normed_two, out_grad, active, pre_grad, *w_out_all)
-    late, relayed = lax.optimization_barrier((late, exchange(normed_parts[3], "tensor", 1)))
-    mixture_parts, weight_grads = late[:tensor_count], late[tensor_count]
+    late, relayed = lax.optimization_barrier((late, relayed))
+    normed_pieces = scatter_parts(normed_parts, relayed)
+    mixture_parts, kept_grads, given_grads = late[:tensor_count], late[-2], late[-1]
+    given_grads = exchange(given_grads, "expert", 1)
+
+    in_rows, out_rows = experts_all * units // 2, experts_all * units // 4
+    in_kept, in_given, out_kept, out_given = pl.pallas_call(
+        add_grads_kernel,
+        out_shape=(
+            shaped((in_rows, model_width), wide),
+            shaped((in_rows, model_width), low),
+            shaped((out_rows, model_width), wide),
+            shaped((out_rows, model_width), low),
+        ),
+        in_specs=in_vmem(2),
+        out_specs=tuple(in_vmem(4)),
+        compiler_params=pltpu.CompilerParams(vmem_limit_bytes=16 * mib),
+        name="add_grads",
+    )(kept_grads, given_grads)
+    residual, in_kept, in_given, out_kept, out_given = lax.optimization_barrier(
+        (residual, in_kept, in_given, out_kept, out_given)
+    )
     residual_grad, low_grad = pl.pallas_call(
         norm_back_kernel,
         out_shape=(shaped((span, model_width), wide), shaped((span, model_width), low)),
@@ -924,7 +979,7 @@
         compiler_params=pltpu.CompilerParams(vmem_limit_bytes=6 * mib),
         name="norm_back",
     )(
-        *scatter_parts(normed_parts, relayed),
+        *normed_pieces,
         residual,
         inverse_two,
         gain_ffn[None],
@@ -932,13 +987,14 @@
     )
     grad_blocks = gather_blocks(low_grad)
 
-    weight_grads = lax.psum_scatter(
-        weight_grads, "expert", scatter_dimension=0, tiled=False
-    ).astype(wide)
-    w_in_grad = weight_grads[: 2 * units].reshape(w_in.shape)
-    w_out_grad = weight_grads[2 * units :].reshape(w_out.shape)
-
-    fetched = (w_output, queries, pairs, probs, cosine, sine, qkv_flat, layer_in)
+    in_arrived = exchange(in_given, "expert", 4)
+    out_arrived = exchange(out_given, "expert", 2)
+    in_summed = in_kept + in_arrived.astype(wide)
+    out_summed = out_kept + out_arrived.astype(wide)
+    in_arrived = exchange(in_summed[in_rows // 2 :].astype(low), "expert", 2)
+    out_arrived = exchange(out_summed[out_rows // 2 :].astype(low), "expert", 4)
+
+    fetched = (w_output, queries, pairs, probs, cosine, sine, qkv_flat)
     back = pl.pallas_call(
         functools.partial(attend_back_kernel, tensor_count),
         out_shape=(shaped((2 * span, model_width), wide),)
@@ -946,18 +1002,17 @@
         + (
             shaped((token_count, model_width), low),
             shaped((token_count, 2 * head_width), low),
-            shaped((1, model_width), wide),
         ),
-        in_specs=in_smem(1) + in_hbm(8) + in_vmem(2 * tensor_count),
-        out_specs=tuple(in_vmem(tensor_count + 3)),
+        in_specs=in_smem(1) + in_hbm(7 + 2 * tensor_count),
+        out_specs=tuple(in_vmem(tensor_count + 2)),
         scratch_shapes=[
             pltpu.VMEM((token_count, head_width), wide),
             pltpu.VMEM((token_count, LANES), wide),
             pltpu.VMEM((token_count, model_width), wide),
         ]
         + [pltpu.VMEM(each.shape, each.dtype) for each in fetched]
-        + [pltpu.SemaphoreType.DMA((len(fetched),))],
-        compiler_params=pltpu.CompilerParams(vmem_limit_bytes=50 * mib),
+        + [pltpu.SemaphoreType.DMA((len(fetched) + 2 * tensor_count,))],
+        compiler_params=pltpu.CompilerParams(vmem_limit_bytes=58 * mib),
         name="attend_back",
     )(
         place,
@@ -965,51 +1020,68 @@
         *grad_blocks,
         *mixture_parts,
     )
-    input_parts, (branch_grad, projected_grad, gain_attn_part) = (
+    input_parts, (branch_grad, projected_grad) = (
         back[:tensor_count],
         back[tensor_count:],
     )
-    w_output_grad = transposed_dot(attended, branch_grad)
-    lanes_each = w_output_grad.shape[1] * kv_here * LANES // model_width * 2
-    summed = sum_experts(
-        jnp.concatenate(
-            [transposed_dot(normed_one, projected_grad)]
-            + [
-                w_output_grad[:, lanes : lanes + lanes_each]
-                for lanes in range(0, model_width, lanes_each)
-            ]
-        )
-    )
-    qkv_summed = summed[:model_width].reshape(w_qkv.shape)
-    output_summed = jnp.concatenate(split_blocks(summed[model_width:], 0, 2), 1)
-
-    small = sum_over_experts(jnp.concatenate([router_part, gain_ffn_part, gain_attn_part]))
-    small = jnp.pad(small, ((0, SMALL_ROWS - small.shape[0]), (0, 0))).astype(low)
+    relayed = exchange(input_parts[3], "tensor", 1)
+    row_count = (model_width + w_output.shape[0] * model_width // (2 * head_width)) // 2
+    kept_sums, given_sums = pl.pallas_call(
+        attend_grad_kernel,
+        out_shape=(
+            shaped((row_count, 2 * head_width), wide),
+            shaped((row_count, 2 * head_width), low),
+        ),
+        in_specs=in_smem(1) + in_vmem(5),
+        out_specs=tuple(in_vmem(2)),
+        scratch_shapes=[pltpu.VMEM((token_count, model_width), low)],
+        compiler_params=pltpu.CompilerParams(vmem_limit_bytes=12 * mib),
+        name="attend_grad",
+    )(place, layer_in, gain_attn[None], projected_grad, attended, branch_grad)
+    relayed, kept_sums, given_sums, in_summed, out_summed = lax.optimization_barrier(
+        (relayed, kept_sums, given_sums, in_summed, out_summed)
+    )
+    sums_half = kept_sums + exchange(given_sums, "expert", 1).astype(wide)
+    sums = exchange_halves(sums_half.astype(low), (2, 4))
+    input_pieces = scatter_parts(input_parts, relayed)
+    residual, in_arrived, out_arrived, sums = lax.optimization_barrier(
+        (residual, in_arrived, out_arrived, sums)
+    )
+    w_in_grad = (in_summed[: in_rows // 2] + in_arrived.astype(wide)).reshape(w_in.shape)
+    w_out_grad = (out_summed[: out_rows // 2] + out_arrived.astype(wide)).reshape(w_out.shape)
     block = pl.pallas_call(
         finish_kernel,
-        out_shape=shaped((2 * span + SMALL_ROWS, model_width), low),
-        in_specs=in_vmem(8),
+        out_shape=shaped((2 * span, model_width), low),
+        in_specs=in_vmem(7),
         out_specs=in_vmem(1)[0],
         compiler_params=pltpu.CompilerParams(vmem_limit_bytes=6 * mib),
         name="finish",
     )(
-        *scatter_parts(input_parts, exchange(input_parts[3], "tensor", 1)),
+        *input_pieces,
         token_block(layer_in),
         gain_attn[None],
         residual_grad,
         residual,
-        small,
     )
     far = exchange(block, "tensor", 2)
     near = exchange(block, "tensor", 1)
-    far, near, qkv_summed, output_summed, w_in_grad, w_out_grad = lax.optimization_barrier(
-        (far, near, qkv_summed, output_summed, w_in_grad, w_out_grad)
-    )
+    small = jnp.concatenate([router_part, gain_ffn_part])
+    sums, small, _ = lax.optimization_barrier((sums, small, block))
+    small = sum_over_experts(small)
+    summed = join_cores(exchange_halves(sums, (4, 2)))
+    qkv_summed = summed[:model_width].reshape(w_qkv.shape)
+    output_summed = jnp.concatenate(split_blocks(summed[model_width:], 0, 2), 1)
+
+    gain_part = jnp.sum(
+        qkv_flat.astype(wide) * summed[:model_width], 1
+    ) / gain_attn
+    small = jnp.concatenate([small, gain_part[None]])
+    far, near, small, summed = lax.optimization_barrier((far, near, small, summed))
+    for bit in (1, 2):
+        small = small + exchange(small, "tensor", bit)
     blocks = [block, near, far, exchange(far, "tensor", 1)]
     layer_here = in_order([block[:span] for block in blocks])
-    in_here = in_order([block[span : 2 * span] for block in blocks])
-    small = in_order([block[2 * span :] for block in blocks], SMALL_ROWS)
-    small = jnp.sum(small.reshape(tensor_count, SMALL_ROWS, -1).astype(wide), 0)
+    in_here = in_order([block[span:] for block in blocks])
     return (
         layer_here,
         in_here,

time: 253 us -> 225 us (0.89)
  waiting for transfers between devices: 109 us -> 94.5 us
  between operations: 14.7 us -> 1.37 us
  local copies, waits for them, and re-layouts: 28.7 us -> 20.4 us
  starting transfers between devices: 37.8 us -> 43.9 us
  other arithmetic: 11.7 us -> 15 us
  matrix products: 2.64 us -> 0 us
    ppermute x36 -> x43, waiting for transfers between devices: 109 us -> 94.5 us  [exchange(): lax.ppermute(array_in, axis_name, [(i, i ^ bits) for i in range(count)])]
    ppermute x36 -> x43, starting transfers between devices: 37.8 us -> 43.9 us  [exchange(): lax.ppermute(array_in, axis_name, [(i, i ^ bits) for i in range(count)])]
    pallas_call x1 -> x3, Pallas kernels: 0.46 us -> 5.17 us  [the longest x1 3.16 us: on_device(): pl.pallas_call(attend_grad_kernel, out_shape=(shaped((row_count, 2 * head...]
    add x0 -> x5, other arithmetic: none -> 4.66 us  [the longest x1 2.47 us: on_device(): in_summed[:in_rows // 2] + in_arrived.astype(wide)]
    pallas_call x1, Pallas kernels: 10.5 us -> 6.78 us  [on_device(): pl.pallas_call(functools.partial(weight_grad_kernel, tensor_count), out_s...]
    slice x5 -> x6, local copies, waits for them, and re-layouts: 3.4 us -> 0.21 us  [the longest x2 0.11 us: exchange_halves(): array_in[:rows]]
    convert_element_type x5 -> x4, other arithmetic: 4.2 us -> 1.14 us  [the longest x2 0.45 us: exchange_halves(): (half.astype(jnp.float32) + arrived.astype(jnp.float32)).astype(jnp.bfloa...]
    dot_general x2 -> x0, matrix products: 2.64 us -> none  [transposed_dot(): lax.dot_general(left, right, (((0,), (0,)), ((), ())), preferred_element_...]
  transfers between devices with their start and end apart: 37 -> 43, of which waited for: 18 -> 26; matrix products, arithmetic and copies ran while one was open for 12% -> 10% of each run, Pallas kernels for 12% -> 14%
where the time goes in v4:
time: 225 us
  waiting for transfers between devices  94.5 us (42%)
  Pallas kernels  49.7 us (22%)
  starting transfers between devices  43.9 us (20%)
  local copies, waits for them, and re-layouts  20.4 us (9%)
  other arithmetic  15 us (7%)
    ppermute x43, waiting for transfers between devices, exchange(): lax.ppermute(array_in, axis_name, [(i, i ^ bits) for i in range(count)])  94.5 us
    ppermute x43, starting transfers between devices, exchange(): lax.ppermute(array_in, axis_name, [(i, i ^ bits) for i in range(count)])  43.9 us
    pallas_call x1, Pallas kernels, on_device(): pl.pallas_call(functools.partial(middle_kernel, tensor_count), out_shape=...  18.3 us
    unnamed x106, local copies, waits for them, and re-layouts  12.3 us
    pallas_call x1, Pallas kernels, on_device(): pl.pallas_call(functools.partial(attend_back_kernel, tensor_count), out_s...  10.7 us
    pallas_call x1, Pallas kernels, on_device(): pl.pallas_call(attend_kernel, out_shape=kept + (shaped((token_count, head...  7.6 us
    pallas_call x1, Pallas kernels, on_device(): pl.pallas_call(functools.partial(weight_grad_kernel, tensor_count), out_s...  6.78 us
  transfers between devices with their start and end apart: 43, of which 26 were waited for; matrix products, arithmetic and copies ran while one was open for 10% of the time, Pallas kernels for 14%

profile of v4, /device:TPU:0, one launch (start us, length us, event | category | flops | bytes accessed | tf_op | source)
XLA Modules:
  0.0 224.9 jit_solution(9523387489359109315)
XLA Ops:
  0.6 3.0 %collective-permute-start = (bf16[256,1024]{1,0:T(8,128)(2,1)}, bf16[256,1024]{1,0:T(8,128)(2,1)S(1)}, u32[]{:S(2)}, u32[]{:S(2)}) collective-permute-start(bf16[256,1024]{1,0:T(8,128)(2,1)} %bitcast.34), channel_id=1, source_target_pairs={{0,8},{4,12},{8,0},{12,4},{16,24},{20,28},{24,16},{28,20},{1,9},{5... | collective-permute-start | bytes 1572872 | tf_op jit(solution)/shard_map/ppermute | solution.py:344
  4.7 2.7 %collective-permute-start.2 = (bf16[128,1024]{1,0:T(8,128)(2,1)S(1)}, bf16[128,1024]{1,0:T(8,128)(2,1)S(1)}, u32[]{:S(2)}, u32[]{:S(2)}) collective-permute-start(bf16[128,1024]{1,0:T(8,128)(2,1)S(1)} %slice_select_fusion), channel_id=1, source_target_pairs={{0,2},{1,3},{2,0},{3,1},{4,6},{5,7},{6,4},{7,5},{8,10},{9,11},{10,... | collective-permute-start | bytes 786440 | tf_op jit(solution)/shard_map/ppermute | solution.py:344
  7.4 1.6 collective-permute-start.3
  8.9 1.5 collective-permute-start.1
  10.5 2.5 %copy.25 = bf16[128,8,2,256]{3,1,2,0:T(8,128)(2,1)} copy(bf16[128,8,2,256]{3,2,1,0:T(2,128)(2,1)} %bitcast.31) | data formatting | bytes 2097152
  12.9 7.6 %attend.1 = (bf16[2,4,256,128]{3,2,1,0:T(8,128)(2,1)}, bf16[2,512,128]{2,1,0:T(8,128)(2,1)}, bf16[2,4,256,512]{3,2,1,0:T(8,128)(2,1)}, bf16[512,256]{1,0:T(8,128)(2,1)}) custom-call(s32[1,3]{1,0:T(1,128)} %lengths.1, bf16[512,1024]{1,0:T(8,128)(2,1)} %layer_in.3, f32[1,1024]{1,0:T(1,128)} %bitcast.22, bf16[1024,512]{1,0:T(8,128)(2,1)} %bitcast.27, ...), custom_call_target="tpu_custom_call" | custom-call | tf_op jit(solution)/shard_map/attend/pallas_call | solution.py:862
  23.3 2.4 %collective-permute-start.5 = (bf16[512,256]{1,0:T(8,128)(2,1)S(1)}, bf16[512,256]{1,0:T(8,128)(2,1)S(1)}, u32[]{:S(2)}, u32[]{:S(2)}) collective-permute-start(bf16[512,256]{1,0:T(8,128)(2,1)S(1)} %copy-done.11), channel_id=1, source_target_pairs={{0,1},{1,0},{2,3},{3,2},{4,5},{5,4},{6,7},{7,6},{8,9},{9,8},{10,11... | collective-permute-start | bytes 786440 | tf_op jit(solution)/shard_map/ppermute | solution.py:344
  26.4 9.0 %collective-permute-done.4 = bf16[512,256]{1,0:T(8,128)(2,1)S(1)} collective-permute-done((bf16[512,256]{1,0:T(8,128)(2,1)S(1)}, bf16[512,256]{1,0:T(8,128)(2,1)S(1)}, u32[]{:S(2)}, u32[]{:S(2)}) %collective-permute-start.4) | collective-permute-done | bytes 262176 | tf_op jit(solution)/shard_map/ppermute | solution.py:344
  35.4 1.3 collective-permute-done.5
  37.6 4.7 %collective-permute-done.7 = bf16[128,1024]{1,0:T(8,128)(2,1)S(1)} collective-permute-done((bf16[128,1024]{1,0:T(8,128)(2,1)S(1)}, bf16[128,1024]{1,0:T(8,128)(2,1)S(1)}, u32[]{:S(2)}, u32[]{:S(2)}) %collective-permute-start.7) | collective-permute-done | bytes 262176 | tf_op jit(solution)/shard_map/ppermute | solution.py:344
  42.4 4.4 %collective-permute-done.6 = bf16[512,256]{1,0:T(8,128)(2,1)S(1)} collective-permute-done((bf16[512,256]{1,0:T(8,128)(2,1)S(1)}, bf16[512,256]{1,0:T(8,128)(2,1)S(1)}, u32[]{:S(2)}, u32[]{:S(2)}) %collective-permute-start.6) | collective-permute-done | bytes 262176 | tf_op jit(solution)/shard_map/ppermute | solution.py:344
  50.5 1.7 collective-permute-done.13.refs_15_.refs_7_
  52.2 1.5 collective-permute-done.14.refs_16_.refs_8_
  53.9 1.5 collective-permute-done.12.refs_12_
  56.5 18.3 %middle.1 = (f32[128,1024]{1,0:T(8,128)S(1)}, bf16[128,1024]{1,0:T(8,128)(2,1)}, bf16[128,1024]{1,0:T(8,128)(2,1)S(1)}, bf16[128,1024]{1,0:T(8,128)(2,1)S(1)}, f...) custom-call(s32[2]{0:T(128)S(1)} %pad_add_fusion.refs_0_.place, ...), custom_call_target="tpu_custom_call" | custom-call | tf_op jit(solution)/shard_map/middle/pallas_call | solution.py:900
  74.8 6.8 %weight_grad.1 = (f32[128,1024]{1,0:T(8,128)S(1)}, bf16[128,1024]{1,0:T(8,128)(2,1)S(1)}, bf16[128,1024]{1,0:T(8,128)(2,1)S(1)}, bf16[128,1024]{1,0:T(8,128)(2,1...) custom-call(s32[2]{0:T(128)S(1)} %pad_add_fusion.refs_0_.place, ...), custom_call_target="tpu_custom_call" | custom-call | tf_op jit(solution)/shard_map/weight_grad/pallas_call | solution.py:943
  81.6 1.5 collective-permute-done.15
  83.9 2.3 %collective-permute-start.17 = (bf16[128,1024]{1,0:T(8,128)(2,1)}, bf16[128,1024]{1,0:T(8,128)(2,1)S(1)}, u32[]{:S(2)}, u32[]{:S(2)}) collective-permute-start(bf16[128,1024]{1,0:T(8,128)(2,1)} %add_convert_fusion.6), channel_id=1, source_target_pairs={{0,2},{1,3},{2,0},{3,1},{4,6},{5,7},{6,4},{7,5},{8,10},{9,11},{10,... | collective-permute-start | bytes 786440 | tf_op jit(solution)/shard_map/ppermute | solution.py:344
  86.3 1.4 collective-permute-start.16
  88.8 1.6 add_grads.1
  90.4 1.3 copy-done.2
  93.5 1.5 collective-permute-start.23
  95.0 4.5 %collective-permute-done.17.far = bf16[128,1024]{1,0:T(8,128)(2,1)S(1)} collective-permute-done((bf16[128,1024]{1,0:T(8,128)(2,1)}, bf16[128,1024]{1,0:T(8,128)(2,1)S(1)}, u32[]{:S(2)}, u32[]{:S(2)}) %collective-permute-start.17) | collective-permute-done | bytes 262176 | tf_op jit(solution)/shard_map/ppermute | solution.py:344
  101.9 2.3 %collective-permute-start.20 = (bf16[128,1024]{1,0:T(8,128)(2,1)S(1)}, bf16[128,1024]{1,0:T(8,128)(2,1)S(1)}, u32[]{:S(2)}, u32[]{:S(2)}) collective-permute-start(bf16[128,1024]{1,0:T(8,128)(2,1)S(1)} %get-tuple-element.134.refs_8_), channel_id=1, source_target_pairs={{0,1},{1,0},{2,3},{3,2},{4,5},{5,4},{6,7},{7,6},{8,9},{9,8},{10,11... | collective-permute-start | bytes 786440 | tf_op jit(solution)/shard_map/ppermute | solution.py:344
  104.8 10.5 %collective-permute-done.19.refs_10_ = bf16[128,1024]{1,0:T(8,128)(2,1)S(1)} collective-permute-done((bf16[128,1024]{1,0:T(8,128)(2,1)S(1)}, bf16[128,1024]{1,0:T(8,128)(2,1)S(1)}, u32[]{:S(2)}, u32[]{:S(2)}) %collective-permute-start.19) | collective-permute-done | bytes 262176 | tf_op jit(solution)/shard_map/ppermute | solution.py:344
  115.7 7.0 %collective-permute-done.21.refs_11_ = bf16[128,1024]{1,0:T(8,128)(2,1)S(1)} collective-permute-done((bf16[128,1024]{1,0:T(8,128)(2,1)S(1)}, bf16[128,1024]{1,0:T(8,128)(2,1)S(1)}, u32[]{:S(2)}, u32[]{:S(2)}) %collective-permute-start.21) | collective-permute-done | bytes 262176 | tf_op jit(solution)/shard_map/ppermute | solution.py:344
  123.4 10.7 %attend_back.1 = (f32[256,1024]{1,0:T(8,128)}, bf16[256,1024]{1,0:T(8,128)(2,1)}, bf16[256,1024]{1,0:T(8,128)(2,1)}, bf16[256,1024]{1,0:T(8,128)(2,1)}, bf16[512...) custom-call(s32[2]{0:T(128)} %copy-done.23, bf16[256,1024]{1,0:T(8,128)(2,1)} %refs_1_.1, ...), custom_call_target="tpu_custom_call" | custom-call | tf_op jit(solution)/shard_map/attend_back/pallas_call | solution.py:998
  136.9 3.2 %attend_grad.1 = (f32[768,512]{1,0:T(8,128)S(1)}, bf16[768,512]{1,0:T(8,128)(2,1)S(1)}) custom-call(s32[2]{0:T(128)S(1)} %copy-done.24, bf16[512,1024]{1,0:T(8,128)(2,1)S(1)} %copy-done, f32[1,1024]{1,0:T(1,128)S(1)} %bitcast.23, bf16[512,512]{1,0:T(8,128)(2,1)S(1)} %copy-done.13, bf16[512,256]{1,0:T(8,128)(2,1)S(1)} %copy-done.12, ...), custom_call_target="tpu_custom_call" | custom-call | tf_op jit(solution)/shard_map/attend_grad/pallas_call | solution.py:1029
  140.2 2.0 convert_add_fusion
  142.3 4.2 %collective-permute-done.22 = bf16[256,1024]{1,0:T(8,128)(2,1)S(1)} collective-permute-done((bf16[256,1024]{1,0:T(8,128)(2,1)}, bf16[256,1024]{1,0:T(8,128)(2,1)S(1)}, u32[]{:S(2)}, u32[]{:S(2)}) %collective-permute-start.22) | collective-permute-done | bytes 524320 | tf_op jit(solution)/shard_map/ppermute | solution.py:344
  147.2 1.6 collective-permute-done.29
  149.7 2.8 %collective-permute-start.31 = (bf16[384,512]{1,0:T(8,128)(2,1)S(1)}, bf16[384,512]{1,0:T(8,128)(2,1)S(1)}, u32[]{:S(2)}, u32[]{:S(2)}) collective-permute-start(bf16[384,512]{1,0:T(8,128)(2,1)S(1)} %get-tuple-element.184), channel_id=1, source_target_pairs={{0,16},{4,20},{8,24},{12,28},{16,0},{20,4},{24,8},{28,12},{1,17},{... | collective-permute-start | bytes 1179656 | tf_op jit(solution)/shard_map/ppermute | solution.py:344
  153.4 1.6 collective-permute-start.25
  155.7 13.7 %collective-permute-done.30 = bf16[384,512]{1,0:T(8,128)(2,1)S(1)} collective-permute-done((bf16[384,512]{1,0:T(8,128)(2,1)S(1)}, bf16[384,512]{1,0:T(8,128)(2,1)S(1)}, u32[]{:S(2)}, u32[]{:S(2)}) %collective-permute-start.30) | collective-permute-done | bytes 393248 | tf_op jit(solution)/shard_map/ppermute | solution.py:344
  169.4 2.8 %collective-permute-start.28 = (bf16[128,1024]{1,0:T(8,128)(2,1)S(1)}, bf16[128,1024]{1,0:T(8,128)(2,1)S(1)}, u32[]{:S(2)}, u32[]{:S(2)}) collective-permute-start(bf16[128,1024]{1,0:T(8,128)(2,1)S(1)} %slice.129), channel_id=1, source_target_pairs={{0,16},{4,20},{8,24},{12,28},{16,0},{20,4},{24,8},{28,12},{1,17},{... | collective-permute-start | bytes 786440 | tf_op jit(solution)/shard_map/ppermute | solution.py:344
  172.5 5.9 %collective-permute-done.28 = bf16[128,1024]{1,0:T(8,128)(2,1)S(1)} collective-permute-done((bf16[128,1024]{1,0:T(8,128)(2,1)S(1)}, bf16[128,1024]{1,0:T(8,128)(2,1)S(1)}, u32[]{:S(2)}, u32[]{:S(2)}) %collective-permute-start.28) | collective-permute-done | bytes 262176 | tf_op jit(solution)/shard_map/ppermute | solution.py:344
  179.2 1.7 collective-permute-start.37
  182.1 1.8 collective-permute-start.33
  184.0 6.0 %collective-permute-done.37 = bf16[384,512]{1,0:T(8,128)(2,1)S(1)} collective-permute-done((bf16[384,512]{1,0:T(8,128)(2,1)S(1)}, bf16[384,512]{1,0:T(8,128)(2,1)S(1)}, u32[]{:S(2)}, u32[]{:S(2)}) %collective-permute-start.37) | collective-permute-done | bytes 393248 | tf_op jit(solution)/shard_map/ppermute | solution.py:344
  191.0 2.5 %convert_add_fusion.1 = f32[256,1024]{1,0:T(8,128)} fusion(bf16[256,1024]{1,0:T(8,128)(2,1)S(1)} %copy-done.36, f32[512,1024]{1,0:T(8,128)} %copy-done.30), kind=kLoop, calls=%fused_computation.8 | loop fusion | flops 524288 | bytes 2621440 | tf_op jit(solution)/shard_map/add | solution.py:1050
  195.5 3.3 %collective-permute-done.35 = f32[9,1024]{1,0:T(8,128)S(1)} collective-permute-done((f32[9,1024]{1,0:T(8,128)S(1)}, f32[9,1024]{1,0:T(8,128)S(1)}, u32[]{:S(2)}, u32[]{:S(2)}) %collective-permute-start.35) | collective-permute-done | bytes 36896 | tf_op jit(solution)/shard_map/ppermute | solution.py:344
  200.1 3.0 %collective-permute-done.36 = f32[9,1024]{1,0:T(8,128)S(1)} collective-permute-done((f32[9,1024]{1,0:T(8,128)S(1)}, f32[9,1024]{1,0:T(8,128)S(1)}, u32[]{:S(2)}, u32[]{:S(2)}) %collective-permute-start.36) | collective-permute-done | bytes 36896 | tf_op jit(solution)/shard_map/ppermute | solution.py:344
  204.7 1.7 fusion
  207.2 1.4 collective-permute-start.40
  208.6 2.9 %collective-permute-done.41 = f32[10,1024]{1,0:T(8,128)S(1)} collective-permute-done((f32[10,1024]{1,0:T(8,128)S(1)}, f32[10,1024]{1,0:T(8,128)S(1)}, u32[]{:S(2)}, u32[]{:S(2)}) %collective-permute-start.41) | collective-permute-done | bytes 40992 | tf_op jit(solution)/shard_map/ppermute | solution.py:344
  214.6 2.3 %reshape.44 = f32[1024,2,256]{2,1,0:T(2,128)} reshape(f32[1024,512]{1,0:T(8,128)S(1)} %copy-done.29) | data formatting | bytes 4194304 | tf_op jit(solution)/shard_map/reshape | solution.py:1072
  218.0 3.6 %collective-permute-done.42 = f32[10,1024]{1,0:T(8,128)S(1)} collective-permute-done((f32[10,1024]{1,0:T(8,128)S(1)}, f32[10,1024]{1,0:T(8,128)S(1)}, u32[]{:S(2)}, u32[]{:S(2)}) %collective-permute-start.42) | collective-permute-done | bytes 40992 | tf_op jit(solution)/shard_map/ppermute | solution.py:344
  223.1 1.9 slice_dynamic-update-slice_fusion
  (200 shorter events, 38.5 us)
Async XLA Ops:
  0.6 19.9 %collective-permute-start = (bf16[256,1024]{1,0:T(8,128)(2,1)}, bf16[256,1024]{1,0:T(8,128)(2,1)S(1)}, u32[]{:S(2)}, u32[]{:S(2)}) collective-permute-start(bf16[256,1024]{1,0:T(8,128)(2,1)} %bitcast.34), channel_id=1, source_target_pairs={{0,8},{4,12},{8,0},{12,4},{16,24},{20,28},{24,16},{28,20},{1,9},{5... | collective-permute-start | bytes 1572872 | tf_op jit(solution)/shard_map/ppermute | solution.py:344
  4.7 15.8 %collective-permute-start.2 = (bf16[128,1024]{1,0:T(8,128)(2,1)S(1)}, bf16[128,1024]{1,0:T(8,128)(2,1)S(1)}, u32[]{:S(2)}, u32[]{:S(2)}) collective-permute-start(bf16[128,1024]{1,0:T(8,128)(2,1)S(1)} %slice_select_fusion), channel_id=1, source_target_pairs={{0,2},{1,3},{2,0},{3,1},{4,6},{5,7},{6,4},{7,5},{8,10},{9,11},{10,... | collective-permute-start | bytes 786440 | tf_op jit(solution)/shard_map/ppermute | solution.py:344
  7.4 13.2 %collective-permute-start.3 = (bf16[128,1024]{1,0:T(8,128)(2,1)S(1)}, bf16[128,1024]{1,0:T(8,128)(2,1)S(1)}, u32[]{:S(2)}, u32[]{:S(2)}) collective-permute-start(bf16[128,1024]{1,0:T(8,128)(2,1)S(1)} %slice_select_fusion), channel_id=1, source_target_pairs={{0,1},{1,0},{2,3},{3,2},{4,5},{5,4},{6,7},{7,6},{8,9},{9,8},{10,11... | collective-permute-start | bytes 786440 | tf_op jit(solution)/shard_map/ppermute | solution.py:344
  8.9 11.6 %collective-permute-start.1 = (bf16[128,1024]{1,0:T(8,128)(2,1)}, bf16[128,1024]{1,0:T(8,128)(2,1)S(1)}, u32[]{:S(2)}, u32[]{:S(2)}) collective-permute-start(bf16[128,1024]{1,0:T(8,128)(2,1)} %bitcast.36), channel_id=1, source_target_pairs={{0,16},{4,20},{8,24},{12,28},{16,0},{20,4},{24,8},{28,12},{1,17},{... | collective-permute-start | bytes 786440 | tf_op jit(solution)/shard_map/ppermute | solution.py:344
  21.6 27.3 %copy-start.50 = (s32[512,2]{0,1:T(2,128)S(1)}, s32[512,2]{0,1:T(2,128)}, u32[]{:S(2)}) copy-start(s32[512,2]{0,1:T(2,128)} %param.15) | copy-start | bytes 12292
  21.6 27.4 %copy-start.49 = (bf16[1024,8]{0,1:T(8,128)(2,1)S(1)}, bf16[1024,8]{0,1:T(8,128)(2,1)}, u32[]{:S(2)}) copy-start(bf16[1024,8]{0,1:T(8,128)(2,1)} %param.20) | copy-start | bytes 49156
  21.6 25.1 %collective-permute-start.8 = (bf16[512,1024]{1,0:T(8,128)(2,1)}, bf16[512,1024]{1,0:T(8,128)(2,1)}, u32[]{:S(2)}, u32[]{:S(2)}) collective-permute-start(bf16[512,1024]{1,0:T(8,128)(2,1)} %pad_maximum_fusion.refs_9_), channel_id=1, source_target_pairs={{0,16},{4,20},{8,24},{12,28},{16,0},{20,4},{24,8},{28,12},{1,17},{... | collective-permute-start | bytes 3145736 | tf_op jit(solution)/shard_map/ppermute | solution.py:344
  22.2 13.3 %collective-permute-start.4 = (bf16[512,256]{1,0:T(8,128)(2,1)S(1)}, bf16[512,256]{1,0:T(8,128)(2,1)S(1)}, u32[]{:S(2)}, u32[]{:S(2)}) collective-permute-start(bf16[512,256]{1,0:T(8,128)(2,1)S(1)} %copy-done.11), channel_id=1, source_target_pairs={{0,2},{1,3},{2,0},{3,1},{4,6},{5,7},{6,4},{7,5},{8,10},{9,11},{10,... | collective-permute-start | bytes 786440 | tf_op jit(solution)/shard_map/ppermute | solution.py:344
  23.3 13.5 %collective-permute-start.5 = (bf16[512,256]{1,0:T(8,128)(2,1)S(1)}, bf16[512,256]{1,0:T(8,128)(2,1)S(1)}, u32[]{:S(2)}, u32[]{:S(2)}) collective-permute-start(bf16[512,256]{1,0:T(8,128)(2,1)S(1)} %copy-done.11), channel_id=1, source_target_pairs={{0,1},{1,0},{2,3},{3,2},{4,5},{5,4},{6,7},{7,6},{8,9},{9,8},{10,11... | collective-permute-start | bytes 786440 | tf_op jit(solution)/shard_map/ppermute | solution.py:344
  25.7 29.7 %copy-start = (bf16[512,1024]{1,0:T(8,128)(2,1)S(1)}, bf16[512,1024]{1,0:T(8,128)(2,1)}, u32[]{:S(2)}) copy-start(bf16[512,1024]{1,0:T(8,128)(2,1)} %layer_in.3) | copy-start | bytes 3145732
  25.8 29.7 %copy-start.1 = (bf16[512,1024]{1,0:T(8,128)(2,1)S(1)}, bf16[512,1024]{1,0:T(8,128)(2,1)}, u32[]{:S(2)}) copy-start(bf16[512,1024]{1,0:T(8,128)(2,1)} %refs_2_.1) | copy-start | bytes 3145732
  25.8 29.7 %copy-start.22 = (f32[1024]{0:T(1024)S(1)}, f32[1024]{0:T(1024)}, u32[]{:S(2)}) copy-start(f32[1024]{0:T(1024)} %param.19) | copy-start | bytes 12292
  25.8 21.0 %collective-permute-start.9 = (bf16[256,1024]{1,0:T(8,128)(2,1)S(1)}, bf16[256,1024]{1,0:T(8,128)(2,1)S(1)}, u32[]{:S(2)}, u32[]{:S(2)}) collective-permute-start(bf16[256,1024]{1,0:T(8,128)(2,1)S(1)} %pad_maximum_fusion.5.refs_13_.refs_5_), channel_id=1, source_target_pairs={{0,8},{4,12},{8,0},{12,4},{16,24},{20,28},{24,16},{28,20},{1,9},{5... | collective-permute-start | bytes 1572872 | tf_op jit(solution)/shard_map/ppermute | solution.py:344
  26.4 16.0 %collective-permute-start.7 = (bf16[128,1024]{1,0:T(8,128)(2,1)S(1)}, bf16[128,1024]{1,0:T(8,128)(2,1)S(1)}, u32[]{:S(2)}, u32[]{:S(2)}) collective-permute-start(bf16[128,1024]{1,0:T(8,128)(2,1)S(1)} %collective-permute-done.2), channel_id=1, source_target_pairs={{0,1},{1,0},{2,3},{3,2},{4,5},{5,4},{6,7},{7,6},{8,9},{9,8},{10,11... | collective-permute-start | bytes 786440 | tf_op jit(solution)/shard_map/ppermute | solution.py:344
  36.8 10.0 %collective-permute-start.6 = (bf16[512,256]{1,0:T(8,128)(2,1)S(1)}, bf16[512,256]{1,0:T(8,128)(2,1)S(1)}, u32[]{:S(2)}, u32[]{:S(2)}) collective-permute-start(bf16[512,256]{1,0:T(8,128)(2,1)S(1)} %collective-permute-done.4), channel_id=1, source_target_pairs={{0,1},{1,0},{2,3},{3,2},{4,5},{5,4},{6,7},{7,6},{8,9},{9,8},{10,11... | collective-permute-start | bytes 786440 | tf_op jit(solution)/shard_map/ppermute | solution.py:344
  47.9 5.8 %collective-permute-start.10 = (bf16[512,1024]{1,0:T(8,128)(2,1)}, bf16[512,1024]{1,0:T(8,128)(2,1)}, u32[]{:S(2)}, u32[]{:S(2)}) collective-permute-start(bf16[512,1024]{1,0:T(8,128)(2,1)} %pad_maximum_fusion.1.refs_6_), channel_id=1, source_target_pairs={{0,4},{4,0},{8,12},{12,8},{16,20},{20,16},{24,28},{28,24},{1,5},{5... | collective-permute-start | bytes 3145736 | tf_op jit(solution)/shard_map/ppermute | solution.py:344
  47.9 6.0 %collective-permute-start.11 = (bf16[512,1024]{1,0:T(8,128)(2,1)}, bf16[512,1024]{1,0:T(8,128)(2,1)}, u32[]{:S(2)}, u32[]{:S(2)}) collective-permute-start(bf16[512,1024]{1,0:T(8,128)(2,1)} %pad_maximum_fusion.refs_9_), channel_id=1, source_target_pairs={{0,4},{4,0},{8,12},{12,8},{16,20},{20,16},{24,28},{28,24},{1,5},{5... | collective-permute-start | bytes 3145736 | tf_op jit(solution)/shard_map/ppermute | solution.py:344
  48.4 7.0 %collective-permute-start.12 = (bf16[512,1024]{1,0:T(8,128)(2,1)}, bf16[512,1024]{1,0:T(8,128)(2,1)}, u32[]{:S(2)}, u32[]{:S(2)}) collective-permute-start(bf16[512,1024]{1,0:T(8,128)(2,1)} %collective-permute-done.8.refs_10_), channel_id=1, source_target_pairs={{0,4},{4,0},{8,12},{12,8},{16,20},{20,16},{24,28},{28,24},{1,5},{5... | collective-permute-start | bytes 3145736 | tf_op jit(solution)/shard_map/ppermute | solution.py:344
  48.4 3.8 %collective-permute-start.13 = (bf16[256,1024]{1,0:T(8,128)(2,1)S(1)}, bf16[256,1024]{1,0:T(8,128)(2,1)}, u32[]{:S(2)}, u32[]{:S(2)}) collective-permute-start(bf16[256,1024]{1,0:T(8,128)(2,1)S(1)} %pad_maximum_fusion.5.refs_13_.refs_5_), channel_id=1, source_target_pairs={{0,4},{4,0},{8,12},{12,8},{16,20},{20,16},{24,28},{28,24},{1,5},{5... | collective-permute-start | bytes 1572872 | tf_op jit(solution)/shard_map/ppermute | solution.py:344
  48.9 4.8 %collective-permute-start.14 = (bf16[256,1024]{1,0:T(8,128)(2,1)S(1)}, bf16[256,1024]{1,0:T(8,128)(2,1)}, u32[]{:S(2)}, u32[]{:S(2)}) collective-permute-start(bf16[256,1024]{1,0:T(8,128)(2,1)S(1)} %collective-permute-done.9.refs_14_.refs_6_), channel_id=1, source_target_pairs={{0,4},{4,0},{8,12},{12,8},{16,20},{20,16},{24,28},{28,24},{1,5},{5... | collective-permute-start | bytes 1572872 | tf_op jit(solution)/shard_map/ppermute | solution.py:344
  74.8 8.4 %collective-permute-start.15 = (bf16[128,1024]{1,0:T(8,128)(2,1)S(1)}, bf16[128,1024]{1,0:T(8,128)(2,1)S(1)}, u32[]{:S(2)}, u32[]{:S(2)}) collective-permute-start(bf16[128,1024]{1,0:T(8,128)(2,1)S(1)} %get-tuple-element.120), channel_id=1, source_target_pairs={{0,1},{1,0},{2,3},{3,2},{4,5},{5,4},{6,7},{7,6},{8,9},{9,8},{10,11... | collective-permute-start | bytes 786440 | tf_op jit(solution)/shard_map/ppermute | solution.py:344
  83.1 5.7 %collective-permute-start.18 = (bf16[1536,1024]{1,0:T(8,128)(2,1)S(1)}, bf16[1536,1024]{1,0:T(8,128)(2,1)S(1)}, u32[]{:S(2)}, u32[]{:S(2)}) collective-permute-start(bf16[1536,1024]{1,0:T(8,128)(2,1)S(1)} %get-tuple-element.127), channel_id=1, source_target_pairs={{0,4},{4,0},{8,12},{12,8},{16,20},{20,16},{24,28},{28,24},{1,5},{5... | collective-permute-start | bytes 9437192 | tf_op jit(solution)/shard_map/ppermute | solution.py:344
  83.9 15.6 %collective-permute-start.17 = (bf16[128,1024]{1,0:T(8,128)(2,1)}, bf16[128,1024]{1,0:T(8,128)(2,1)S(1)}, u32[]{:S(2)}, u32[]{:S(2)}) collective-permute-start(bf16[128,1024]{1,0:T(8,128)(2,1)} %add_convert_fusion.6), channel_id=1, source_target_pairs={{0,2},{1,3},{2,0},{3,1},{4,6},{5,7},{6,4},{7,5},{8,10},{9,11},{10,... | collective-permute-start | bytes 786440 | tf_op jit(solution)/shard_map/ppermute | solution.py:344
  86.3 13.5 %collective-permute-start.16 = (bf16[128,1024]{1,0:T(8,128)(2,1)}, bf16[128,1024]{1,0:T(8,128)(2,1)}, u32[]{:S(2)}, u32[]{:S(2)}) collective-permute-start(bf16[128,1024]{1,0:T(8,128)(2,1)} %get-tuple-element.122), channel_id=1, source_target_pairs={{0,1},{1,0},{2,3},{3,2},{4,5},{5,4},{6,7},{7,6},{8,9},{9,8},{10,11... | collective-permute-start | bytes 786440 | tf_op jit(solution)/shard_map/ppermute | solution.py:344
  93.5 46.8 %collective-permute-start.23 = (bf16[512,1024]{1,0:T(8,128)(2,1)}, bf16[512,1024]{1,0:T(8,128)(2,1)}, u32[]{:S(2)}, u32[]{:S(2)}) collective-permute-start(bf16[512,1024]{1,0:T(8,128)(2,1)} %get-tuple-element.150), channel_id=1, source_target_pairs={{0,16},{4,20},{8,24},{12,28},{16,0},{20,4},{24,8},{28,12},{1,17},{... | collective-permute-start | bytes 3145736 | tf_op jit(solution)/shard_map/ppermute | solution.py:344
  101.0 14.3 %collective-permute-start.19 = (bf16[128,1024]{1,0:T(8,128)(2,1)S(1)}, bf16[128,1024]{1,0:T(8,128)(2,1)S(1)}, u32[]{:S(2)}, u32[]{:S(2)}) collective-permute-start(bf16[128,1024]{1,0:T(8,128)(2,1)S(1)} %get-tuple-element.134.refs_8_), channel_id=1, source_target_pairs={{0,2},{1,3},{2,0},{3,1},{4,6},{5,7},{6,4},{7,5},{8,10},{9,11},{10,... | collective-permute-start | bytes 786440 | tf_op jit(solution)/shard_map/ppermute | solution.py:344
  101.9 13.4 %collective-permute-start.20 = (bf16[128,1024]{1,0:T(8,128)(2,1)S(1)}, bf16[128,1024]{1,0:T(8,128)(2,1)S(1)}, u32[]{:S(2)}, u32[]{:S(2)}) collective-permute-start(bf16[128,1024]{1,0:T(8,128)(2,1)S(1)} %get-tuple-element.134.refs_8_), channel_id=1, source_target_pairs={{0,1},{1,0},{2,3},{3,2},{4,5},{5,4},{6,7},{7,6},{8,9},{9,8},{10,11... | collective-permute-start | bytes 786440 | tf_op jit(solution)/shard_map/ppermute | solution.py:344
  104.3 35.8 %collective-permute-start.24 = (bf16[256,1024]{1,0:T(8,128)(2,1)S(1)}, bf16[256,1024]{1,0:T(8,128)(2,1)S(1)}, u32[]{:S(2)}, u32[]{:S(2)}) collective-permute-start(bf16[256,1024]{1,0:T(8,128)(2,1)S(1)} %copy-done.26), channel_id=1, source_target_pairs={{0,8},{4,12},{8,0},{12,4},{16,24},{20,28},{24,16},{28,20},{1,9},{5... | collective-permute-start | bytes 1572872 | tf_op jit(solution)/shard_map/ppermute | solution.py:344
  115.3 7.4 %collective-permute-start.21 = (bf16[128,1024]{1,0:T(8,128)(2,1)S(1)}, bf16[128,1024]{1,0:T(8,128)(2,1)S(1)}, u32[]{:S(2)}, u32[]{:S(2)}) collective-permute-start(bf16[128,1024]{1,0:T(8,128)(2,1)S(1)} %collective-permute-done.19.refs_10_), channel_id=1, source_target_pairs={{0,1},{1,0},{2,3},{3,2},{4,5},{5,4},{6,7},{7,6},{8,9},{9,8},{10,11... | collective-permute-start | bytes 786440 | tf_op jit(solution)/shard_map/ppermute | solution.py:344
  134.2 12.4 %collective-permute-start.22 = (bf16[256,1024]{1,0:T(8,128)(2,1)}, bf16[256,1024]{1,0:T(8,128)(2,1)S(1)}, u32[]{:S(2)}, u32[]{:S(2)}) collective-permute-start(bf16[256,1024]{1,0:T(8,128)(2,1)} %get-tuple-element.144), channel_id=1, source_target_pairs={{0,1},{1,0},{2,3},{3,2},{4,5},{5,4},{6,7},{7,6},{8,9},{9,8},{10,11... | collective-permute-start | bytes 1572872 | tf_op jit(solution)/shard_map/ppermute | solution.py:344
  146.5 2.3 %collective-permute-start.29 = (bf16[768,512]{1,0:T(8,128)(2,1)S(1)}, bf16[768,512]{1,0:T(8,128)(2,1)S(1)}, u32[]{:S(2)}, u32[]{:S(2)}) collective-permute-start(bf16[768,512]{1,0:T(8,128)(2,1)S(1)} %get-tuple-element.159), channel_id=1, source_target_pairs={{0,4},{4,0},{8,12},{12,8},{16,20},{20,16},{24,28},{28,24},{1,5},{5... | collective-permute-start | bytes 2359304 | tf_op jit(solution)/shard_map/ppermute | solution.py:344
  146.6 31.8 %collective-permute-start.27 = (bf16[256,1024]{1,0:T(8,128)(2,1)S(1)}, bf16[256,1024]{1,0:T(8,128)(2,1)S(1)}, u32[]{:S(2)}, u32[]{:S(2)}) collective-permute-start(bf16[256,1024]{1,0:T(8,128)(2,1)S(1)} %slice.128), channel_id=1, source_target_pairs={{0,8},{4,12},{8,0},{12,4},{16,24},{20,28},{24,16},{28,20},{1,9},{5... | collective-permute-start | bytes 1572872 | tf_op jit(solution)/shard_map/ppermute | solution.py:344
  149.1 20.3 %collective-permute-start.30 = (bf16[384,512]{1,0:T(8,128)(2,1)S(1)}, bf16[384,512]{1,0:T(8,128)(2,1)S(1)}, u32[]{:S(2)}, u32[]{:S(2)}) collective-permute-start(bf16[384,512]{1,0:T(8,128)(2,1)S(1)} %get-tuple-element.183), channel_id=1, source_target_pairs={{0,8},{4,12},{8,0},{12,4},{16,24},{20,28},{24,16},{28,20},{1,9},{5... | collective-permute-start | bytes 1179656 | tf_op jit(solution)/shard_map/ppermute | solution.py:344
  149.7 22.4 %collective-permute-start.31 = (bf16[384,512]{1,0:T(8,128)(2,1)S(1)}, bf16[384,512]{1,0:T(8,128)(2,1)S(1)}, u32[]{:S(2)}, u32[]{:S(2)}) collective-permute-start(bf16[384,512]{1,0:T(8,128)(2,1)S(1)} %get-tuple-element.184), channel_id=1, source_target_pairs={{0,16},{4,20},{8,24},{12,28},{16,0},{20,4},{24,8},{28,12},{1,17},{... | collective-permute-start | bytes 1179656 | tf_op jit(solution)/shard_map/ppermute | solution.py:344
  152.7 25.7 %collective-permute-start.26 = (bf16[256,1024]{1,0:T(8,128)(2,1)S(1)}, bf16[256,1024]{1,0:T(8,128)(2,1)S(1)}, u32[]{:S(2)}, u32[]{:S(2)}) collective-permute-start(bf16[256,1024]{1,0:T(8,128)(2,1)S(1)} %add_convert_fusion.1), channel_id=1, source_target_pairs={{0,2},{1,3},{2,0},{3,1},{4,6},{5,7},{6,4},{7,5},{8,10},{9,11},{10,... | collective-permute-start | bytes 1572872 | tf_op jit(solution)/shard_map/ppermute | solution.py:344
  153.4 25.0 %collective-permute-start.25 = (bf16[256,1024]{1,0:T(8,128)(2,1)S(1)}, bf16[256,1024]{1,0:T(8,128)(2,1)S(1)}, u32[]{:S(2)}, u32[]{:S(2)}) collective-permute-start(bf16[256,1024]{1,0:T(8,128)(2,1)S(1)} %copy-done.51), channel_id=1, source_target_pairs={{0,1},{1,0},{2,3},{3,2},{4,5},{5,4},{6,7},{7,6},{8,9},{9,8},{10,11... | collective-permute-start | bytes 1572872 | tf_op jit(solution)/shard_map/ppermute | solution.py:344
  169.4 8.9 %collective-permute-start.28 = (bf16[128,1024]{1,0:T(8,128)(2,1)S(1)}, bf16[128,1024]{1,0:T(8,128)(2,1)S(1)}, u32[]{:S(2)}, u32[]{:S(2)}) collective-permute-start(bf16[128,1024]{1,0:T(8,128)(2,1)S(1)} %slice.129), channel_id=1, source_target_pairs={{0,16},{4,20},{8,24},{12,28},{16,0},{20,4},{24,8},{28,12},{1,17},{... | collective-permute-start | bytes 786440 | tf_op jit(solution)/shard_map/ppermute | solution.py:344
  179.2 10.7 %collective-permute-start.37 = (bf16[384,512]{1,0:T(8,128)(2,1)S(1)}, bf16[384,512]{1,0:T(8,128)(2,1)S(1)}, u32[]{:S(2)}, u32[]{:S(2)}) collective-permute-start(bf16[384,512]{1,0:T(8,128)(2,1)S(1)} %get-tuple-element.179), channel_id=1, source_target_pairs={{0,16},{4,20},{8,24},{12,28},{16,0},{20,4},{24,8},{28,12},{1,17},{... | collective-permute-start | bytes 1179656 | tf_op jit(solution)/shard_map/ppermute | solution.py:344
  181.0 9.6 %collective-permute-start.38 = (bf16[384,512]{1,0:T(8,128)(2,1)S(1)}, bf16[384,512]{1,0:T(8,128)(2,1)S(1)}, u32[]{:S(2)}, u32[]{:S(2)}) collective-permute-start(bf16[384,512]{1,0:T(8,128)(2,1)S(1)} %get-tuple-element.180), channel_id=1, source_target_pairs={{0,8},{4,12},{8,0},{12,4},{16,24},{20,28},{24,16},{28,20},{1,9},{5... | collective-permute-start | bytes 1179656 | tf_op jit(solution)/shard_map/ppermute | solution.py:344
  181.5 24.9 %collective-permute-start.32 = (bf16[256,1024]{1,0:T(8,128)(2,1)S(1)}, bf16[256,1024]{1,0:T(8,128)(2,1)}, u32[]{:S(2)}, u32[]{:S(2)}) collective-permute-start(bf16[256,1024]{1,0:T(8,128)(2,1)S(1)} %finish.1), channel_id=1, source_target_pairs={{0,2},{1,3},{2,0},{3,1},{4,6},{5,7},{6,4},{7,5},{8,10},{9,11},{10,... | collective-permute-start | bytes 1572872 | tf_op jit(solution)/shard_map/ppermute | solution.py:344
  182.1 24.3 %collective-permute-start.33 = (bf16[256,1024]{1,0:T(8,128)(2,1)S(1)}, bf16[256,1024]{1,0:T(8,128)(2,1)S(1)}, u32[]{:S(2)}, u32[]{:S(2)}) collective-permute-start(bf16[256,1024]{1,0:T(8,128)(2,1)S(1)} %finish.1), channel_id=1, source_target_pairs={{0,1},{1,0},{2,3},{3,2},{4,5},{5,4},{6,7},{7,6},{8,9},{9,8},{10,11... | collective-permute-start | bytes 1572872 | tf_op jit(solution)/shard_map/ppermute | solution.py:344
  184.0 10.3 %collective-permute-start.34 = (f32[9,1024]{1,0:T(8,128)S(1)}, f32[9,1024]{1,0:T(8,128)S(1)}, u32[]{:S(2)}, u32[]{:S(2)}) collective-permute-start(f32[9,1024]{1,0:T(8,128)S(1)} %copy-done.41), channel_id=1, source_target_pairs={{0,4},{4,0},{8,12},{12,8},{16,20},{20,16},{24,28},{28,24},{1,5},{5... | collective-permute-start | bytes 110600 | tf_op jit(solution)/shard_map/ppermute | solution.py:344
  190.9 12.3 %collective-permute-start.39 = (bf16[768,512]{1,0:T(8,128)(2,1)S(1)}, bf16[768,512]{1,0:T(8,128)(2,1)S(1)}, u32[]{:S(2)}, u32[]{:S(2)}) collective-permute-start(bf16[768,512]{1,0:T(8,128)(2,1)S(1)} %pad_maximum_fusion.4), channel_id=1, source_target_pairs={{0,4},{4,0},{8,12},{12,8},{16,20},{20,16},{24,28},{28,24},{1,5},{5... | collective-permute-start | bytes 2359304 | tf_op jit(solution)/shard_map/ppermute | solution.py:344
  194.3 4.5 %collective-permute-start.35 = (f32[9,1024]{1,0:T(8,128)S(1)}, f32[9,1024]{1,0:T(8,128)S(1)}, u32[]{:S(2)}, u32[]{:S(2)}) collective-permute-start(f32[9,1024]{1,0:T(8,128)S(1)} %add.76), channel_id=1, source_target_pairs={{0,8},{4,12},{8,0},{12,4},{16,24},{20,28},{24,16},{28,20},{1,9},{5... | collective-permute-start | bytes 110600 | tf_op jit(solution)/shard_map/ppermute | solution.py:344
  198.8 4.3 %collective-permute-start.36 = (f32[9,1024]{1,0:T(8,128)S(1)}, f32[9,1024]{1,0:T(8,128)S(1)}, u32[]{:S(2)}, u32[]{:S(2)}) collective-permute-start(f32[9,1024]{1,0:T(8,128)S(1)} %add.77), channel_id=1, source_target_pairs={{0,16},{4,20},{8,24},{12,28},{16,0},{20,4},{24,8},{28,12},{1,17},{... | collective-permute-start | bytes 110600 | tf_op jit(solution)/shard_map/ppermute | solution.py:344
  206.5 5.1 %collective-permute-start.41 = (f32[10,1024]{1,0:T(8,128)S(1)}, f32[10,1024]{1,0:T(8,128)S(1)}, u32[]{:S(2)}, u32[]{:S(2)}) collective-permute-start(f32[10,1024]{1,0:T(8,128)S(1)} %pad_maximum_fusion.7), channel_id=1, source_target_pairs={{0,1},{1,0},{2,3},{3,2},{4,5},{5,4},{6,7},{7,6},{8,9},{9,8},{10,11... | collective-permute-start | bytes 122888 | tf_op jit(solution)/shard_map/ppermute | solution.py:344
  207.2 15.9 %collective-permute-start.40 = (bf16[256,1024]{1,0:T(8,128)(2,1)}, bf16[256,1024]{1,0:T(8,128)(2,1)}, u32[]{:S(2)}, u32[]{:S(2)}) collective-permute-start(bf16[256,1024]{1,0:T(8,128)(2,1)} %collective-permute-done.32), channel_id=1, source_target_pairs={{0,1},{1,0},{2,3},{3,2},{4,5},{5,4},{6,7},{7,6},{8,9},{9,8},{10,11... | collective-permute-start | bytes 1572872 | tf_op jit(solution)/shard_map/ppermute | solution.py:344
  211.5 10.0 %collective-permute-start.42 = (f32[10,1024]{1,0:T(8,128)S(1)}, f32[10,1024]{1,0:T(8,128)S(1)}, u32[]{:S(2)}, u32[]{:S(2)}) collective-permute-start(f32[10,1024]{1,0:T(8,128)S(1)} %add.84), channel_id=1, source_target_pairs={{0,2},{1,3},{2,0},{3,1},{4,6},{5,7},{6,4},{7,5},{8,10},{9,11},{10,... | collective-permute-start | bytes 122888 | tf_op jit(solution)/shard_map/ppermute | solution.py:344
  (48 other events, 349.8 us)

commit v5 on v4

--- a/solution.py
+++ b/solution.py
@@ -533,24 +533,32 @@
     core = place[1] & 1
     mine_lanes = pl.ds(pl.multiple_of(core * half, half), half)
     other_lanes = pl.ds(pl.multiple_of((1 - core) * half, half), half)
+
+    def branch_step(number, carry):
+        columns = pl.ds(pl.multiple_of(number * 2 * LANES, 2 * LANES), 2 * LANES)
+        summed = layer_in[:, columns].astype(jnp.float32)
+        for number in range(tensor_count):
+            head_rows = pl.ds(number * token_count, token_count)
+            half_rows = pl.ds(number * half, half)
+            summed = summed + dot_plain(heads[head_rows, mine_lanes], w_mine[half_rows, columns])
+            summed = summed + dot_plain(heads[head_rows, other_lanes], w_other[half_rows, columns])
+        residual[:, columns] = summed
+        return carry
+
+    lax.fori_loop(0, model_width // (2 * LANES), branch_step, 0)
     for row in range(0, token_count, ROWS):
         rows = pl.ds(row, ROWS)
-        values = layer_in[rows, :].astype(jnp.float32)
-        for number in range(tensor_count):
-            head_rows = pl.ds(number * token_count + row, ROWS)
-            half_rows = pl.ds(number * half, half)
-            values = values + dot_plain(heads[head_rows, mine_lanes], w_mine[half_rows, :])
-            values = values + dot_plain(heads[head_rows, other_lanes], w_other[half_rows, :])
-        residual[rows, :] = values
+        values = residual[rows, :]
         scale = lax.rsqrt(jnp.mean(values * values, axis=-1, keepdims=True) + epsilon)
         inverse[rows, :] = scale
-        normed_low = (values * scale * gain[...]).astype(jnp.bfloat16)
-        normed[rows, :] = normed_low
-        logits = dot_transposed(normed_low, router[...])
+        normed[rows, :] = (values * scale * gain[...]).astype(jnp.bfloat16)
+    gates[...] = dot_transposed(normed[...], router[...])
+    for row in range(0, token_count, ROWS):
+        rows = pl.ds(row, ROWS)
         picked = routes[rows, 0:1] == lane
         for top in range(1, routes.shape[1]):
             picked = picked | (routes[rows, top : top + 1] == lane)
-        logits = jnp.where(picked, logits, masked_out)
+        logits = jnp.where(picked, gates[rows, :], masked_out)
         weight = jnp.where(picked, jnp.exp(logits - jnp.max(logits, -1, keepdims=True)), 0.0)
         gates[rows, :] = weight / jnp.sum(weight, -1, keepdims=True)
     gate_grad[...] = jnp.zeros_like(gate_grad)
@@ -565,7 +573,7 @@
             rows = pl.ds(row, ROWS)
             gate = jnp.sum(jnp.where(lane == name, gates[rows, :], 0.0), -1, keepdims=True)
             gate_vals, up_vals = hidden[rows, :units], hidden[rows, units:]
-            sig_vals = 1.0 / (1.0 + jnp.exp(-gate_vals))
+            sig_vals = 0.5 + 0.5 * jnp.tanh(0.5 * gate_vals)
             silu_vals = gate_vals * sig_vals
             active = silu_vals * up_vals
             grad = plain[rows, :]
@@ -656,7 +664,7 @@
 def attend_back_kernel(tensor_count, *refs):
     place, far_refs, refs = refs[0], refs[1:8], refs[8:]
     blocks, refs = refs[:tensor_count], refs[tensor_count:]
-    mixtures, refs = refs[:tensor_count], refs[tensor_count:]
+    mixtures, refs = refs[: tensor_count - 1], refs[tensor_count - 1 :]
     parts, refs = refs[:tensor_count], refs[tensor_count:]
     branch_grad, projected_grad, heads_grad, pair_grad, total = refs[:5]
     near_refs, sems = refs[5:12], refs[12]
@@ -669,7 +677,7 @@
     span = token_count // tensor_count
     mixture_copies = [
         pltpu.make_async_copy(mixture, part.at[pl.ds(span, span)], sems.at[len(copies) + number])
-        for number, (mixture, part) in enumerate(zip(mixtures, parts))
+        for number, (mixture, part) in enumerate(zip(mixtures, parts[:-1]))
     ]
     block_copies = []
     for number, block in enumerate(blocks):
@@ -734,7 +742,7 @@
         return carry
 
     lax.fori_loop(0, model_width // (2 * LANES), column_step, 0)
-    write_parts(place, total, [part.at[:span] for part in parts], span)
+    write_parts(place, total, [part.at[:span] for part in parts[:-1]] + [parts[-1]], span)
     for copy in mixture_copies:
         copy.wait()
 
@@ -881,12 +889,12 @@
     heads_far = exchange(attended, "tensor", 2)
     heads_near = exchange(attended, "tensor", 1)
     output_both = exchange(output_far, "tensor", 1)
-    heads_far, heads_near = lax.optimization_barrier((heads_far, heads_near))
+    heads_far, heads_near, w_in_near, w_out_near = lax.optimization_barrier(
+        (heads_far, heads_near, w_in_near, w_out_near)
+    )
     heads_both = exchange(heads_far, "tensor", 1)
-    heads_both, output_both, w_in_near, w_in_far, w_out_near, w_out_far = (
-        lax.optimization_barrier(
-            (heads_both, output_both, w_in_near, w_in_far, w_out_near, w_out_far)
-        )
+    heads_both, output_both, w_in_far, w_out_far = lax.optimization_barrier(
+        (heads_both, output_both, w_in_far, w_out_far)
     )
     w_in_all = gather_pairs(w_in_near, w_in_far)
     w_out_all = gather_pairs(w_out_near, w_out_far)
@@ -989,21 +997,19 @@
 
     in_arrived = exchange(in_given, "expert", 4)
     out_arrived = exchange(out_given, "expert", 2)
-    in_summed = in_kept + in_arrived.astype(wide)
-    out_summed = out_kept + out_arrived.astype(wide)
-    in_arrived = exchange(in_summed[in_rows // 2 :].astype(low), "expert", 2)
-    out_arrived = exchange(out_summed[out_rows // 2 :].astype(low), "expert", 4)
-
+    mixture_last, *grad_blocks = lax.optimization_barrier((mixture_parts[3], *grad_blocks))
+    mixture_relayed = exchange(mixture_last, "tensor", 1)
     fetched = (w_output, queries, pairs, probs, cosine, sine, qkv_flat)
     back = pl.pallas_call(
         functools.partial(attend_back_kernel, tensor_count),
         out_shape=(shaped((2 * span, model_width), wide),)
-        + (shaped((2 * span, model_width), low),) * (tensor_count - 1)
+        + (shaped((2 * span, model_width), low),) * (tensor_count - 2)
+        + (shaped((span, model_width), low),)
         + (
             shaped((token_count, model_width), low),
             shaped((token_count, 2 * head_width), low),
         ),
-        in_specs=in_smem(1) + in_hbm(7 + 2 * tensor_count),
+        in_specs=in_smem(1) + in_hbm(6 + 2 * tensor_count),
         out_specs=tuple(in_vmem(tensor_count + 2)),
         scratch_shapes=[
             pltpu.VMEM((token_count, head_width), wide),
@@ -1018,12 +1024,22 @@
         place,
         *fetched,
         *grad_blocks,
-        *mixture_parts,
+        *mixture_parts[:-1],
     )
     input_parts, (branch_grad, projected_grad) = (
         back[:tensor_count],
         back[tensor_count:],
     )
+    *input_parts, projected_grad, in_arrived, out_arrived, mixture_relayed = (
+        lax.optimization_barrier(
+            (*input_parts, projected_grad, in_arrived, out_arrived, mixture_relayed)
+        )
+    )
+    in_summed = in_kept + in_arrived.astype(wide)
+    out_summed = out_kept + out_arrived.astype(wide)
+    in_arrived = exchange(in_summed[in_rows // 2 :].astype(low), "expert", 2)
+    out_arrived = exchange(out_summed[out_rows // 2 :].astype(low), "expert", 4)
+
     relayed = exchange(input_parts[3], "tensor", 1)
     row_count = (model_width + w_output.shape[0] * model_width // (2 * head_width)) // 2
     kept_sums, given_sums = pl.pallas_call(
@@ -1043,7 +1059,7 @@
     )
     sums_half = kept_sums + exchange(given_sums, "expert", 1).astype(wide)
     sums = exchange_halves(sums_half.astype(low), (2, 4))
-    input_pieces = scatter_parts(input_parts, relayed)
+    input_pieces = scatter_parts(input_parts, jnp.concatenate([relayed, mixture_relayed]))
     residual, in_arrived, out_arrived, sums = lax.optimization_barrier(
         (residual, in_arrived, out_arrived, sums)
     )

time: 225 us -> 216 us (0.960)
  waiting for transfers between devices: 94.5 us -> 85.3 us
  local copies, waits for them, and re-layouts: 20.4 us -> 17.6 us
    ppermute x43 -> x44, waiting for transfers between devices: 94.5 us -> 85.3 us  [exchange(): lax.ppermute(array_in, axis_name, [(i, i ^ bits) for i in range(count)])]
    unnamed x106 -> x104, local copies, waits for them, and re-layouts: 12.3 us -> 9.46 us
    ppermute x43 -> x44, starting transfers between devices: 43.9 us -> 46.1 us  [exchange(): lax.ppermute(array_in, axis_name, [(i, i ^ bits) for i in range(count)])]
  transfers between devices with their start and end apart: 43 -> 44, of which waited for: 26 -> 26; matrix products, arithmetic and copies ran while one was open for 10% -> 11% of each run, Pallas kernels for 14% -> 15%
where the time goes in v5:
time: 216 us; the launch traced here: 215 us
  waiting for transfers between devices  85.3 us (39%)
  Pallas kernels  48.6 us (22%)
  starting transfers between devices  46.1 us (21%)
  local copies, waits for them, and re-layouts  17.6 us (8%)
  other arithmetic  15.5 us (7%)
    ppermute x44, waiting for transfers between devices, exchange(): lax.ppermute(array_in, axis_name, [(i, i ^ bits) for i in range(count)])  85.3 us
    ppermute x44, starting transfers between devices, exchange(): lax.ppermute(array_in, axis_name, [(i, i ^ bits) for i in range(count)])  46.1 us
    pallas_call x1, Pallas kernels, on_device(): pl.pallas_call(functools.partial(middle_kernel, tensor_count), out_shape=...  16.4 us
    pallas_call x1, Pallas kernels, on_device(): pl.pallas_call(functools.partial(attend_back_kernel, tensor_count), out_s...  10.6 us
    unnamed x104, local copies, waits for them, and re-layouts  9.46 us
    pallas_call x1, Pallas kernels, on_device(): pl.pallas_call(functools.partial(weight_grad_kernel, tensor_count), out_s...  7.62 us
    pallas_call x1, Pallas kernels, on_device(): pl.pallas_call(attend_kernel, out_shape=kept + (shaped((token_count, head...  7.61 us
  transfers between devices with their start and end apart: 44, of which 26 were waited for; matrix products, arithmetic and copies ran while one was open for 11% of the time, Pallas kernels for 15%

profile of v5, /device:TPU:0, one launch (start us, length us, event | category | flops | bytes accessed | tf_op | source)
XLA Modules:
  0.0 214.6 jit_solution(16344079149034790698)
XLA Ops:
  0.6 3.0 %collective-permute-start = (bf16[256,1024]{1,0:T(8,128)(2,1)}, bf16[256,1024]{1,0:T(8,128)(2,1)S(1)}, u32[]{:S(2)}, u32[]{:S(2)}) collective-permute-start(bf16[256,1024]{1,0:T(8,128)(2,1)} %bitcast.34), channel_id=1, source_target_pairs={{0,8},{4,12},{8,0},{12,4},{16,24},{20,28},{24,16},{28,20},{1,9},{5... | collective-permute-start | bytes 1572872 | tf_op jit(solution)/shard_map/ppermute | solution.py:344
  4.7 2.7 %collective-permute-start.2 = (bf16[128,1024]{1,0:T(8,128)(2,1)S(1)}, bf16[128,1024]{1,0:T(8,128)(2,1)S(1)}, u32[]{:S(2)}, u32[]{:S(2)}) collective-permute-start(bf16[128,1024]{1,0:T(8,128)(2,1)S(1)} %slice_select_fusion), channel_id=1, source_target_pairs={{0,2},{1,3},{2,0},{3,1},{4,6},{5,7},{6,4},{7,5},{8,10},{9,11},{10,... | collective-permute-start | bytes 786440 | tf_op jit(solution)/shard_map/ppermute | solution.py:344
  7.4 1.6 collective-permute-start.3
  8.9 1.5 collective-permute-start.1
  10.5 2.5 %copy.25 = bf16[128,8,2,256]{3,1,2,0:T(8,128)(2,1)} copy(bf16[128,8,2,256]{3,2,1,0:T(2,128)(2,1)} %bitcast.31) | data formatting | bytes 2097152
  12.9 7.6 %attend.1 = (bf16[2,4,256,128]{3,2,1,0:T(8,128)(2,1)}, bf16[2,512,128]{2,1,0:T(8,128)(2,1)}, bf16[2,4,256,512]{3,2,1,0:T(8,128)(2,1)}, bf16[512,256]{1,0:T(8,128)(2,1)}) custom-call(s32[1,3]{1,0:T(1,128)} %lengths.1, bf16[512,1024]{1,0:T(8,128)(2,1)} %layer_in.3, f32[1,1024]{1,0:T(1,128)} %bitcast.22, bf16[1024,512]{1,0:T(8,128)(2,1)} %bitcast.27, ...), custom_call_target="tpu_custom_call" | custom-call | tf_op jit(solution)/shard_map/attend/pallas_call | solution.py:870
  23.3 2.4 %collective-permute-start.5 = (bf16[512,256]{1,0:T(8,128)(2,1)S(1)}, bf16[512,256]{1,0:T(8,128)(2,1)S(1)}, u32[]{:S(2)}, u32[]{:S(2)}) collective-permute-start(bf16[512,256]{1,0:T(8,128)(2,1)S(1)} %copy-done.11), channel_id=1, source_target_pairs={{0,1},{1,0},{2,3},{3,2},{4,5},{5,4},{6,7},{7,6},{8,9},{9,8},{10,11... | collective-permute-start | bytes 786440 | tf_op jit(solution)/shard_map/ppermute | solution.py:344
  26.4 9.1 %collective-permute-done.4 = bf16[512,256]{1,0:T(8,128)(2,1)S(1)} collective-permute-done((bf16[512,256]{1,0:T(8,128)(2,1)S(1)}, bf16[512,256]{1,0:T(8,128)(2,1)S(1)}, u32[]{:S(2)}, u32[]{:S(2)}) %collective-permute-start.4) | collective-permute-done | bytes 262176 | tf_op jit(solution)/shard_map/ppermute | solution.py:344
  35.4 1.3 collective-permute-done.5
  37.6 4.8 %collective-permute-done.7 = bf16[128,1024]{1,0:T(8,128)(2,1)S(1)} collective-permute-done((bf16[128,1024]{1,0:T(8,128)(2,1)S(1)}, bf16[128,1024]{1,0:T(8,128)(2,1)S(1)}, u32[]{:S(2)}, u32[]{:S(2)}) %collective-permute-start.7) | collective-permute-done | bytes 262176 | tf_op jit(solution)/shard_map/ppermute | solution.py:344
  42.4 4.4 %collective-permute-done.6 = bf16[512,256]{1,0:T(8,128)(2,1)S(1)} collective-permute-done((bf16[512,256]{1,0:T(8,128)(2,1)S(1)}, bf16[512,256]{1,0:T(8,128)(2,1)S(1)}, u32[]{:S(2)}, u32[]{:S(2)}) %collective-permute-start.6) | collective-permute-done | bytes 262176 | tf_op jit(solution)/shard_map/ppermute | solution.py:344
  46.8 1.1 pad_maximum_fusion.1.refs_6_
  49.2 1.3 pad_maximum_fusion.2.refs_8_
  50.5 1.7 collective-permute-done.13.refs_15_.refs_7_
  52.2 1.5 collective-permute-done.14.refs_16_.refs_8_
  55.0 16.4 %middle.1 = (f32[128,1024]{1,0:T(8,128)S(1)}, bf16[128,1024]{1,0:T(8,128)(2,1)}, bf16[128,1024]{1,0:T(8,128)(2,1)S(1)}, bf16[128,1024]{1,0:T(8,128)(2,1)S(1)}, f...) custom-call(s32[2]{0:T(128)S(1)} %pad_add_fusion.refs_0_.place, ...), custom_call_target="tpu_custom_call" | custom-call | tf_op jit(solution)/shard_map/middle/pallas_call | solution.py:908
  71.4 7.6 %weight_grad.1 = (f32[128,1024]{1,0:T(8,128)S(1)}, bf16[128,1024]{1,0:T(8,128)(2,1)S(1)}, bf16[128,1024]{1,0:T(8,128)(2,1)S(1)}, bf16[128,1024]{1,0:T(8,128)(2,1...) custom-call(s32[2]{0:T(128)S(1)} %pad_add_fusion.refs_0_.place, ...), custom_call_target="tpu_custom_call" | custom-call | tf_op jit(solution)/shard_map/weight_grad/pallas_call | solution.py:951
  80.5 3.2 %collective-permute-start.17 = (bf16[128,1024]{1,0:T(8,128)(2,1)}, bf16[128,1024]{1,0:T(8,128)(2,1)S(1)}, u32[]{:S(2)}, u32[]{:S(2)}) collective-permute-start(bf16[128,1024]{1,0:T(8,128)(2,1)} %add_convert_fusion.6), channel_id=1, source_target_pairs={{0,2},{1,3},{2,0},{3,1},{4,6},{5,7},{6,4},{7,5},{8,10},{9,11},{10,... | collective-permute-start | bytes 786440 | tf_op jit(solution)/shard_map/ppermute | solution.py:344
  84.2 1.1 collective-permute-done.18.given
  85.3 1.6 add_grads.1
  86.9 1.3 copy-done.2
  90.0 1.5 collective-permute-start.22
  91.6 4.8 %collective-permute-done.17.far = bf16[128,1024]{1,0:T(8,128)(2,1)S(1)} collective-permute-done((bf16[128,1024]{1,0:T(8,128)(2,1)}, bf16[128,1024]{1,0:T(8,128)(2,1)S(1)}, u32[]{:S(2)}, u32[]{:S(2)}) %collective-permute-start.17) | collective-permute-done | bytes 262176 | tf_op jit(solution)/shard_map/ppermute | solution.py:344
  97.4 1.2 norm_back.1
  98.7 2.3 %collective-permute-start.20 = (bf16[128,1024]{1,0:T(8,128)(2,1)S(1)}, bf16[128,1024]{1,0:T(8,128)(2,1)S(1)}, u32[]{:S(2)}, u32[]{:S(2)}) collective-permute-start(bf16[128,1024]{1,0:T(8,128)(2,1)S(1)} %get-tuple-element.151.refs_8_), channel_id=1, source_target_pairs={{0,1},{1,0},{2,3},{3,2},{4,5},{5,4},{6,7},{7,6},{8,9},{9,8},{10,11... | collective-permute-start | bytes 786440 | tf_op jit(solution)/shard_map/ppermute | solution.py:344
  101.0 11.1 %collective-permute-done.19.refs_10_ = bf16[128,1024]{1,0:T(8,128)(2,1)S(1)} collective-permute-done((bf16[128,1024]{1,0:T(8,128)(2,1)S(1)}, bf16[128,1024]{1,0:T(8,128)(2,1)S(1)}, u32[]{:S(2)}, u32[]{:S(2)}) %collective-permute-start.19) | collective-permute-done | bytes 262176 | tf_op jit(solution)/shard_map/ppermute | solution.py:344
  112.8 6.6 %collective-permute-done.21.refs_11_ = bf16[128,1024]{1,0:T(8,128)(2,1)S(1)} collective-permute-done((bf16[128,1024]{1,0:T(8,128)(2,1)S(1)}, bf16[128,1024]{1,0:T(8,128)(2,1)S(1)}, u32[]{:S(2)}, u32[]{:S(2)}) %collective-permute-start.21) | collective-permute-done | bytes 262176 | tf_op jit(solution)/shard_map/ppermute | solution.py:344
  120.1 10.6 %attend_back.1 = (f32[256,1024]{1,0:T(8,128)}, bf16[256,1024]{1,0:T(8,128)(2,1)}, bf16[256,1024]{1,0:T(8,128)(2,1)}, bf16[128,1024]{1,0:T(8,128)(2,1)}, bf16[512...) custom-call(s32[2]{0:T(128)} %copy-done.22, bf16[256,1024]{1,0:T(8,128)(2,1)} %refs_1_.1, ...), custom_call_target="tpu_custom_call" | custom-call | tf_op jit(solution)/shard_map/attend_back/pallas_call | solution.py:1003
  130.8 1.4 collective-permute-start.25
  132.2 1.5 convert_add_fusion
  133.8 3.2 %attend_grad.1 = (f32[768,512]{1,0:T(8,128)S(1)}, bf16[768,512]{1,0:T(8,128)(2,1)S(1)}) custom-call(s32[2]{0:T(128)S(1)} %copy-done.23, bf16[512,1024]{1,0:T(8,128)(2,1)S(1)} %copy-done, f32[1,1024]{1,0:T(1,128)S(1)} %bitcast.23, bf16[512,512]{1,0:T(8,128)(2,1)S(1)} %copy-done.14, bf16[512,256]{1,0:T(8,128)(2,1)S(1)} %copy-done.12, ...), custom_call_target="tpu_custom_call" | custom-call | tf_op jit(solution)/shard_map/attend_grad/pallas_call | solution.py:1045
  141.1 2.1 %collective-permute-start.32 = (bf16[384,512]{1,0:T(8,128)(2,1)S(1)}, bf16[384,512]{1,0:T(8,128)(2,1)S(1)}, u32[]{:S(2)}, u32[]{:S(2)}) collective-permute-start(bf16[384,512]{1,0:T(8,128)(2,1)S(1)} %get-tuple-element.210), channel_id=1, source_target_pairs={{0,16},{4,20},{8,24},{12,28},{16,0},{20,4},{24,8},{28,12},{1,17},{... | collective-permute-start | bytes 1179656 | tf_op jit(solution)/shard_map/ppermute | solution.py:344
  143.4 2.6 %collective-permute-start.27 = (bf16[256,1024]{1,0:T(8,128)(2,1)S(1)}, bf16[256,1024]{1,0:T(8,128)(2,1)S(1)}, u32[]{:S(2)}, u32[]{:S(2)}) collective-permute-start(bf16[256,1024]{1,0:T(8,128)(2,1)S(1)} %add_convert_fusion.1), channel_id=1, source_target_pairs={{0,2},{1,3},{2,0},{3,1},{4,6},{5,7},{6,4},{7,5},{8,10},{9,11},{10,... | collective-permute-start | bytes 1572872 | tf_op jit(solution)/shard_map/ppermute | solution.py:344
  147.7 12.7 %collective-permute-done.31 = bf16[384,512]{1,0:T(8,128)(2,1)S(1)} collective-permute-done((bf16[384,512]{1,0:T(8,128)(2,1)S(1)}, bf16[384,512]{1,0:T(8,128)(2,1)S(1)}, u32[]{:S(2)}, u32[]{:S(2)}) %collective-permute-start.31) | collective-permute-done | bytes 393248 | tf_op jit(solution)/shard_map/ppermute | solution.py:344
  160.4 2.1 %collective-permute-start.29 = (bf16[128,1024]{1,0:T(8,128)(2,1)S(1)}, bf16[128,1024]{1,0:T(8,128)(2,1)S(1)}, u32[]{:S(2)}, u32[]{:S(2)}) collective-permute-start(bf16[128,1024]{1,0:T(8,128)(2,1)S(1)} %slice.129), channel_id=1, source_target_pairs={{0,16},{4,20},{8,24},{12,28},{16,0},{20,4},{24,8},{28,12},{1,17},{... | collective-permute-start | bytes 786440 | tf_op jit(solution)/shard_map/ppermute | solution.py:344
  162.8 5.9 %collective-permute-done.29 = bf16[128,1024]{1,0:T(8,128)(2,1)S(1)} collective-permute-done((bf16[128,1024]{1,0:T(8,128)(2,1)S(1)}, bf16[128,1024]{1,0:T(8,128)(2,1)S(1)}, u32[]{:S(2)}, u32[]{:S(2)}) %collective-permute-start.29) | collective-permute-done | bytes 262176 | tf_op jit(solution)/shard_map/ppermute | solution.py:344
  171.8 2.6 %collective-permute-start.33 = (bf16[256,1024]{1,0:T(8,128)(2,1)S(1)}, bf16[256,1024]{1,0:T(8,128)(2,1)}, u32[]{:S(2)}, u32[]{:S(2)}) collective-permute-start(bf16[256,1024]{1,0:T(8,128)(2,1)S(1)} %finish.1), channel_id=1, source_target_pairs={{0,2},{1,3},{2,0},{3,1},{4,6},{5,7},{6,4},{7,5},{8,10},{9,11},{10,... | collective-permute-start | bytes 1572872 | tf_op jit(solution)/shard_map/ppermute | solution.py:344
  175.4 4.9 %collective-permute-done.38 = bf16[384,512]{1,0:T(8,128)(2,1)S(1)} collective-permute-done((bf16[384,512]{1,0:T(8,128)(2,1)S(1)}, bf16[384,512]{1,0:T(8,128)(2,1)S(1)}, u32[]{:S(2)}, u32[]{:S(2)}) %collective-permute-start.38) | collective-permute-done | bytes 393248 | tf_op jit(solution)/shard_map/ppermute | solution.py:344
  181.3 2.5 %convert_add_fusion.1 = f32[256,1024]{1,0:T(8,128)} fusion(bf16[256,1024]{1,0:T(8,128)(2,1)S(1)} %copy-done.35, f32[512,1024]{1,0:T(8,128)} %copy-done.29), kind=kLoop, calls=%fused_computation.8 | loop fusion | flops 524288 | bytes 2621440 | tf_op jit(solution)/shard_map/add | solution.py:1066
  185.4 3.8 %collective-permute-done.36 = f32[9,1024]{1,0:T(8,128)S(1)} collective-permute-done((f32[9,1024]{1,0:T(8,128)S(1)}, f32[9,1024]{1,0:T(8,128)S(1)}, u32[]{:S(2)}, u32[]{:S(2)}) %collective-permute-start.36) | collective-permute-done | bytes 36896 | tf_op jit(solution)/shard_map/ppermute | solution.py:344
  189.2 1.2 collective-permute-start.37
  190.5 3.0 %collective-permute-done.37 = f32[9,1024]{1,0:T(8,128)S(1)} collective-permute-done((f32[9,1024]{1,0:T(8,128)S(1)}, f32[9,1024]{1,0:T(8,128)S(1)}, u32[]{:S(2)}, u32[]{:S(2)}) %collective-permute-start.37) | collective-permute-done | bytes 36896 | tf_op jit(solution)/shard_map/ppermute | solution.py:344
  195.1 1.7 fusion
  196.8 1.1 collective-permute-start.42
  199.0 2.9 %collective-permute-done.42 = f32[10,1024]{1,0:T(8,128)S(1)} collective-permute-done((f32[10,1024]{1,0:T(8,128)S(1)}, f32[10,1024]{1,0:T(8,128)S(1)}, u32[]{:S(2)}, u32[]{:S(2)}) %collective-permute-start.42) | collective-permute-done | bytes 40992 | tf_op jit(solution)/shard_map/ppermute | solution.py:344
  201.9 2.6 %collective-permute-start.43 = (f32[10,1024]{1,0:T(8,128)S(1)}, f32[10,1024]{1,0:T(8,128)S(1)}, u32[]{:S(2)}, u32[]{:S(2)}) collective-permute-start(f32[10,1024]{1,0:T(8,128)S(1)} %add.84), channel_id=1, source_target_pairs={{0,2},{1,3},{2,0},{3,1},{4,6},{5,7},{6,4},{7,5},{8,10},{9,11},{10,... | collective-permute-start | bytes 122888 | tf_op jit(solution)/shard_map/ppermute | solution.py:344
  206.9 2.3 %reshape.44 = f32[1024,2,256]{2,1,0:T(2,128)} reshape(f32[1024,512]{1,0:T(8,128)S(1)} %copy-done.28) | data formatting | bytes 4194304 | tf_op jit(solution)/shard_map/reshape | solution.py:1088
  212.7 1.9 slice_dynamic-update-slice_fusion
  (201 shorter events, 35.5 us)
Async XLA Ops:
  0.6 20.0 %collective-permute-start = (bf16[256,1024]{1,0:T(8,128)(2,1)}, bf16[256,1024]{1,0:T(8,128)(2,1)S(1)}, u32[]{:S(2)}, u32[]{:S(2)}) collective-permute-start(bf16[256,1024]{1,0:T(8,128)(2,1)} %bitcast.34), channel_id=1, source_target_pairs={{0,8},{4,12},{8,0},{12,4},{16,24},{20,28},{24,16},{28,20},{1,9},{5... | collective-permute-start | bytes 1572872 | tf_op jit(solution)/shard_map/ppermute | solution.py:344
  4.7 15.9 %collective-permute-start.2 = (bf16[128,1024]{1,0:T(8,128)(2,1)S(1)}, bf16[128,1024]{1,0:T(8,128)(2,1)S(1)}, u32[]{:S(2)}, u32[]{:S(2)}) collective-permute-start(bf16[128,1024]{1,0:T(8,128)(2,1)S(1)} %slice_select_fusion), channel_id=1, source_target_pairs={{0,2},{1,3},{2,0},{3,1},{4,6},{5,7},{6,4},{7,5},{8,10},{9,11},{10,... | collective-permute-start | bytes 786440 | tf_op jit(solution)/shard_map/ppermute | solution.py:344
  7.4 13.2 %collective-permute-start.3 = (bf16[128,1024]{1,0:T(8,128)(2,1)S(1)}, bf16[128,1024]{1,0:T(8,128)(2,1)S(1)}, u32[]{:S(2)}, u32[]{:S(2)}) collective-permute-start(bf16[128,1024]{1,0:T(8,128)(2,1)S(1)} %slice_select_fusion), channel_id=1, source_target_pairs={{0,1},{1,0},{2,3},{3,2},{4,5},{5,4},{6,7},{7,6},{8,9},{9,8},{10,11... | collective-permute-start | bytes 786440 | tf_op jit(solution)/shard_map/ppermute | solution.py:344
  8.9 11.7 %collective-permute-start.1 = (bf16[128,1024]{1,0:T(8,128)(2,1)}, bf16[128,1024]{1,0:T(8,128)(2,1)S(1)}, u32[]{:S(2)}, u32[]{:S(2)}) collective-permute-start(bf16[128,1024]{1,0:T(8,128)(2,1)} %bitcast.36), channel_id=1, source_target_pairs={{0,16},{4,20},{8,24},{12,28},{16,0},{20,4},{24,8},{28,12},{1,17},{... | collective-permute-start | bytes 786440 | tf_op jit(solution)/shard_map/ppermute | solution.py:344
  21.7 27.4 %copy-start.48 = (bf16[1024,8]{0,1:T(8,128)(2,1)S(1)}, bf16[1024,8]{0,1:T(8,128)(2,1)}, u32[]{:S(2)}) copy-start(bf16[1024,8]{0,1:T(8,128)(2,1)} %param.20) | copy-start | bytes 49156
  21.7 25.1 %collective-permute-start.8 = (bf16[512,1024]{1,0:T(8,128)(2,1)}, bf16[512,1024]{1,0:T(8,128)(2,1)}, u32[]{:S(2)}, u32[]{:S(2)}) collective-permute-start(bf16[512,1024]{1,0:T(8,128)(2,1)} %pad_maximum_fusion.refs_9_), channel_id=1, source_target_pairs={{0,16},{4,20},{8,24},{12,28},{16,0},{20,4},{24,8},{28,12},{1,17},{... | collective-permute-start | bytes 3145736 | tf_op jit(solution)/shard_map/ppermute | solution.py:344
  22.2 13.3 %collective-permute-start.4 = (bf16[512,256]{1,0:T(8,128)(2,1)S(1)}, bf16[512,256]{1,0:T(8,128)(2,1)S(1)}, u32[]{:S(2)}, u32[]{:S(2)}) collective-permute-start(bf16[512,256]{1,0:T(8,128)(2,1)S(1)} %copy-done.11), channel_id=1, source_target_pairs={{0,2},{1,3},{2,0},{3,1},{4,6},{5,7},{6,4},{7,5},{8,10},{9,11},{10,... | collective-permute-start | bytes 786440 | tf_op jit(solution)/shard_map/ppermute | solution.py:344
  23.3 13.5 %collective-permute-start.5 = (bf16[512,256]{1,0:T(8,128)(2,1)S(1)}, bf16[512,256]{1,0:T(8,128)(2,1)S(1)}, u32[]{:S(2)}, u32[]{:S(2)}) collective-permute-start(bf16[512,256]{1,0:T(8,128)(2,1)S(1)} %copy-done.11), channel_id=1, source_target_pairs={{0,1},{1,0},{2,3},{3,2},{4,5},{5,4},{6,7},{7,6},{8,9},{9,8},{10,11... | collective-permute-start | bytes 786440 | tf_op jit(solution)/shard_map/ppermute | solution.py:344
  25.7 28.2 %copy-start = (bf16[512,1024]{1,0:T(8,128)(2,1)S(1)}, bf16[512,1024]{1,0:T(8,128)(2,1)}, u32[]{:S(2)}) copy-start(bf16[512,1024]{1,0:T(8,128)(2,1)} %layer_in.3) | copy-start | bytes 3145732
  25.8 28.2 %copy-start.1 = (bf16[512,1024]{1,0:T(8,128)(2,1)S(1)}, bf16[512,1024]{1,0:T(8,128)(2,1)}, u32[]{:S(2)}) copy-start(bf16[512,1024]{1,0:T(8,128)(2,1)} %refs_2_.1) | copy-start | bytes 3145732
  25.8 28.2 %copy-start.21 = (f32[1024]{0:T(1024)S(1)}, f32[1024]{0:T(1024)}, u32[]{:S(2)}) copy-start(f32[1024]{0:T(1024)} %param.19) | copy-start | bytes 12292
  25.8 21.0 %collective-permute-start.9 = (bf16[256,1024]{1,0:T(8,128)(2,1)S(1)}, bf16[256,1024]{1,0:T(8,128)(2,1)S(1)}, u32[]{:S(2)}, u32[]{:S(2)}) collective-permute-start(bf16[256,1024]{1,0:T(8,128)(2,1)S(1)} %pad_maximum_fusion.5.refs_13_.refs_5_), channel_id=1, source_target_pairs={{0,8},{4,12},{8,0},{12,4},{16,24},{20,28},{24,16},{28,20},{1,9},{5... | collective-permute-start | bytes 1572872 | tf_op jit(solution)/shard_map/ppermute | solution.py:344
  26.4 16.0 %collective-permute-start.7 = (bf16[128,1024]{1,0:T(8,128)(2,1)S(1)}, bf16[128,1024]{1,0:T(8,128)(2,1)S(1)}, u32[]{:S(2)}, u32[]{:S(2)}) collective-permute-start(bf16[128,1024]{1,0:T(8,128)(2,1)S(1)} %collective-permute-done.2), channel_id=1, source_target_pairs={{0,1},{1,0},{2,3},{3,2},{4,5},{5,4},{6,7},{7,6},{8,9},{9,8},{10,11... | collective-permute-start | bytes 786440 | tf_op jit(solution)/shard_map/ppermute | solution.py:344
  36.8 10.0 %collective-permute-start.6 = (bf16[512,256]{1,0:T(8,128)(2,1)S(1)}, bf16[512,256]{1,0:T(8,128)(2,1)S(1)}, u32[]{:S(2)}, u32[]{:S(2)}) collective-permute-start(bf16[512,256]{1,0:T(8,128)(2,1)S(1)} %collective-permute-done.4), channel_id=1, source_target_pairs={{0,1},{1,0},{2,3},{3,2},{4,5},{5,4},{6,7},{7,6},{8,9},{9,8},{10,11... | collective-permute-start | bytes 786440 | tf_op jit(solution)/shard_map/ppermute | solution.py:344
  37.6 14.6 %collective-permute-start.11 = (bf16[512,1024]{1,0:T(8,128)(2,1)}, bf16[512,1024]{1,0:T(8,128)(2,1)}, u32[]{:S(2)}, u32[]{:S(2)}) collective-permute-start(bf16[512,1024]{1,0:T(8,128)(2,1)} %pad_maximum_fusion.refs_9_), channel_id=1, source_target_pairs={{0,4},{4,0},{8,12},{12,8},{16,20},{20,16},{24,28},{28,24},{1,5},{5... | collective-permute-start | bytes 3145736 | tf_op jit(solution)/shard_map/ppermute | solution.py:344
  47.9 5.8 %collective-permute-start.10 = (bf16[512,1024]{1,0:T(8,128)(2,1)}, bf16[512,1024]{1,0:T(8,128)(2,1)}, u32[]{:S(2)}, u32[]{:S(2)}) collective-permute-start(bf16[512,1024]{1,0:T(8,128)(2,1)} %pad_maximum_fusion.1.refs_6_), channel_id=1, source_target_pairs={{0,4},{4,0},{8,12},{12,8},{16,20},{20,16},{24,28},{28,24},{1,5},{5... | collective-permute-start | bytes 3145736 | tf_op jit(solution)/shard_map/ppermute | solution.py:344
  47.9 6.0 %collective-permute-start.12 = (bf16[512,1024]{1,0:T(8,128)(2,1)}, bf16[512,1024]{1,0:T(8,128)(2,1)}, u32[]{:S(2)}, u32[]{:S(2)}) collective-permute-start(bf16[512,1024]{1,0:T(8,128)(2,1)} %collective-permute-done.8.refs_10_), channel_id=1, source_target_pairs={{0,4},{4,0},{8,12},{12,8},{16,20},{20,16},{24,28},{28,24},{1,5},{5... | collective-permute-start | bytes 3145736 | tf_op jit(solution)/shard_map/ppermute | solution.py:344
  48.4 3.8 %collective-permute-start.13 = (bf16[256,1024]{1,0:T(8,128)(2,1)S(1)}, bf16[256,1024]{1,0:T(8,128)(2,1)}, u32[]{:S(2)}, u32[]{:S(2)}) collective-permute-start(bf16[256,1024]{1,0:T(8,128)(2,1)S(1)} %pad_maximum_fusion.5.refs_13_.refs_5_), channel_id=1, source_target_pairs={{0,4},{4,0},{8,12},{12,8},{16,20},{20,16},{24,28},{28,24},{1,5},{5... | collective-permute-start | bytes 1572872 | tf_op jit(solution)/shard_map/ppermute | solution.py:344
  48.4 5.3 %collective-permute-start.14 = (bf16[256,1024]{1,0:T(8,128)(2,1)S(1)}, bf16[256,1024]{1,0:T(8,128)(2,1)}, u32[]{:S(2)}, u32[]{:S(2)}) collective-permute-start(bf16[256,1024]{1,0:T(8,128)(2,1)S(1)} %collective-permute-done.9.refs_14_.refs_6_), channel_id=1, source_target_pairs={{0,4},{4,0},{8,12},{12,8},{16,20},{20,16},{24,28},{28,24},{1,5},{5... | collective-permute-start | bytes 1572872 | tf_op jit(solution)/shard_map/ppermute | solution.py:344
  71.4 8.3 %collective-permute-start.15 = (bf16[128,1024]{1,0:T(8,128)(2,1)S(1)}, bf16[128,1024]{1,0:T(8,128)(2,1)S(1)}, u32[]{:S(2)}, u32[]{:S(2)}) collective-permute-start(bf16[128,1024]{1,0:T(8,128)(2,1)S(1)} %get-tuple-element.130), channel_id=1, source_target_pairs={{0,1},{1,0},{2,3},{3,2},{4,5},{5,4},{6,7},{7,6},{8,9},{9,8},{10,11... | collective-permute-start | bytes 786440 | tf_op jit(solution)/shard_map/ppermute | solution.py:344
  79.7 5.7 %collective-permute-start.18 = (bf16[1536,1024]{1,0:T(8,128)(2,1)S(1)}, bf16[1536,1024]{1,0:T(8,128)(2,1)S(1)}, u32[]{:S(2)}, u32[]{:S(2)}) collective-permute-start(bf16[1536,1024]{1,0:T(8,128)(2,1)S(1)} %get-tuple-element.141), channel_id=1, source_target_pairs={{0,4},{4,0},{8,12},{12,8},{16,20},{20,16},{24,28},{28,24},{1,5},{5... | collective-permute-start | bytes 9437192 | tf_op jit(solution)/shard_map/ppermute | solution.py:344
  80.5 15.9 %collective-permute-start.17 = (bf16[128,1024]{1,0:T(8,128)(2,1)}, bf16[128,1024]{1,0:T(8,128)(2,1)S(1)}, u32[]{:S(2)}, u32[]{:S(2)}) collective-permute-start(bf16[128,1024]{1,0:T(8,128)(2,1)} %add_convert_fusion.6), channel_id=1, source_target_pairs={{0,2},{1,3},{2,0},{3,1},{4,6},{5,7},{6,4},{7,5},{8,10},{9,11},{10,... | collective-permute-start | bytes 786440 | tf_op jit(solution)/shard_map/ppermute | solution.py:344
  83.7 13.7 %collective-permute-start.16 = (bf16[128,1024]{1,0:T(8,128)(2,1)}, bf16[128,1024]{1,0:T(8,128)(2,1)}, u32[]{:S(2)}, u32[]{:S(2)}) collective-permute-start(bf16[128,1024]{1,0:T(8,128)(2,1)} %get-tuple-element.136), channel_id=1, source_target_pairs={{0,1},{1,0},{2,3},{3,2},{4,5},{5,4},{6,7},{7,6},{8,9},{9,8},{10,11... | collective-permute-start | bytes 786440 | tf_op jit(solution)/shard_map/ppermute | solution.py:344
  90.0 40.7 %collective-permute-start.22 = (bf16[512,1024]{1,0:T(8,128)(2,1)}, bf16[512,1024]{1,0:T(8,128)(2,1)}, u32[]{:S(2)}, u32[]{:S(2)}) collective-permute-start(bf16[512,1024]{1,0:T(8,128)(2,1)} %get-tuple-element.163), channel_id=1, source_target_pairs={{0,16},{4,20},{8,24},{12,28},{16,0},{20,4},{24,8},{28,12},{1,17},{... | collective-permute-start | bytes 3145736 | tf_op jit(solution)/shard_map/ppermute | solution.py:344
  98.6 13.5 %collective-permute-start.19 = (bf16[128,1024]{1,0:T(8,128)(2,1)S(1)}, bf16[128,1024]{1,0:T(8,128)(2,1)S(1)}, u32[]{:S(2)}, u32[]{:S(2)}) collective-permute-start(bf16[128,1024]{1,0:T(8,128)(2,1)S(1)} %get-tuple-element.151.refs_8_), channel_id=1, source_target_pairs={{0,2},{1,3},{2,0},{3,1},{4,6},{5,7},{6,4},{7,5},{8,10},{9,11},{10,... | collective-permute-start | bytes 786440 | tf_op jit(solution)/shard_map/ppermute | solution.py:344
  98.7 13.4 %collective-permute-start.20 = (bf16[128,1024]{1,0:T(8,128)(2,1)S(1)}, bf16[128,1024]{1,0:T(8,128)(2,1)S(1)}, u32[]{:S(2)}, u32[]{:S(2)}) collective-permute-start(bf16[128,1024]{1,0:T(8,128)(2,1)S(1)} %get-tuple-element.151.refs_8_), channel_id=1, source_target_pairs={{0,1},{1,0},{2,3},{3,2},{4,5},{5,4},{6,7},{7,6},{8,9},{9,8},{10,11... | collective-permute-start | bytes 786440 | tf_op jit(solution)/shard_map/ppermute | solution.py:344
  112.1 7.3 %collective-permute-start.21 = (bf16[128,1024]{1,0:T(8,128)(2,1)S(1)}, bf16[128,1024]{1,0:T(8,128)(2,1)S(1)}, u32[]{:S(2)}, u32[]{:S(2)}) collective-permute-start(bf16[128,1024]{1,0:T(8,128)(2,1)S(1)} %collective-permute-done.19.refs_10_), channel_id=1, source_target_pairs={{0,1},{1,0},{2,3},{3,2},{4,5},{5,4},{6,7},{7,6},{8,9},{9,8},{10,11... | collective-permute-start | bytes 786440 | tf_op jit(solution)/shard_map/ppermute | solution.py:344
  112.2 18.5 %collective-permute-start.23 = (bf16[256,1024]{1,0:T(8,128)(2,1)S(1)}, bf16[256,1024]{1,0:T(8,128)(2,1)S(1)}, u32[]{:S(2)}, u32[]{:S(2)}) collective-permute-start(bf16[256,1024]{1,0:T(8,128)(2,1)S(1)} %copy-done.25), channel_id=1, source_target_pairs={{0,8},{4,12},{8,0},{12,4},{16,24},{20,28},{24,16},{28,20},{1,9},{5... | collective-permute-start | bytes 1572872 | tf_op jit(solution)/shard_map/ppermute | solution.py:344
  119.4 11.3 %collective-permute-start.24 = (bf16[128,1024]{1,0:T(8,128)(2,1)}, bf16[128,1024]{1,0:T(8,128)(2,1)}, u32[]{:S(2)}, u32[]{:S(2)}) collective-permute-start(bf16[128,1024]{1,0:T(8,128)(2,1)} %get-tuple-element.165), channel_id=1, source_target_pairs={{0,1},{1,0},{2,3},{3,2},{4,5},{5,4},{6,7},{7,6},{8,9},{9,8},{10,11... | collective-permute-start | bytes 786440 | tf_op jit(solution)/shard_map/ppermute | solution.py:344
  130.8 6.6 %collective-permute-start.25 = (bf16[128,1024]{1,0:T(8,128)(2,1)}, bf16[128,1024]{1,0:T(8,128)(2,1)S(1)}, u32[]{:S(2)}, u32[]{:S(2)}) collective-permute-start(bf16[128,1024]{1,0:T(8,128)(2,1)} %get-tuple-element.169), channel_id=1, source_target_pairs={{0,1},{1,0},{2,3},{3,2},{4,5},{5,4},{6,7},{7,6},{8,9},{9,8},{10,11... | collective-permute-start | bytes 786440 | tf_op jit(solution)/shard_map/ppermute | solution.py:344
  137.5 2.3 %collective-permute-start.30 = (bf16[768,512]{1,0:T(8,128)(2,1)S(1)}, bf16[768,512]{1,0:T(8,128)(2,1)S(1)}, u32[]{:S(2)}, u32[]{:S(2)}) collective-permute-start(bf16[768,512]{1,0:T(8,128)(2,1)S(1)} %get-tuple-element.185), channel_id=1, source_target_pairs={{0,4},{4,0},{8,12},{12,8},{16,20},{20,16},{24,28},{28,24},{1,5},{5... | collective-permute-start | bytes 2359304 | tf_op jit(solution)/shard_map/ppermute | solution.py:344
  137.5 31.2 %collective-permute-start.28 = (bf16[256,1024]{1,0:T(8,128)(2,1)S(1)}, bf16[256,1024]{1,0:T(8,128)(2,1)S(1)}, u32[]{:S(2)}, u32[]{:S(2)}) collective-permute-start(bf16[256,1024]{1,0:T(8,128)(2,1)S(1)} %slice.128), channel_id=1, source_target_pairs={{0,8},{4,12},{8,0},{12,4},{16,24},{20,28},{24,16},{28,20},{1,9},{5... | collective-permute-start | bytes 1572872 | tf_op jit(solution)/shard_map/ppermute | solution.py:344
  140.1 20.3 %collective-permute-start.31 = (bf16[384,512]{1,0:T(8,128)(2,1)S(1)}, bf16[384,512]{1,0:T(8,128)(2,1)S(1)}, u32[]{:S(2)}, u32[]{:S(2)}) collective-permute-start(bf16[384,512]{1,0:T(8,128)(2,1)S(1)} %get-tuple-element.209), channel_id=1, source_target_pairs={{0,8},{4,12},{8,0},{12,4},{16,24},{20,28},{24,16},{28,20},{1,9},{5... | collective-permute-start | bytes 1179656 | tf_op jit(solution)/shard_map/ppermute | solution.py:344
  141.1 21.5 %collective-permute-start.32 = (bf16[384,512]{1,0:T(8,128)(2,1)S(1)}, bf16[384,512]{1,0:T(8,128)(2,1)S(1)}, u32[]{:S(2)}, u32[]{:S(2)}) collective-permute-start(bf16[384,512]{1,0:T(8,128)(2,1)S(1)} %get-tuple-element.210), channel_id=1, source_target_pairs={{0,16},{4,20},{8,24},{12,28},{16,0},{20,4},{24,8},{28,12},{1,17},{... | collective-permute-start | bytes 1179656 | tf_op jit(solution)/shard_map/ppermute | solution.py:344
  143.4 25.8 %collective-permute-start.27 = (bf16[256,1024]{1,0:T(8,128)(2,1)S(1)}, bf16[256,1024]{1,0:T(8,128)(2,1)S(1)}, u32[]{:S(2)}, u32[]{:S(2)}) collective-permute-start(bf16[256,1024]{1,0:T(8,128)(2,1)S(1)} %add_convert_fusion.1), channel_id=1, source_target_pairs={{0,2},{1,3},{2,0},{3,1},{4,6},{5,7},{6,4},{7,5},{8,10},{9,11},{10,... | collective-permute-start | bytes 1572872 | tf_op jit(solution)/shard_map/ppermute | solution.py:344
  146.0 23.9 %collective-permute-start.26 = (bf16[256,1024]{1,0:T(8,128)(2,1)S(1)}, bf16[256,1024]{1,0:T(8,128)(2,1)S(1)}, u32[]{:S(2)}, u32[]{:S(2)}) collective-permute-start(bf16[256,1024]{1,0:T(8,128)(2,1)S(1)} %copy-done.50), channel_id=1, source_target_pairs={{0,1},{1,0},{2,3},{3,2},{4,5},{5,4},{6,7},{7,6},{8,9},{9,8},{10,11... | collective-permute-start | bytes 1572872 | tf_op jit(solution)/shard_map/ppermute | solution.py:344
  160.4 8.3 %collective-permute-start.29 = (bf16[128,1024]{1,0:T(8,128)(2,1)S(1)}, bf16[128,1024]{1,0:T(8,128)(2,1)S(1)}, u32[]{:S(2)}, u32[]{:S(2)}) collective-permute-start(bf16[128,1024]{1,0:T(8,128)(2,1)S(1)} %slice.129), channel_id=1, source_target_pairs={{0,16},{4,20},{8,24},{12,28},{16,0},{20,4},{24,8},{28,12},{1,17},{... | collective-permute-start | bytes 786440 | tf_op jit(solution)/shard_map/ppermute | solution.py:344
  170.4 9.9 %collective-permute-start.38 = (bf16[384,512]{1,0:T(8,128)(2,1)S(1)}, bf16[384,512]{1,0:T(8,128)(2,1)S(1)}, u32[]{:S(2)}, u32[]{:S(2)}) collective-permute-start(bf16[384,512]{1,0:T(8,128)(2,1)S(1)} %get-tuple-element.205), channel_id=1, source_target_pairs={{0,16},{4,20},{8,24},{12,28},{16,0},{20,4},{24,8},{28,12},{1,17},{... | collective-permute-start | bytes 1179656 | tf_op jit(solution)/shard_map/ppermute | solution.py:344
  171.3 9.6 %collective-permute-start.39 = (bf16[384,512]{1,0:T(8,128)(2,1)S(1)}, bf16[384,512]{1,0:T(8,128)(2,1)S(1)}, u32[]{:S(2)}, u32[]{:S(2)}) collective-permute-start(bf16[384,512]{1,0:T(8,128)(2,1)S(1)} %get-tuple-element.206), channel_id=1, source_target_pairs={{0,8},{4,12},{8,0},{12,4},{16,24},{20,28},{24,16},{28,20},{1,9},{5... | collective-permute-start | bytes 1179656 | tf_op jit(solution)/shard_map/ppermute | solution.py:344
  171.8 25.0 %collective-permute-start.33 = (bf16[256,1024]{1,0:T(8,128)(2,1)S(1)}, bf16[256,1024]{1,0:T(8,128)(2,1)}, u32[]{:S(2)}, u32[]{:S(2)}) collective-permute-start(bf16[256,1024]{1,0:T(8,128)(2,1)S(1)} %finish.1), channel_id=1, source_target_pairs={{0,2},{1,3},{2,0},{3,1},{4,6},{5,7},{6,4},{7,5},{8,10},{9,11},{10,... | collective-permute-start | bytes 1572872 | tf_op jit(solution)/shard_map/ppermute | solution.py:344
  174.4 22.4 %collective-permute-start.34 = (bf16[256,1024]{1,0:T(8,128)(2,1)S(1)}, bf16[256,1024]{1,0:T(8,128)(2,1)S(1)}, u32[]{:S(2)}, u32[]{:S(2)}) collective-permute-start(bf16[256,1024]{1,0:T(8,128)(2,1)S(1)} %finish.1), channel_id=1, source_target_pairs={{0,1},{1,0},{2,3},{3,2},{4,5},{5,4},{6,7},{7,6},{8,9},{9,8},{10,11... | collective-permute-start | bytes 1572872 | tf_op jit(solution)/shard_map/ppermute | solution.py:344
  175.4 9.3 %collective-permute-start.35 = (f32[9,1024]{1,0:T(8,128)S(1)}, f32[9,1024]{1,0:T(8,128)S(1)}, u32[]{:S(2)}, u32[]{:S(2)}) collective-permute-start(f32[9,1024]{1,0:T(8,128)S(1)} %copy-done.43), channel_id=1, source_target_pairs={{0,4},{4,0},{8,12},{12,8},{16,20},{20,16},{24,28},{28,24},{1,5},{5... | collective-permute-start | bytes 110600 | tf_op jit(solution)/shard_map/ppermute | solution.py:344
  181.2 12.3 %collective-permute-start.40 = (bf16[768,512]{1,0:T(8,128)(2,1)S(1)}, bf16[768,512]{1,0:T(8,128)(2,1)S(1)}, u32[]{:S(2)}, u32[]{:S(2)}) collective-permute-start(bf16[768,512]{1,0:T(8,128)(2,1)S(1)} %pad_maximum_fusion.4), channel_id=1, source_target_pairs={{0,4},{4,0},{8,12},{12,8},{16,20},{20,16},{24,28},{28,24},{1,5},{5... | collective-permute-start | bytes 2359304 | tf_op jit(solution)/shard_map/ppermute | solution.py:344
  184.7 4.5 %collective-permute-start.36 = (f32[9,1024]{1,0:T(8,128)S(1)}, f32[9,1024]{1,0:T(8,128)S(1)}, u32[]{:S(2)}, u32[]{:S(2)}) collective-permute-start(f32[9,1024]{1,0:T(8,128)S(1)} %add.76), channel_id=1, source_target_pairs={{0,8},{4,12},{8,0},{12,4},{16,24},{20,28},{24,16},{28,20},{1,9},{5... | collective-permute-start | bytes 110600 | tf_op jit(solution)/shard_map/ppermute | solution.py:344
  189.2 4.3 %collective-permute-start.37 = (f32[9,1024]{1,0:T(8,128)S(1)}, f32[9,1024]{1,0:T(8,128)S(1)}, u32[]{:S(2)}, u32[]{:S(2)}) collective-permute-start(f32[9,1024]{1,0:T(8,128)S(1)} %add.77), channel_id=1, source_target_pairs={{0,16},{4,20},{8,24},{12,28},{16,0},{20,4},{24,8},{28,12},{1,17},{... | collective-permute-start | bytes 110600 | tf_op jit(solution)/shard_map/ppermute | solution.py:344
  196.8 5.1 %collective-permute-start.42 = (f32[10,1024]{1,0:T(8,128)S(1)}, f32[10,1024]{1,0:T(8,128)S(1)}, u32[]{:S(2)}, u32[]{:S(2)}) collective-permute-start(f32[10,1024]{1,0:T(8,128)S(1)} %pad_maximum_fusion.8), channel_id=1, source_target_pairs={{0,1},{1,0},{2,3},{3,2},{4,5},{5,4},{6,7},{7,6},{8,9},{9,8},{10,11... | collective-permute-start | bytes 122888 | tf_op jit(solution)/shard_map/ppermute | solution.py:344
  197.9 14.8 %collective-permute-start.41 = (bf16[256,1024]{1,0:T(8,128)(2,1)}, bf16[256,1024]{1,0:T(8,128)(2,1)}, u32[]{:S(2)}, u32[]{:S(2)}) collective-permute-start(bf16[256,1024]{1,0:T(8,128)(2,1)} %collective-permute-done.33), channel_id=1, source_target_pairs={{0,1},{1,0},{2,3},{3,2},{4,5},{5,4},{6,7},{7,6},{8,9},{9,8},{10,11... | collective-permute-start | bytes 1572872 | tf_op jit(solution)/shard_map/ppermute | solution.py:344
  201.9 9.4 %collective-permute-start.43 = (f32[10,1024]{1,0:T(8,128)S(1)}, f32[10,1024]{1,0:T(8,128)S(1)}, u32[]{:S(2)}, u32[]{:S(2)}) collective-permute-start(f32[10,1024]{1,0:T(8,128)S(1)} %add.84), channel_id=1, source_target_pairs={{0,2},{1,3},{2,0},{3,1},{4,6},{5,7},{6,4},{7,5},{8,10},{9,11},{10,... | collective-permute-start | bytes 122888 | tf_op jit(solution)/shard_map/ppermute | solution.py:344
  (48 other events, 356.6 us)

commit v6 on v5

--- a/solution.py
+++ b/solution.py
@@ -517,32 +517,34 @@
         part[...] = total[pl.ds(row, span), :].astype(part.dtype)
 
 
-def middle_kernel(tensor_count, *refs):
-    place, gain, router, routes, layer_in, out_grad = refs[:6]
-    w_mine, w_other, heads, refs = refs[6], refs[7], refs[8], refs[9:]
-    w_ins, w_outs, refs = refs[:4], refs[4:8], refs[8:]
-    parts, refs = refs[:tensor_count], refs[tensor_count:]
-    (residual_block, inverse_block, normed, active_out, pre_out, gain_part, router_part) = refs[:7]
-    (residual, inverse, gates, gate_grad, hidden, plain, total) = refs[7:]
+def branch_kernel(
+    place,
+    gain,
+    router,
+    routes,
+    layer_in,
+    w_mine,
+    w_other,
+    heads,
+    residual,
+    inverse,
+    normed,
+    gates,
+    w_output,
+):
     token_count, model_width = layer_in.shape
-    experts_all = router_part.shape[0]
-    units = w_outs[0].shape[0] // 2
-    span = token_count // tensor_count
-    lane = lane_index((ROWS, LANES))
-    half = w_mine.shape[0] // tensor_count
-    core = place[1] & 1
-    mine_lanes = pl.ds(pl.multiple_of(core * half, half), half)
-    other_lanes = pl.ds(pl.multiple_of((1 - core) * half, half), half)
+    half = LANES
+    mine = (place[1] & 1) * half
+    for row in range(0, model_width, 2 * half):
+        rows = pl.ds(row // 2, half)
+        w_output[pl.ds(pl.multiple_of(row + mine, half), half), :] = w_mine[rows, :]
+        w_output[pl.ds(pl.multiple_of(row + half - mine, half), half), :] = w_other[rows, :]
 
     def branch_step(number, carry):
         columns = pl.ds(pl.multiple_of(number * 2 * LANES, 2 * LANES), 2 * LANES)
-        summed = layer_in[:, columns].astype(jnp.float32)
-        for number in range(tensor_count):
-            head_rows = pl.ds(number * token_count, token_count)
-            half_rows = pl.ds(number * half, half)
-            summed = summed + dot_plain(heads[head_rows, mine_lanes], w_mine[half_rows, columns])
-            summed = summed + dot_plain(heads[head_rows, other_lanes], w_other[half_rows, columns])
-        residual[:, columns] = summed
+        residual[:, columns] = layer_in[:, columns].astype(jnp.float32) + dot_plain(
+            heads[...], w_output[:, columns]
+        )
         return carry
 
     lax.fori_loop(0, model_width // (2 * LANES), branch_step, 0)
@@ -553,6 +555,7 @@
         inverse[rows, :] = scale
         normed[rows, :] = (values * scale * gain[...]).astype(jnp.bfloat16)
     gates[...] = dot_transposed(normed[...], router[...])
+    lane = lane_index((ROWS, LANES))
     for row in range(0, token_count, ROWS):
         rows = pl.ds(row, ROWS)
         picked = routes[rows, 0:1] == lane
@@ -561,25 +564,43 @@
         logits = jnp.where(picked, gates[rows, :], masked_out)
         weight = jnp.where(picked, jnp.exp(logits - jnp.max(logits, -1, keepdims=True)), 0.0)
         gates[rows, :] = weight / jnp.sum(weight, -1, keepdims=True)
-    gate_grad[...] = jnp.zeros_like(gate_grad)
+
+
+def middle_kernel(tensor_count, *refs):
+    place, router, out_grad, residual, inverse, normed, gates = refs[:7]
+    w_ins, w_outs, refs = refs[7:11], refs[11:15], refs[15:]
+    parts, refs = refs[:tensor_count], refs[tensor_count:]
+    (residual_block, inverse_block, active_out, pre_out, gain_part, router_part) = refs[:6]
+    (gate_wide, product, hidden, plain, total) = refs[6:]
+    token_count, model_width = normed.shape
+    experts_all = router_part.shape[0]
+    units = w_outs[0].shape[0] // 2
+    span = token_count // tensor_count
+    for pair, weights in enumerate(w_outs):
+        plain[:, 2 * pair * units : 2 * (pair + 1) * units] = dot_transposed(
+            out_grad[...], weights[...]
+        )
+    gates_high = gates[...].astype(jnp.bfloat16)
+    gates_low = (gates[...] - gates_high.astype(jnp.float32)).astype(jnp.bfloat16)
+    total_grad = jnp.zeros((token_count, LANES), jnp.float32)
     for number in range(experts_all):
         name = place[1] ^ IN_ORDER[number]
         in_rows = pl.ds(number % 2 * 2 * units, 2 * units)
         out_number = OUT_ORDER.index(IN_ORDER[number])
-        out_rows = pl.ds(out_number % 2 * units, units)
         hidden[...] = dot_transposed(normed[...], w_ins[number // 2][in_rows, :])
-        plain[...] = dot_transposed(out_grad[...], w_outs[out_number // 2][out_rows, :])
+        out_lanes = pl.ds(out_number * units, units)
+        chosen = lax.broadcasted_iota(jnp.int32, (LANES, units), 0) == name
+        chosen = jnp.where(chosen, 1.0, 0.0).astype(jnp.bfloat16)
+        gate_wide[...] = dot_plain(gates_high, chosen) + dot_plain(gates_low, chosen)
         for row in range(0, token_count, ROWS):
             rows = pl.ds(row, ROWS)
-            gate = jnp.sum(jnp.where(lane == name, gates[rows, :], 0.0), -1, keepdims=True)
+            gate = gate_wide[rows, :]
             gate_vals, up_vals = hidden[rows, :units], hidden[rows, units:]
             sig_vals = 0.5 + 0.5 * jnp.tanh(0.5 * gate_vals)
             silu_vals = gate_vals * sig_vals
             active = silu_vals * up_vals
-            grad = plain[rows, :]
-            gate_grad[rows, :] = gate_grad[rows, :] + jnp.where(
-                lane == name, jnp.sum(active * grad, -1, keepdims=True), 0.0
-            )
+            grad = plain[rows, out_lanes]
+            product[rows, :] = (active * grad).astype(jnp.bfloat16)
             active_grad = grad * gate
             active_out[rows, out_number * units : (out_number + 1) * units] = (
                 active * gate
@@ -590,7 +611,8 @@
             pre_out[rows, (2 * number + 1) * units : (2 * number + 2) * units] = (
                 active_grad * silu_vals
             ).astype(jnp.bfloat16)
-    gate_all, grad_all = gates[...], gate_grad[...]
+        total_grad = total_grad + dot_transposed(product[...], chosen)
+    gate_all, grad_all = gates[...], total_grad
     logit_part = (
         gate_all * (grad_all - jnp.sum(gate_all * grad_all, -1, keepdims=True))
     ).astype(jnp.bfloat16)
@@ -669,14 +691,23 @@
     branch_grad, projected_grad, heads_grad, pair_grad, total = refs[:5]
     near_refs, sems = refs[5:12], refs[12]
     w_output, queries, pairs, probs, cosine, sine, w_qkv = near_refs
-    copies = [
-        pltpu.make_async_copy(source, target, sems.at[number])
-        for number, (source, target) in enumerate(zip(far_refs, near_refs))
-    ]
+    copies, prob_copies = [], []
+    for number, (source, target) in enumerate(zip(far_refs, near_refs)):
+        if target is probs:
+            for block in range(probs.shape[1]):
+                part = (slice(None), block, slice(None), slice((block + 1) * ROWS))
+                prob_copies.append(
+                    pltpu.make_async_copy(
+                        source.at[part], target.at[part], sems.at[len(near_refs) + block]
+                    )
+                )
+        else:
+            copies.append(pltpu.make_async_copy(source, target, sems.at[number]))
+    more = len(near_refs) + len(prob_copies)
     token_count, model_width = branch_grad.shape
     span = token_count // tensor_count
     mixture_copies = [
-        pltpu.make_async_copy(mixture, part.at[pl.ds(span, span)], sems.at[len(copies) + number])
+        pltpu.make_async_copy(mixture, part.at[pl.ds(span, span)], sems.at[more + number])
         for number, (mixture, part) in enumerate(zip(mixtures, parts[:-1]))
     ]
     block_copies = []
@@ -686,15 +717,15 @@
             pltpu.make_async_copy(
                 block,
                 branch_grad.at[pl.ds(row, span)],
-                sems.at[len(copies) + tensor_count + number],
+                sems.at[more + tensor_count + number],
             )
         )
-    for copy in block_copies + copies + mixture_copies:
+    for copy in block_copies + copies[:5] + prob_copies + copies[5:] + mixture_copies:
         copy.start()
     for copy in copies[:1] + block_copies:
         copy.wait()
     heads_grad[...] = dot_transposed(branch_grad[...], w_output[...])
-    for copy in copies[1:6]:
+    for copy in copies[1:5]:
         copy.wait()
     is_first = first_head((ROWS, LANES))
     for kv in range(pairs.shape[0]):
@@ -709,6 +740,8 @@
                     jnp.where(is_first, 0.0, upper),
                 ]
             ).astype(jnp.bfloat16)
+            if kv == 0:
+                prob_copies[block].wait()
             share_low = probs[kv, block, :, :keys]
             share = share_low.astype(jnp.float32)
             prob_grad = dot_transposed(upper, pairs[kv, :keys, :])
@@ -733,7 +766,7 @@
                 is_first, grad * cosine[rows, :] - turn(grad) * sine[rows, :], grad
             ).astype(jnp.bfloat16)
 
-    for copy in copies[6:]:
+    for copy in copies[5:]:
         copy.wait()
 
     def column_step(number, carry):
@@ -889,13 +922,11 @@
     heads_far = exchange(attended, "tensor", 2)
     heads_near = exchange(attended, "tensor", 1)
     output_both = exchange(output_far, "tensor", 1)
-    heads_far, heads_near, w_in_near, w_out_near = lax.optimization_barrier(
-        (heads_far, heads_near, w_in_near, w_out_near)
+    heads_far, heads_near, w_in_near, w_out_near, output_both = lax.optimization_barrier(
+        (heads_far, heads_near, w_in_near, w_out_near, output_both)
     )
     heads_both = exchange(heads_far, "tensor", 1)
-    heads_both, output_both, w_in_far, w_out_far = lax.optimization_barrier(
-        (heads_both, output_both, w_in_far, w_out_far)
-    )
+    heads_both, w_in_far, w_out_far = lax.optimization_barrier((heads_both, w_in_far, w_out_far))
     w_in_all = gather_pairs(w_in_near, w_in_far)
     w_out_all = gather_pairs(w_out_near, w_out_far)
     heads_all = [attended, heads_near, heads_far, heads_both]
@@ -905,46 +936,64 @@
     part_shapes = (shaped((span, model_width), wide),) + (
         shaped((span, model_width), low),
     ) * (tensor_count - 1)
+    residual_all, inverse_all, normed_two, gates = pl.pallas_call(
+        branch_kernel,
+        out_shape=(
+            shaped((token_count, model_width), wide),
+            shaped((token_count, 1), wide),
+            shaped((token_count, model_width), low),
+            shaped((token_count, LANES), wide),
+        ),
+        in_specs=in_smem(1) + in_vmem(7),
+        out_specs=tuple(in_vmem(4)),
+        scratch_shapes=[pltpu.VMEM((model_width, model_width), low)],
+        compiler_params=pltpu.CompilerParams(vmem_limit_bytes=12 * mib),
+        name="branch",
+    )(
+        place,
+        gain_ffn[None],
+        router_rows,
+        routes,
+        layer_in,
+        output_mine,
+        output_other,
+        jnp.concatenate(heads_all, 1),
+    )
     middle = pl.pallas_call(
         functools.partial(middle_kernel, tensor_count),
         out_shape=part_shapes
         + (
             shaped((span, model_width), wide),
             shaped((span, 1), wide),
-            shaped((token_count, model_width), low),
             shaped((token_count, experts_all * units), low),
             shaped((token_count, experts_all * 2 * units), low),
             shaped((1, model_width), wide),
             shaped((experts_all, model_width), wide),
         ),
-        in_specs=in_smem(1) + in_vmem(16),
-        out_specs=tuple(in_vmem(tensor_count + 7)),
+        in_specs=in_smem(1) + in_vmem(14),
+        out_specs=tuple(in_vmem(tensor_count + 6)),
         scratch_shapes=[
-            pltpu.VMEM((token_count, model_width), wide),
-            pltpu.VMEM((token_count, 1), wide),
-            pltpu.VMEM((token_count, LANES), wide),
-            pltpu.VMEM((token_count, LANES), wide),
+            pltpu.VMEM((token_count, units), wide),
+            pltpu.VMEM((token_count, units), low),
             pltpu.VMEM((token_count, 2 * units), wide),
-            pltpu.VMEM((token_count, units), wide),
+            pltpu.VMEM((token_count, experts_all * units), wide),
             pltpu.VMEM((token_count, model_width), wide),
         ],
-        compiler_params=pltpu.CompilerParams(vmem_limit_bytes=20 * mib),
+        compiler_params=pltpu.CompilerParams(vmem_limit_bytes=24 * mib),
         name="middle",
     )(
         place,
-        gain_ffn[None],
         router_rows,
-        routes,
-        layer_in,
         out_grad,
-        output_mine,
-        output_other,
-        jnp.concatenate(heads_all),
+        residual_all,
+        inverse_all,
+        normed_two,
+        gates,
         *w_in_all,
         *w_out_all,
     )
     normed_parts, middle = middle[:tensor_count], middle[tensor_count:]
-    residual, inverse_two, normed_two, active, pre_grad, gain_ffn_part, router_part = middle
+    residual, inverse_two, active, pre_grad, gain_ffn_part, router_part = middle
 
     relayed = exchange(normed_parts[3], "tensor", 1)
     half_grads = shaped((experts_all // 2 * 3 * units, model_width), low)
@@ -1017,7 +1066,7 @@
             pltpu.VMEM((token_count, model_width), wide),
         ]
         + [pltpu.VMEM(each.shape, each.dtype) for each in fetched]
-        + [pltpu.SemaphoreType.DMA((len(fetched) + 2 * tensor_count,))],
+        + [pltpu.SemaphoreType.DMA((len(fetched) + block_count + 2 * tensor_count,))],
         compiler_params=pltpu.CompilerParams(vmem_limit_bytes=58 * mib),
         name="attend_back",
     )(

time: 216 us -> 215 us (level)
    pallas_call x0 -> x1, Pallas kernels: none -> 4.2 us  [on_device(): pl.pallas_call(branch_kernel, out_shape=(shaped((token_count, model_width...]
    pallas_call x1, Pallas kernels: 16.4 us -> 12.4 us  [on_device(): pl.pallas_call(functools.partial(middle_kernel, tensor_count), out_shape=...]
    unnamed x104 -> x106, local copies, waits for them, and re-layouts: 9.46 us -> 11 us
  transfers between devices with their start and end apart: 44 -> 44, of which waited for: 26 -> 22; matrix products, arithmetic and copies ran while one was open for 11% -> 10% of each run, Pallas kernels for 15% -> 17%
where the time goes in v6:
time: 215 us; the launch traced here: 214 us
  waiting for transfers between devices  85.3 us (40%)
  Pallas kernels  49.2 us (23%)
  starting transfers between devices  44.6 us (21%)
  local copies, waits for them, and re-layouts  19.2 us (9%)
  other arithmetic  14.5 us (7%)
    ppermute x44, waiting for transfers between devices, exchange(): lax.ppermute(array_in, axis_name, [(i, i ^ bits) for i in range(count)])  85.3 us
    ppermute x44, starting transfers between devices, exchange(): lax.ppermute(array_in, axis_name, [(i, i ^ bits) for i in range(count)])  44.6 us
    pallas_call x1, Pallas kernels, on_device(): pl.pallas_call(functools.partial(middle_kernel, tensor_count), out_shape=...  12.4 us
    pallas_call x1, Pallas kernels, on_device(): pl.pallas_call(functools.partial(attend_back_kernel, tensor_count), out_s...  11.2 us
    unnamed x106, local copies, waits for them, and re-layouts  11 us
    pallas_call x1, Pallas kernels, on_device(): pl.pallas_call(attend_kernel, out_shape=kept + (shaped((token_count, head...  7.61 us
    pallas_call x1, Pallas kernels, on_device(): pl.pallas_call(functools.partial(weight_grad_kernel, tensor_count), out_s...  7.4 us
  transfers between devices with their start and end apart: 44, of which 22 were waited for; matrix products, arithmetic and copies ran while one was open for 10% of the time, Pallas kernels for 17%

profile of v6, /device:TPU:0, one launch (start us, length us, event | category | flops | bytes accessed | tf_op | source)
XLA Modules:
  0.0 214.3 jit_solution(18059653468654309868)
XLA Ops:
  0.6 3.0 %collective-permute-start = (bf16[256,1024]{1,0:T(8,128)(2,1)}, bf16[256,1024]{1,0:T(8,128)(2,1)S(1)}, u32[]{:S(2)}, u32[]{:S(2)}) collective-permute-start(bf16[256,1024]{1,0:T(8,128)(2,1)} %bitcast.34), channel_id=1, source_target_pairs={{0,8},{4,12},{8,0},{12,4},{16,24},{20,28},{24,16},{28,20},{1,9},{5... | collective-permute-start | bytes 1572872 | tf_op jit(solution)/shard_map/ppermute | solution.py:344
  4.7 2.7 %collective-permute-start.2 = (bf16[128,1024]{1,0:T(8,128)(2,1)S(1)}, bf16[128,1024]{1,0:T(8,128)(2,1)S(1)}, u32[]{:S(2)}, u32[]{:S(2)}) collective-permute-start(bf16[128,1024]{1,0:T(8,128)(2,1)S(1)} %slice_select_fusion), channel_id=1, source_target_pairs={{0,2},{1,3},{2,0},{3,1},{4,6},{5,7},{6,4},{7,5},{8,10},{9,11},{10,... | collective-permute-start | bytes 786440 | tf_op jit(solution)/shard_map/ppermute | solution.py:344
  7.4 1.6 collective-permute-start.3
  8.9 1.5 collective-permute-start.1
  10.5 2.5 %copy.25 = bf16[128,8,2,256]{3,1,2,0:T(8,128)(2,1)} copy(bf16[128,8,2,256]{3,2,1,0:T(2,128)(2,1)} %bitcast.31) | data formatting | bytes 2097152
  12.9 7.6 %attend.1 = (bf16[2,4,256,128]{3,2,1,0:T(8,128)(2,1)}, bf16[2,512,128]{2,1,0:T(8,128)(2,1)}, bf16[2,4,256,512]{3,2,1,0:T(8,128)(2,1)}, bf16[512,256]{1,0:T(8,128)(2,1)}) custom-call(s32[1,3]{1,0:T(1,128)} %lengths.1, bf16[512,1024]{1,0:T(8,128)(2,1)} %layer_in.5, f32[1,1024]{1,0:T(1,128)} %bitcast.22, bf16[1024,512]{1,0:T(8,128)(2,1)} %bitcast.27, ...), custom_call_target="tpu_custom_call" | custom-call | tf_op jit(solution)/shard_map/attend/pallas_call | solution.py:903
  22.2 1.1 collective-permute-start.4
  23.3 2.4 %collective-permute-start.5 = (bf16[512,256]{1,0:T(8,128)(2,1)S(1)}, bf16[512,256]{1,0:T(8,128)(2,1)S(1)}, u32[]{:S(2)}, u32[]{:S(2)}) collective-permute-start(bf16[512,256]{1,0:T(8,128)(2,1)S(1)} %copy-done.12), channel_id=1, source_target_pairs={{0,1},{1,0},{2,3},{3,2},{4,5},{5,4},{6,7},{7,6},{8,9},{9,8},{10,11... | collective-permute-start | bytes 786440 | tf_op jit(solution)/shard_map/ppermute | solution.py:344
  26.4 9.0 %collective-permute-done.4 = bf16[512,256]{1,0:T(8,128)(2,1)S(1)} collective-permute-done((bf16[512,256]{1,0:T(8,128)(2,1)S(1)}, bf16[512,256]{1,0:T(8,128)(2,1)S(1)}, u32[]{:S(2)}, u32[]{:S(2)}) %collective-permute-start.4) | collective-permute-done | bytes 262176 | tf_op jit(solution)/shard_map/ppermute | solution.py:344
  35.4 1.3 collective-permute-done.5
  36.8 4.4 %collective-permute-done.6 = bf16[128,1024]{1,0:T(8,128)(2,1)S(1)} collective-permute-done((bf16[128,1024]{1,0:T(8,128)(2,1)S(1)}, bf16[128,1024]{1,0:T(8,128)(2,1)S(1)}, u32[]{:S(2)}, u32[]{:S(2)}) %collective-permute-start.6) | collective-permute-done | bytes 262176 | tf_op jit(solution)/shard_map/ppermute | solution.py:344
  41.8 6.5 %collective-permute-done.8 = bf16[512,256]{1,0:T(8,128)(2,1)S(1)} collective-permute-done((bf16[512,256]{1,0:T(8,128)(2,1)S(1)}, bf16[512,256]{1,0:T(8,128)(2,1)S(1)}, u32[]{:S(2)}, u32[]{:S(2)}) %collective-permute-start.8) | collective-permute-done | bytes 262176 | tf_op jit(solution)/shard_map/ppermute | solution.py:344
  49.3 1.3 pad_maximum_fusion.2.heads
  50.7 1.2 copy-done.3
  51.9 4.2 %branch.1 = (f32[512,1024]{1,0:T(8,128)S(1)}, f32[512,1]{1,0:T(8,128)S(1)}, bf16[512,1024]{1,0:T(8,128)(2,1)S(1)}, f32[512,128]{1,0:T(8,128)S(1)}) custom-call(s32[2]{0:T(128)S(1)} %pad_add_fusion.place.refs_0_, f32[1,1024]{1,0:T(1,128)S(1)} %bitcast.25, bf16[128,1024]{1,0:T(8,128)(2,1)S(1)} %pad.4.router.refs_1_, s32[512,2]{1,0:T(8,128)S(1)} %copy.22.routes, ...), custom_call_target="tpu_custom_call" | custom-call | tf_op jit(solution)/shard_map/branch/pallas_call | solution.py:939
  57.2 12.4 %middle.1 = (f32[128,1024]{1,0:T(8,128)S(1)}, bf16[128,1024]{1,0:T(8,128)(2,1)}, bf16[128,1024]{1,0:T(8,128)(2,1)S(1)}, bf16[128,1024]{1,0:T(8,128)(2,1)S(1)}, f...) custom-call(s32[2]{0:T(128)S(1)} %pad_add_fusion.place.refs_0_, ...), custom_call_target="tpu_custom_call" | custom-call | tf_op jit(solution)/shard_map/middle/pallas_call | solution.py:962
  69.9 7.4 %weight_grad.1 = (f32[128,1024]{1,0:T(8,128)S(1)}, bf16[128,1024]{1,0:T(8,128)(2,1)S(1)}, bf16[128,1024]{1,0:T(8,128)(2,1)S(1)}, bf16[128,1024]{1,0:T(8,128)(2,1...) custom-call(s32[2]{0:T(128)S(1)} %pad_add_fusion.place.refs_0_, ...), custom_call_target="tpu_custom_call" | custom-call | tf_op jit(solution)/shard_map/weight_grad/pallas_call | solution.py:1000
  79.2 2.7 %collective-permute-start.17 = (bf16[128,1024]{1,0:T(8,128)(2,1)}, bf16[128,1024]{1,0:T(8,128)(2,1)S(1)}, u32[]{:S(2)}, u32[]{:S(2)}) collective-permute-start(bf16[128,1024]{1,0:T(8,128)(2,1)} %add_convert_fusion.6), channel_id=1, source_target_pairs={{0,2},{1,3},{2,0},{3,1},{4,6},{5,7},{6,4},{7,5},{8,10},{9,11},{10,... | collective-permute-start | bytes 786440 | tf_op jit(solution)/shard_map/ppermute | solution.py:344
  82.5 1.4 collective-permute-done.18.given
  84.0 1.6 add_grads.1
  85.5 1.3 copy-done.4
  88.6 1.5 collective-permute-start.22
  90.2 4.5 %collective-permute-done.17.far = bf16[128,1024]{1,0:T(8,128)(2,1)S(1)} collective-permute-done((bf16[128,1024]{1,0:T(8,128)(2,1)}, bf16[128,1024]{1,0:T(8,128)(2,1)S(1)}, u32[]{:S(2)}, u32[]{:S(2)}) %collective-permute-start.17) | collective-permute-done | bytes 262176 | tf_op jit(solution)/shard_map/ppermute | solution.py:344
  95.1 1.2 norm_back.1
  97.4 1.6 collective-permute-start.20
  99.1 11.1 %collective-permute-done.19.refs_10_ = bf16[128,1024]{1,0:T(8,128)(2,1)S(1)} collective-permute-done((bf16[128,1024]{1,0:T(8,128)(2,1)S(1)}, bf16[128,1024]{1,0:T(8,128)(2,1)S(1)}, u32[]{:S(2)}, u32[]{:S(2)}) %collective-permute-start.19) | collective-permute-done | bytes 262176 | tf_op jit(solution)/shard_map/ppermute | solution.py:344
  111.3 5.9 %collective-permute-done.21.refs_11_ = bf16[128,1024]{1,0:T(8,128)(2,1)S(1)} collective-permute-done((bf16[128,1024]{1,0:T(8,128)(2,1)S(1)}, bf16[128,1024]{1,0:T(8,128)(2,1)S(1)}, u32[]{:S(2)}, u32[]{:S(2)}) %collective-permute-start.21) | collective-permute-done | bytes 262176 | tf_op jit(solution)/shard_map/ppermute | solution.py:344
  118.0 11.2 %attend_back.1 = (f32[256,1024]{1,0:T(8,128)}, bf16[256,1024]{1,0:T(8,128)(2,1)}, bf16[256,1024]{1,0:T(8,128)(2,1)}, bf16[128,1024]{1,0:T(8,128)(2,1)}, bf16[512...) custom-call(s32[2]{0:T(128)} %copy-done.23, bf16[256,1024]{1,0:T(8,128)(2,1)} %refs_1_.1, ...), custom_call_target="tpu_custom_call" | custom-call | tf_op jit(solution)/shard_map/attend_back/pallas_call | solution.py:1052
  129.3 1.3 collective-permute-start.25
  130.6 1.5 convert_add_fusion
  132.2 3.2 %attend_grad.1 = (f32[768,512]{1,0:T(8,128)S(1)}, bf16[768,512]{1,0:T(8,128)(2,1)S(1)}) custom-call(s32[2]{0:T(128)S(1)} %copy-done.24, bf16[512,1024]{1,0:T(8,128)(2,1)S(1)} %copy-done, f32[1,1024]{1,0:T(1,128)S(1)} %bitcast.23, bf16[512,512]{1,0:T(8,128)(2,1)S(1)} %copy-done.15, bf16[512,256]{1,0:T(8,128)(2,1)S(1)} %copy-done.13, ...), custom_call_target="tpu_custom_call" | custom-call | tf_op jit(solution)/shard_map/attend_grad/pallas_call | solution.py:1094
  139.5 3.4 %collective-permute-start.32 = (bf16[384,512]{1,0:T(8,128)(2,1)S(1)}, bf16[384,512]{1,0:T(8,128)(2,1)S(1)}, u32[]{:S(2)}, u32[]{:S(2)}) collective-permute-start(bf16[384,512]{1,0:T(8,128)(2,1)S(1)} %get-tuple-element.216), channel_id=1, source_target_pairs={{0,16},{4,20},{8,24},{12,28},{16,0},{20,4},{24,8},{28,12},{1,17},{... | collective-permute-start | bytes 1179656 | tf_op jit(solution)/shard_map/ppermute | solution.py:344
  145.2 13.7 %collective-permute-done.31 = bf16[384,512]{1,0:T(8,128)(2,1)S(1)} collective-permute-done((bf16[384,512]{1,0:T(8,128)(2,1)S(1)}, bf16[384,512]{1,0:T(8,128)(2,1)S(1)}, u32[]{:S(2)}, u32[]{:S(2)}) %collective-permute-start.31) | collective-permute-done | bytes 393248 | tf_op jit(solution)/shard_map/ppermute | solution.py:344
  158.8 3.4 %collective-permute-start.29 = (bf16[128,1024]{1,0:T(8,128)(2,1)S(1)}, bf16[128,1024]{1,0:T(8,128)(2,1)S(1)}, u32[]{:S(2)}, u32[]{:S(2)}) collective-permute-start(bf16[128,1024]{1,0:T(8,128)(2,1)S(1)} %slice.129), channel_id=1, source_target_pairs={{0,16},{4,20},{8,24},{12,28},{16,0},{20,4},{24,8},{28,12},{1,17},{... | collective-permute-start | bytes 786440 | tf_op jit(solution)/shard_map/ppermute | solution.py:344
  162.5 5.9 %collective-permute-done.29 = bf16[128,1024]{1,0:T(8,128)(2,1)S(1)} collective-permute-done((bf16[128,1024]{1,0:T(8,128)(2,1)S(1)}, bf16[128,1024]{1,0:T(8,128)(2,1)S(1)}, u32[]{:S(2)}, u32[]{:S(2)}) %collective-permute-start.29) | collective-permute-done | bytes 262176 | tf_op jit(solution)/shard_map/ppermute | solution.py:344
  169.4 1.7 collective-permute-start.38
  172.2 1.6 collective-permute-start.34
  173.8 6.2 %collective-permute-done.38 = bf16[384,512]{1,0:T(8,128)(2,1)S(1)} collective-permute-done((bf16[384,512]{1,0:T(8,128)(2,1)S(1)}, bf16[384,512]{1,0:T(8,128)(2,1)S(1)}, u32[]{:S(2)}, u32[]{:S(2)}) %collective-permute-start.38) | collective-permute-done | bytes 393248 | tf_op jit(solution)/shard_map/ppermute | solution.py:344
  181.0 2.5 %convert_add_fusion.1 = f32[256,1024]{1,0:T(8,128)} fusion(bf16[256,1024]{1,0:T(8,128)(2,1)S(1)} %copy-done.36, f32[512,1024]{1,0:T(8,128)} %copy-done.30), kind=kLoop, calls=%fused_computation.8 | loop fusion | flops 524288 | bytes 2621440 | tf_op jit(solution)/shard_map/add | solution.py:1115
  185.2 3.7 %collective-permute-done.36 = f32[9,1024]{1,0:T(8,128)S(1)} collective-permute-done((f32[9,1024]{1,0:T(8,128)S(1)}, f32[9,1024]{1,0:T(8,128)S(1)}, u32[]{:S(2)}, u32[]{:S(2)}) %collective-permute-start.36) | collective-permute-done | bytes 36896 | tf_op jit(solution)/shard_map/ppermute | solution.py:344
  188.9 1.1 collective-permute-start.37
  190.2 3.0 %collective-permute-done.37 = f32[9,1024]{1,0:T(8,128)S(1)} collective-permute-done((f32[9,1024]{1,0:T(8,128)S(1)}, f32[9,1024]{1,0:T(8,128)S(1)}, u32[]{:S(2)}, u32[]{:S(2)}) %collective-permute-start.37) | collective-permute-done | bytes 36896 | tf_op jit(solution)/shard_map/ppermute | solution.py:344
  194.8 1.7 fusion
  196.5 1.1 collective-permute-start.42
  198.7 2.9 %collective-permute-done.42 = f32[10,1024]{1,0:T(8,128)S(1)} collective-permute-done((f32[10,1024]{1,0:T(8,128)S(1)}, f32[10,1024]{1,0:T(8,128)S(1)}, u32[]{:S(2)}, u32[]{:S(2)}) %collective-permute-start.42) | collective-permute-done | bytes 40992 | tf_op jit(solution)/shard_map/ppermute | solution.py:344
  204.9 2.3 %reshape.44 = f32[1024,2,256]{2,1,0:T(2,128)} reshape(f32[1024,512]{1,0:T(8,128)S(1)} %copy-done.29) | data formatting | bytes 4194304 | tf_op jit(solution)/shard_map/reshape | solution.py:1137
  208.3 2.7 %collective-permute-done.43 = f32[10,1024]{1,0:T(8,128)S(1)} collective-permute-done((f32[10,1024]{1,0:T(8,128)S(1)}, f32[10,1024]{1,0:T(8,128)S(1)}, u32[]{:S(2)}, u32[]{:S(2)}) %collective-permute-start.43) | collective-permute-done | bytes 40992 | tf_op jit(solution)/shard_map/ppermute | solution.py:344
  212.4 1.9 slice_dynamic-update-slice_fusion
  (204 shorter events, 33.7 us)
Async XLA Ops:
  0.6 20.0 %collective-permute-start = (bf16[256,1024]{1,0:T(8,128)(2,1)}, bf16[256,1024]{1,0:T(8,128)(2,1)S(1)}, u32[]{:S(2)}, u32[]{:S(2)}) collective-permute-start(bf16[256,1024]{1,0:T(8,128)(2,1)} %bitcast.34), channel_id=1, source_target_pairs={{0,8},{4,12},{8,0},{12,4},{16,24},{20,28},{24,16},{28,20},{1,9},{5... | collective-permute-start | bytes 1572872 | tf_op jit(solution)/shard_map/ppermute | solution.py:344
  4.7 15.9 %collective-permute-start.2 = (bf16[128,1024]{1,0:T(8,128)(2,1)S(1)}, bf16[128,1024]{1,0:T(8,128)(2,1)S(1)}, u32[]{:S(2)}, u32[]{:S(2)}) collective-permute-start(bf16[128,1024]{1,0:T(8,128)(2,1)S(1)} %slice_select_fusion), channel_id=1, source_target_pairs={{0,2},{1,3},{2,0},{3,1},{4,6},{5,7},{6,4},{7,5},{8,10},{9,11},{10,... | collective-permute-start | bytes 786440 | tf_op jit(solution)/shard_map/ppermute | solution.py:344
  7.4 13.2 %collective-permute-start.3 = (bf16[128,1024]{1,0:T(8,128)(2,1)S(1)}, bf16[128,1024]{1,0:T(8,128)(2,1)S(1)}, u32[]{:S(2)}, u32[]{:S(2)}) collective-permute-start(bf16[128,1024]{1,0:T(8,128)(2,1)S(1)} %slice_select_fusion), channel_id=1, source_target_pairs={{0,1},{1,0},{2,3},{3,2},{4,5},{5,4},{6,7},{7,6},{8,9},{9,8},{10,11... | collective-permute-start | bytes 786440 | tf_op jit(solution)/shard_map/ppermute | solution.py:344
  8.9 11.7 %collective-permute-start.1 = (bf16[128,1024]{1,0:T(8,128)(2,1)}, bf16[128,1024]{1,0:T(8,128)(2,1)S(1)}, u32[]{:S(2)}, u32[]{:S(2)}) collective-permute-start(bf16[128,1024]{1,0:T(8,128)(2,1)} %bitcast.36), channel_id=1, source_target_pairs={{0,16},{4,20},{8,24},{12,28},{16,0},{20,4},{24,8},{28,12},{1,17},{... | collective-permute-start | bytes 786440 | tf_op jit(solution)/shard_map/ppermute | solution.py:344
  21.7 27.3 %copy-start.50 = (s32[512,2]{0,1:T(2,128)S(1)}, s32[512,2]{0,1:T(2,128)}, u32[]{:S(2)}) copy-start(s32[512,2]{0,1:T(2,128)} %param.15) | copy-start | bytes 12292
  21.7 27.5 %copy-start.49 = (bf16[1024,8]{0,1:T(8,128)(2,1)S(1)}, bf16[1024,8]{0,1:T(8,128)(2,1)}, u32[]{:S(2)}) copy-start(bf16[1024,8]{0,1:T(8,128)(2,1)} %param.20) | copy-start | bytes 49156
  21.7 26.6 %collective-permute-start.9 = (bf16[512,1024]{1,0:T(8,128)(2,1)}, bf16[512,1024]{1,0:T(8,128)(2,1)}, u32[]{:S(2)}, u32[]{:S(2)}) collective-permute-start(bf16[512,1024]{1,0:T(8,128)(2,1)} %pad_maximum_fusion.refs_7_), channel_id=1, source_target_pairs={{0,16},{4,20},{8,24},{12,28},{16,0},{20,4},{24,8},{28,12},{1,17},{... | collective-permute-start | bytes 3145736 | tf_op jit(solution)/shard_map/ppermute | solution.py:344
  22.2 13.3 %collective-permute-start.4 = (bf16[512,256]{1,0:T(8,128)(2,1)S(1)}, bf16[512,256]{1,0:T(8,128)(2,1)S(1)}, u32[]{:S(2)}, u32[]{:S(2)}) collective-permute-start(bf16[512,256]{1,0:T(8,128)(2,1)S(1)} %copy-done.12), channel_id=1, source_target_pairs={{0,2},{1,3},{2,0},{3,1},{4,6},{5,7},{6,4},{7,5},{8,10},{9,11},{10,... | collective-permute-start | bytes 786440 | tf_op jit(solution)/shard_map/ppermute | solution.py:344
  23.3 13.5 %collective-permute-start.5 = (bf16[512,256]{1,0:T(8,128)(2,1)S(1)}, bf16[512,256]{1,0:T(8,128)(2,1)S(1)}, u32[]{:S(2)}, u32[]{:S(2)}) collective-permute-start(bf16[512,256]{1,0:T(8,128)(2,1)S(1)} %copy-done.12), channel_id=1, source_target_pairs={{0,1},{1,0},{2,3},{3,2},{4,5},{5,4},{6,7},{7,6},{8,9},{9,8},{10,11... | collective-permute-start | bytes 786440 | tf_op jit(solution)/shard_map/ppermute | solution.py:344
  25.7 15.4 %collective-permute-start.6 = (bf16[128,1024]{1,0:T(8,128)(2,1)S(1)}, bf16[128,1024]{1,0:T(8,128)(2,1)S(1)}, u32[]{:S(2)}, u32[]{:S(2)}) collective-permute-start(bf16[128,1024]{1,0:T(8,128)(2,1)S(1)} %collective-permute-done.2), channel_id=1, source_target_pairs={{0,1},{1,0},{2,3},{3,2},{4,5},{5,4},{6,7},{7,6},{8,9},{9,8},{10,11... | collective-permute-start | bytes 786440 | tf_op jit(solution)/shard_map/ppermute | solution.py:344
  25.8 24.9 %copy-start = (bf16[512,1024]{1,0:T(8,128)(2,1)S(1)}, bf16[512,1024]{1,0:T(8,128)(2,1)}, u32[]{:S(2)}) copy-start(bf16[512,1024]{1,0:T(8,128)(2,1)} %layer_in.5) | copy-start | bytes 3145732
  25.8 24.9 %copy-start.22 = (f32[1024]{0:T(1024)S(1)}, f32[1024]{0:T(1024)}, u32[]{:S(2)}) copy-start(f32[1024]{0:T(1024)} %param.19) | copy-start | bytes 12292
  25.8 22.5 %collective-permute-start.10 = (bf16[256,1024]{1,0:T(8,128)(2,1)S(1)}, bf16[256,1024]{1,0:T(8,128)(2,1)S(1)}, u32[]{:S(2)}, u32[]{:S(2)}) collective-permute-start(bf16[256,1024]{1,0:T(8,128)(2,1)S(1)} %pad_maximum_fusion.5.refs_11_.refs_5_), channel_id=1, source_target_pairs={{0,8},{4,12},{8,0},{12,4},{16,24},{20,28},{24,16},{28,20},{1,9},{5... | collective-permute-start | bytes 1572872 | tf_op jit(solution)/shard_map/ppermute | solution.py:344
  41.1 7.2 %collective-permute-start.8 = (bf16[512,256]{1,0:T(8,128)(2,1)S(1)}, bf16[512,256]{1,0:T(8,128)(2,1)S(1)}, u32[]{:S(2)}, u32[]{:S(2)}) collective-permute-start(bf16[512,256]{1,0:T(8,128)(2,1)S(1)} %collective-permute-done.4), channel_id=1, source_target_pairs={{0,1},{1,0},{2,3},{3,2},{4,5},{5,4},{6,7},{7,6},{8,9},{9,8},{10,11... | collective-permute-start | bytes 786440 | tf_op jit(solution)/shard_map/ppermute | solution.py:344
  41.2 9.4 %collective-permute-start.7 = (bf16[512,1024]{1,0:T(8,128)(2,1)S(1)}, bf16[512,1024]{1,0:T(8,128)(2,1)}, u32[]{:S(2)}, u32[]{:S(2)}) collective-permute-start(bf16[512,1024]{1,0:T(8,128)(2,1)S(1)} %pad_maximum_fusion.1.w_mine), channel_id=1, source_target_pairs={{0,4},{4,0},{8,12},{12,8},{16,20},{20,16},{24,28},{28,24},{1,5},{5... | collective-permute-start | bytes 3145736 | tf_op jit(solution)/shard_map/ppermute | solution.py:344
  41.3 14.8 %collective-permute-start.11 = (bf16[512,1024]{1,0:T(8,128)(2,1)}, bf16[512,1024]{1,0:T(8,128)(2,1)}, u32[]{:S(2)}, u32[]{:S(2)}) collective-permute-start(bf16[512,1024]{1,0:T(8,128)(2,1)} %pad_maximum_fusion.refs_7_), channel_id=1, source_target_pairs={{0,4},{4,0},{8,12},{12,8},{16,20},{20,16},{24,28},{28,24},{1,5},{5... | collective-permute-start | bytes 3145736 | tf_op jit(solution)/shard_map/ppermute | solution.py:344
  48.3 7.8 %collective-permute-start.12 = (bf16[512,1024]{1,0:T(8,128)(2,1)}, bf16[512,1024]{1,0:T(8,128)(2,1)}, u32[]{:S(2)}, u32[]{:S(2)}) collective-permute-start(bf16[512,1024]{1,0:T(8,128)(2,1)} %collective-permute-done.9.refs_8_), channel_id=1, source_target_pairs={{0,4},{4,0},{8,12},{12,8},{16,20},{20,16},{24,28},{28,24},{1,5},{5... | collective-permute-start | bytes 3145736 | tf_op jit(solution)/shard_map/ppermute | solution.py:344
  48.4 7.7 %collective-permute-start.13 = (bf16[256,1024]{1,0:T(8,128)(2,1)S(1)}, bf16[256,1024]{1,0:T(8,128)(2,1)}, u32[]{:S(2)}, u32[]{:S(2)}) collective-permute-start(bf16[256,1024]{1,0:T(8,128)(2,1)S(1)} %pad_maximum_fusion.5.refs_11_.refs_5_), channel_id=1, source_target_pairs={{0,4},{4,0},{8,12},{12,8},{16,20},{20,16},{24,28},{28,24},{1,5},{5... | collective-permute-start | bytes 1572872 | tf_op jit(solution)/shard_map/ppermute | solution.py:344
  49.0 7.1 %collective-permute-start.14 = (bf16[256,1024]{1,0:T(8,128)(2,1)S(1)}, bf16[256,1024]{1,0:T(8,128)(2,1)}, u32[]{:S(2)}, u32[]{:S(2)}) collective-permute-start(bf16[256,1024]{1,0:T(8,128)(2,1)S(1)} %collective-permute-done.10.refs_12_.refs_6_), channel_id=1, source_target_pairs={{0,4},{4,0},{8,12},{12,8},{16,20},{20,16},{24,28},{28,24},{1,5},{5... | collective-permute-start | bytes 1572872 | tf_op jit(solution)/shard_map/ppermute | solution.py:344
  69.6 8.7 %collective-permute-start.15 = (bf16[128,1024]{1,0:T(8,128)(2,1)S(1)}, bf16[128,1024]{1,0:T(8,128)(2,1)S(1)}, u32[]{:S(2)}, u32[]{:S(2)}) collective-permute-start(bf16[128,1024]{1,0:T(8,128)(2,1)S(1)} %get-tuple-element.136), channel_id=1, source_target_pairs={{0,1},{1,0},{2,3},{3,2},{4,5},{5,4},{6,7},{7,6},{8,9},{9,8},{10,11... | collective-permute-start | bytes 786440 | tf_op jit(solution)/shard_map/ppermute | solution.py:344
  78.3 5.7 %collective-permute-start.18 = (bf16[1536,1024]{1,0:T(8,128)(2,1)S(1)}, bf16[1536,1024]{1,0:T(8,128)(2,1)S(1)}, u32[]{:S(2)}, u32[]{:S(2)}) collective-permute-start(bf16[1536,1024]{1,0:T(8,128)(2,1)S(1)} %get-tuple-element.147), channel_id=1, source_target_pairs={{0,4},{4,0},{8,12},{12,8},{16,20},{20,16},{24,28},{28,24},{1,5},{5... | collective-permute-start | bytes 9437192 | tf_op jit(solution)/shard_map/ppermute | solution.py:344
  79.2 15.4 %collective-permute-start.17 = (bf16[128,1024]{1,0:T(8,128)(2,1)}, bf16[128,1024]{1,0:T(8,128)(2,1)S(1)}, u32[]{:S(2)}, u32[]{:S(2)}) collective-permute-start(bf16[128,1024]{1,0:T(8,128)(2,1)} %add_convert_fusion.6), channel_id=1, source_target_pairs={{0,2},{1,3},{2,0},{3,1},{4,6},{5,7},{6,4},{7,5},{8,10},{9,11},{10,... | collective-permute-start | bytes 786440 | tf_op jit(solution)/shard_map/ppermute | solution.py:344
  82.0 13.2 %collective-permute-start.16 = (bf16[128,1024]{1,0:T(8,128)(2,1)}, bf16[128,1024]{1,0:T(8,128)(2,1)}, u32[]{:S(2)}, u32[]{:S(2)}) collective-permute-start(bf16[128,1024]{1,0:T(8,128)(2,1)} %get-tuple-element.142), channel_id=1, source_target_pairs={{0,1},{1,0},{2,3},{3,2},{4,5},{5,4},{6,7},{7,6},{8,9},{9,8},{10,11... | collective-permute-start | bytes 786440 | tf_op jit(solution)/shard_map/ppermute | solution.py:344
  88.6 40.6 %collective-permute-start.22 = (bf16[512,1024]{1,0:T(8,128)(2,1)}, bf16[512,1024]{1,0:T(8,128)(2,1)}, u32[]{:S(2)}, u32[]{:S(2)}) collective-permute-start(bf16[512,1024]{1,0:T(8,128)(2,1)} %get-tuple-element.169), channel_id=1, source_target_pairs={{0,16},{4,20},{8,24},{12,28},{16,0},{20,4},{24,8},{28,12},{1,17},{... | collective-permute-start | bytes 3145736 | tf_op jit(solution)/shard_map/ppermute | solution.py:344
  96.4 13.8 %collective-permute-start.19 = (bf16[128,1024]{1,0:T(8,128)(2,1)S(1)}, bf16[128,1024]{1,0:T(8,128)(2,1)S(1)}, u32[]{:S(2)}, u32[]{:S(2)}) collective-permute-start(bf16[128,1024]{1,0:T(8,128)(2,1)S(1)} %get-tuple-element.157.refs_8_), channel_id=1, source_target_pairs={{0,2},{1,3},{2,0},{3,1},{4,6},{5,7},{6,4},{7,5},{8,10},{9,11},{10,... | collective-permute-start | bytes 786440 | tf_op jit(solution)/shard_map/ppermute | solution.py:344
  97.4 12.8 %collective-permute-start.20 = (bf16[128,1024]{1,0:T(8,128)(2,1)S(1)}, bf16[128,1024]{1,0:T(8,128)(2,1)S(1)}, u32[]{:S(2)}, u32[]{:S(2)}) collective-permute-start(bf16[128,1024]{1,0:T(8,128)(2,1)S(1)} %get-tuple-element.157.refs_8_), channel_id=1, source_target_pairs={{0,1},{1,0},{2,3},{3,2},{4,5},{5,4},{6,7},{7,6},{8,9},{9,8},{10,11... | collective-permute-start | bytes 786440 | tf_op jit(solution)/shard_map/ppermute | solution.py:344
  110.2 7.1 %collective-permute-start.21 = (bf16[128,1024]{1,0:T(8,128)(2,1)S(1)}, bf16[128,1024]{1,0:T(8,128)(2,1)S(1)}, u32[]{:S(2)}, u32[]{:S(2)}) collective-permute-start(bf16[128,1024]{1,0:T(8,128)(2,1)S(1)} %collective-permute-done.19.refs_10_), channel_id=1, source_target_pairs={{0,1},{1,0},{2,3},{3,2},{4,5},{5,4},{6,7},{7,6},{8,9},{9,8},{10,11... | collective-permute-start | bytes 786440 | tf_op jit(solution)/shard_map/ppermute | solution.py:344
  110.8 18.4 %collective-permute-start.23 = (bf16[256,1024]{1,0:T(8,128)(2,1)S(1)}, bf16[256,1024]{1,0:T(8,128)(2,1)S(1)}, u32[]{:S(2)}, u32[]{:S(2)}) collective-permute-start(bf16[256,1024]{1,0:T(8,128)(2,1)S(1)} %copy-done.26), channel_id=1, source_target_pairs={{0,8},{4,12},{8,0},{12,4},{16,24},{20,28},{24,16},{28,20},{1,9},{5... | collective-permute-start | bytes 1572872 | tf_op jit(solution)/shard_map/ppermute | solution.py:344
  117.2 12.0 %collective-permute-start.24 = (bf16[128,1024]{1,0:T(8,128)(2,1)}, bf16[128,1024]{1,0:T(8,128)(2,1)}, u32[]{:S(2)}, u32[]{:S(2)}) collective-permute-start(bf16[128,1024]{1,0:T(8,128)(2,1)} %get-tuple-element.171), channel_id=1, source_target_pairs={{0,1},{1,0},{2,3},{3,2},{4,5},{5,4},{6,7},{7,6},{8,9},{9,8},{10,11... | collective-permute-start | bytes 786440 | tf_op jit(solution)/shard_map/ppermute | solution.py:344
  129.3 6.6 %collective-permute-start.25 = (bf16[128,1024]{1,0:T(8,128)(2,1)}, bf16[128,1024]{1,0:T(8,128)(2,1)S(1)}, u32[]{:S(2)}, u32[]{:S(2)}) collective-permute-start(bf16[128,1024]{1,0:T(8,128)(2,1)} %get-tuple-element.175), channel_id=1, source_target_pairs={{0,1},{1,0},{2,3},{3,2},{4,5},{5,4},{6,7},{7,6},{8,9},{9,8},{10,11... | collective-permute-start | bytes 786440 | tf_op jit(solution)/shard_map/ppermute | solution.py:344
  135.9 2.3 %collective-permute-start.30 = (bf16[768,512]{1,0:T(8,128)(2,1)S(1)}, bf16[768,512]{1,0:T(8,128)(2,1)S(1)}, u32[]{:S(2)}, u32[]{:S(2)}) collective-permute-start(bf16[768,512]{1,0:T(8,128)(2,1)S(1)} %get-tuple-element.191), channel_id=1, source_target_pairs={{0,4},{4,0},{8,12},{12,8},{16,20},{20,16},{24,28},{28,24},{1,5},{5... | collective-permute-start | bytes 2359304 | tf_op jit(solution)/shard_map/ppermute | solution.py:344
  136.0 32.4 %collective-permute-start.28 = (bf16[256,1024]{1,0:T(8,128)(2,1)S(1)}, bf16[256,1024]{1,0:T(8,128)(2,1)S(1)}, u32[]{:S(2)}, u32[]{:S(2)}) collective-permute-start(bf16[256,1024]{1,0:T(8,128)(2,1)S(1)} %slice.128), channel_id=1, source_target_pairs={{0,8},{4,12},{8,0},{12,4},{16,24},{20,28},{24,16},{28,20},{1,9},{5... | collective-permute-start | bytes 1572872 | tf_op jit(solution)/shard_map/ppermute | solution.py:344
  138.6 20.3 %collective-permute-start.31 = (bf16[384,512]{1,0:T(8,128)(2,1)S(1)}, bf16[384,512]{1,0:T(8,128)(2,1)S(1)}, u32[]{:S(2)}, u32[]{:S(2)}) collective-permute-start(bf16[384,512]{1,0:T(8,128)(2,1)S(1)} %get-tuple-element.215), channel_id=1, source_target_pairs={{0,8},{4,12},{8,0},{12,4},{16,24},{20,28},{24,16},{28,20},{1,9},{5... | collective-permute-start | bytes 1179656 | tf_op jit(solution)/shard_map/ppermute | solution.py:344
  139.5 22.7 %collective-permute-start.32 = (bf16[384,512]{1,0:T(8,128)(2,1)S(1)}, bf16[384,512]{1,0:T(8,128)(2,1)S(1)}, u32[]{:S(2)}, u32[]{:S(2)}) collective-permute-start(bf16[384,512]{1,0:T(8,128)(2,1)S(1)} %get-tuple-element.216), channel_id=1, source_target_pairs={{0,16},{4,20},{8,24},{12,28},{16,0},{20,4},{24,8},{28,12},{1,17},{... | collective-permute-start | bytes 1179656 | tf_op jit(solution)/shard_map/ppermute | solution.py:344
  143.1 25.7 %collective-permute-start.27 = (bf16[256,1024]{1,0:T(8,128)(2,1)S(1)}, bf16[256,1024]{1,0:T(8,128)(2,1)S(1)}, u32[]{:S(2)}, u32[]{:S(2)}) collective-permute-start(bf16[256,1024]{1,0:T(8,128)(2,1)S(1)} %add_convert_fusion.1), channel_id=1, source_target_pairs={{0,2},{1,3},{2,0},{3,1},{4,6},{5,7},{6,4},{7,5},{8,10},{9,11},{10,... | collective-permute-start | bytes 1572872 | tf_op jit(solution)/shard_map/ppermute | solution.py:344
  143.5 25.3 %collective-permute-start.26 = (bf16[256,1024]{1,0:T(8,128)(2,1)S(1)}, bf16[256,1024]{1,0:T(8,128)(2,1)S(1)}, u32[]{:S(2)}, u32[]{:S(2)}) collective-permute-start(bf16[256,1024]{1,0:T(8,128)(2,1)S(1)} %copy-done.51), channel_id=1, source_target_pairs={{0,1},{1,0},{2,3},{3,2},{4,5},{5,4},{6,7},{7,6},{8,9},{9,8},{10,11... | collective-permute-start | bytes 1572872 | tf_op jit(solution)/shard_map/ppermute | solution.py:344
  158.8 9.6 %collective-permute-start.29 = (bf16[128,1024]{1,0:T(8,128)(2,1)S(1)}, bf16[128,1024]{1,0:T(8,128)(2,1)S(1)}, u32[]{:S(2)}, u32[]{:S(2)}) collective-permute-start(bf16[128,1024]{1,0:T(8,128)(2,1)S(1)} %slice.129), channel_id=1, source_target_pairs={{0,16},{4,20},{8,24},{12,28},{16,0},{20,4},{24,8},{28,12},{1,17},{... | collective-permute-start | bytes 786440 | tf_op jit(solution)/shard_map/ppermute | solution.py:344
  169.4 10.6 %collective-permute-start.38 = (bf16[384,512]{1,0:T(8,128)(2,1)S(1)}, bf16[384,512]{1,0:T(8,128)(2,1)S(1)}, u32[]{:S(2)}, u32[]{:S(2)}) collective-permute-start(bf16[384,512]{1,0:T(8,128)(2,1)S(1)} %get-tuple-element.211), channel_id=1, source_target_pairs={{0,16},{4,20},{8,24},{12,28},{16,0},{20,4},{24,8},{28,12},{1,17},{... | collective-permute-start | bytes 1179656 | tf_op jit(solution)/shard_map/ppermute | solution.py:344
  171.0 9.6 %collective-permute-start.39 = (bf16[384,512]{1,0:T(8,128)(2,1)S(1)}, bf16[384,512]{1,0:T(8,128)(2,1)S(1)}, u32[]{:S(2)}, u32[]{:S(2)}) collective-permute-start(bf16[384,512]{1,0:T(8,128)(2,1)S(1)} %get-tuple-element.212), channel_id=1, source_target_pairs={{0,8},{4,12},{8,0},{12,4},{16,24},{20,28},{24,16},{28,20},{1,9},{5... | collective-permute-start | bytes 1179656 | tf_op jit(solution)/shard_map/ppermute | solution.py:344
  171.6 24.9 %collective-permute-start.33 = (bf16[256,1024]{1,0:T(8,128)(2,1)S(1)}, bf16[256,1024]{1,0:T(8,128)(2,1)}, u32[]{:S(2)}, u32[]{:S(2)}) collective-permute-start(bf16[256,1024]{1,0:T(8,128)(2,1)S(1)} %finish.1), channel_id=1, source_target_pairs={{0,2},{1,3},{2,0},{3,1},{4,6},{5,7},{6,4},{7,5},{8,10},{9,11},{10,... | collective-permute-start | bytes 1572872 | tf_op jit(solution)/shard_map/ppermute | solution.py:344
  172.2 24.4 %collective-permute-start.34 = (bf16[256,1024]{1,0:T(8,128)(2,1)S(1)}, bf16[256,1024]{1,0:T(8,128)(2,1)S(1)}, u32[]{:S(2)}, u32[]{:S(2)}) collective-permute-start(bf16[256,1024]{1,0:T(8,128)(2,1)S(1)} %finish.1), channel_id=1, source_target_pairs={{0,1},{1,0},{2,3},{3,2},{4,5},{5,4},{6,7},{7,6},{8,9},{9,8},{10,11... | collective-permute-start | bytes 1572872 | tf_op jit(solution)/shard_map/ppermute | solution.py:344
  173.8 10.6 %collective-permute-start.35 = (f32[9,1024]{1,0:T(8,128)S(1)}, f32[9,1024]{1,0:T(8,128)S(1)}, u32[]{:S(2)}, u32[]{:S(2)}) collective-permute-start(f32[9,1024]{1,0:T(8,128)S(1)} %copy-done.44), channel_id=1, source_target_pairs={{0,4},{4,0},{8,12},{12,8},{16,20},{20,16},{24,28},{28,24},{1,5},{5... | collective-permute-start | bytes 110600 | tf_op jit(solution)/shard_map/ppermute | solution.py:344
  180.9 12.3 %collective-permute-start.40 = (bf16[768,512]{1,0:T(8,128)(2,1)S(1)}, bf16[768,512]{1,0:T(8,128)(2,1)S(1)}, u32[]{:S(2)}, u32[]{:S(2)}) collective-permute-start(bf16[768,512]{1,0:T(8,128)(2,1)S(1)} %pad_maximum_fusion.4), channel_id=1, source_target_pairs={{0,4},{4,0},{8,12},{12,8},{16,20},{20,16},{24,28},{28,24},{1,5},{5... | collective-permute-start | bytes 2359304 | tf_op jit(solution)/shard_map/ppermute | solution.py:344
  184.4 4.5 %collective-permute-start.36 = (f32[9,1024]{1,0:T(8,128)S(1)}, f32[9,1024]{1,0:T(8,128)S(1)}, u32[]{:S(2)}, u32[]{:S(2)}) collective-permute-start(f32[9,1024]{1,0:T(8,128)S(1)} %add.76), channel_id=1, source_target_pairs={{0,8},{4,12},{8,0},{12,4},{16,24},{20,28},{24,16},{28,20},{1,9},{5... | collective-permute-start | bytes 110600 | tf_op jit(solution)/shard_map/ppermute | solution.py:344
  188.9 4.3 %collective-permute-start.37 = (f32[9,1024]{1,0:T(8,128)S(1)}, f32[9,1024]{1,0:T(8,128)S(1)}, u32[]{:S(2)}, u32[]{:S(2)}) collective-permute-start(f32[9,1024]{1,0:T(8,128)S(1)} %add.77), channel_id=1, source_target_pairs={{0,16},{4,20},{8,24},{12,28},{16,0},{20,4},{24,8},{28,12},{1,17},{... | collective-permute-start | bytes 110600 | tf_op jit(solution)/shard_map/ppermute | solution.py:344
  196.5 5.1 %collective-permute-start.42 = (f32[10,1024]{1,0:T(8,128)S(1)}, f32[10,1024]{1,0:T(8,128)S(1)}, u32[]{:S(2)}, u32[]{:S(2)}) collective-permute-start(f32[10,1024]{1,0:T(8,128)S(1)} %pad_maximum_fusion.8), channel_id=1, source_target_pairs={{0,1},{1,0},{2,3},{3,2},{4,5},{5,4},{6,7},{7,6},{8,9},{9,8},{10,11... | collective-permute-start | bytes 122888 | tf_op jit(solution)/shard_map/ppermute | solution.py:344
  197.7 14.8 %collective-permute-start.41 = (bf16[256,1024]{1,0:T(8,128)(2,1)}, bf16[256,1024]{1,0:T(8,128)(2,1)}, u32[]{:S(2)}, u32[]{:S(2)}) collective-permute-start(bf16[256,1024]{1,0:T(8,128)(2,1)} %collective-permute-done.33), channel_id=1, source_target_pairs={{0,1},{1,0},{2,3},{3,2},{4,5},{5,4},{6,7},{7,6},{8,9},{9,8},{10,11... | collective-permute-start | bytes 1572872 | tf_op jit(solution)/shard_map/ppermute | solution.py:344
  201.6 9.4 %collective-permute-start.43 = (f32[10,1024]{1,0:T(8,128)S(1)}, f32[10,1024]{1,0:T(8,128)S(1)}, u32[]{:S(2)}, u32[]{:S(2)}) collective-permute-start(f32[10,1024]{1,0:T(8,128)S(1)} %add.84), channel_id=1, source_target_pairs={{0,2},{1,3},{2,0},{3,1},{4,6},{5,7},{6,4},{7,5},{8,10},{9,11},{10,... | collective-permute-start | bytes 122888 | tf_op jit(solution)/shard_map/ppermute | solution.py:344
  (49 other events, 306.8 us)

commit v7 on v6

--- a/solution.py
+++ b/solution.py
@@ -908,7 +908,7 @@
         scratch_shapes=[pltpu.VMEM((token_count, model_width), low)]
         + [pltpu.VMEM(each.shape, low) for each in kept]
         + [pltpu.SemaphoreType.DMA((2 + block_count,))],
-        compiler_params=pltpu.CompilerParams(vmem_limit_bytes=56 * mib),
+        compiler_params=pltpu.CompilerParams(vmem_limit_bytes=46 * mib),
         name="attend",
     )(seq_lengths, layer_in, gain_attn[None], qkv_flat, cosine, sine)
 

time: 215 us -> 214 us (level)
  waiting for transfers between devices: 85.3 us -> 88.7 us
  Pallas kernels: 49.2 us -> 46.8 us
    ppermute x44, waiting for transfers between devices: 85.3 us -> 88.7 us  [exchange(): lax.ppermute(array_in, axis_name, [(i, i ^ bits) for i in range(count)])]
    pallas_call x1, Pallas kernels: 7.61 us -> 5.43 us  [on_device(): pl.pallas_call(attend_kernel, out_shape=kept + (shaped((token_count, head...]
    unnamed x106 -> x116, local copies, waits for them, and re-layouts: 11 us -> 10.8 us
  transfers between devices with their start and end apart: 44 -> 44, of which waited for: 22 -> 25; matrix products, arithmetic and copies ran while one was open for 10% -> 10% of each run, Pallas kernels for 17% -> 16%
where the time goes in v7:
time: 214 us; the launch traced here: 212 us
  waiting for transfers between devices  88.7 us (41%)
  Pallas kernels  46.8 us (22%)
  starting transfers between devices  43.1 us (20%)
  local copies, waits for them, and re-layouts  18.9 us (9%)
  other arithmetic  13.5 us (6%)
    ppermute x44, waiting for transfers between devices, exchange(): lax.ppermute(array_in, axis_name, [(i, i ^ bits) for i in range(count)])  88.7 us
    ppermute x44, starting transfers between devices, exchange(): lax.ppermute(array_in, axis_name, [(i, i ^ bits) for i in range(count)])  43.1 us
    pallas_call x1, Pallas kernels, on_device(): pl.pallas_call(functools.partial(middle_kernel, tensor_count), out_shape=...  12.4 us
    pallas_call x1, Pallas kernels, on_device(): pl.pallas_call(functools.partial(attend_back_kernel, tensor_count), out_s...  11.2 us
    unnamed x116, local copies, waits for them, and re-layouts  10.8 us
    pallas_call x1, Pallas kernels, on_device(): pl.pallas_call(functools.partial(weight_grad_kernel, tensor_count), out_s...  7.38 us
    pallas_call x1, Pallas kernels, on_device(): pl.pallas_call(attend_kernel, out_shape=kept + (shaped((token_count, head...  5.43 us
  transfers between devices with their start and end apart: 44, of which 25 were waited for; matrix products, arithmetic and copies ran while one was open for 10% of the time, Pallas kernels for 16%

profile of v7, /device:TPU:0, one launch (start us, length us, event | category | flops | bytes accessed | tf_op | source)
XLA Modules:
  0.0 212.5 jit_solution(16091611872905672730)
XLA Ops:
  0.7 3.0 %collective-permute-start = (bf16[256,1024]{1,0:T(8,128)(2,1)}, bf16[256,1024]{1,0:T(8,128)(2,1)S(1)}, u32[]{:S(2)}, u32[]{:S(2)}) collective-permute-start(bf16[256,1024]{1,0:T(8,128)(2,1)} %bitcast.34), channel_id=1, source_target_pairs={{0,8},{4,12},{8,0},{12,4},{16,24},{20,28},{24,16},{28,20},{1,9},{5... | collective-permute-start | bytes 1572872 | tf_op jit(solution)/shard_map/ppermute | solution.py:344
  4.8 2.7 %collective-permute-start.2 = (bf16[128,1024]{1,0:T(8,128)(2,1)S(1)}, bf16[128,1024]{1,0:T(8,128)(2,1)S(1)}, u32[]{:S(2)}, u32[]{:S(2)}) collective-permute-start(bf16[128,1024]{1,0:T(8,128)(2,1)S(1)} %slice_select_fusion), channel_id=1, source_target_pairs={{0,2},{1,3},{2,0},{3,1},{4,6},{5,7},{6,4},{7,5},{8,10},{9,11},{10,... | collective-permute-start | bytes 786440 | tf_op jit(solution)/shard_map/ppermute | solution.py:344
  7.4 1.6 collective-permute-start.3
  9.0 1.5 collective-permute-start.1
  10.5 1.5 copy.25
  12.1 5.4 %attend.1 = (bf16[2,4,256,128]{3,2,1,0:T(8,128)(2,1)S(1)}, bf16[2,512,128]{2,1,0:T(8,128)(2,1)S(1)}, bf16[2,4,256,512]{3,2,1,0:T(8,128)(2,1)S(1)}, bf16[512,256]{1,0:T(8,128)(2,1)S(1)}) custom-call(s32[1,3]{1,0:T(1,128)S(1)} %copy-done.32, bf16[512,1024]{1,0:T(8,128)(2,1)S(1)} %copy-done.2, f32[1,1024]{1,0:T(1,128)S(1)} %bitcast.25, ...), custom_call_target="tpu_custom_call" | custom-call | tf_op jit(solution)/shard_map/attend/pallas_call | solution.py:903
  17.6 1.6 collective-permute-done.2
  20.5 1.5 collective-permute-start.9
  22.0 1.3 collective-permute-start.4
  23.3 2.4 %collective-permute-start.5 = (bf16[512,256]{1,0:T(8,128)(2,1)S(1)}, bf16[512,256]{1,0:T(8,128)(2,1)S(1)}, u32[]{:S(2)}, u32[]{:S(2)}) collective-permute-start(bf16[512,256]{1,0:T(8,128)(2,1)S(1)} %get-tuple-element.113.attended), channel_id=1, source_target_pairs={{0,1},{1,0},{2,3},{3,2},{4,5},{5,4},{6,7},{7,6},{8,9},{9,8},{10,11... | collective-permute-start | bytes 786440 | tf_op jit(solution)/shard_map/ppermute | solution.py:344
  26.6 8.7 %collective-permute-done.4 = bf16[512,256]{1,0:T(8,128)(2,1)S(1)} collective-permute-done((bf16[512,256]{1,0:T(8,128)(2,1)S(1)}, bf16[512,256]{1,0:T(8,128)(2,1)S(1)}, u32[]{:S(2)}, u32[]{:S(2)}) %collective-permute-start.4) | collective-permute-done | bytes 262176 | tf_op jit(solution)/shard_map/ppermute | solution.py:344
  35.3 1.3 collective-permute-done.5
  36.6 4.4 %collective-permute-done.6 = bf16[128,1024]{1,0:T(8,128)(2,1)S(1)} collective-permute-done((bf16[128,1024]{1,0:T(8,128)(2,1)S(1)}, bf16[128,1024]{1,0:T(8,128)(2,1)S(1)}, u32[]{:S(2)}, u32[]{:S(2)}) %collective-permute-start.6) | collective-permute-done | bytes 262176 | tf_op jit(solution)/shard_map/ppermute | solution.py:344
  41.9 6.2 %collective-permute-done.8 = bf16[512,256]{1,0:T(8,128)(2,1)S(1)} collective-permute-done((bf16[512,256]{1,0:T(8,128)(2,1)S(1)}, bf16[512,256]{1,0:T(8,128)(2,1)S(1)}, u32[]{:S(2)}, u32[]{:S(2)}) %collective-permute-start.8) | collective-permute-done | bytes 262176 | tf_op jit(solution)/shard_map/ppermute | solution.py:344
  49.1 1.3 pad_maximum_fusion.2.heads
  50.4 1.2 copy-done.5
  51.7 4.0 %branch.1 = (f32[512,1024]{1,0:T(8,128)S(1)}, f32[512,1]{1,0:T(8,128)S(1)}, bf16[512,1024]{1,0:T(8,128)(2,1)S(1)}, f32[512,128]{1,0:T(8,128)S(1)}) custom-call(s32[2]{0:T(128)S(1)} %pad_add_fusion.place.refs_0_, f32[1,1024]{1,0:T(1,128)S(1)} %bitcast.28, bf16[128,1024]{1,0:T(8,128)(2,1)S(1)} %pad.4.router.refs_1_, s32[512,2]{1,0:T(8,128)S(1)} %copy.22.routes, ...), custom_call_target="tpu_custom_call" | custom-call | tf_op jit(solution)/shard_map/branch/pallas_call | solution.py:939
  56.8 12.4 %middle.1 = (f32[128,1024]{1,0:T(8,128)S(1)}, bf16[128,1024]{1,0:T(8,128)(2,1)}, bf16[128,1024]{1,0:T(8,128)(2,1)S(1)}, bf16[128,1024]{1,0:T(8,128)(2,1)S(1)}, f...) custom-call(s32[2]{0:T(128)S(1)} %pad_add_fusion.place.refs_0_, ...), custom_call_target="tpu_custom_call" | custom-call | tf_op jit(solution)/shard_map/middle/pallas_call | solution.py:962
  69.5 7.4 %weight_grad.1 = (f32[128,1024]{1,0:T(8,128)S(1)}, bf16[128,1024]{1,0:T(8,128)(2,1)S(1)}, bf16[128,1024]{1,0:T(8,128)(2,1)S(1)}, bf16[128,1024]{1,0:T(8,128)(2,1...) custom-call(s32[2]{0:T(128)S(1)} %pad_add_fusion.place.refs_0_, ...), custom_call_target="tpu_custom_call" | custom-call | tf_op jit(solution)/shard_map/weight_grad/pallas_call | solution.py:1000
  78.8 3.0 %collective-permute-start.17 = (bf16[128,1024]{1,0:T(8,128)(2,1)}, bf16[128,1024]{1,0:T(8,128)(2,1)S(1)}, u32[]{:S(2)}, u32[]{:S(2)}) collective-permute-start(bf16[128,1024]{1,0:T(8,128)(2,1)} %add_convert_fusion.6), channel_id=1, source_target_pairs={{0,2},{1,3},{2,0},{3,1},{4,6},{5,7},{6,4},{7,5},{8,10},{9,11},{10,... | collective-permute-start | bytes 786440 | tf_op jit(solution)/shard_map/ppermute | solution.py:344
  82.4 1.2 collective-permute-done.18.given
  83.6 1.6 add_grads.1
  85.1 1.3 copy-done.7
  88.7 5.7 %collective-permute-done.17.far = bf16[128,1024]{1,0:T(8,128)(2,1)S(1)} collective-permute-done((bf16[128,1024]{1,0:T(8,128)(2,1)}, bf16[128,1024]{1,0:T(8,128)(2,1)S(1)}, u32[]{:S(2)}, u32[]{:S(2)}) %collective-permute-start.17) | collective-permute-done | bytes 262176 | tf_op jit(solution)/shard_map/ppermute | solution.py:344
  95.2 1.2 norm_back.1
  97.0 1.9 collective-permute-start.20
  98.9 11.3 %collective-permute-done.19.refs_10_ = bf16[128,1024]{1,0:T(8,128)(2,1)S(1)} collective-permute-done((bf16[128,1024]{1,0:T(8,128)(2,1)S(1)}, bf16[128,1024]{1,0:T(8,128)(2,1)S(1)}, u32[]{:S(2)}, u32[]{:S(2)}) %collective-permute-start.19) | collective-permute-done | bytes 262176 | tf_op jit(solution)/shard_map/ppermute | solution.py:344
  111.0 6.4 %collective-permute-done.21.refs_11_ = bf16[128,1024]{1,0:T(8,128)(2,1)S(1)} collective-permute-done((bf16[128,1024]{1,0:T(8,128)(2,1)S(1)}, bf16[128,1024]{1,0:T(8,128)(2,1)S(1)}, u32[]{:S(2)}, u32[]{:S(2)}) %collective-permute-start.21) | collective-permute-done | bytes 262176 | tf_op jit(solution)/shard_map/ppermute | solution.py:344
  118.2 11.2 %attend_back.1 = (f32[256,1024]{1,0:T(8,128)}, bf16[256,1024]{1,0:T(8,128)(2,1)}, bf16[256,1024]{1,0:T(8,128)(2,1)}, bf16[128,1024]{1,0:T(8,128)(2,1)}, bf16[512...) custom-call(s32[2]{0:T(128)} %copy-done.30, bf16[256,1024]{1,0:T(8,128)(2,1)} %refs_1_.1, ...), custom_call_target="tpu_custom_call" | custom-call | tf_op jit(solution)/shard_map/attend_back/pallas_call | solution.py:1052
  129.5 1.4 collective-permute-start.25
  130.8 1.5 convert_add_fusion
  132.4 3.2 %attend_grad.1 = (f32[768,512]{1,0:T(8,128)S(1)}, bf16[768,512]{1,0:T(8,128)(2,1)S(1)}) custom-call(s32[2]{0:T(128)S(1)} %copy-done.31, bf16[512,1024]{1,0:T(8,128)(2,1)S(1)} %copy-done.2, f32[1,1024]{1,0:T(1,128)S(1)} %bitcast.26, bf16[512,512]{1,0:T(8,128)(2,1)S(1)} %copy-done.21, bf16[512,256]{1,0:T(8,128)(2,1)S(1)} %copy-done.18, ...), custom_call_target="tpu_custom_call" | custom-call | tf_op jit(solution)/shard_map/attend_grad/pallas_call | solution.py:1094
  140.4 2.9 %collective-permute-start.27 = (bf16[256,1024]{1,0:T(8,128)(2,1)S(1)}, bf16[256,1024]{1,0:T(8,128)(2,1)S(1)}, u32[]{:S(2)}, u32[]{:S(2)}) collective-permute-start(bf16[256,1024]{1,0:T(8,128)(2,1)S(1)} %add_convert_fusion.1), channel_id=1, source_target_pairs={{0,2},{1,3},{2,0},{3,1},{4,6},{5,7},{6,4},{7,5},{8,10},{9,11},{10,... | collective-permute-start | bytes 1572872 | tf_op jit(solution)/shard_map/ppermute | solution.py:344
  144.3 14.7 %collective-permute-done.31 = bf16[384,512]{1,0:T(8,128)(2,1)S(1)} collective-permute-done((bf16[384,512]{1,0:T(8,128)(2,1)S(1)}, bf16[384,512]{1,0:T(8,128)(2,1)S(1)}, u32[]{:S(2)}, u32[]{:S(2)}) %collective-permute-start.31) | collective-permute-done | bytes 393248 | tf_op jit(solution)/shard_map/ppermute | solution.py:344
  159.8 7.2 %collective-permute-done.29 = bf16[128,1024]{1,0:T(8,128)(2,1)S(1)} collective-permute-done((bf16[128,1024]{1,0:T(8,128)(2,1)S(1)}, bf16[128,1024]{1,0:T(8,128)(2,1)S(1)}, u32[]{:S(2)}, u32[]{:S(2)}) %collective-permute-start.29) | collective-permute-done | bytes 262176 | tf_op jit(solution)/shard_map/ppermute | solution.py:344
  167.8 1.3 collective-permute-start.38
  170.2 1.8 collective-permute-start.33
  173.0 4.7 %collective-permute-done.38 = bf16[384,512]{1,0:T(8,128)(2,1)S(1)} collective-permute-done((bf16[384,512]{1,0:T(8,128)(2,1)S(1)}, bf16[384,512]{1,0:T(8,128)(2,1)S(1)}, u32[]{:S(2)}, u32[]{:S(2)}) %collective-permute-start.38) | collective-permute-done | bytes 393248 | tf_op jit(solution)/shard_map/ppermute | solution.py:344
  178.7 1.2 add_convert_fusion.3
  180.1 2.5 %convert_add_fusion.1 = f32[256,1024]{1,0:T(8,128)} fusion(bf16[256,1024]{1,0:T(8,128)(2,1)S(1)} %copy-done.42, f32[512,1024]{1,0:T(8,128)} %copy-done.36), kind=kLoop, calls=%fused_computation.8 | loop fusion | flops 524288 | bytes 2621440 | tf_op jit(solution)/shard_map/add | solution.py:1115
  183.4 1.1 collective-permute-start.36
  184.7 3.2 %collective-permute-done.36 = f32[9,1024]{1,0:T(8,128)S(1)} collective-permute-done((f32[9,1024]{1,0:T(8,128)S(1)}, f32[9,1024]{1,0:T(8,128)S(1)}, u32[]{:S(2)}, u32[]{:S(2)}) %collective-permute-start.36) | collective-permute-done | bytes 36896 | tf_op jit(solution)/shard_map/ppermute | solution.py:344
  189.0 3.3 %collective-permute-done.37 = f32[9,1024]{1,0:T(8,128)S(1)} collective-permute-done((f32[9,1024]{1,0:T(8,128)S(1)}, f32[9,1024]{1,0:T(8,128)S(1)}, u32[]{:S(2)}, u32[]{:S(2)}) %collective-permute-start.37) | collective-permute-done | bytes 36896 | tf_op jit(solution)/shard_map/ppermute | solution.py:344
  196.6 2.9 %collective-permute-done.42 = f32[10,1024]{1,0:T(8,128)S(1)} collective-permute-done((f32[10,1024]{1,0:T(8,128)S(1)}, f32[10,1024]{1,0:T(8,128)S(1)}, u32[]{:S(2)}, u32[]{:S(2)}) %collective-permute-start.42) | collective-permute-done | bytes 40992 | tf_op jit(solution)/shard_map/ppermute | solution.py:344
  199.5 1.6 collective-permute-start.43
  203.6 2.3 %reshape.44 = f32[1024,2,256]{2,1,0:T(2,128)} reshape(f32[1024,512]{1,0:T(8,128)S(1)} %get-tuple-element.205) | data formatting | bytes 4194304 | tf_op jit(solution)/shard_map/reshape | solution.py:1137
  207.0 2.3 %collective-permute-done.43 = f32[10,1024]{1,0:T(8,128)S(1)} collective-permute-done((f32[10,1024]{1,0:T(8,128)S(1)}, f32[10,1024]{1,0:T(8,128)S(1)}, u32[]{:S(2)}, u32[]{:S(2)}) %collective-permute-start.43) | collective-permute-done | bytes 40992 | tf_op jit(solution)/shard_map/ppermute | solution.py:344
  210.6 1.9 slice_dynamic-update-slice_fusion
  (214 shorter events, 35.6 us)
Async XLA Ops:
  0.7 18.7 %collective-permute-start = (bf16[256,1024]{1,0:T(8,128)(2,1)}, bf16[256,1024]{1,0:T(8,128)(2,1)S(1)}, u32[]{:S(2)}, u32[]{:S(2)}) collective-permute-start(bf16[256,1024]{1,0:T(8,128)(2,1)} %bitcast.34), channel_id=1, source_target_pairs={{0,8},{4,12},{8,0},{12,4},{16,24},{20,28},{24,16},{28,20},{1,9},{5... | collective-permute-start | bytes 1572872 | tf_op jit(solution)/shard_map/ppermute | solution.py:344
  4.8 14.5 %collective-permute-start.2 = (bf16[128,1024]{1,0:T(8,128)(2,1)S(1)}, bf16[128,1024]{1,0:T(8,128)(2,1)S(1)}, u32[]{:S(2)}, u32[]{:S(2)}) collective-permute-start(bf16[128,1024]{1,0:T(8,128)(2,1)S(1)} %slice_select_fusion), channel_id=1, source_target_pairs={{0,2},{1,3},{2,0},{3,1},{4,6},{5,7},{6,4},{7,5},{8,10},{9,11},{10,... | collective-permute-start | bytes 786440 | tf_op jit(solution)/shard_map/ppermute | solution.py:344
  7.4 12.0 %collective-permute-start.3 = (bf16[128,1024]{1,0:T(8,128)(2,1)S(1)}, bf16[128,1024]{1,0:T(8,128)(2,1)S(1)}, u32[]{:S(2)}, u32[]{:S(2)}) collective-permute-start(bf16[128,1024]{1,0:T(8,128)(2,1)S(1)} %slice_select_fusion), channel_id=1, source_target_pairs={{0,1},{1,0},{2,3},{3,2},{4,5},{5,4},{6,7},{7,6},{8,9},{9,8},{10,11... | collective-permute-start | bytes 786440 | tf_op jit(solution)/shard_map/ppermute | solution.py:344
  9.0 10.4 %collective-permute-start.1 = (bf16[128,1024]{1,0:T(8,128)(2,1)}, bf16[128,1024]{1,0:T(8,128)(2,1)S(1)}, u32[]{:S(2)}, u32[]{:S(2)}) collective-permute-start(bf16[128,1024]{1,0:T(8,128)(2,1)} %bitcast.36), channel_id=1, source_target_pairs={{0,16},{4,20},{8,24},{12,28},{16,0},{20,4},{24,8},{28,12},{1,17},{... | collective-permute-start | bytes 786440 | tf_op jit(solution)/shard_map/ppermute | solution.py:344
  17.5 23.7 %copy-start.6 = (bf16[2,4,256,512]{3,2,1,0:T(8,128)(2,1)}, bf16[2,4,256,512]{3,2,1,0:T(8,128)(2,1)S(1)}, u32[]{:S(2)}) copy-start(bf16[2,4,256,512]{3,2,1,0:T(8,128)(2,1)S(1)} %get-tuple-element.109.refs_4_) | copy-start | bytes 6291460
  20.5 28.3 %copy-start.55 = (s32[512,2]{0,1:T(2,128)S(1)}, s32[512,2]{0,1:T(2,128)}, u32[]{:S(2)}) copy-start(s32[512,2]{0,1:T(2,128)} %param.15) | copy-start | bytes 12292
  20.5 28.5 %copy-start.54 = (bf16[1024,8]{0,1:T(8,128)(2,1)S(1)}, bf16[1024,8]{0,1:T(8,128)(2,1)}, u32[]{:S(2)}) copy-start(bf16[1024,8]{0,1:T(8,128)(2,1)} %param.20) | copy-start | bytes 49156
  20.5 27.6 %collective-permute-start.9 = (bf16[512,1024]{1,0:T(8,128)(2,1)}, bf16[512,1024]{1,0:T(8,128)(2,1)}, u32[]{:S(2)}, u32[]{:S(2)}) collective-permute-start(bf16[512,1024]{1,0:T(8,128)(2,1)} %pad_maximum_fusion.refs_7_), channel_id=1, source_target_pairs={{0,16},{4,20},{8,24},{12,28},{16,0},{20,4},{24,8},{28,12},{1,17},{... | collective-permute-start | bytes 3145736 | tf_op jit(solution)/shard_map/ppermute | solution.py:344
  22.0 13.3 %collective-permute-start.4 = (bf16[512,256]{1,0:T(8,128)(2,1)S(1)}, bf16[512,256]{1,0:T(8,128)(2,1)S(1)}, u32[]{:S(2)}, u32[]{:S(2)}) collective-permute-start(bf16[512,256]{1,0:T(8,128)(2,1)S(1)} %get-tuple-element.113.attended), channel_id=1, source_target_pairs={{0,2},{1,3},{2,0},{3,1},{4,6},{5,7},{6,4},{7,5},{8,10},{9,11},{10,... | collective-permute-start | bytes 786440 | tf_op jit(solution)/shard_map/ppermute | solution.py:344
  23.3 13.3 %collective-permute-start.5 = (bf16[512,256]{1,0:T(8,128)(2,1)S(1)}, bf16[512,256]{1,0:T(8,128)(2,1)S(1)}, u32[]{:S(2)}, u32[]{:S(2)}) collective-permute-start(bf16[512,256]{1,0:T(8,128)(2,1)S(1)} %get-tuple-element.113.attended), channel_id=1, source_target_pairs={{0,1},{1,0},{2,3},{3,2},{4,5},{5,4},{6,7},{7,6},{8,9},{9,8},{10,11... | collective-permute-start | bytes 786440 | tf_op jit(solution)/shard_map/ppermute | solution.py:344
  25.8 15.2 %collective-permute-start.6 = (bf16[128,1024]{1,0:T(8,128)(2,1)S(1)}, bf16[128,1024]{1,0:T(8,128)(2,1)S(1)}, u32[]{:S(2)}, u32[]{:S(2)}) collective-permute-start(bf16[128,1024]{1,0:T(8,128)(2,1)S(1)} %collective-permute-done.2), channel_id=1, source_target_pairs={{0,1},{1,0},{2,3},{3,2},{4,5},{5,4},{6,7},{7,6},{8,9},{9,8},{10,11... | collective-permute-start | bytes 786440 | tf_op jit(solution)/shard_map/ppermute | solution.py:344
  25.8 24.6 %copy-start.29 = (f32[1024]{0:T(1024)S(1)}, f32[1024]{0:T(1024)}, u32[]{:S(2)}) copy-start(f32[1024]{0:T(1024)} %param.19) | copy-start | bytes 12292
  25.8 22.3 %collective-permute-start.10 = (bf16[256,1024]{1,0:T(8,128)(2,1)S(1)}, bf16[256,1024]{1,0:T(8,128)(2,1)S(1)}, u32[]{:S(2)}, u32[]{:S(2)}) collective-permute-start(bf16[256,1024]{1,0:T(8,128)(2,1)S(1)} %pad_maximum_fusion.5.refs_11_.refs_5_), channel_id=1, source_target_pairs={{0,8},{4,12},{8,0},{12,4},{16,24},{20,28},{24,16},{28,20},{1,9},{5... | collective-permute-start | bytes 1572872 | tf_op jit(solution)/shard_map/ppermute | solution.py:344
  40.9 7.2 %collective-permute-start.8 = (bf16[512,256]{1,0:T(8,128)(2,1)S(1)}, bf16[512,256]{1,0:T(8,128)(2,1)S(1)}, u32[]{:S(2)}, u32[]{:S(2)}) collective-permute-start(bf16[512,256]{1,0:T(8,128)(2,1)S(1)} %collective-permute-done.4), channel_id=1, source_target_pairs={{0,1},{1,0},{2,3},{3,2},{4,5},{5,4},{6,7},{7,6},{8,9},{9,8},{10,11... | collective-permute-start | bytes 786440 | tf_op jit(solution)/shard_map/ppermute | solution.py:344
  41.3 9.1 %collective-permute-start.7 = (bf16[512,1024]{1,0:T(8,128)(2,1)S(1)}, bf16[512,1024]{1,0:T(8,128)(2,1)}, u32[]{:S(2)}, u32[]{:S(2)}) collective-permute-start(bf16[512,1024]{1,0:T(8,128)(2,1)S(1)} %pad_maximum_fusion.1.w_mine), channel_id=1, source_target_pairs={{0,4},{4,0},{8,12},{12,8},{16,20},{20,16},{24,28},{28,24},{1,5},{5... | collective-permute-start | bytes 3145736 | tf_op jit(solution)/shard_map/ppermute | solution.py:344
  41.4 14.3 %collective-permute-start.11 = (bf16[512,1024]{1,0:T(8,128)(2,1)}, bf16[512,1024]{1,0:T(8,128)(2,1)}, u32[]{:S(2)}, u32[]{:S(2)}) collective-permute-start(bf16[512,1024]{1,0:T(8,128)(2,1)} %pad_maximum_fusion.refs_7_), channel_id=1, source_target_pairs={{0,4},{4,0},{8,12},{12,8},{16,20},{20,16},{24,28},{28,24},{1,5},{5... | collective-permute-start | bytes 3145736 | tf_op jit(solution)/shard_map/ppermute | solution.py:344
  48.1 7.6 %collective-permute-start.12 = (bf16[512,1024]{1,0:T(8,128)(2,1)}, bf16[512,1024]{1,0:T(8,128)(2,1)}, u32[]{:S(2)}, u32[]{:S(2)}) collective-permute-start(bf16[512,1024]{1,0:T(8,128)(2,1)} %collective-permute-done.9.refs_8_), channel_id=1, source_target_pairs={{0,4},{4,0},{8,12},{12,8},{16,20},{20,16},{24,28},{28,24},{1,5},{5... | collective-permute-start | bytes 3145736 | tf_op jit(solution)/shard_map/ppermute | solution.py:344
  48.2 7.5 %collective-permute-start.13 = (bf16[256,1024]{1,0:T(8,128)(2,1)S(1)}, bf16[256,1024]{1,0:T(8,128)(2,1)}, u32[]{:S(2)}, u32[]{:S(2)}) collective-permute-start(bf16[256,1024]{1,0:T(8,128)(2,1)S(1)} %pad_maximum_fusion.5.refs_11_.refs_5_), channel_id=1, source_target_pairs={{0,4},{4,0},{8,12},{12,8},{16,20},{20,16},{24,28},{28,24},{1,5},{5... | collective-permute-start | bytes 1572872 | tf_op jit(solution)/shard_map/ppermute | solution.py:344
  48.8 6.9 %collective-permute-start.14 = (bf16[256,1024]{1,0:T(8,128)(2,1)S(1)}, bf16[256,1024]{1,0:T(8,128)(2,1)}, u32[]{:S(2)}, u32[]{:S(2)}) collective-permute-start(bf16[256,1024]{1,0:T(8,128)(2,1)S(1)} %collective-permute-done.10.refs_12_.refs_6_), channel_id=1, source_target_pairs={{0,4},{4,0},{8,12},{12,8},{16,20},{20,16},{24,28},{28,24},{1,5},{5... | collective-permute-start | bytes 1572872 | tf_op jit(solution)/shard_map/ppermute | solution.py:344
  69.2 8.7 %collective-permute-start.15 = (bf16[128,1024]{1,0:T(8,128)(2,1)S(1)}, bf16[128,1024]{1,0:T(8,128)(2,1)S(1)}, u32[]{:S(2)}, u32[]{:S(2)}) collective-permute-start(bf16[128,1024]{1,0:T(8,128)(2,1)S(1)} %get-tuple-element.136), channel_id=1, source_target_pairs={{0,1},{1,0},{2,3},{3,2},{4,5},{5,4},{6,7},{7,6},{8,9},{9,8},{10,11... | collective-permute-start | bytes 786440 | tf_op jit(solution)/shard_map/ppermute | solution.py:344
  77.9 5.7 %collective-permute-start.18 = (bf16[1536,1024]{1,0:T(8,128)(2,1)S(1)}, bf16[1536,1024]{1,0:T(8,128)(2,1)S(1)}, u32[]{:S(2)}, u32[]{:S(2)}) collective-permute-start(bf16[1536,1024]{1,0:T(8,128)(2,1)S(1)} %get-tuple-element.147), channel_id=1, source_target_pairs={{0,4},{4,0},{8,12},{12,8},{16,20},{20,16},{24,28},{28,24},{1,5},{5... | collective-permute-start | bytes 9437192 | tf_op jit(solution)/shard_map/ppermute | solution.py:344
  78.8 15.7 %collective-permute-start.17 = (bf16[128,1024]{1,0:T(8,128)(2,1)}, bf16[128,1024]{1,0:T(8,128)(2,1)S(1)}, u32[]{:S(2)}, u32[]{:S(2)}) collective-permute-start(bf16[128,1024]{1,0:T(8,128)(2,1)} %add_convert_fusion.6), channel_id=1, source_target_pairs={{0,2},{1,3},{2,0},{3,1},{4,6},{5,7},{6,4},{7,5},{8,10},{9,11},{10,... | collective-permute-start | bytes 786440 | tf_op jit(solution)/shard_map/ppermute | solution.py:344
  81.8 13.4 %collective-permute-start.16 = (bf16[128,1024]{1,0:T(8,128)(2,1)}, bf16[128,1024]{1,0:T(8,128)(2,1)}, u32[]{:S(2)}, u32[]{:S(2)}) collective-permute-start(bf16[128,1024]{1,0:T(8,128)(2,1)} %get-tuple-element.142), channel_id=1, source_target_pairs={{0,1},{1,0},{2,3},{3,2},{4,5},{5,4},{6,7},{7,6},{8,9},{9,8},{10,11... | collective-permute-start | bytes 786440 | tf_op jit(solution)/shard_map/ppermute | solution.py:344
  88.2 41.2 %collective-permute-start.22 = (bf16[512,1024]{1,0:T(8,128)(2,1)}, bf16[512,1024]{1,0:T(8,128)(2,1)}, u32[]{:S(2)}, u32[]{:S(2)}) collective-permute-start(bf16[512,1024]{1,0:T(8,128)(2,1)} %get-tuple-element.169), channel_id=1, source_target_pairs={{0,16},{4,20},{8,24},{12,28},{16,0},{20,4},{24,8},{28,12},{1,17},{... | collective-permute-start | bytes 3145736 | tf_op jit(solution)/shard_map/ppermute | solution.py:344
  96.4 13.8 %collective-permute-start.19 = (bf16[128,1024]{1,0:T(8,128)(2,1)S(1)}, bf16[128,1024]{1,0:T(8,128)(2,1)S(1)}, u32[]{:S(2)}, u32[]{:S(2)}) collective-permute-start(bf16[128,1024]{1,0:T(8,128)(2,1)S(1)} %get-tuple-element.157.refs_8_), channel_id=1, source_target_pairs={{0,2},{1,3},{2,0},{3,1},{4,6},{5,7},{6,4},{7,5},{8,10},{9,11},{10,... | collective-permute-start | bytes 786440 | tf_op jit(solution)/shard_map/ppermute | solution.py:344
  97.0 13.2 %collective-permute-start.20 = (bf16[128,1024]{1,0:T(8,128)(2,1)S(1)}, bf16[128,1024]{1,0:T(8,128)(2,1)S(1)}, u32[]{:S(2)}, u32[]{:S(2)}) collective-permute-start(bf16[128,1024]{1,0:T(8,128)(2,1)S(1)} %get-tuple-element.157.refs_8_), channel_id=1, source_target_pairs={{0,1},{1,0},{2,3},{3,2},{4,5},{5,4},{6,7},{7,6},{8,9},{9,8},{10,11... | collective-permute-start | bytes 786440 | tf_op jit(solution)/shard_map/ppermute | solution.py:344
  110.2 7.3 %collective-permute-start.21 = (bf16[128,1024]{1,0:T(8,128)(2,1)S(1)}, bf16[128,1024]{1,0:T(8,128)(2,1)S(1)}, u32[]{:S(2)}, u32[]{:S(2)}) collective-permute-start(bf16[128,1024]{1,0:T(8,128)(2,1)S(1)} %collective-permute-done.19.refs_10_), channel_id=1, source_target_pairs={{0,1},{1,0},{2,3},{3,2},{4,5},{5,4},{6,7},{7,6},{8,9},{9,8},{10,11... | collective-permute-start | bytes 786440 | tf_op jit(solution)/shard_map/ppermute | solution.py:344
  110.3 19.1 %collective-permute-start.23 = (bf16[256,1024]{1,0:T(8,128)(2,1)S(1)}, bf16[256,1024]{1,0:T(8,128)(2,1)S(1)}, u32[]{:S(2)}, u32[]{:S(2)}) collective-permute-start(bf16[256,1024]{1,0:T(8,128)(2,1)S(1)} %copy-done.34), channel_id=1, source_target_pairs={{0,8},{4,12},{8,0},{12,4},{16,24},{20,28},{24,16},{28,20},{1,9},{5... | collective-permute-start | bytes 1572872 | tf_op jit(solution)/shard_map/ppermute | solution.py:344
  117.5 11.9 %collective-permute-start.24 = (bf16[128,1024]{1,0:T(8,128)(2,1)}, bf16[128,1024]{1,0:T(8,128)(2,1)}, u32[]{:S(2)}, u32[]{:S(2)}) collective-permute-start(bf16[128,1024]{1,0:T(8,128)(2,1)} %get-tuple-element.171), channel_id=1, source_target_pairs={{0,1},{1,0},{2,3},{3,2},{4,5},{5,4},{6,7},{7,6},{8,9},{9,8},{10,11... | collective-permute-start | bytes 786440 | tf_op jit(solution)/shard_map/ppermute | solution.py:344
  129.5 6.6 %collective-permute-start.25 = (bf16[128,1024]{1,0:T(8,128)(2,1)}, bf16[128,1024]{1,0:T(8,128)(2,1)S(1)}, u32[]{:S(2)}, u32[]{:S(2)}) collective-permute-start(bf16[128,1024]{1,0:T(8,128)(2,1)} %get-tuple-element.175), channel_id=1, source_target_pairs={{0,1},{1,0},{2,3},{3,2},{4,5},{5,4},{6,7},{7,6},{8,9},{9,8},{10,11... | collective-permute-start | bytes 786440 | tf_op jit(solution)/shard_map/ppermute | solution.py:344
  136.1 2.3 %collective-permute-start.30 = (bf16[768,512]{1,0:T(8,128)(2,1)S(1)}, bf16[768,512]{1,0:T(8,128)(2,1)S(1)}, u32[]{:S(2)}, u32[]{:S(2)}) collective-permute-start(bf16[768,512]{1,0:T(8,128)(2,1)S(1)} %get-tuple-element.191), channel_id=1, source_target_pairs={{0,4},{4,0},{8,12},{12,8},{16,20},{20,16},{24,28},{28,24},{1,5},{5... | collective-permute-start | bytes 2359304 | tf_op jit(solution)/shard_map/ppermute | solution.py:344
  136.2 30.8 %collective-permute-start.28 = (bf16[256,1024]{1,0:T(8,128)(2,1)S(1)}, bf16[256,1024]{1,0:T(8,128)(2,1)S(1)}, u32[]{:S(2)}, u32[]{:S(2)}) collective-permute-start(bf16[256,1024]{1,0:T(8,128)(2,1)S(1)} %slice.128), channel_id=1, source_target_pairs={{0,8},{4,12},{8,0},{12,4},{16,24},{20,28},{24,16},{28,20},{1,9},{5... | collective-permute-start | bytes 1572872 | tf_op jit(solution)/shard_map/ppermute | solution.py:344
  138.7 20.3 %collective-permute-start.31 = (bf16[384,512]{1,0:T(8,128)(2,1)S(1)}, bf16[384,512]{1,0:T(8,128)(2,1)S(1)}, u32[]{:S(2)}, u32[]{:S(2)}) collective-permute-start(bf16[384,512]{1,0:T(8,128)(2,1)S(1)} %get-tuple-element.215), channel_id=1, source_target_pairs={{0,8},{4,12},{8,0},{12,4},{16,24},{20,28},{24,16},{28,20},{1,9},{5... | collective-permute-start | bytes 1179656 | tf_op jit(solution)/shard_map/ppermute | solution.py:344
  139.7 19.8 %collective-permute-start.32 = (bf16[384,512]{1,0:T(8,128)(2,1)S(1)}, bf16[384,512]{1,0:T(8,128)(2,1)S(1)}, u32[]{:S(2)}, u32[]{:S(2)}) collective-permute-start(bf16[384,512]{1,0:T(8,128)(2,1)S(1)} %get-tuple-element.216), channel_id=1, source_target_pairs={{0,16},{4,20},{8,24},{12,28},{16,0},{20,4},{24,8},{28,12},{1,17},{... | collective-permute-start | bytes 1179656 | tf_op jit(solution)/shard_map/ppermute | solution.py:344
  140.4 26.6 %collective-permute-start.27 = (bf16[256,1024]{1,0:T(8,128)(2,1)S(1)}, bf16[256,1024]{1,0:T(8,128)(2,1)S(1)}, u32[]{:S(2)}, u32[]{:S(2)}) collective-permute-start(bf16[256,1024]{1,0:T(8,128)(2,1)S(1)} %add_convert_fusion.1), channel_id=1, source_target_pairs={{0,2},{1,3},{2,0},{3,1},{4,6},{5,7},{6,4},{7,5},{8,10},{9,11},{10,... | collective-permute-start | bytes 1572872 | tf_op jit(solution)/shard_map/ppermute | solution.py:344
  143.3 23.7 %collective-permute-start.26 = (bf16[256,1024]{1,0:T(8,128)(2,1)S(1)}, bf16[256,1024]{1,0:T(8,128)(2,1)S(1)}, u32[]{:S(2)}, u32[]{:S(2)}) collective-permute-start(bf16[256,1024]{1,0:T(8,128)(2,1)S(1)} %copy-done.56), channel_id=1, source_target_pairs={{0,1},{1,0},{2,3},{3,2},{4,5},{5,4},{6,7},{7,6},{8,9},{9,8},{10,11... | collective-permute-start | bytes 1572872 | tf_op jit(solution)/shard_map/ppermute | solution.py:344
  159.0 7.9 %collective-permute-start.29 = (bf16[128,1024]{1,0:T(8,128)(2,1)S(1)}, bf16[128,1024]{1,0:T(8,128)(2,1)S(1)}, u32[]{:S(2)}, u32[]{:S(2)}) collective-permute-start(bf16[128,1024]{1,0:T(8,128)(2,1)S(1)} %slice.129), channel_id=1, source_target_pairs={{0,16},{4,20},{8,24},{12,28},{16,0},{20,4},{24,8},{28,12},{1,17},{... | collective-permute-start | bytes 786440 | tf_op jit(solution)/shard_map/ppermute | solution.py:344
  167.8 9.9 %collective-permute-start.38 = (bf16[384,512]{1,0:T(8,128)(2,1)S(1)}, bf16[384,512]{1,0:T(8,128)(2,1)S(1)}, u32[]{:S(2)}, u32[]{:S(2)}) collective-permute-start(bf16[384,512]{1,0:T(8,128)(2,1)S(1)} %get-tuple-element.211), channel_id=1, source_target_pairs={{0,16},{4,20},{8,24},{12,28},{16,0},{20,4},{24,8},{28,12},{1,17},{... | collective-permute-start | bytes 1179656 | tf_op jit(solution)/shard_map/ppermute | solution.py:344
  169.2 9.5 %collective-permute-start.39 = (bf16[384,512]{1,0:T(8,128)(2,1)S(1)}, bf16[384,512]{1,0:T(8,128)(2,1)}, u32[]{:S(2)}, u32[]{:S(2)}) collective-permute-start(bf16[384,512]{1,0:T(8,128)(2,1)S(1)} %get-tuple-element.212), channel_id=1, source_target_pairs={{0,8},{4,12},{8,0},{12,4},{16,24},{20,28},{24,16},{28,20},{1,9},{5... | collective-permute-start | bytes 1179656 | tf_op jit(solution)/shard_map/ppermute | solution.py:344
  170.2 24.3 %collective-permute-start.33 = (bf16[256,1024]{1,0:T(8,128)(2,1)S(1)}, bf16[256,1024]{1,0:T(8,128)(2,1)}, u32[]{:S(2)}, u32[]{:S(2)}) collective-permute-start(bf16[256,1024]{1,0:T(8,128)(2,1)S(1)} %finish.1), channel_id=1, source_target_pairs={{0,2},{1,3},{2,0},{3,1},{4,6},{5,7},{6,4},{7,5},{8,10},{9,11},{10,... | collective-permute-start | bytes 1572872 | tf_op jit(solution)/shard_map/ppermute | solution.py:344
  172.0 22.5 %collective-permute-start.34 = (bf16[256,1024]{1,0:T(8,128)(2,1)S(1)}, bf16[256,1024]{1,0:T(8,128)(2,1)S(1)}, u32[]{:S(2)}, u32[]{:S(2)}) collective-permute-start(bf16[256,1024]{1,0:T(8,128)(2,1)S(1)} %finish.1), channel_id=1, source_target_pairs={{0,1},{1,0},{2,3},{3,2},{4,5},{5,4},{6,7},{7,6},{8,9},{9,8},{10,11... | collective-permute-start | bytes 1572872 | tf_op jit(solution)/shard_map/ppermute | solution.py:344
  173.0 10.4 %collective-permute-start.35 = (f32[9,1024]{1,0:T(8,128)S(1)}, f32[9,1024]{1,0:T(8,128)S(1)}, u32[]{:S(2)}, u32[]{:S(2)}) collective-permute-start(f32[9,1024]{1,0:T(8,128)S(1)} %pad_maximum_fusion.7), channel_id=1, source_target_pairs={{0,4},{4,0},{8,12},{12,8},{16,20},{20,16},{24,28},{28,24},{1,5},{5... | collective-permute-start | bytes 110600 | tf_op jit(solution)/shard_map/ppermute | solution.py:344
  180.0 12.3 %collective-permute-start.40 = (bf16[768,512]{1,0:T(8,128)(2,1)S(1)}, bf16[768,512]{1,0:T(8,128)(2,1)S(1)}, u32[]{:S(2)}, u32[]{:S(2)}) collective-permute-start(bf16[768,512]{1,0:T(8,128)(2,1)S(1)} %pad_maximum_fusion.4), channel_id=1, source_target_pairs={{0,4},{4,0},{8,12},{12,8},{16,20},{20,16},{24,28},{28,24},{1,5},{5... | collective-permute-start | bytes 2359304 | tf_op jit(solution)/shard_map/ppermute | solution.py:344
  183.4 4.5 %collective-permute-start.36 = (f32[9,1024]{1,0:T(8,128)S(1)}, f32[9,1024]{1,0:T(8,128)S(1)}, u32[]{:S(2)}, u32[]{:S(2)}) collective-permute-start(f32[9,1024]{1,0:T(8,128)S(1)} %add.76), channel_id=1, source_target_pairs={{0,8},{4,12},{8,0},{12,4},{16,24},{20,28},{24,16},{28,20},{1,9},{5... | collective-permute-start | bytes 110600 | tf_op jit(solution)/shard_map/ppermute | solution.py:344
  187.9 4.3 %collective-permute-start.37 = (f32[9,1024]{1,0:T(8,128)S(1)}, f32[9,1024]{1,0:T(8,128)S(1)}, u32[]{:S(2)}, u32[]{:S(2)}) collective-permute-start(f32[9,1024]{1,0:T(8,128)S(1)} %add.77), channel_id=1, source_target_pairs={{0,16},{4,20},{8,24},{12,28},{16,0},{20,4},{24,8},{28,12},{1,17},{... | collective-permute-start | bytes 110600 | tf_op jit(solution)/shard_map/ppermute | solution.py:344
  194.5 5.0 %collective-permute-start.42 = (f32[10,1024]{1,0:T(8,128)S(1)}, f32[10,1024]{1,0:T(8,128)S(1)}, u32[]{:S(2)}, u32[]{:S(2)}) collective-permute-start(f32[10,1024]{1,0:T(8,128)S(1)} %pad_maximum_fusion.8), channel_id=1, source_target_pairs={{0,1},{1,0},{2,3},{3,2},{4,5},{5,4},{6,7},{7,6},{8,9},{9,8},{10,11... | collective-permute-start | bytes 122888 | tf_op jit(solution)/shard_map/ppermute | solution.py:344
  195.4 15.2 %collective-permute-start.41 = (bf16[256,1024]{1,0:T(8,128)(2,1)}, bf16[256,1024]{1,0:T(8,128)(2,1)}, u32[]{:S(2)}, u32[]{:S(2)}) collective-permute-start(bf16[256,1024]{1,0:T(8,128)(2,1)} %collective-permute-done.33), channel_id=1, source_target_pairs={{0,1},{1,0},{2,3},{3,2},{4,5},{5,4},{6,7},{7,6},{8,9},{9,8},{10,11... | collective-permute-start | bytes 1572872 | tf_op jit(solution)/shard_map/ppermute | solution.py:344
  199.5 9.8 %collective-permute-start.43 = (f32[10,1024]{1,0:T(8,128)S(1)}, f32[10,1024]{1,0:T(8,128)S(1)}, u32[]{:S(2)}, u32[]{:S(2)}) collective-permute-start(f32[10,1024]{1,0:T(8,128)S(1)} %add.84), channel_id=1, source_target_pairs={{0,2},{1,3},{2,0},{3,1},{4,6},{5,7},{6,4},{7,5},{8,10},{9,11},{10,... | collective-permute-start | bytes 122888 | tf_op jit(solution)/shard_map/ppermute | solution.py:344
  (54 other events, 428.9 us)

commit v8 on v7

--- a/solution.py
+++ b/solution.py
@@ -1141,10 +1141,13 @@
         qkv_flat.astype(wide) * summed[:model_width], 1
     ) / gain_attn
     small = jnp.concatenate([small, gain_part[None]])
-    far, near, small, summed = lax.optimization_barrier((far, near, small, summed))
+    far, near = lax.optimization_barrier((far, near))
     for bit in (1, 2):
         small = small + exchange(small, "tensor", bit)
-    blocks = [block, near, far, exchange(far, "tensor", 1)]
+    both, qkv_summed, output_summed = lax.optimization_barrier(
+        (exchange(far, "tensor", 1), qkv_summed, output_summed)
+    )
+    blocks = [block, near, far, both]
     layer_here = in_order([block[:span] for block in blocks])
     in_here = in_order([block[span:] for block in blocks])
     return (

time: 214 us -> 218 us (1.019)
  local copies, waits for them, and re-layouts: 18.9 us -> 22.1 us
    unnamed x116 -> x110, local copies, waits for them, and re-layouts: 10.8 us -> 11.1 us
  transfers between devices with their start and end apart: 44 -> 44, of which waited for: 25 -> 24; matrix products, arithmetic and copies ran while one was open for 10% -> 12% of each run, Pallas kernels for 16% -> 16%
where the time goes in v8:
time: 218 us; the launch traced here: 217 us
  waiting for transfers between devices  89 us (41%)
  Pallas kernels  46.8 us (21%)
  starting transfers between devices  42.6 us (20%)
  local copies, waits for them, and re-layouts  22.1 us (10%)
  other arithmetic  15.4 us (7%)
    ppermute x44, waiting for transfers between devices, exchange(): lax.ppermute(array_in, axis_name, [(i, i ^ bits) for i in range(count)])  89 us
    ppermute x44, starting transfers between devices, exchange(): lax.ppermute(array_in, axis_name, [(i, i ^ bits) for i in range(count)])  42.6 us
    pallas_call x1, Pallas kernels, on_device(): pl.pallas_call(functools.partial(middle_kernel, tensor_count), out_shape=...  12.4 us
    pallas_call x1, Pallas kernels, on_device(): pl.pallas_call(functools.partial(attend_back_kernel, tensor_count), out_s...  11.2 us
    unnamed x110, local copies, waits for them, and re-layouts  11.1 us
    pallas_call x1, Pallas kernels, on_device(): pl.pallas_call(functools.partial(weight_grad_kernel, tensor_count), out_s...  7.37 us
    pallas_call x1, Pallas kernels, on_device(): pl.pallas_call(attend_kernel, out_shape=kept + (shaped((token_count, head...  5.43 us
  transfers between devices with their start and end apart: 44, of which 24 were waited for; matrix products, arithmetic and copies ran while one was open for 12% of the time, Pallas kernels for 16%

profile of v8, /device:TPU:0, one launch (start us, length us, event | category | flops | bytes accessed | tf_op | source)
XLA Modules:
  0.0 217.5 jit_solution(3016674724720253271)
XLA Ops:
  0.7 3.0 %collective-permute-start = (bf16[256,1024]{1,0:T(8,128)(2,1)}, bf16[256,1024]{1,0:T(8,128)(2,1)S(1)}, u32[]{:S(2)}, u32[]{:S(2)}) collective-permute-start(bf16[256,1024]{1,0:T(8,128)(2,1)} %bitcast.34), channel_id=1, source_target_pairs={{0,8},{4,12},{8,0},{12,4},{16,24},{20,28},{24,16},{28,20},{1,9},{5... | collective-permute-start | bytes 1572872 | tf_op jit(solution)/shard_map/ppermute | solution.py:344
  4.8 2.7 %collective-permute-start.2 = (bf16[128,1024]{1,0:T(8,128)(2,1)S(1)}, bf16[128,1024]{1,0:T(8,128)(2,1)S(1)}, u32[]{:S(2)}, u32[]{:S(2)}) collective-permute-start(bf16[128,1024]{1,0:T(8,128)(2,1)S(1)} %slice_select_fusion), channel_id=1, source_target_pairs={{0,2},{1,3},{2,0},{3,1},{4,6},{5,7},{6,4},{7,5},{8,10},{9,11},{10,... | collective-permute-start | bytes 786440 | tf_op jit(solution)/shard_map/ppermute | solution.py:344
  7.4 1.6 collective-permute-start.3
  9.0 1.5 collective-permute-start.1
  10.5 1.5 copy.25
  12.1 5.4 %attend.1 = (bf16[2,4,256,128]{3,2,1,0:T(8,128)(2,1)S(1)}, bf16[2,512,128]{2,1,0:T(8,128)(2,1)S(1)}, bf16[2,4,256,512]{3,2,1,0:T(8,128)(2,1)S(1)}, bf16[512,256]{1,0:T(8,128)(2,1)S(1)}) custom-call(s32[1,3]{1,0:T(1,128)S(1)} %copy-done.32, bf16[512,1024]{1,0:T(8,128)(2,1)S(1)} %copy-done.2, f32[1,1024]{1,0:T(1,128)S(1)} %bitcast.25, ...), custom_call_target="tpu_custom_call" | custom-call | tf_op jit(solution)/shard_map/attend/pallas_call | solution.py:903
  17.6 1.6 collective-permute-done.2
  20.5 1.5 collective-permute-start.9
  22.0 1.3 collective-permute-start.4
  23.3 2.4 %collective-permute-start.5 = (bf16[512,256]{1,0:T(8,128)(2,1)S(1)}, bf16[512,256]{1,0:T(8,128)(2,1)S(1)}, u32[]{:S(2)}, u32[]{:S(2)}) collective-permute-start(bf16[512,256]{1,0:T(8,128)(2,1)S(1)} %get-tuple-element.115.attended), channel_id=1, source_target_pairs={{0,1},{1,0},{2,3},{3,2},{4,5},{5,4},{6,7},{7,6},{8,9},{9,8},{10,11... | collective-permute-start | bytes 786440 | tf_op jit(solution)/shard_map/ppermute | solution.py:344
  26.6 8.7 %collective-permute-done.4 = bf16[512,256]{1,0:T(8,128)(2,1)S(1)} collective-permute-done((bf16[512,256]{1,0:T(8,128)(2,1)S(1)}, bf16[512,256]{1,0:T(8,128)(2,1)S(1)}, u32[]{:S(2)}, u32[]{:S(2)}) %collective-permute-start.4) | collective-permute-done | bytes 262176 | tf_op jit(solution)/shard_map/ppermute | solution.py:344
  35.3 1.3 collective-permute-done.5
  36.6 4.4 %collective-permute-done.6 = bf16[128,1024]{1,0:T(8,128)(2,1)S(1)} collective-permute-done((bf16[128,1024]{1,0:T(8,128)(2,1)S(1)}, bf16[128,1024]{1,0:T(8,128)(2,1)S(1)}, u32[]{:S(2)}, u32[]{:S(2)}) %collective-permute-start.6) | collective-permute-done | bytes 262176 | tf_op jit(solution)/shard_map/ppermute | solution.py:344
  41.9 6.2 %collective-permute-done.8 = bf16[512,256]{1,0:T(8,128)(2,1)S(1)} collective-permute-done((bf16[512,256]{1,0:T(8,128)(2,1)S(1)}, bf16[512,256]{1,0:T(8,128)(2,1)S(1)}, u32[]{:S(2)}, u32[]{:S(2)}) %collective-permute-start.8) | collective-permute-done | bytes 262176 | tf_op jit(solution)/shard_map/ppermute | solution.py:344
  49.1 1.3 pad_maximum_fusion.2.heads
  51.7 4.0 %branch.1 = (f32[512,1024]{1,0:T(8,128)S(1)}, f32[512,1]{1,0:T(8,128)S(1)}, bf16[512,1024]{1,0:T(8,128)(2,1)S(1)}, f32[512,128]{1,0:T(8,128)S(1)}) custom-call(s32[2]{0:T(128)S(1)} %pad_add_fusion.place.refs_0_, f32[1,1024]{1,0:T(1,128)S(1)} %bitcast.28, bf16[128,1024]{1,0:T(8,128)(2,1)S(1)} %pad.4.router.refs_1_, s32[512,2]{1,0:T(8,128)S(1)} %copy.22.routes, ...), custom_call_target="tpu_custom_call" | custom-call | tf_op jit(solution)/shard_map/branch/pallas_call | solution.py:939
  56.8 12.4 %middle.1 = (f32[128,1024]{1,0:T(8,128)S(1)}, bf16[128,1024]{1,0:T(8,128)(2,1)}, bf16[128,1024]{1,0:T(8,128)(2,1)S(1)}, bf16[128,1024]{1,0:T(8,128)(2,1)S(1)}, f...) custom-call(s32[2]{0:T(128)S(1)} %pad_add_fusion.place.refs_0_, ...), custom_call_target="tpu_custom_call" | custom-call | tf_op jit(solution)/shard_map/middle/pallas_call | solution.py:962
  69.5 7.4 %weight_grad.1 = (f32[128,1024]{1,0:T(8,128)S(1)}, bf16[128,1024]{1,0:T(8,128)(2,1)S(1)}, bf16[128,1024]{1,0:T(8,128)(2,1)S(1)}, bf16[128,1024]{1,0:T(8,128)(2,1...) custom-call(s32[2]{0:T(128)S(1)} %pad_add_fusion.place.refs_0_, ...), custom_call_target="tpu_custom_call" | custom-call | tf_op jit(solution)/shard_map/weight_grad/pallas_call | solution.py:1000
  78.8 3.0 %collective-permute-start.17 = (bf16[128,1024]{1,0:T(8,128)(2,1)}, bf16[128,1024]{1,0:T(8,128)(2,1)S(1)}, u32[]{:S(2)}, u32[]{:S(2)}) collective-permute-start(bf16[128,1024]{1,0:T(8,128)(2,1)} %add_convert_fusion.6), channel_id=1, source_target_pairs={{0,2},{1,3},{2,0},{3,1},{4,6},{5,7},{6,4},{7,5},{8,10},{9,11},{10,... | collective-permute-start | bytes 786440 | tf_op jit(solution)/shard_map/ppermute | solution.py:344
  83.6 1.6 add_grads.1
  85.1 1.3 copy-done.7
  88.7 5.7 %collective-permute-done.17.far = bf16[128,1024]{1,0:T(8,128)(2,1)S(1)} collective-permute-done((bf16[128,1024]{1,0:T(8,128)(2,1)}, bf16[128,1024]{1,0:T(8,128)(2,1)S(1)}, u32[]{:S(2)}, u32[]{:S(2)}) %collective-permute-start.17) | collective-permute-done | bytes 262176 | tf_op jit(solution)/shard_map/ppermute | solution.py:344
  97.0 1.9 collective-permute-start.20
  98.9 11.3 %collective-permute-done.19.refs_10_ = bf16[128,1024]{1,0:T(8,128)(2,1)S(1)} collective-permute-done((bf16[128,1024]{1,0:T(8,128)(2,1)S(1)}, bf16[128,1024]{1,0:T(8,128)(2,1)S(1)}, u32[]{:S(2)}, u32[]{:S(2)}) %collective-permute-start.19) | collective-permute-done | bytes 262176 | tf_op jit(solution)/shard_map/ppermute | solution.py:344
  111.0 6.4 %collective-permute-done.21.refs_11_ = bf16[128,1024]{1,0:T(8,128)(2,1)S(1)} collective-permute-done((bf16[128,1024]{1,0:T(8,128)(2,1)S(1)}, bf16[128,1024]{1,0:T(8,128)(2,1)S(1)}, u32[]{:S(2)}, u32[]{:S(2)}) %collective-permute-start.21) | collective-permute-done | bytes 262176 | tf_op jit(solution)/shard_map/ppermute | solution.py:344
  118.2 11.2 %attend_back.1 = (f32[256,1024]{1,0:T(8,128)}, bf16[256,1024]{1,0:T(8,128)(2,1)}, bf16[256,1024]{1,0:T(8,128)(2,1)}, bf16[128,1024]{1,0:T(8,128)(2,1)}, bf16[512...) custom-call(s32[2]{0:T(128)} %copy-done.30, bf16[256,1024]{1,0:T(8,128)(2,1)} %refs_1_.1, ...), custom_call_target="tpu_custom_call" | custom-call | tf_op jit(solution)/shard_map/attend_back/pallas_call | solution.py:1052
  129.5 1.4 collective-permute-start.25
  130.9 1.5 convert_add_fusion
  132.5 3.2 %attend_grad.1 = (f32[768,512]{1,0:T(8,128)S(1)}, bf16[768,512]{1,0:T(8,128)(2,1)S(1)}) custom-call(s32[2]{0:T(128)S(1)} %copy-done.31, bf16[512,1024]{1,0:T(8,128)(2,1)S(1)} %copy-done.2, f32[1,1024]{1,0:T(1,128)S(1)} %bitcast.26, bf16[512,512]{1,0:T(8,128)(2,1)S(1)} %copy-done.21, bf16[512,256]{1,0:T(8,128)(2,1)S(1)} %copy-done.18, ...), custom_call_target="tpu_custom_call" | custom-call | tf_op jit(solution)/shard_map/attend_grad/pallas_call | solution.py:1094
  140.6 1.4 collective-permute-start.31
  143.5 2.2 %collective-permute-start.27 = (bf16[256,1024]{1,0:T(8,128)(2,1)}, bf16[256,1024]{1,0:T(8,128)(2,1)S(1)}, u32[]{:S(2)}, u32[]{:S(2)}) collective-permute-start(bf16[256,1024]{1,0:T(8,128)(2,1)} %add_convert_fusion.1), channel_id=1, source_target_pairs={{0,2},{1,3},{2,0},{3,1},{4,6},{5,7},{6,4},{7,5},{8,10},{9,11},{10,... | collective-permute-start | bytes 1572872 | tf_op jit(solution)/shard_map/ppermute | solution.py:344
  145.7 1.3 collective-permute-start.26
  148.2 12.6 %collective-permute-done.31 = bf16[384,512]{1,0:T(8,128)(2,1)} collective-permute-done((bf16[384,512]{1,0:T(8,128)(2,1)}, bf16[384,512]{1,0:T(8,128)(2,1)}, u32[]{:S(2)}, u32[]{:S(2)}) %collective-permute-start.31) | collective-permute-done | bytes 393248 | tf_op jit(solution)/shard_map/ppermute | solution.py:344
  161.3 1.6 add_convert_fusion.5
  162.9 5.8 %collective-permute-done.29 = bf16[128,1024]{1,0:T(8,128)(2,1)S(1)} collective-permute-done((bf16[128,1024]{1,0:T(8,128)(2,1)S(1)}, bf16[128,1024]{1,0:T(8,128)(2,1)S(1)}, u32[]{:S(2)}, u32[]{:S(2)}) %collective-permute-start.29) | collective-permute-done | bytes 262176 | tf_op jit(solution)/shard_map/ppermute | solution.py:344
  171.5 2.0 collective-permute-start.34
  173.5 1.6 collective-permute-start.36
  175.8 2.1 convert_add_fusion.1
  178.8 1.4 collective-permute-start.40
  180.2 4.9 %collective-permute-done.36 = bf16[384,512]{1,0:T(8,128)(2,1)S(1)} collective-permute-done((bf16[384,512]{1,0:T(8,128)(2,1)S(1)}, bf16[384,512]{1,0:T(8,128)(2,1)S(1)}, u32[]{:S(2)}, u32[]{:S(2)}) %collective-permute-start.36) | collective-permute-done | bytes 393248 | tf_op jit(solution)/shard_map/ppermute | solution.py:344
  185.1 1.9 collective-permute-done.37
  188.5 3.6 %collective-permute-done.41 = f32[9,1024]{1,0:T(8,128)S(1)} collective-permute-done((f32[9,1024]{1,0:T(8,128)S(1)}, f32[9,1024]{1,0:T(8,128)S(1)}, u32[]{:S(2)}, u32[]{:S(2)}) %collective-permute-start.41) | collective-permute-done | bytes 36896 | tf_op jit(solution)/shard_map/ppermute | solution.py:344
  192.1 3.6 %collective-permute-done.33 = bf16[256,1024]{1,0:T(8,128)(2,1)} collective-permute-done((bf16[256,1024]{1,0:T(8,128)(2,1)S(1)}, bf16[256,1024]{1,0:T(8,128)(2,1)}, u32[]{:S(2)}, u32[]{:S(2)}) %collective-permute-start.33) | collective-permute-done | bytes 524320 | tf_op jit(solution)/shard_map/ppermute | solution.py:344
  200.8 2.1 collective-permute-start.42
  204.1 2.3 %reshape.44 = f32[1024,2,256]{2,1,0:T(2,128)} reshape(f32[1024,512]{1,0:T(8,128)S(1)} %get-tuple-element.210) | data formatting | bytes 4194304 | tf_op jit(solution)/shard_map/reshape | solution.py:1137
  206.4 3.6 %collective-permute-done.35 = bf16[256,1024]{1,0:T(8,128)(2,1)} collective-permute-done((bf16[256,1024]{1,0:T(8,128)(2,1)}, bf16[256,1024]{1,0:T(8,128)(2,1)}, u32[]{:S(2)}, u32[]{:S(2)}) %collective-permute-start.35) | collective-permute-done | bytes 524320 | tf_op jit(solution)/shard_map/ppermute | solution.py:344
  211.7 1.9 slice_dynamic-update-slice_fusion.2
  213.5 2.7 %collective-permute-done.43 = f32[10,1024]{1,0:T(8,128)S(1)} collective-permute-done((f32[10,1024]{1,0:T(8,128)S(1)}, f32[10,1024]{1,0:T(8,128)S(1)}, u32[]{:S(2)}, u32[]{:S(2)}) %collective-permute-start.43) | collective-permute-done | bytes 40992 | tf_op jit(solution)/shard_map/ppermute | solution.py:344
  (207 shorter events, 40.6 us)
Async XLA Ops:
  0.7 18.7 %collective-permute-start = (bf16[256,1024]{1,0:T(8,128)(2,1)}, bf16[256,1024]{1,0:T(8,128)(2,1)S(1)}, u32[]{:S(2)}, u32[]{:S(2)}) collective-permute-start(bf16[256,1024]{1,0:T(8,128)(2,1)} %bitcast.34), channel_id=1, source_target_pairs={{0,8},{4,12},{8,0},{12,4},{16,24},{20,28},{24,16},{28,20},{1,9},{5... | collective-permute-start | bytes 1572872 | tf_op jit(solution)/shard_map/ppermute | solution.py:344
  4.8 14.5 %collective-permute-start.2 = (bf16[128,1024]{1,0:T(8,128)(2,1)S(1)}, bf16[128,1024]{1,0:T(8,128)(2,1)S(1)}, u32[]{:S(2)}, u32[]{:S(2)}) collective-permute-start(bf16[128,1024]{1,0:T(8,128)(2,1)S(1)} %slice_select_fusion), channel_id=1, source_target_pairs={{0,2},{1,3},{2,0},{3,1},{4,6},{5,7},{6,4},{7,5},{8,10},{9,11},{10,... | collective-permute-start | bytes 786440 | tf_op jit(solution)/shard_map/ppermute | solution.py:344
  7.4 12.0 %collective-permute-start.3 = (bf16[128,1024]{1,0:T(8,128)(2,1)S(1)}, bf16[128,1024]{1,0:T(8,128)(2,1)S(1)}, u32[]{:S(2)}, u32[]{:S(2)}) collective-permute-start(bf16[128,1024]{1,0:T(8,128)(2,1)S(1)} %slice_select_fusion), channel_id=1, source_target_pairs={{0,1},{1,0},{2,3},{3,2},{4,5},{5,4},{6,7},{7,6},{8,9},{9,8},{10,11... | collective-permute-start | bytes 786440 | tf_op jit(solution)/shard_map/ppermute | solution.py:344
  9.0 10.4 %collective-permute-start.1 = (bf16[128,1024]{1,0:T(8,128)(2,1)}, bf16[128,1024]{1,0:T(8,128)(2,1)S(1)}, u32[]{:S(2)}, u32[]{:S(2)}) collective-permute-start(bf16[128,1024]{1,0:T(8,128)(2,1)} %bitcast.36), channel_id=1, source_target_pairs={{0,16},{4,20},{8,24},{12,28},{16,0},{20,4},{24,8},{28,12},{1,17},{... | collective-permute-start | bytes 786440 | tf_op jit(solution)/shard_map/ppermute | solution.py:344
  17.5 23.7 %copy-start.6 = (bf16[2,4,256,512]{3,2,1,0:T(8,128)(2,1)}, bf16[2,4,256,512]{3,2,1,0:T(8,128)(2,1)S(1)}, u32[]{:S(2)}) copy-start(bf16[2,4,256,512]{3,2,1,0:T(8,128)(2,1)S(1)} %get-tuple-element.111.refs_4_) | copy-start | bytes 6291460
  20.5 28.3 %copy-start.53 = (s32[512,2]{0,1:T(2,128)S(1)}, s32[512,2]{0,1:T(2,128)}, u32[]{:S(2)}) copy-start(s32[512,2]{0,1:T(2,128)} %param.15) | copy-start | bytes 12292
  20.5 28.5 %copy-start.52 = (bf16[1024,8]{0,1:T(8,128)(2,1)S(1)}, bf16[1024,8]{0,1:T(8,128)(2,1)}, u32[]{:S(2)}) copy-start(bf16[1024,8]{0,1:T(8,128)(2,1)} %param.20) | copy-start | bytes 49156
  20.5 27.6 %collective-permute-start.9 = (bf16[512,1024]{1,0:T(8,128)(2,1)}, bf16[512,1024]{1,0:T(8,128)(2,1)}, u32[]{:S(2)}, u32[]{:S(2)}) collective-permute-start(bf16[512,1024]{1,0:T(8,128)(2,1)} %pad_maximum_fusion.refs_7_), channel_id=1, source_target_pairs={{0,16},{4,20},{8,24},{12,28},{16,0},{20,4},{24,8},{28,12},{1,17},{... | collective-permute-start | bytes 3145736 | tf_op jit(solution)/shard_map/ppermute | solution.py:344
  22.0 13.3 %collective-permute-start.4 = (bf16[512,256]{1,0:T(8,128)(2,1)S(1)}, bf16[512,256]{1,0:T(8,128)(2,1)S(1)}, u32[]{:S(2)}, u32[]{:S(2)}) collective-permute-start(bf16[512,256]{1,0:T(8,128)(2,1)S(1)} %get-tuple-element.115.attended), channel_id=1, source_target_pairs={{0,2},{1,3},{2,0},{3,1},{4,6},{5,7},{6,4},{7,5},{8,10},{9,11},{10,... | collective-permute-start | bytes 786440 | tf_op jit(solution)/shard_map/ppermute | solution.py:344
  23.3 13.3 %collective-permute-start.5 = (bf16[512,256]{1,0:T(8,128)(2,1)S(1)}, bf16[512,256]{1,0:T(8,128)(2,1)S(1)}, u32[]{:S(2)}, u32[]{:S(2)}) collective-permute-start(bf16[512,256]{1,0:T(8,128)(2,1)S(1)} %get-tuple-element.115.attended), channel_id=1, source_target_pairs={{0,1},{1,0},{2,3},{3,2},{4,5},{5,4},{6,7},{7,6},{8,9},{9,8},{10,11... | collective-permute-start | bytes 786440 | tf_op jit(solution)/shard_map/ppermute | solution.py:344
  25.8 15.2 %collective-permute-start.6 = (bf16[128,1024]{1,0:T(8,128)(2,1)S(1)}, bf16[128,1024]{1,0:T(8,128)(2,1)S(1)}, u32[]{:S(2)}, u32[]{:S(2)}) collective-permute-start(bf16[128,1024]{1,0:T(8,128)(2,1)S(1)} %collective-permute-done.2), channel_id=1, source_target_pairs={{0,1},{1,0},{2,3},{3,2},{4,5},{5,4},{6,7},{7,6},{8,9},{9,8},{10,11... | collective-permute-start | bytes 786440 | tf_op jit(solution)/shard_map/ppermute | solution.py:344
  25.8 24.6 %copy-start.29 = (f32[1024]{0:T(1024)S(1)}, f32[1024]{0:T(1024)}, u32[]{:S(2)}) copy-start(f32[1024]{0:T(1024)} %param.19) | copy-start | bytes 12292
  25.8 22.3 %collective-permute-start.10 = (bf16[256,1024]{1,0:T(8,128)(2,1)S(1)}, bf16[256,1024]{1,0:T(8,128)(2,1)S(1)}, u32[]{:S(2)}, u32[]{:S(2)}) collective-permute-start(bf16[256,1024]{1,0:T(8,128)(2,1)S(1)} %pad_maximum_fusion.5.refs_11_.refs_5_), channel_id=1, source_target_pairs={{0,8},{4,12},{8,0},{12,4},{16,24},{20,28},{24,16},{28,20},{1,9},{5... | collective-permute-start | bytes 1572872 | tf_op jit(solution)/shard_map/ppermute | solution.py:344
  40.9 7.2 %collective-permute-start.8 = (bf16[512,256]{1,0:T(8,128)(2,1)S(1)}, bf16[512,256]{1,0:T(8,128)(2,1)S(1)}, u32[]{:S(2)}, u32[]{:S(2)}) collective-permute-start(bf16[512,256]{1,0:T(8,128)(2,1)S(1)} %collective-permute-done.4), channel_id=1, source_target_pairs={{0,1},{1,0},{2,3},{3,2},{4,5},{5,4},{6,7},{7,6},{8,9},{9,8},{10,11... | collective-permute-start | bytes 786440 | tf_op jit(solution)/shard_map/ppermute | solution.py:344
  41.3 9.1 %collective-permute-start.7 = (bf16[512,1024]{1,0:T(8,128)(2,1)S(1)}, bf16[512,1024]{1,0:T(8,128)(2,1)}, u32[]{:S(2)}, u32[]{:S(2)}) collective-permute-start(bf16[512,1024]{1,0:T(8,128)(2,1)S(1)} %pad_maximum_fusion.1.w_mine), channel_id=1, source_target_pairs={{0,4},{4,0},{8,12},{12,8},{16,20},{20,16},{24,28},{28,24},{1,5},{5... | collective-permute-start | bytes 3145736 | tf_op jit(solution)/shard_map/ppermute | solution.py:344
  41.4 14.3 %collective-permute-start.11 = (bf16[512,1024]{1,0:T(8,128)(2,1)}, bf16[512,1024]{1,0:T(8,128)(2,1)}, u32[]{:S(2)}, u32[]{:S(2)}) collective-permute-start(bf16[512,1024]{1,0:T(8,128)(2,1)} %pad_maximum_fusion.refs_7_), channel_id=1, source_target_pairs={{0,4},{4,0},{8,12},{12,8},{16,20},{20,16},{24,28},{28,24},{1,5},{5... | collective-permute-start | bytes 3145736 | tf_op jit(solution)/shard_map/ppermute | solution.py:344
  48.1 7.6 %collective-permute-start.12 = (bf16[512,1024]{1,0:T(8,128)(2,1)}, bf16[512,1024]{1,0:T(8,128)(2,1)}, u32[]{:S(2)}, u32[]{:S(2)}) collective-permute-start(bf16[512,1024]{1,0:T(8,128)(2,1)} %collective-permute-done.9.refs_8_), channel_id=1, source_target_pairs={{0,4},{4,0},{8,12},{12,8},{16,20},{20,16},{24,28},{28,24},{1,5},{5... | collective-permute-start | bytes 3145736 | tf_op jit(solution)/shard_map/ppermute | solution.py:344
  48.2 7.5 %collective-permute-start.13 = (bf16[256,1024]{1,0:T(8,128)(2,1)S(1)}, bf16[256,1024]{1,0:T(8,128)(2,1)}, u32[]{:S(2)}, u32[]{:S(2)}) collective-permute-start(bf16[256,1024]{1,0:T(8,128)(2,1)S(1)} %pad_maximum_fusion.5.refs_11_.refs_5_), channel_id=1, source_target_pairs={{0,4},{4,0},{8,12},{12,8},{16,20},{20,16},{24,28},{28,24},{1,5},{5... | collective-permute-start | bytes 1572872 | tf_op jit(solution)/shard_map/ppermute | solution.py:344
  48.8 6.9 %collective-permute-start.14 = (bf16[256,1024]{1,0:T(8,128)(2,1)S(1)}, bf16[256,1024]{1,0:T(8,128)(2,1)}, u32[]{:S(2)}, u32[]{:S(2)}) collective-permute-start(bf16[256,1024]{1,0:T(8,128)(2,1)S(1)} %collective-permute-done.10.refs_12_.refs_6_), channel_id=1, source_target_pairs={{0,4},{4,0},{8,12},{12,8},{16,20},{20,16},{24,28},{28,24},{1,5},{5... | collective-permute-start | bytes 1572872 | tf_op jit(solution)/shard_map/ppermute | solution.py:344
  69.2 8.7 %collective-permute-start.15 = (bf16[128,1024]{1,0:T(8,128)(2,1)S(1)}, bf16[128,1024]{1,0:T(8,128)(2,1)S(1)}, u32[]{:S(2)}, u32[]{:S(2)}) collective-permute-start(bf16[128,1024]{1,0:T(8,128)(2,1)S(1)} %get-tuple-element.138), channel_id=1, source_target_pairs={{0,1},{1,0},{2,3},{3,2},{4,5},{5,4},{6,7},{7,6},{8,9},{9,8},{10,11... | collective-permute-start | bytes 786440 | tf_op jit(solution)/shard_map/ppermute | solution.py:344
  77.9 5.7 %collective-permute-start.18 = (bf16[1536,1024]{1,0:T(8,128)(2,1)S(1)}, bf16[1536,1024]{1,0:T(8,128)(2,1)S(1)}, u32[]{:S(2)}, u32[]{:S(2)}) collective-permute-start(bf16[1536,1024]{1,0:T(8,128)(2,1)S(1)} %get-tuple-element.149), channel_id=1, source_target_pairs={{0,4},{4,0},{8,12},{12,8},{16,20},{20,16},{24,28},{28,24},{1,5},{5... | collective-permute-start | bytes 9437192 | tf_op jit(solution)/shard_map/ppermute | solution.py:344
  78.8 15.7 %collective-permute-start.17 = (bf16[128,1024]{1,0:T(8,128)(2,1)}, bf16[128,1024]{1,0:T(8,128)(2,1)S(1)}, u32[]{:S(2)}, u32[]{:S(2)}) collective-permute-start(bf16[128,1024]{1,0:T(8,128)(2,1)} %add_convert_fusion.6), channel_id=1, source_target_pairs={{0,2},{1,3},{2,0},{3,1},{4,6},{5,7},{6,4},{7,5},{8,10},{9,11},{10,... | collective-permute-start | bytes 786440 | tf_op jit(solution)/shard_map/ppermute | solution.py:344
  81.8 13.4 %collective-permute-start.16 = (bf16[128,1024]{1,0:T(8,128)(2,1)}, bf16[128,1024]{1,0:T(8,128)(2,1)}, u32[]{:S(2)}, u32[]{:S(2)}) collective-permute-start(bf16[128,1024]{1,0:T(8,128)(2,1)} %get-tuple-element.144), channel_id=1, source_target_pairs={{0,1},{1,0},{2,3},{3,2},{4,5},{5,4},{6,7},{7,6},{8,9},{9,8},{10,11... | collective-permute-start | bytes 786440 | tf_op jit(solution)/shard_map/ppermute | solution.py:344
  88.2 41.2 %collective-permute-start.22 = (bf16[512,1024]{1,0:T(8,128)(2,1)}, bf16[512,1024]{1,0:T(8,128)(2,1)}, u32[]{:S(2)}, u32[]{:S(2)}) collective-permute-start(bf16[512,1024]{1,0:T(8,128)(2,1)} %get-tuple-element.171), channel_id=1, source_target_pairs={{0,16},{4,20},{8,24},{12,28},{16,0},{20,4},{24,8},{28,12},{1,17},{... | collective-permute-start | bytes 3145736 | tf_op jit(solution)/shard_map/ppermute | solution.py:344
  96.4 13.8 %collective-permute-start.19 = (bf16[128,1024]{1,0:T(8,128)(2,1)S(1)}, bf16[128,1024]{1,0:T(8,128)(2,1)S(1)}, u32[]{:S(2)}, u32[]{:S(2)}) collective-permute-start(bf16[128,1024]{1,0:T(8,128)(2,1)S(1)} %get-tuple-element.159.refs_8_), channel_id=1, source_target_pairs={{0,2},{1,3},{2,0},{3,1},{4,6},{5,7},{6,4},{7,5},{8,10},{9,11},{10,... | collective-permute-start | bytes 786440 | tf_op jit(solution)/shard_map/ppermute | solution.py:344
  97.0 13.2 %collective-permute-start.20 = (bf16[128,1024]{1,0:T(8,128)(2,1)S(1)}, bf16[128,1024]{1,0:T(8,128)(2,1)S(1)}, u32[]{:S(2)}, u32[]{:S(2)}) collective-permute-start(bf16[128,1024]{1,0:T(8,128)(2,1)S(1)} %get-tuple-element.159.refs_8_), channel_id=1, source_target_pairs={{0,1},{1,0},{2,3},{3,2},{4,5},{5,4},{6,7},{7,6},{8,9},{9,8},{10,11... | collective-permute-start | bytes 786440 | tf_op jit(solution)/shard_map/ppermute | solution.py:344
  110.2 7.3 %collective-permute-start.21 = (bf16[128,1024]{1,0:T(8,128)(2,1)S(1)}, bf16[128,1024]{1,0:T(8,128)(2,1)S(1)}, u32[]{:S(2)}, u32[]{:S(2)}) collective-permute-start(bf16[128,1024]{1,0:T(8,128)(2,1)S(1)} %collective-permute-done.19.refs_10_), channel_id=1, source_target_pairs={{0,1},{1,0},{2,3},{3,2},{4,5},{5,4},{6,7},{7,6},{8,9},{9,8},{10,11... | collective-permute-start | bytes 786440 | tf_op jit(solution)/shard_map/ppermute | solution.py:344
  110.3 19.1 %collective-permute-start.23 = (bf16[256,1024]{1,0:T(8,128)(2,1)S(1)}, bf16[256,1024]{1,0:T(8,128)(2,1)S(1)}, u32[]{:S(2)}, u32[]{:S(2)}) collective-permute-start(bf16[256,1024]{1,0:T(8,128)(2,1)S(1)} %copy-done.34), channel_id=1, source_target_pairs={{0,8},{4,12},{8,0},{12,4},{16,24},{20,28},{24,16},{28,20},{1,9},{5... | collective-permute-start | bytes 1572872 | tf_op jit(solution)/shard_map/ppermute | solution.py:344
  117.5 11.9 %collective-permute-start.24 = (bf16[128,1024]{1,0:T(8,128)(2,1)}, bf16[128,1024]{1,0:T(8,128)(2,1)}, u32[]{:S(2)}, u32[]{:S(2)}) collective-permute-start(bf16[128,1024]{1,0:T(8,128)(2,1)} %get-tuple-element.173), channel_id=1, source_target_pairs={{0,1},{1,0},{2,3},{3,2},{4,5},{5,4},{6,7},{7,6},{8,9},{9,8},{10,11... | collective-permute-start | bytes 786440 | tf_op jit(solution)/shard_map/ppermute | solution.py:344
  129.5 7.3 %collective-permute-start.25 = (bf16[128,1024]{1,0:T(8,128)(2,1)}, bf16[128,1024]{1,0:T(8,128)(2,1)S(1)}, u32[]{:S(2)}, u32[]{:S(2)}) collective-permute-start(bf16[128,1024]{1,0:T(8,128)(2,1)} %get-tuple-element.177), channel_id=1, source_target_pairs={{0,1},{1,0},{2,3},{3,2},{4,5},{5,4},{6,7},{7,6},{8,9},{9,8},{10,11... | collective-permute-start | bytes 786440 | tf_op jit(solution)/shard_map/ppermute | solution.py:344
  136.8 2.6 %collective-permute-start.30 = (bf16[768,512]{1,0:T(8,128)(2,1)S(1)}, bf16[768,512]{1,0:T(8,128)(2,1)S(1)}, u32[]{:S(2)}, u32[]{:S(2)}) collective-permute-start(bf16[768,512]{1,0:T(8,128)(2,1)S(1)} %get-tuple-element.193), channel_id=1, source_target_pairs={{0,4},{4,0},{8,12},{12,8},{16,20},{20,16},{24,28},{28,24},{1,5},{5... | collective-permute-start | bytes 2359304 | tf_op jit(solution)/shard_map/ppermute | solution.py:344
  137.7 31.0 %collective-permute-start.28 = (bf16[256,1024]{1,0:T(8,128)(2,1)}, bf16[256,1024]{1,0:T(8,128)(2,1)}, u32[]{:S(2)}, u32[]{:S(2)}) collective-permute-start(bf16[256,1024]{1,0:T(8,128)(2,1)} %slice.125), channel_id=1, source_target_pairs={{0,8},{4,12},{8,0},{12,4},{16,24},{20,28},{24,16},{28,20},{1,9},{5... | collective-permute-start | bytes 1572872 | tf_op jit(solution)/shard_map/ppermute | solution.py:344
  140.6 20.1 %collective-permute-start.31 = (bf16[384,512]{1,0:T(8,128)(2,1)}, bf16[384,512]{1,0:T(8,128)(2,1)}, u32[]{:S(2)}, u32[]{:S(2)}) collective-permute-start(bf16[384,512]{1,0:T(8,128)(2,1)} %get-tuple-element.219), channel_id=1, source_target_pairs={{0,8},{4,12},{8,0},{12,4},{16,24},{20,28},{24,16},{28,20},{1,9},{5... | collective-permute-start | bytes 1179656 | tf_op jit(solution)/shard_map/ppermute | solution.py:344
  142.0 19.3 %collective-permute-start.32 = (bf16[384,512]{1,0:T(8,128)(2,1)}, bf16[384,512]{1,0:T(8,128)(2,1)}, u32[]{:S(2)}, u32[]{:S(2)}) collective-permute-start(bf16[384,512]{1,0:T(8,128)(2,1)} %get-tuple-element.220), channel_id=1, source_target_pairs={{0,16},{4,20},{8,24},{12,28},{16,0},{20,4},{24,8},{28,12},{1,17},{... | collective-permute-start | bytes 1179656 | tf_op jit(solution)/shard_map/ppermute | solution.py:344
  143.5 25.9 %collective-permute-start.27 = (bf16[256,1024]{1,0:T(8,128)(2,1)}, bf16[256,1024]{1,0:T(8,128)(2,1)S(1)}, u32[]{:S(2)}, u32[]{:S(2)}) collective-permute-start(bf16[256,1024]{1,0:T(8,128)(2,1)} %add_convert_fusion.1), channel_id=1, source_target_pairs={{0,2},{1,3},{2,0},{3,1},{4,6},{5,7},{6,4},{7,5},{8,10},{9,11},{10,... | collective-permute-start | bytes 1572872 | tf_op jit(solution)/shard_map/ppermute | solution.py:344
  145.7 24.2 %collective-permute-start.26 = (bf16[256,1024]{1,0:T(8,128)(2,1)}, bf16[256,1024]{1,0:T(8,128)(2,1)S(1)}, u32[]{:S(2)}, u32[]{:S(2)}) collective-permute-start(bf16[256,1024]{1,0:T(8,128)(2,1)} %get-tuple-element.188), channel_id=1, source_target_pairs={{0,1},{1,0},{2,3},{3,2},{4,5},{5,4},{6,7},{7,6},{8,9},{9,8},{10,11... | collective-permute-start | bytes 1572872 | tf_op jit(solution)/shard_map/ppermute | solution.py:344
  160.8 7.9 %collective-permute-start.29 = (bf16[128,1024]{1,0:T(8,128)(2,1)S(1)}, bf16[128,1024]{1,0:T(8,128)(2,1)S(1)}, u32[]{:S(2)}, u32[]{:S(2)}) collective-permute-start(bf16[128,1024]{1,0:T(8,128)(2,1)S(1)} %slice.126), channel_id=1, source_target_pairs={{0,16},{4,20},{8,24},{12,28},{16,0},{20,4},{24,8},{28,12},{1,17},{... | collective-permute-start | bytes 786440 | tf_op jit(solution)/shard_map/ppermute | solution.py:344
  170.4 25.3 %collective-permute-start.33 = (bf16[256,1024]{1,0:T(8,128)(2,1)S(1)}, bf16[256,1024]{1,0:T(8,128)(2,1)}, u32[]{:S(2)}, u32[]{:S(2)}) collective-permute-start(bf16[256,1024]{1,0:T(8,128)(2,1)S(1)} %finish.1), channel_id=1, source_target_pairs={{0,2},{1,3},{2,0},{3,1},{4,6},{5,7},{6,4},{7,5},{8,10},{9,11},{10,... | collective-permute-start | bytes 1572872 | tf_op jit(solution)/shard_map/ppermute | solution.py:344
  171.5 24.3 %collective-permute-start.34 = (bf16[256,1024]{1,0:T(8,128)(2,1)S(1)}, bf16[256,1024]{1,0:T(8,128)(2,1)S(1)}, u32[]{:S(2)}, u32[]{:S(2)}) collective-permute-start(bf16[256,1024]{1,0:T(8,128)(2,1)S(1)} %finish.1), channel_id=1, source_target_pairs={{0,1},{1,0},{2,3},{3,2},{4,5},{5,4},{6,7},{7,6},{8,9},{9,8},{10,11... | collective-permute-start | bytes 1572872 | tf_op jit(solution)/shard_map/ppermute | solution.py:344
  173.4 5.3 %collective-permute-start.39 = (f32[9,1024]{1,0:T(8,128)S(1)}, f32[9,1024]{1,0:T(8,128)S(1)}, u32[]{:S(2)}, u32[]{:S(2)}) collective-permute-start(f32[9,1024]{1,0:T(8,128)S(1)} %pad_maximum_fusion.7), channel_id=1, source_target_pairs={{0,4},{4,0},{8,12},{12,8},{16,20},{20,16},{24,28},{28,24},{1,5},{5... | collective-permute-start | bytes 110600 | tf_op jit(solution)/shard_map/ppermute | solution.py:344
  173.5 11.6 %collective-permute-start.36 = (bf16[384,512]{1,0:T(8,128)(2,1)S(1)}, bf16[384,512]{1,0:T(8,128)(2,1)S(1)}, u32[]{:S(2)}, u32[]{:S(2)}) collective-permute-start(bf16[384,512]{1,0:T(8,128)(2,1)S(1)} %get-tuple-element.215), channel_id=1, source_target_pairs={{0,16},{4,20},{8,24},{12,28},{16,0},{20,4},{24,8},{28,12},{1,17},{... | collective-permute-start | bytes 1179656 | tf_op jit(solution)/shard_map/ppermute | solution.py:344
  175.1 11.9 %collective-permute-start.37 = (bf16[384,512]{1,0:T(8,128)(2,1)S(1)}, bf16[384,512]{1,0:T(8,128)(2,1)S(1)}, u32[]{:S(2)}, u32[]{:S(2)}) collective-permute-start(bf16[384,512]{1,0:T(8,128)(2,1)S(1)} %get-tuple-element.216), channel_id=1, source_target_pairs={{0,8},{4,12},{8,0},{12,4},{16,24},{20,28},{24,16},{28,20},{1,9},{5... | collective-permute-start | bytes 1179656 | tf_op jit(solution)/shard_map/ppermute | solution.py:344
  178.8 8.9 %collective-permute-start.40 = (f32[9,1024]{1,0:T(8,128)S(1)}, f32[9,1024]{1,0:T(8,128)S(1)}, u32[]{:S(2)}, u32[]{:S(2)}) collective-permute-start(f32[9,1024]{1,0:T(8,128)S(1)} %add.81), channel_id=1, source_target_pairs={{0,8},{4,12},{8,0},{12,4},{16,24},{20,28},{24,16},{28,20},{1,9},{5... | collective-permute-start | bytes 110600 | tf_op jit(solution)/shard_map/ppermute | solution.py:344
  187.3 11.6 %collective-permute-start.38 = (bf16[768,512]{1,0:T(8,128)(2,1)S(1)}, bf16[768,512]{1,0:T(8,128)(2,1)S(1)}, u32[]{:S(2)}, u32[]{:S(2)}) collective-permute-start(bf16[768,512]{1,0:T(8,128)(2,1)S(1)} %pad_maximum_fusion.4), channel_id=1, source_target_pairs={{0,4},{4,0},{8,12},{12,8},{16,20},{20,16},{24,28},{28,24},{1,5},{5... | collective-permute-start | bytes 2359304 | tf_op jit(solution)/shard_map/ppermute | solution.py:344
  187.7 4.4 %collective-permute-start.41 = (f32[9,1024]{1,0:T(8,128)S(1)}, f32[9,1024]{1,0:T(8,128)S(1)}, u32[]{:S(2)}, u32[]{:S(2)}) collective-permute-start(f32[9,1024]{1,0:T(8,128)S(1)} %add.82), channel_id=1, source_target_pairs={{0,16},{4,20},{8,24},{12,28},{16,0},{20,4},{24,8},{28,12},{1,17},{... | collective-permute-start | bytes 110600 | tf_op jit(solution)/shard_map/ppermute | solution.py:344
  195.8 14.2 %collective-permute-start.35 = (bf16[256,1024]{1,0:T(8,128)(2,1)}, bf16[256,1024]{1,0:T(8,128)(2,1)}, u32[]{:S(2)}, u32[]{:S(2)}) collective-permute-start(bf16[256,1024]{1,0:T(8,128)(2,1)} %collective-permute-done.33), channel_id=1, source_target_pairs={{0,1},{1,0},{2,3},{3,2},{4,5},{5,4},{6,7},{7,6},{8,9},{9,8},{10,11... | collective-permute-start | bytes 1572872 | tf_op jit(solution)/shard_map/ppermute | solution.py:344
  200.8 9.8 %collective-permute-start.42 = (f32[10,1024]{1,0:T(8,128)S(1)}, f32[10,1024]{1,0:T(8,128)S(1)}, u32[]{:S(2)}, u32[]{:S(2)}) collective-permute-start(f32[10,1024]{1,0:T(8,128)S(1)} %pad_maximum_fusion.8), channel_id=1, source_target_pairs={{0,1},{1,0},{2,3},{3,2},{4,5},{5,4},{6,7},{7,6},{8,9},{9,8},{10,11... | collective-permute-start | bytes 122888 | tf_op jit(solution)/shard_map/ppermute | solution.py:344
  210.6 5.7 %collective-permute-start.43 = (f32[10,1024]{1,0:T(8,128)S(1)}, f32[10,1024]{1,0:T(8,128)S(1)}, u32[]{:S(2)}, u32[]{:S(2)}) collective-permute-start(f32[10,1024]{1,0:T(8,128)S(1)} %fusion.3), channel_id=1, source_target_pairs={{0,2},{1,3},{2,0},{3,1},{4,6},{5,7},{6,4},{7,5},{8,10},{9,11},{10,... | collective-permute-start | bytes 122888 | tf_op jit(solution)/shard_map/ppermute | solution.py:344
  (50 other events, 408.6 us)
